TPU v7x, 32 devices: a whole 2x2x4 slice. The times are simulated.
32 devices in a mesh: groups: 2 (over x), tm: 8 (over z, y), block: 2 (over core).
Axes of the slice: x: 2, y: 2, z: 4, core: 2. Of those that a mesh axis runs over, the one named last changes fastest.
Arguments:
- scaled_residual_maps: bfloat16 [32, 128, 16, 512], P(('groups', 'tm'), 'block'), parts along dimension 0, may hold values from -1.5 to 1.5
- measurement_stencil: bfloat16 [16, 7, 7], replicated, may hold values from -0.21875 to 0.21875
- observed_partition: int32 [32, 128], P(('groups', 'tm'), 'block'), parts along dimension 0, may hold values from 0 to 1
- active_probe_total: int32 [32, 2], P(('groups', 'tm'), 'block'), parts along dimension 0, may hold values from 1 to 64, as said below
- filtering_operator: bfloat16 [32, 2, 512, 512], P(('groups', 'tm'), 'block'), parts along dimension 0
- updated_covariance: bfloat16 [32, 2, 512, 512], P(('groups', 'tm'), 'block'), parts along dimension 0
- backward_factor: bfloat16 [32, 2, 512, 512], P(('groups', 'tm'), 'block'), parts along dimension 0
- propagator: bfloat16 [2, 512, 512], P('block'), may hold values from -0.25 to 0.25
- initial_mean: float32 [4, 512], P(('groups', 'block')), parts along dimension 0, may hold values from -6 to 6
Outputs:
- updated_means: float32 [32, 2, 512], P(('groups', 'tm'), 'block'), parts along dimension 0
- smoothed: float32 [32, 2, 512], P(('groups', 'tm'), 'block'), parts along dimension 0
There are 2 independent parts, one for each index of `groups`. A program takes and returns all parts, laid end to end along the dimension named above; an argument that names none is the same for every part. Nothing has to cross between parts.
Inputs may be any that keep to these rules, and one draw needn't show every extreme that they name: active_probe_total[t, k] is the number of leading slots of index k of block at step t that carry a sensor; some entry equals 64.
All inputs are finite; a program needn't handle non-finite values.
Results may differ from a plain program's by a relative error of at most 0.0003.
Values sent between devices are 32-bit elements; how exact they have to be, the bound alone decides.
No kernel may reach another device: no remote copies, remote signals or barrier semaphores. Data moves between devices by JAX's collectives and lax.ppermute only.
A program may use at most 192 MiB of HBM per device.

v0:
```python
import jax
import jax.numpy as jnp
from jax import lax
from jax.sharding import PartitionSpec as P

GH = 16


EXACT_ARITHMETIC = lax.Precision.HIGHEST


def entering(array, axis, combine, identity, reverse):
    count, here = (lax.axis_size(axis), lax.axis_index(axis))
    everything = jax.tree.map(lambda part: lax.all_gather(part, axis), array)
    start = jax.tree.map(
        lambda part, zero: jnp.broadcast_to(jnp.asarray(zero, part.dtype), part.shape),
        array,
        identity,
    )

    def hop(k, before):
        at = count - 1 - k if reverse else k
        reached = at > here if reverse else at < here
        new = combine(before, jax.tree.map(lambda part: part[at], everything))
        return jax.tree.map(lambda a, b: jnp.where(reached, a, b), new, before)

    return lax.fori_loop(0, count, hop, start)


def apply_matrix(matrix, vector):
    return jnp.einsum("bij,bj->bi", matrix.astype(jnp.float32), vector, precision=EXACT_ARITHMETIC)


def compose(earlier, later):
    product = jnp.einsum("bij,bjk->bik", later[0], earlier[0], precision=EXACT_ARITHMETIC)
    offset = jnp.einsum("bij,bj->bi", later[0], earlier[1], precision=EXACT_ARITHMETIC) + later[1]
    return (product, offset)


def run_filter(start, filtering_operator, inputs):
    state = start
    states = []
    for step in range(inputs.shape[0]):
        state = apply_matrix(filtering_operator[step], state) + inputs[step]
        states.append(state)
    return jnp.stack(states)


def run_smoother(incoming, mats, vecs):
    state = incoming
    states = []
    for step in reversed(range(vecs.shape[0])):
        state = apply_matrix(mats[step], state) + vecs[step]
        states.append(state)
    return jnp.stack(states[::-1])


def sensor_info(scaled_residual_maps, measurement_stencil, observed_partition, active_probe_total):
    steps, slots, channels, cells = scaled_residual_maps.shape
    grid = scaled_residual_maps.reshape(steps * slots, channels, GH, cells // GH)
    flipped = measurement_stencil[:, ::-1, ::-1][None]
    adjoint = lax.conv_general_dilated(
        grid,
        flipped,
        (1, 1),
        "SAME",
        dimension_numbers=("NCHW", "OIHW", "NCHW"),
        preferred_element_type=jnp.float32,
    )
    adjoint = adjoint.reshape(steps, slots, cells)
    blocks = lax.axis_size("block")
    alive = lax.broadcasted_iota(jnp.int32, (steps, slots), 1) < active_probe_total
    owners = lax.broadcasted_iota(jnp.int32, (steps, slots, blocks), 2)
    weight = jnp.where(
        (observed_partition[:, :, None] == owners) & alive[:, :, None], 1.0, 0.0
    ).astype(jnp.float32)
    partial_value = jnp.einsum("tsn,tsc->tnc", weight, adjoint, precision=EXACT_ARITHMETIC)
    return lax.psum_scatter(partial_value, "block", scatter_dimension=1, tiled=True)


def local(
    scaled_residual_maps,
    measurement_stencil,
    observed_partition,
    active_probe_total,
    filtering_operator,
    updated_covariance,
    backward_factor,
    propagator,
    initial_mean,
):
    info = sensor_info(
        scaled_residual_maps, measurement_stencil, observed_partition, active_probe_total
    )
    inputs = jnp.einsum(
        "gupl,gul->gup", updated_covariance.astype(jnp.float32), info, precision=EXACT_ARITHMETIC
    )
    steps = inputs.shape[0]
    place = lax.axis_index("tm")
    length = lax.axis_size("tm")
    element = (filtering_operator[0].astype(jnp.float32), inputs[0])
    for step in range(1, steps):
        element = compose(element, (filtering_operator[step].astype(jnp.float32), inputs[step]))
    identity = (
        jnp.broadcast_to(jnp.eye(element[0].shape[-1], dtype=jnp.float32), element[0].shape),
        jnp.zeros_like(element[1]),
    )
    before = entering(element, "tm", compose, identity, False)
    start = apply_matrix(before[0], initial_mean) + before[1]
    updated_means = run_filter(start, filtering_operator, inputs)
    propagate_mean = jnp.einsum(
        "pmz,ypz->ypm", propagator.astype(jnp.float32), updated_means, precision=EXACT_ARITHMETIC
    )
    displacements = updated_means - jnp.einsum(
        "gupl,gul->gup",
        backward_factor.astype(jnp.float32),
        propagate_mean,
        precision=EXACT_ARITHMETIC,
    )
    final = place == length - 1
    mats = backward_factor.astype(jnp.float32)
    last_mat = jnp.where(final, jnp.zeros_like(mats[-1]), mats[-1])
    last_vec = jnp.where(final, updated_means[-1], displacements[-1])
    mats = jnp.concatenate([mats[:-1], last_mat[None]], axis=0)
    vecs = jnp.concatenate([displacements[:-1], last_vec[None]], axis=0)
    element = (mats[-1], vecs[-1])
    for step in reversed(range(steps - 1)):
        element = compose(element, (mats[step], vecs[step]))
    identity = (
        jnp.broadcast_to(jnp.eye(element[0].shape[-1], dtype=jnp.float32), element[0].shape),
        jnp.zeros_like(element[1]),
    )
    after = entering(element, "tm", compose, identity, True)
    smoothed = run_smoother(after[1], mats, vecs)
    return (updated_means, smoothed)


def solution(mesh):
    placed = (
        P(("groups", "tm"), "block", None, None),
        P(),
        P(("groups", "tm"), "block"),
        P(("groups", "tm"), "block"),
        P(("groups", "tm"), "block", None, None),
        P(("groups", "tm"), "block", None, None),
        P(("groups", "tm"), "block", None, None),
        P("block", None, None),
        P(("groups", "block"), None),
    )
    return jax.shard_map(
        local,
        mesh=mesh,
        in_specs=placed,
        out_specs=(P(("groups", "tm"), "block", None), P(("groups", "tm"), "block", None)),
        check_vma=False,
    )
```

profile of v0, /device:TPU:0, one launch (start us, length us, event | category | flops | bytes accessed | tf_op | source)
XLA Modules:
  0.0 299.7 jit_solution(10974437785834543901)
XLA Ops:
  7.2 2.7 fusion.35
  10.0 3.7 %convolution_bitcast_fusion.1 = f32[512,512]{0,1:T(8,128)} fusion(pred[]{:T(512)S(6)} %eq.24, bf16[2,1,512,512]{3,2,1,0:T(8,128)(2,1)} %param.19), kind=kOutput, calls=%fused_computation.24 | convolution fusion | flops 1611137024 | bytes 2097153 | tf_op jit(solution)/shard_map/bij,bjk->bik/dot_general | solution.py:35
  13.8 8.0 %copy.33 = bf16[2,64,16,512]{1,0,2,3:T(2,128)(2,1)} copy(bf16[2,64,16,512]{3,2,1,0:T(8,128)(2,1)} %param.13) | data formatting | bytes 4194304 | tf_op jit(solution)/shard_map/reshape | solution.py:60
  21.8 7.8 %reshape.268 = bf16[128,16,16,32]{0,1,3,2:T(8,128)(2,1)} reshape(bf16[2,64,16,512]{1,0,2,3:T(2,128)(2,1)} %copy.33) | data formatting | bytes 4194304 | tf_op jit(solution)/shard_map/reshape | solution.py:60
  29.7 16.1 %convolution_reduce_fusion = f32[128,16,32]{0,2,1:T(8,128)S(1)} fusion(bf16[128,16,16,32]{0,1,3,2:T(8,128)(2,1)} %reshape.268, bf16[1,16,7,7]{1,3,2,0:T(8,128)(2,1)S(1)} %bitcast.177), kind=kOutput, calls=%fused_computation.25 | convolution fusion | flops 86835200 | bytes 2360864 | tf_op jit(solution)/shard_map/conv_general_dilated | solution.py:62
  47.3 2.6 all-reduce
  52.0 28.2 %all-gather.4 = f32[8,1,512]{2,1,0:T(1,128)S(1)} all-gather(f32[1,1,512]{2,1,0:T(1,128)S(1)} %fusion.17), channel_id=3, replica_groups=mesh['groups'=2,'tm'=8,'block'=2] {'tm'}, dimensions={0}, use_global_device_ids=true | all-gather | bytes 18432 | tf_op jit(solution)/shard_map/all_gather | solution.py:14
  80.3 57.7 %all-gather.9.cloned.1.call-done = f32[4096,512]{1,0:T(8,128)} async-done(((f32[512,512]{1,0:T(8,128)}), f32[4096,512]{1,0:T(8,128)}) %all-gather.9.cloned.1.call-update) | async-done | bytes 8388624 | tf_op jit(solution)/shard_map/all_gather | solution.py:14
  138.0 43.4 %while.32 = (s32[]{:T(128)}, f32[1,512,512]{2,1,0:T(8,128)S(1)}, f32[1,512]{1,0:T(1,128)S(1)}, s32[]{:T(128)}, f32[8,1,512,512]{3,2,1,0:T(8,128)}, /*index=5*/f32[8,1,512]{2,1,0:T(1,128)S(1)}, s32[]{:T(128)}, s32[]{:T(128)}) while((s32[]{:T(128)}, f32[1,512,512]{2,1,0:T(8,128)S(1)}, f32[1,512]{1,0:T(1,128)S(1)}, s32[]{:T(128)}, ...), condition=%wide.region_2.3_spmd.clone, body=%wide.region_1.2_spmd.clone.sunk | while | flops 1614022656 | bytes 7360639 | solution.py:27
  138.1 3.1 %fusion.92 = f32[1,512,512]{2,1,0:T(8,128)S(1)} fusion(f32[1,512,512]{2,1,0:T(8,128)S(1)} %copy.68, f32[8,1,512,512]{3,2,1,0:T(8,128)} %get-tuple-element.429, s32[]{:T(128)S(6)} %copy.55, pred[]{:T(512)S(6)} %lt.60), kind=kOutput, calls=%fused_computation.1.clone.1 | convolution fusion | flops 1610874880 | bytes 4194309 | tf_op jit(solution)/shard_map/while/body/eval_jaxpr/bij,bjk->bik/dot_general | solution.py:35
  141.2 2.2 fusion.93
  143.5 3.1 %fusion.92 = f32[1,512,512]{2,1,0:T(8,128)S(1)} fusion(f32[1,512,512]{2,1,0:T(8,128)S(1)} %copy.68, f32[8,1,512,512]{3,2,1,0:T(8,128)} %get-tuple-element.429, s32[]{:T(128)S(6)} %copy.55, pred[]{:T(512)S(6)} %lt.60), kind=kOutput, calls=%fused_computation.1.clone.1 | convolution fusion | flops 1610874880 | bytes 4194309 | tf_op jit(solution)/shard_map/while/body/eval_jaxpr/bij,bjk->bik/dot_general | solution.py:35
  146.6 2.3 fusion.93
  149.0 3.1 %fusion.92 = f32[1,512,512]{2,1,0:T(8,128)S(1)} fusion(f32[1,512,512]{2,1,0:T(8,128)S(1)} %copy.68, f32[8,1,512,512]{3,2,1,0:T(8,128)} %get-tuple-element.429, s32[]{:T(128)S(6)} %copy.55, pred[]{:T(512)S(6)} %lt.60), kind=kOutput, calls=%fused_computation.1.clone.1 | convolution fusion | flops 1610874880 | bytes 4194309 | tf_op jit(solution)/shard_map/while/body/eval_jaxpr/bij,bjk->bik/dot_general | solution.py:35
  152.1 2.2 fusion.93
  154.4 3.1 %fusion.92 = f32[1,512,512]{2,1,0:T(8,128)S(1)} fusion(f32[1,512,512]{2,1,0:T(8,128)S(1)} %copy.68, f32[8,1,512,512]{3,2,1,0:T(8,128)} %get-tuple-element.429, s32[]{:T(128)S(6)} %copy.55, pred[]{:T(512)S(6)} %lt.60), kind=kOutput, calls=%fused_computation.1.clone.1 | convolution fusion | flops 1610874880 | bytes 4194309 | tf_op jit(solution)/shard_map/while/body/eval_jaxpr/bij,bjk->bik/dot_general | solution.py:35
  157.5 2.2 fusion.93
  159.8 3.1 %fusion.92 = f32[1,512,512]{2,1,0:T(8,128)S(1)} fusion(f32[1,512,512]{2,1,0:T(8,128)S(1)} %copy.68, f32[8,1,512,512]{3,2,1,0:T(8,128)} %get-tuple-element.429, s32[]{:T(128)S(6)} %copy.55, pred[]{:T(512)S(6)} %lt.60), kind=kOutput, calls=%fused_computation.1.clone.1 | convolution fusion | flops 1610874880 | bytes 4194309 | tf_op jit(solution)/shard_map/while/body/eval_jaxpr/bij,bjk->bik/dot_general | solution.py:35
  162.9 2.2 fusion.93
  165.3 3.1 %fusion.92 = f32[1,512,512]{2,1,0:T(8,128)S(1)} fusion(f32[1,512,512]{2,1,0:T(8,128)S(1)} %copy.68, f32[8,1,512,512]{3,2,1,0:T(8,128)} %get-tuple-element.429, s32[]{:T(128)S(6)} %copy.55, pred[]{:T(512)S(6)} %lt.60), kind=kOutput, calls=%fused_computation.1.clone.1 | convolution fusion | flops 1610874880 | bytes 4194309 | tf_op jit(solution)/shard_map/while/body/eval_jaxpr/bij,bjk->bik/dot_general | solution.py:35
  168.3 2.2 fusion.93
  170.7 3.1 %fusion.92 = f32[1,512,512]{2,1,0:T(8,128)S(1)} fusion(f32[1,512,512]{2,1,0:T(8,128)S(1)} %copy.68, f32[8,1,512,512]{3,2,1,0:T(8,128)} %get-tuple-element.429, s32[]{:T(128)S(6)} %copy.55, pred[]{:T(512)S(6)} %lt.60), kind=kOutput, calls=%fused_computation.1.clone.1 | convolution fusion | flops 1610874880 | bytes 4194309 | tf_op jit(solution)/shard_map/while/body/eval_jaxpr/bij,bjk->bik/dot_general | solution.py:35
  173.8 2.2 fusion.93
  176.1 3.1 %fusion.92 = f32[1,512,512]{2,1,0:T(8,128)S(1)} fusion(f32[1,512,512]{2,1,0:T(8,128)S(1)} %copy.68, f32[8,1,512,512]{3,2,1,0:T(8,128)} %get-tuple-element.429, s32[]{:T(128)S(6)} %copy.55, pred[]{:T(512)S(6)} %lt.60), kind=kOutput, calls=%fused_computation.1.clone.1 | convolution fusion | flops 1610874880 | bytes 4194309 | tf_op jit(solution)/shard_map/while/body/eval_jaxpr/bij,bjk->bik/dot_general | solution.py:35
  179.2 2.2 fusion.93
  191.0 26.6 %all-gather.5 = f32[8,1,512]{2,1,0:T(1,128)S(1)} all-gather(f32[1,1,512]{2,1,0:T(1,128)S(1)} %bitcast.182), channel_id=5, replica_groups=mesh['groups'=2,'tm'=8,'block'=2] {'tm'}, dimensions={0}, use_global_device_ids=true | all-gather | bytes 18432 | tf_op jit(solution)/shard_map/all_gather | solution.py:14
  217.6 46.0 %all-gather.11.cloned.1.call-done = f32[4096,512]{0,1:T(8,128)} async-done(((f32[512,512]{0,1:T(8,128)}), f32[4096,512]{0,1:T(8,128)}) %all-gather.11.cloned.1.call-update) | async-done | bytes 8388624 | tf_op jit(solution)/shard_map/all_gather | solution.py:14
  263.6 9.0 %copy.34 = f32[4096,512]{1,0:T(8,128)} copy(f32[4096,512]{0,1:T(8,128)} %all-gather.11.cloned.1.call-done) | data formatting | bytes 16777216
  272.6 18.0 %while.33 = (s32[]{:T(128)}, f32[1,512]{1,0:T(1,128)S(1)}, s32[]{:T(128)}, f32[8,1,512,512]{3,2,1,0:T(8,128)}, f32[8,1,512]{2,1,0:T(1,128)S(1)}, /*index=5*/s32[]{:T(128)}, s32[]{:T(128)}, s32[]{:T(128)}, s32[]{:T(128)}) while((s32[]{:T(128)}, f32[1,512]{1,0:T(1,128)S(1)}, s32[]{:T(128)}, f32[8,1,512,512]{3,2,1,0:T(8,128)}, ...), condition=%wide.region_4.5_spmd.clone, body=%wide.region_3.4_spmd.clone.sunk | while | flops 3147784 | bytes 1069232 | solution.py:27
  274.9 2.2 fusion.96
  277.2 2.2 fusion.96
  288.4 2.2 fusion.96
  (112 shorter events, 27.5 us)
Async XLA Ops:
  7.2 43.4 %copy-start = (bf16[2,1,512,512]{3,2,1,0:T(8,128)(2,1)S(1)}, bf16[2,1,512,512]{3,2,1,0:T(8,128)(2,1)}, u32[]{:S(2)}) copy-start(bf16[2,1,512,512]{3,2,1,0:T(8,128)(2,1)} %param.18) | copy-start | bytes 3145732
  7.2 130.8 %all-gather.9.cloned.1.call-start = ((), (), s32[]{:S(2)}) async-start(), calls=%async_computation | async-start | bytes 9437184 | tf_op jit(solution)/shard_map/all_gather | solution.py:14
  9.9 19.7 %copy-start.4 = (bf16[16,7,7]{0,2,1:T(8,128)(2,1)S(1)}, bf16[16,7,7]{0,2,1:T(8,128)(2,1)}, u32[]{:S(2)}) copy-start(bf16[16,7,7]{0,2,1:T(8,128)(2,1)} %param.14) | copy-start | bytes 4708
  10.0 253.7 %all-gather.11.cloned.1.call-start = ((), (), s32[]{:S(2)}) async-start(), calls=%async_computation.1 | async-start | bytes 9437184 | tf_op jit(solution)/shard_map/all_gather | solution.py:14
  29.6 16.4 %copy-start.7 = (s32[2,1]{0,1:T(1,128)S(1)}, s32[2,1]{0,1:T(1,128)}, u32[]{:S(2)}) copy-start(s32[2,1]{0,1:T(1,128)} %param.16) | copy-start | bytes 28
  29.6 16.5 %copy-start.6 = (s32[2,64]{1,0:T(2,128)S(1)}, s32[2,64]{1,0:T(2,128)}, u32[]{:S(2)}) copy-start(s32[2,64]{1,0:T(2,128)} %param.15) | copy-start | bytes 1540
  29.7 17.0 %copy-start.8 = (u32[32]{0:T(128)S(1)}, u32[32]{0:T(128)}, u32[]{:S(2)}) copy-start(u32[32]{0:T(128)} %constant.90) | copy-start | bytes 388
  29.7 21.8 %copy-start.1 = (bf16[2,1,512,512]{3,2,1,0:T(8,128)(2,1)S(1)}, bf16[2,1,512,512]{3,2,1,0:T(8,128)(2,1)}, u32[]{:S(2)}) copy-start(bf16[2,1,512,512]{3,2,1,0:T(8,128)(2,1)} %param.17) | copy-start | bytes 3145732
  138.0 43.4 %copy-start.5 = (f32[1,512]{1,0:T(1,128)S(1)}, f32[1,512]{1,0:T(1,128)}, u32[]{:S(2)}) copy-start(f32[1,512]{1,0:T(1,128)} %param.21) | copy-start | bytes 6148
  185.6 87.1 %copy-start.3 = (f32[2,1,512]{2,1,0:T(1,128)}, f32[2,1,512]{2,1,0:T(1,128)S(1)}, u32[]{:S(2)}) copy-start(f32[2,1,512]{2,1,0:T(1,128)S(1)} %pad_maximum_fusion) | copy-start | bytes 12292
  217.6 73.1 %copy-start.2 = (bf16[2,1,512,512]{3,2,1,0:T(8,128)(2,1)S(1)}, bf16[2,1,512,512]{3,2,1,0:T(8,128)(2,1)}, u32[]{:S(2)}) copy-start(bf16[2,1,512,512]{3,2,1,0:T(8,128)(2,1)} %param.19) | copy-start | bytes 3145732
Sparse Core Ops, SparseCore 0:
  10.1 127.8 all-gather.8
  140.2 123.3 all-gather.10
where the time goes:
time: 302 us; the launch traced here: 300 us
  waiting for transfers between devices  104 us (34%)
  matrix products  95.3 us (32%)
  blocking collectives  57.4 us (19%)
  local copies, waits for them, and re-layouts  27.1 us (9%)
  between operations  14.2 us (5%)
    all_gather x2, waiting for transfers between devices, entering(): everything = jax.tree.map(lambda part: lax.all_gather(part, axis), array)  104 us
    all_gather x2, blocking collectives, entering(): everything = jax.tree.map(lambda part: lax.all_gather(part, axis), array)  54.7 us
    dot_general x18, matrix products, compose(): jnp.einsum('bij,bj->bi', later[0], earlier[1], precision=EXACT_ARITHMETIC)  37.6 us
    dot_general x10, matrix products, compose(): jnp.einsum('bij,bjk->bik', later[0], earlier[0], precision=EXACT_ARITHMETIC)  31 us
    conv_general_dilated x1, matrix products, sensor_info(): lax.conv_general_dilated(grid, flipped, (1, 1), 'SAME', dimension_numbers...  16.1 us
    reshape x2, local copies, waits for them, and re-layouts, sensor_info(): scaled_residual_maps.reshape(steps * slots, channels, GH, cells // GH)  15.8 us
    unnamed x20, local copies, waits for them, and re-layouts  9.68 us
  transfers between devices with their start and end apart: 2, of which 2 were waited for; matrix products, arithmetic and copies ran while one was open for 31% of the time, Pallas kernels for 0%

commit v1 on v0

v1 whole, which is shorter than its diff:
```python
import functools

import jax
import jax.numpy as jnp
from jax import lax
from jax.experimental import pallas as pl
from jax.experimental.pallas import tpu as pltpu
from jax.sharding import PartitionSpec as P

GH = 16
VMEM = pl.BlockSpec(memory_space=pltpu.VMEM)
PARAMS = pltpu.CompilerParams(vmem_limit_bytes=16 * 2**20)


def pieces(row, rows=8, count=3):
    at = lax.broadcasted_iota(jnp.int32, (rows, row.shape[1]), 0)
    block = jnp.zeros((rows, row.shape[1]), jnp.float32)
    rest = row
    for i in range(count):
        piece = rest.astype(jnp.bfloat16).astype(jnp.float32)
        block = jnp.where(at == i, piece, block)
        rest = rest - piece
    return block.astype(jnp.bfloat16)


def times(matrix, row):
    product = lax.dot_general(
        pieces(row), matrix, (((1,), (1,)), ((), ())), preferred_element_type=jnp.float32
    )
    return jnp.sum(product, axis=0, keepdims=True)


def info_kernel(maps_hbm, stencil_ref, observed_ref, active_ref, mine_ref, theirs_ref, maps, taps, sems):
    steps, rows, cells = maps.shape
    slots = observed_ref.shape[1]
    channels, side, _ = stencil_ref.shape
    half = side // 2
    copies = []
    for t in range(steps):
        copies.append(pltpu.make_async_copy(maps_hbm.at[t], maps.at[t], sems.at[t]))
        copies[-1].start()

    repeat = jnp.where(
        lax.broadcasted_iota(jnp.int32, (channels, rows), 1) % channels
        == lax.broadcasted_iota(jnp.int32, (channels, rows), 0),
        1.0,
        0.0,
    ).astype(jnp.bfloat16)
    taps[...] = jnp.zeros_like(taps)
    for p in range(side):
        taps[p * 8 : p * 8 + side, :] = lax.dot_general(
            stencil_ref[:, p, :], repeat, (((0,), (0,)), ((), ())), preferred_element_type=jnp.float32
        )
    spread = jnp.where(
        lax.broadcasted_iota(jnp.int32, (slots, rows), 1) // channels
        == lax.broadcasted_iota(jnp.int32, (slots, rows), 0),
        1.0,
        0.0,
    ).astype(jnp.bfloat16)

    cell = lax.broadcasted_iota(jnp.int32, (8, cells), 1)
    width = cells // GH
    down = cell // width
    across = cell % width
    tap = lax.broadcasted_iota(jnp.int32, (8, cells), 0)
    column = across - tap + half
    column_inside = (column >= 0) & (column < width) & (tap < side)
    me = lax.axis_index("block")
    for t in range(steps):
        owner = lax.broadcasted_iota(jnp.int32, (8, slots), 0)
        slot = lax.broadcasted_iota(jnp.int32, (8, slots), 1)
        live = (observed_ref[t : t + 1, :] == owner) & (slot < active_ref[t, 0])
        weight = jnp.dot(
            jnp.where(live, 1.0, 0.0).astype(jnp.bfloat16), spread, preferred_element_type=jnp.float32
        )
        left = jnp.concatenate([taps[...] * weight[b : b + 1, :] for b in range(2)], axis=0)
        copies[t].wait()
        shifted = jnp.dot(left.astype(jnp.bfloat16), maps[t], preferred_element_type=jnp.float32)
        found = []
        for b in range(2):
            total = jnp.zeros((8, cells), jnp.float32)
            for p in range(side):
                at = (b * side + p) * 8
                part = pltpu.roll(shifted[at : at + 8, :], ((p - half) * width) % cells, 1)
                row = down - p + half
                total = total + jnp.where((row >= 0) & (row < GH), part, 0.0)
            sides = jnp.zeros((8, cells), jnp.float32)
            for q in range(side):
                part = pltpu.roll(total, (q - half) % cells, 1)
                sides = jnp.where(column_inside & (tap == q), part, sides)
            found.append(jnp.sum(sides, axis=0, keepdims=True))
        mine_ref[t : t + 1, :] = jnp.where(me == 0, found[0], found[1])
        theirs_ref[t : t + 1, :] = jnp.where(me == 0, found[1], found[0])


def sensor_info(scaled_residual_maps, measurement_stencil, observed_partition, active_probe_total):
    steps, slots, channels, cells = scaled_residual_maps.shape
    side = measurement_stencil.shape[1]
    mine, theirs = pl.pallas_call(
        info_kernel,
        out_shape=[jax.ShapeDtypeStruct((steps, cells), jnp.float32)] * 2,
        in_specs=[
            pl.BlockSpec(memory_space=pl.ANY),
            VMEM,
            VMEM,
            pl.BlockSpec(memory_space=pltpu.SMEM),
        ],
        out_specs=[VMEM] * 2,
        scratch_shapes=[
            pltpu.VMEM((steps, slots * channels, cells), jnp.bfloat16),
            pltpu.VMEM((side * 8, slots * channels), jnp.float32),
            pltpu.SemaphoreType.DMA((steps,)),
        ],
        compiler_params=PARAMS,
        name="sensor_info",
    )(
        scaled_residual_maps.reshape(steps, slots * channels, cells),
        measurement_stencil,
        observed_partition,
        active_probe_total,
    )
    return mine, lax.ppermute(theirs, "block", [(0, 1), (1, 0)])


def inputs_kernel(mine_ref, other_ref, covariance_ref, operator_ref, start_ref, inputs_ref, states_ref, send_ref):
    state = start_ref[...]
    for t in range(mine_ref.shape[0]):
        drive = times(covariance_ref[t], mine_ref[t : t + 1, :] + other_ref[t : t + 1, :])
        inputs_ref[t : t + 1, :] = drive
        state = times(operator_ref[t], state) + drive
        states_ref[t : t + 1, :] = state
    send_ref[...] = state


def hop_kernel(turn, reverse, came_ref, matrices_ref, offsets_ref, kept_ref, states_ref, send_ref):
    here = lax.axis_index("tm") == turn

    @pl.when(here)
    def _():
        state = came_ref[...]
        order = range(matrices_ref.shape[0])
        for t in reversed(order) if reverse else order:
            state = times(matrices_ref[t], state) + offsets_ref[t : t + 1, :]
            states_ref[t : t + 1, :] = state
        send_ref[...] = state

    @pl.when(jnp.logical_not(here))
    def _():
        states_ref[...] = kept_ref[...]
        send_ref[...] = came_ref[...]


def turn_kernel(last, means_ref, gain_ref, propagator_ref, offsets_ref, states_ref, send_ref):
    steps = means_ref.shape[0]
    for t in range(steps):
        moved = times(gain_ref[t], times(propagator_ref[...], means_ref[t : t + 1, :]))
        offsets_ref[t : t + 1, :] = means_ref[t : t + 1, :] - moved
    state = means_ref[steps - 1 : steps, :]
    states_ref[steps - 1 : steps, :] = state
    for t in reversed(range(steps - 1)):
        state = times(gain_ref[t], state) + offsets_ref[t : t + 1, :]
        states_ref[t : t + 1, :] = state
    send_ref[...] = state


def call(kernel, name, outs, *args):
    return pl.pallas_call(
        kernel,
        out_shape=[jax.ShapeDtypeStruct(shape, jnp.float32) for shape in outs],
        in_specs=[VMEM] * len(args),
        out_specs=[VMEM] * len(outs),
        compiler_params=PARAMS,
        name=name,
    )(*args)


def hop(row, source, target, places):
    pairs = []
    for core in range(2):
        pairs += [(source * 2 + core, target * 2 + core), (target * 2 + core, source * 2 + core)]
    for place in range(places):
        if place not in (source, target):
            pairs += [(place * 2, place * 2 + 1), (place * 2 + 1, place * 2)]
    return lax.ppermute(row, ("tm", "block"), pairs)


def local(
    scaled_residual_maps,
    measurement_stencil,
    observed_partition,
    active_probe_total,
    filtering_operator,
    updated_covariance,
    backward_factor,
    propagator,
    initial_mean,
):
    steps, size = filtering_operator.shape[0], filtering_operator.shape[-1]
    places = lax.axis_size("tm")
    many, one = (steps, size), (1, size)
    operator = filtering_operator.reshape(steps, size, size)
    covariance = updated_covariance.reshape(steps, size, size)
    gain = backward_factor.reshape(steps, size, size)
    mine, other = sensor_info(
        scaled_residual_maps, measurement_stencil, observed_partition, active_probe_total
    )
    inputs, means, send = call(
        inputs_kernel, "inputs", (many, many, one), mine, other, covariance, operator, initial_mean
    )
    for place in range(1, places):
        came = hop(send, place - 1, place, places)
        means, send = call(
            functools.partial(hop_kernel, place, False), "forward", (many, one), came, operator, inputs, means
        )
    offsets, states, send = call(
        functools.partial(turn_kernel, places - 1),
        "turn",
        (many, many, one),
        means,
        gain,
        propagator.reshape(size, size),
    )
    for place in reversed(range(places - 1)):
        came = hop(send, place + 1, place, places)
        states, send = call(
            functools.partial(hop_kernel, place, True), "backward", (many, one), came, gain, offsets, states
        )
    return (means.reshape(steps, 1, size), states.reshape(steps, 1, size))


def solution(mesh):
    placed = (
        P(("groups", "tm"), "block", None, None),
        P(),
        P(("groups", "tm"), "block"),
        P(("groups", "tm"), "block"),
        P(("groups", "tm"), "block", None, None),
        P(("groups", "tm"), "block", None, None),
        P(("groups", "tm"), "block", None, None),
        P("block", None, None),
        P(("groups", "block"), None),
    )
    return jax.shard_map(
        local,
        mesh=mesh,
        in_specs=placed,
        out_specs=(P(("groups", "tm"), "block", None), P(("groups", "tm"), "block", None)),
        check_vma=False,
    )
```

time: 302 us -> 62.2 us (0.21)
  matrix products: 95.3 us -> 0 us
  waiting for transfers between devices: 104 us -> 15.3 us
  blocking collectives: 57.4 us -> 0 us
  starting transfers between devices: 0.08 us -> 35.6 us
  local copies, waits for them, and re-layouts: 27.1 us -> 5.15 us
  between operations: 14.2 us -> 0.7 us
  Pallas kernels: 0 us -> 5.23 us
    all_gather x2 -> x0, waiting for transfers between devices: 104 us -> none  [entering(): everything = jax.tree.map(lambda part: lax.all_gather(part, axis), array)]
    dot_general x37 -> x0, matrix products: 79.3 us -> none  [the longest x18 37.6 us: compose(): jnp.einsum('bij,bj->bi', later[0], earlier[1], precision=EXACT_ARITHMETIC)]
    all_gather x2 -> x0, blocking collectives: 54.7 us -> none  [entering(): everything = jax.tree.map(lambda part: lax.all_gather(part, axis), array)]
    ppermute x0 -> x15, starting transfers between devices: none -> 35.6 us  [the longest x14 35 us: hop(): return lax.ppermute(row, ('tm', 'block'), pairs)]
    reshape x3 -> x0, local copies, waits for them, and re-layouts: 16.1 us -> none  [the longest x2 15.8 us: sensor_info(): scaled_residual_maps.reshape(steps * slots, channels, GH, cells // GH)]
    conv_general_dilated x1 -> x0, matrix products: 16.1 us -> none  [sensor_info(): lax.conv_general_dilated(grid, flipped, (1, 1), 'SAME', dimension_numbers...]
    ppermute x0 -> x15, waiting for transfers between devices: none -> 15.3 us  [the longest x14 14.5 us: hop(): return lax.ppermute(row, ('tm', 'block'), pairs)]
    pallas_call x0 -> x17, Pallas kernels: none -> 5.23 us  [the longest x16 3.24 us: call(): pl.pallas_call(kernel, out_shape=[jax.ShapeDtypeStruct(shape, jnp.float32...]
  transfers between devices with their start and end apart: 2 -> 15, of which waited for: 2 -> 15; matrix products, arithmetic and copies ran while one was open for 31% -> 1% of each run, Pallas kernels for 0% -> 0%
where the time goes in v1:
time: 62.2 us; the launch traced here: 62 us
  starting transfers between devices  35.6 us (57%)
  waiting for transfers between devices  15.3 us (25%)
  Pallas kernels  5.23 us (8%)
  local copies, waits for them, and re-layouts  5.15 us (8%)
  between operations  0.7 us (1%)
    ppermute x14, starting transfers between devices, hop(): return lax.ppermute(row, ('tm', 'block'), pairs)  35 us
    ppermute x14, waiting for transfers between devices, hop(): return lax.ppermute(row, ('tm', 'block'), pairs)  14.5 us
    unnamed x18, local copies, waits for them, and re-layouts  5.15 us
    pallas_call x16, Pallas kernels, call(): pl.pallas_call(kernel, out_shape=[jax.ShapeDtypeStruct(shape, jnp.float32...  3.24 us
    pallas_call x1, Pallas kernels, sensor_info(): pl.pallas_call(info_kernel, out_shape=[jax.ShapeDtypeStruct((steps, cells...  1.99 us
  transfers between devices with their start and end apart: 15, of which 15 were waited for; matrix products, arithmetic and copies ran while one was open for 1% of the time, Pallas kernels for 0%

profile of v1, /device:TPU:0, one launch (start us, length us, event | category | flops | bytes accessed | tf_op | source)
XLA Modules:
  0.0 62.0 jit_solution(457715837395899642)
XLA Ops:
  0.6 0.8 %copy.12.active_ref = s32[2,1]{1,0:T(2,128)S(1)} copy(s32[2,1]{0,1:T(1,128)} %param.12) | data formatting | bytes 16 | tf_op args[3]
  1.5 0.8 %copy.11.stencil_ref = bf16[16,7,7]{2,1,0:T(8,128)(2,1)S(1)} copy(bf16[16,7,7]{0,2,1:T(8,128)(2,1)} %param.10) | data formatting | bytes 3136 | tf_op args[1]
  2.3 1.6 %copy-done.2 = bf16[2,64,16,512]{3,2,1,0:T(8,128)(2,1)S(1)} copy-done((bf16[2,64,16,512]{3,2,1,0:T(8,128)(2,1)S(1)}, bf16[2,64,16,512]{3,2,1,0:T(8,128)(2,1)}, u32[]{:S(2)}) %copy-start.2) | copy-done | bytes 2097176
  3.9 0.7 %copy-done.6 = s32[2,64]{1,0:T(2,128)S(1)} copy-done((s32[2,64]{1,0:T(2,128)S(1)}, s32[2,64]{1,0:T(2,128)}, u32[]{:S(2)}) %copy-start.6) | copy-done | bytes 536
  4.6 2.0 %sensor_info.1 = (f32[2,512]{1,0:T(2,128)S(1)}, f32[2,512]{1,0:T(2,128)S(1)}) custom-call(bf16[2,1024,512]{2,1,0:T(8,128)(2,1)S(1)} %bitcast.23, bf16[16,7,7]{2,1,0:T(8,128)(2,1)S(1)} %copy.11.stencil_ref, s32[2,64]{1,0:T(2,128)S(1)} %copy-done.6, s32[2,1]{1,0:T(2,128)S(1)} %copy.12.active_ref), custom_call_target="tpu_custom_call" | custom-call | tf_op jit(solution)/shard_map/sensor_info/pallas_call | solution.py:99
  6.6 0.5 collective-permute-start
  7.1 0.8 %collective-permute-done.other_ref = f32[2,512]{1,0:T(2,128)S(1)} collective-permute-done((f32[2,512]{1,0:T(2,128)S(1)}, f32[2,512]{1,0:T(2,128)S(1)}, u32[]{:S(2)}, u32[]{:S(2)}) %collective-permute-start) | collective-permute-done | bytes 4128 | tf_op jit(solution)/shard_map/ppermute | solution.py:122
  8.0 0.7 %inputs.1 = (f32[2,512]{1,0:T(2,128)S(1)}, f32[2,512]{1,0:T(2,128)S(1)}, f32[1,512]{1,0:T(1,128)S(1)}) custom-call(f32[2,512]{1,0:T(2,128)S(1)} %get-tuple-element.36.mine_ref, f32[2,512]{1,0:T(2,128)S(1)} %collective-permute-done.other_ref, bf16[2,512,512]{2,1,0:T(8,128)(2,1)S(1)} %bitcast.24, bf16[2,512,512]{2,1,0:T(8,128)(2,1)S(1)} %bitcast.7, ...), custom_call_target="tpu_custom_call" | custom-call | tf_op jit(solution)/shard_map/inputs/pallas_call | solution.py:167
  8.6 2.9 %collective-permute-start.1 = (f32[1,512]{1,0:T(1,128)S(1)}, f32[1,512]{1,0:T(1,128)S(1)}, u32[]{:S(2)}, u32[]{:S(2)}) collective-permute-start(f32[1,512]{1,0:T(1,128)S(1)} %get-tuple-element.38), channel_id=1, source_target_pairs={{0,2},{2,0},{1,3},{3,1},{4,5},{5,4},{6,7},{7,6},{8,9},{9,8},{10,11... | collective-permute-start | bytes 6152 | tf_op jit(solution)/shard_map/ppermute | solution.py:184
  11.5 1.6 %collective-permute-done.1.came_ref = f32[1,512]{1,0:T(1,128)S(1)} collective-permute-done((f32[1,512]{1,0:T(1,128)S(1)}, f32[1,512]{1,0:T(1,128)S(1)}, u32[]{:S(2)}, u32[]{:S(2)}) %collective-permute-start.1) | collective-permute-done | bytes 2080 | tf_op jit(solution)/shard_map/ppermute | solution.py:184
  13.1 1.2 %collective-permute-done.2.came_ref = f32[1,512]{1,0:T(1,128)S(1)} collective-permute-done((f32[1,512]{1,0:T(1,128)S(1)}, f32[1,512]{1,0:T(1,128)S(1)}, u32[]{:S(2)}, u32[]{:S(2)}) %collective-permute-start.2) | collective-permute-done | bytes 2080 | tf_op jit(solution)/shard_map/ppermute | solution.py:184
  14.3 0.2 collective-permute-start.3
  14.4 1.0 %collective-permute-done.3.came_ref = f32[1,512]{1,0:T(1,128)S(1)} collective-permute-done((f32[1,512]{1,0:T(1,128)S(1)}, f32[1,512]{1,0:T(1,128)S(1)}, u32[]{:S(2)}, u32[]{:S(2)}) %collective-permute-start.3) | collective-permute-done | bytes 2080 | tf_op jit(solution)/shard_map/ppermute | solution.py:184
  15.6 1.0 %collective-permute-done.4.came_ref = f32[1,512]{1,0:T(1,128)S(1)} collective-permute-done((f32[1,512]{1,0:T(1,128)S(1)}, f32[1,512]{1,0:T(1,128)S(1)}, u32[]{:S(2)}, u32[]{:S(2)}) %collective-permute-start.4) | collective-permute-done | bytes 2080 | tf_op jit(solution)/shard_map/ppermute | solution.py:184
  16.6 0.2 collective-permute-start.5
  16.8 1.0 %collective-permute-done.5.came_ref = f32[1,512]{1,0:T(1,128)S(1)} collective-permute-done((f32[1,512]{1,0:T(1,128)S(1)}, f32[1,512]{1,0:T(1,128)S(1)}, u32[]{:S(2)}, u32[]{:S(2)}) %collective-permute-start.5) | collective-permute-done | bytes 2080 | tf_op jit(solution)/shard_map/ppermute | solution.py:184
  18.0 1.0 %collective-permute-done.6.came_ref = f32[1,512]{1,0:T(1,128)S(1)} collective-permute-done((f32[1,512]{1,0:T(1,128)S(1)}, f32[1,512]{1,0:T(1,128)S(1)}, u32[]{:S(2)}, u32[]{:S(2)}) %collective-permute-start.6) | collective-permute-done | bytes 2080 | tf_op jit(solution)/shard_map/ppermute | solution.py:184
  19.2 1.0 %collective-permute-done.7.came_ref = f32[1,512]{1,0:T(1,128)S(1)} collective-permute-done((f32[1,512]{1,0:T(1,128)S(1)}, f32[1,512]{1,0:T(1,128)S(1)}, u32[]{:S(2)}, u32[]{:S(2)}) %collective-permute-start.7) | collective-permute-done | bytes 2080 | tf_op jit(solution)/shard_map/ppermute | solution.py:184
  20.1 0.6 forward.13
  20.7 0.9 %turn.1 = (f32[2,512]{1,0:T(2,128)S(1)}, f32[2,512]{1,0:T(2,128)S(1)}, f32[1,512]{1,0:T(1,128)S(1)}) custom-call(f32[2,512]{1,0:T(2,128)S(1)} %get-tuple-element.53.means_ref, bf16[2,512,512]{2,1,0:T(8,128)(2,1)S(1)} %bitcast.15, bf16[512,512]{1,0:T(8,128)(2,1)S(1)} %bitcast.25), custom_call_target="tpu_custom_call" | custom-call | tf_op jit(solution)/shard_map/turn/pallas_call | solution.py:167
  21.7 0.2 collective-permute-start.8
  21.9 1.0 %collective-permute-done.8.came_ref = f32[1,512]{1,0:T(1,128)S(1)} collective-permute-done((f32[1,512]{1,0:T(1,128)S(1)}, f32[1,512]{1,0:T(1,128)S(1)}, u32[]{:S(2)}, u32[]{:S(2)}) %collective-permute-start.8) | collective-permute-done | bytes 2080 | tf_op jit(solution)/shard_map/ppermute | solution.py:184
  23.1 1.0 %collective-permute-done.9.came_ref = f32[1,512]{1,0:T(1,128)S(1)} collective-permute-done((f32[1,512]{1,0:T(1,128)S(1)}, f32[1,512]{1,0:T(1,128)S(1)}, u32[]{:S(2)}, u32[]{:S(2)}) %collective-permute-start.9) | collective-permute-done | bytes 2080 | tf_op jit(solution)/shard_map/ppermute | solution.py:184
  24.2 1.0 %collective-permute-done.10.came_ref = f32[1,512]{1,0:T(1,128)S(1)} collective-permute-done((f32[1,512]{1,0:T(1,128)S(1)}, f32[1,512]{1,0:T(1,128)S(1)}, u32[]{:S(2)}, u32[]{:S(2)}) %collective-permute-start.10) | collective-permute-done | bytes 2080 | tf_op jit(solution)/shard_map/ppermute | solution.py:184
  25.4 1.0 %collective-permute-done.11.came_ref = f32[1,512]{1,0:T(1,128)S(1)} collective-permute-done((f32[1,512]{1,0:T(1,128)S(1)}, f32[1,512]{1,0:T(1,128)S(1)}, u32[]{:S(2)}, u32[]{:S(2)}) %collective-permute-start.11) | collective-permute-done | bytes 2080 | tf_op jit(solution)/shard_map/ppermute | solution.py:184
  26.5 1.0 %collective-permute-done.12.came_ref = f32[1,512]{1,0:T(1,128)S(1)} collective-permute-done((f32[1,512]{1,0:T(1,128)S(1)}, f32[1,512]{1,0:T(1,128)S(1)}, u32[]{:S(2)}, u32[]{:S(2)}) %collective-permute-start.12) | collective-permute-done | bytes 2080 | tf_op jit(solution)/shard_map/ppermute | solution.py:184
  27.7 1.0 %collective-permute-done.13.came_ref = f32[1,512]{1,0:T(1,128)S(1)} collective-permute-done((f32[1,512]{1,0:T(1,128)S(1)}, f32[1,512]{1,0:T(1,128)S(1)}, u32[]{:S(2)}, u32[]{:S(2)}) %collective-permute-start.13) | collective-permute-done | bytes 2080 | tf_op jit(solution)/shard_map/ppermute | solution.py:184
  28.7 30.1 %collective-permute-start.14 = (f32[1,512]{1,0:T(1,128)S(1)}, f32[1,512]{1,0:T(1,128)S(1)}, u32[]{:S(2)}, u32[]{:S(2)}) collective-permute-start(f32[1,512]{1,0:T(1,128)S(1)} %get-tuple-element.67), channel_id=1, source_target_pairs={{2,0},{0,2},{3,1},{1,3},{4,5},{5,4},{6,7},{7,6},{8,9},{9,8},{10,11... | collective-permute-start | bytes 6152 | tf_op jit(solution)/shard_map/ppermute | solution.py:184
  58.8 0.6 copy.13
  59.4 1.0 %collective-permute-done.14.came_ref = f32[1,512]{1,0:T(1,128)S(1)} collective-permute-done((f32[1,512]{1,0:T(1,128)S(1)}, f32[1,512]{1,0:T(1,128)S(1)}, u32[]{:S(2)}, u32[]{:S(2)}) %collective-permute-start.14) | collective-permute-done | bytes 2080 | tf_op jit(solution)/shard_map/ppermute | solution.py:184
  60.3 1.0 %backward.13 = (f32[2,512]{1,0:T(2,128)S(1)}, f32[1,512]{1,0:T(1,128)}) custom-call(f32[1,512]{1,0:T(1,128)S(1)} %collective-permute-done.14.came_ref, bf16[2,512,512]{2,1,0:T(8,128)(2,1)S(1)} %bitcast.22, f32[2,512]{1,0:T(2,128)S(1)} %get-tuple-element.55.offsets_ref, f32[2,512]{1,0:T(2,128)S(1)} %get-tuple-element.68.kept_ref), custom_call_target="tpu_custom_call" | custom-call | tf_op jit(solution)/shard_map/backward/pallas_call | solution.py:167
  61.4 0.6 copy.14
  (33 shorter events, 1.5 us)
Async XLA Ops:
  0.6 7.3 %copy-start = (bf16[2,1,512,512]{3,2,1,0:T(8,128)(2,1)S(1)}, bf16[2,1,512,512]{3,2,1,0:T(8,128)(2,1)}, u32[]{:S(2)}) copy-start(bf16[2,1,512,512]{3,2,1,0:T(8,128)(2,1)} %param.13) | copy-start | bytes 3145732
  2.3 1.6 %copy-start.2 = (bf16[2,64,16,512]{3,2,1,0:T(8,128)(2,1)S(1)}, bf16[2,64,16,512]{3,2,1,0:T(8,128)(2,1)}, u32[]{:S(2)}) copy-start(bf16[2,64,16,512]{3,2,1,0:T(8,128)(2,1)} %param.9) | copy-start | bytes 6291460
  3.9 0.7 %copy-start.6 = (s32[2,64]{1,0:T(2,128)S(1)}, s32[2,64]{1,0:T(2,128)}, u32[]{:S(2)}) copy-start(s32[2,64]{1,0:T(2,128)} %observed_ref.1) | copy-start | bytes 1540
  4.6 3.4 %copy-start.3 = (bf16[2,1,512,512]{3,2,1,0:T(8,128)(2,1)S(1)}, bf16[2,1,512,512]{3,2,1,0:T(8,128)(2,1)}, u32[]{:S(2)}) copy-start(bf16[2,1,512,512]{3,2,1,0:T(8,128)(2,1)} %param.14) | copy-start | bytes 3145732
  4.6 3.4 %copy-start.5 = (f32[1,512]{1,0:T(1,128)S(1)}, f32[1,512]{1,0:T(1,128)}, u32[]{:S(2)}) copy-start(f32[1,512]{1,0:T(1,128)} %start_ref.1) | copy-start | bytes 6148
  6.6 1.3 %collective-permute-start = (f32[2,512]{1,0:T(2,128)S(1)}, f32[2,512]{1,0:T(2,128)S(1)}, u32[]{:S(2)}, u32[]{:S(2)}) collective-permute-start(f32[2,512]{1,0:T(2,128)S(1)} %get-tuple-element.37), channel_id=1, source_target_pairs={{0,1},{1,0},{2,3},{3,2},{4,5},{5,4},{6,7},{7,6},{8,9},{9,8},{10,11... | collective-permute-start | bytes 12296 | tf_op jit(solution)/shard_map/ppermute | solution.py:122
  8.6 4.5 %collective-permute-start.1 = (f32[1,512]{1,0:T(1,128)S(1)}, f32[1,512]{1,0:T(1,128)S(1)}, u32[]{:S(2)}, u32[]{:S(2)}) collective-permute-start(f32[1,512]{1,0:T(1,128)S(1)} %get-tuple-element.38), channel_id=1, source_target_pairs={{0,2},{2,0},{1,3},{3,1},{4,5},{5,4},{6,7},{7,6},{8,9},{9,8},{10,11... | collective-permute-start | bytes 6152 | tf_op jit(solution)/shard_map/ppermute | solution.py:184
  13.1 1.2 %collective-permute-start.2 = (f32[1,512]{1,0:T(1,128)S(1)}, f32[1,512]{1,0:T(1,128)S(1)}, u32[]{:S(2)}, u32[]{:S(2)}) collective-permute-start(f32[1,512]{1,0:T(1,128)S(1)} %get-tuple-element.41), channel_id=1, source_target_pairs={{2,4},{4,2},{3,5},{5,3},{0,1},{1,0},{6,7},{7,6},{8,9},{9,8},{10,11... | collective-permute-start | bytes 6152 | tf_op jit(solution)/shard_map/ppermute | solution.py:184
  14.3 1.2 %collective-permute-start.3 = (f32[1,512]{1,0:T(1,128)S(1)}, f32[1,512]{1,0:T(1,128)S(1)}, u32[]{:S(2)}, u32[]{:S(2)}) collective-permute-start(f32[1,512]{1,0:T(1,128)S(1)} %get-tuple-element.43), channel_id=1, source_target_pairs={{4,6},{6,4},{5,7},{7,5},{0,1},{1,0},{2,3},{3,2},{8,9},{9,8},{10,11... | collective-permute-start | bytes 6152 | tf_op jit(solution)/shard_map/ppermute | solution.py:184
  15.4 1.2 %collective-permute-start.4 = (f32[1,512]{1,0:T(1,128)S(1)}, f32[1,512]{1,0:T(1,128)S(1)}, u32[]{:S(2)}, u32[]{:S(2)}) collective-permute-start(f32[1,512]{1,0:T(1,128)S(1)} %get-tuple-element.45), channel_id=1, source_target_pairs={{6,8},{8,6},{7,9},{9,7},{0,1},{1,0},{2,3},{3,2},{4,5},{5,4},{10,11... | collective-permute-start | bytes 6152 | tf_op jit(solution)/shard_map/ppermute | solution.py:184
  16.6 4.1 %copy-start.1 = (bf16[2,1,512,512]{3,2,1,0:T(8,128)(2,1)S(1)}, bf16[2,1,512,512]{3,2,1,0:T(8,128)(2,1)}, u32[]{:S(2)}) copy-start(bf16[2,1,512,512]{3,2,1,0:T(8,128)(2,1)} %param.15) | copy-start | bytes 3145732
  16.6 4.1 %copy-start.4 = (bf16[1,512,512]{2,1,0:T(8,128)(2,1)S(1)}, bf16[1,512,512]{2,1,0:T(8,128)(2,1)}, u32[]{:S(2)}) copy-start(bf16[1,512,512]{2,1,0:T(8,128)(2,1)} %param.16) | copy-start | bytes 1572868
  16.6 1.2 %collective-permute-start.5 = (f32[1,512]{1,0:T(1,128)S(1)}, f32[1,512]{1,0:T(1,128)S(1)}, u32[]{:S(2)}, u32[]{:S(2)}) collective-permute-start(f32[1,512]{1,0:T(1,128)S(1)} %get-tuple-element.47), channel_id=1, source_target_pairs={{8,10},{10,8},{9,11},{11,9},{0,1},{1,0},{2,3},{3,2},{4,5},{5,4},{6... | collective-permute-start | bytes 6152 | tf_op jit(solution)/shard_map/ppermute | solution.py:184
  17.8 1.2 %collective-permute-start.6 = (f32[1,512]{1,0:T(1,128)S(1)}, f32[1,512]{1,0:T(1,128)S(1)}, u32[]{:S(2)}, u32[]{:S(2)}) collective-permute-start(f32[1,512]{1,0:T(1,128)S(1)} %get-tuple-element.49), channel_id=1, source_target_pairs={{10,12},{12,10},{11,13},{13,11},{0,1},{1,0},{2,3},{3,2},{4,5},{5,4... | collective-permute-start | bytes 6152 | tf_op jit(solution)/shard_map/ppermute | solution.py:184
  19.0 1.2 %collective-permute-start.7 = (f32[1,512]{1,0:T(1,128)S(1)}, f32[1,512]{1,0:T(1,128)S(1)}, u32[]{:S(2)}, u32[]{:S(2)}) collective-permute-start(f32[1,512]{1,0:T(1,128)S(1)} %get-tuple-element.51), channel_id=1, source_target_pairs={{12,14},{14,12},{13,15},{15,13},{0,1},{1,0},{2,3},{3,2},{4,5},{5,4... | collective-permute-start | bytes 6152 | tf_op jit(solution)/shard_map/ppermute | solution.py:184
  21.7 1.2 %collective-permute-start.8 = (f32[1,512]{1,0:T(1,128)S(1)}, f32[1,512]{1,0:T(1,128)S(1)}, u32[]{:S(2)}, u32[]{:S(2)}) collective-permute-start(f32[1,512]{1,0:T(1,128)S(1)} %get-tuple-element.54), channel_id=1, source_target_pairs={{14,12},{12,14},{15,13},{13,15},{0,1},{1,0},{2,3},{3,2},{4,5},{5,4... | collective-permute-start | bytes 6152 | tf_op jit(solution)/shard_map/ppermute | solution.py:184
  22.9 1.2 %collective-permute-start.9 = (f32[1,512]{1,0:T(1,128)S(1)}, f32[1,512]{1,0:T(1,128)S(1)}, u32[]{:S(2)}, u32[]{:S(2)}) collective-permute-start(f32[1,512]{1,0:T(1,128)S(1)} %get-tuple-element.57), channel_id=1, source_target_pairs={{12,10},{10,12},{13,11},{11,13},{0,1},{1,0},{2,3},{3,2},{4,5},{5,4... | collective-permute-start | bytes 6152 | tf_op jit(solution)/shard_map/ppermute | solution.py:184
  24.0 1.2 %collective-permute-start.10 = (f32[1,512]{1,0:T(1,128)S(1)}, f32[1,512]{1,0:T(1,128)S(1)}, u32[]{:S(2)}, u32[]{:S(2)}) collective-permute-start(f32[1,512]{1,0:T(1,128)S(1)} %get-tuple-element.59), channel_id=1, source_target_pairs={{10,8},{8,10},{11,9},{9,11},{0,1},{1,0},{2,3},{3,2},{4,5},{5,4},{6... | collective-permute-start | bytes 6152 | tf_op jit(solution)/shard_map/ppermute | solution.py:184
  25.2 1.2 %collective-permute-start.11 = (f32[1,512]{1,0:T(1,128)S(1)}, f32[1,512]{1,0:T(1,128)S(1)}, u32[]{:S(2)}, u32[]{:S(2)}) collective-permute-start(f32[1,512]{1,0:T(1,128)S(1)} %get-tuple-element.61), channel_id=1, source_target_pairs={{8,6},{6,8},{9,7},{7,9},{0,1},{1,0},{2,3},{3,2},{4,5},{5,4},{10,11... | collective-permute-start | bytes 6152 | tf_op jit(solution)/shard_map/ppermute | solution.py:184
  26.4 1.2 %collective-permute-start.12 = (f32[1,512]{1,0:T(1,128)S(1)}, f32[1,512]{1,0:T(1,128)S(1)}, u32[]{:S(2)}, u32[]{:S(2)}) collective-permute-start(f32[1,512]{1,0:T(1,128)S(1)} %get-tuple-element.63), channel_id=1, source_target_pairs={{6,4},{4,6},{7,5},{5,7},{0,1},{1,0},{2,3},{3,2},{8,9},{9,8},{10,11... | collective-permute-start | bytes 6152 | tf_op jit(solution)/shard_map/ppermute | solution.py:184
  27.5 1.2 %collective-permute-start.13 = (f32[1,512]{1,0:T(1,128)S(1)}, f32[1,512]{1,0:T(1,128)S(1)}, u32[]{:S(2)}, u32[]{:S(2)}) collective-permute-start(f32[1,512]{1,0:T(1,128)S(1)} %get-tuple-element.65), channel_id=1, source_target_pairs={{4,2},{2,4},{5,3},{3,5},{0,1},{1,0},{6,7},{7,6},{8,9},{9,8},{10,11... | collective-permute-start | bytes 6152 | tf_op jit(solution)/shard_map/ppermute | solution.py:184
  28.7 31.6 %collective-permute-start.14 = (f32[1,512]{1,0:T(1,128)S(1)}, f32[1,512]{1,0:T(1,128)S(1)}, u32[]{:S(2)}, u32[]{:S(2)}) collective-permute-start(f32[1,512]{1,0:T(1,128)S(1)} %get-tuple-element.67), channel_id=1, source_target_pairs={{2,0},{0,2},{3,1},{1,3},{4,5},{5,4},{6,7},{7,6},{8,9},{9,8},{10,11... | collective-permute-start | bytes 6152 | tf_op jit(solution)/shard_map/ppermute | solution.py:184

commit v2 on v1

--- a/solution.py
+++ b/solution.py
@@ -8,6 +8,7 @@
 from jax.sharding import PartitionSpec as P
 
 GH = 16
+MAP_COPIES = 4
 VMEM = pl.BlockSpec(memory_space=pltpu.VMEM)
 PARAMS = pltpu.CompilerParams(vmem_limit_bytes=16 * 2**20)
 
@@ -30,15 +31,40 @@
     return jnp.sum(product, axis=0, keepdims=True)
 
 
-def info_kernel(maps_hbm, stencil_ref, observed_ref, active_ref, mine_ref, theirs_ref, maps, taps, sems):
+def info_kernel(
+    maps_hbm,
+    stencil_hbm,
+    observed_hbm,
+    active_hbm,
+    mine_ref,
+    theirs_ref,
+    maps,
+    stencil_ref,
+    observed_ref,
+    active_ref,
+    taps,
+    map_sems,
+    sems,
+):
     steps, rows, cells = maps.shape
     slots = observed_ref.shape[1]
-    channels, side, _ = stencil_ref.shape
+    side, _, channels = stencil_ref.shape
     half = side // 2
+    small = []
+    for i, (source, target) in enumerate(
+        ((stencil_hbm, stencil_ref), (observed_hbm, observed_ref), (active_hbm, active_ref))
+    ):
+        small.append(pltpu.make_async_copy(source, target, sems.at[i]))
+        small[-1].start()
+    part = rows // MAP_COPIES
     copies = []
     for t in range(steps):
-        copies.append(pltpu.make_async_copy(maps_hbm.at[t], maps.at[t], sems.at[t]))
-        copies[-1].start()
+        for i in range(MAP_COPIES):
+            at = pl.ds(i * part, part)
+            copies.append(
+                pltpu.make_async_copy(maps_hbm.at[t, at], maps.at[t, at], map_sems.at[t, i])
+            )
+            copies[-1].start()
 
     repeat = jnp.where(
         lax.broadcasted_iota(jnp.int32, (channels, rows), 1) % channels
@@ -47,10 +73,6 @@
         0.0,
     ).astype(jnp.bfloat16)
     taps[...] = jnp.zeros_like(taps)
-    for p in range(side):
-        taps[p * 8 : p * 8 + side, :] = lax.dot_general(
-            stencil_ref[:, p, :], repeat, (((0,), (0,)), ((), ())), preferred_element_type=jnp.float32
-        )
     spread = jnp.where(
         lax.broadcasted_iota(jnp.int32, (slots, rows), 1) // channels
         == lax.broadcasted_iota(jnp.int32, (slots, rows), 0),
@@ -66,15 +88,22 @@
     column = across - tap + half
     column_inside = (column >= 0) & (column < width) & (tap < side)
     me = lax.axis_index("block")
+    for copy in small:
+        copy.wait()
+    for p in range(side):
+        taps[p * 8 : p * 8 + side, :] = jnp.dot(
+            stencil_ref[p], repeat, preferred_element_type=jnp.float32
+        )
     for t in range(steps):
         owner = lax.broadcasted_iota(jnp.int32, (8, slots), 0)
         slot = lax.broadcasted_iota(jnp.int32, (8, slots), 1)
-        live = (observed_ref[t : t + 1, :] == owner) & (slot < active_ref[t, 0])
+        live = (observed_ref[t : t + 1, :] == owner) & (slot < active_ref[0:1, t : t + 1])
         weight = jnp.dot(
             jnp.where(live, 1.0, 0.0).astype(jnp.bfloat16), spread, preferred_element_type=jnp.float32
         )
         left = jnp.concatenate([taps[...] * weight[b : b + 1, :] for b in range(2)], axis=0)
-        copies[t].wait()
+        for copy in copies[t * MAP_COPIES : (t + 1) * MAP_COPIES]:
+            copy.wait()
         shifted = jnp.dot(left.astype(jnp.bfloat16), maps[t], preferred_element_type=jnp.float32)
         found = []
         for b in range(2):
@@ -99,25 +128,29 @@
     mine, theirs = pl.pallas_call(
         info_kernel,
         out_shape=[jax.ShapeDtypeStruct((steps, cells), jnp.float32)] * 2,
-        in_specs=[
-            pl.BlockSpec(memory_space=pl.ANY),
-            VMEM,
-            VMEM,
-            pl.BlockSpec(memory_space=pltpu.SMEM),
-        ],
+        in_specs=[pl.BlockSpec(memory_space=pltpu.HBM)] * 4,
         out_specs=[VMEM] * 2,
         scratch_shapes=[
             pltpu.VMEM((steps, slots * channels, cells), jnp.bfloat16),
+            pltpu.VMEM((side, side, channels), jnp.bfloat16),
+            pltpu.VMEM((steps, slots), jnp.int32),
+            pltpu.VMEM((1, steps), jnp.int32),
             pltpu.VMEM((side * 8, slots * channels), jnp.float32),
-            pltpu.SemaphoreType.DMA((steps,)),
+            pltpu.SemaphoreType.DMA((steps, MAP_COPIES)),
+            pltpu.SemaphoreType.DMA((3,)),
         ],
         compiler_params=PARAMS,
         name="sensor_info",
     )(
-        scaled_residual_maps.reshape(steps, slots * channels, cells),
-        measurement_stencil,
-        observed_partition,
-        active_probe_total,
+        *(
+            pltpu.with_memory_space_constraint(array, pltpu.HBM)
+            for array in (
+                scaled_residual_maps.reshape(steps, slots * channels, cells),
+                measurement_stencil.transpose(1, 2, 0),
+                observed_partition,
+                active_probe_total.T,
+            )
+        )
     )
     return mine, lax.ppermute(theirs, "block", [(0, 1), (1, 0)])
 

time: 62.2 us -> 58.9 us (0.947)
  local copies, waits for them, and re-layouts: 5.15 us -> 1.21 us
  Pallas kernels: 5.23 us -> 5.95 us
    unnamed x18 -> x12, local copies, waits for them, and re-layouts: 5.15 us -> 1.21 us
    pallas_call x1, Pallas kernels: 1.99 us -> 2.71 us  [sensor_info(): pl.pallas_call(info_kernel, out_shape=[jax.ShapeDtypeStruct((steps, cells...]
where the time goes in v2:
time: 58.9 us; the launch traced here: 58.8 us
  starting transfers between devices  35.6 us (60%)
  waiting for transfers between devices  15.3 us (26%)
  Pallas kernels  5.95 us (10%)
  local copies, waits for them, and re-layouts  1.21 us (2%)
  between operations  0.71 us (1%)
    ppermute x14, starting transfers between devices, hop(): return lax.ppermute(row, ('tm', 'block'), pairs)  35 us
    ppermute x14, waiting for transfers between devices, hop(): return lax.ppermute(row, ('tm', 'block'), pairs)  14.5 us
    pallas_call x16, Pallas kernels, call(): pl.pallas_call(kernel, out_shape=[jax.ShapeDtypeStruct(shape, jnp.float32...  3.24 us
    pallas_call x1, Pallas kernels, sensor_info(): pl.pallas_call(info_kernel, out_shape=[jax.ShapeDtypeStruct((steps, cells...  2.71 us
    unnamed x12, local copies, waits for them, and re-layouts  1.21 us
  transfers between devices with their start and end apart: 15, of which 15 were waited for; matrix products, arithmetic and copies ran while one was open for 1% of the time, Pallas kernels for 0%

profile of v2, /device:TPU:0, one launch (start us, length us, event | category | flops | bytes accessed | tf_op | source)
XLA Modules:
  0.0 58.8 jit_solution(1853386450838601650)
XLA Ops:
  0.7 2.7 %sensor_info.1 = (f32[2,512]{1,0:T(2,128)S(1)}, f32[2,512]{1,0:T(2,128)S(1)}) custom-call(bf16[2,1024,512]{2,1,0:T(8,128)(2,1)} %bitcast.29, bf16[7,7,16]{2,1,0:T(8,128)(2,1)} %bitcast.30, s32[2,64]{1,0:T(2,128)} %observed_hbm.1, s32[1,2]{1,0:T(1,128)} %bitcast.31), custom_call_target="tpu_custom_call" | custom-call | tf_op jit(solution)/shard_map/sensor_info/pallas_call | solution.py:128
  3.4 0.5 collective-permute-start
  3.9 0.8 %collective-permute-done.other_ref = f32[2,512]{1,0:T(2,128)S(1)} collective-permute-done((f32[2,512]{1,0:T(2,128)S(1)}, f32[2,512]{1,0:T(2,128)S(1)}, u32[]{:S(2)}, u32[]{:S(2)}) %collective-permute-start) | collective-permute-done | bytes 4128 | tf_op jit(solution)/shard_map/ppermute | solution.py:155
  4.7 0.7 %inputs.1 = (f32[2,512]{1,0:T(2,128)S(1)}, f32[2,512]{1,0:T(2,128)S(1)}, f32[1,512]{1,0:T(1,128)S(1)}) custom-call(f32[2,512]{1,0:T(2,128)S(1)} %get-tuple-element.36.mine_ref, f32[2,512]{1,0:T(2,128)S(1)} %collective-permute-done.other_ref, bf16[2,512,512]{2,1,0:T(8,128)(2,1)S(1)} %bitcast.25, bf16[2,512,512]{2,1,0:T(8,128)(2,1)S(1)} %bitcast.9, ...), custom_call_target="tpu_custom_call" | custom-call | tf_op jit(solution)/shard_map/inputs/pallas_call | solution.py:200
  5.4 2.9 %collective-permute-start.1 = (f32[1,512]{1,0:T(1,128)S(1)}, f32[1,512]{1,0:T(1,128)S(1)}, u32[]{:S(2)}, u32[]{:S(2)}) collective-permute-start(f32[1,512]{1,0:T(1,128)S(1)} %get-tuple-element.38), channel_id=1, source_target_pairs={{0,2},{2,0},{1,3},{3,1},{4,5},{5,4},{6,7},{7,6},{8,9},{9,8},{10,11... | collective-permute-start | bytes 6152 | tf_op jit(solution)/shard_map/ppermute | solution.py:217
  8.3 1.6 %collective-permute-done.1.came_ref = f32[1,512]{1,0:T(1,128)S(1)} collective-permute-done((f32[1,512]{1,0:T(1,128)S(1)}, f32[1,512]{1,0:T(1,128)S(1)}, u32[]{:S(2)}, u32[]{:S(2)}) %collective-permute-start.1) | collective-permute-done | bytes 2080 | tf_op jit(solution)/shard_map/ppermute | solution.py:217
  9.9 1.2 %collective-permute-done.2.came_ref = f32[1,512]{1,0:T(1,128)S(1)} collective-permute-done((f32[1,512]{1,0:T(1,128)S(1)}, f32[1,512]{1,0:T(1,128)S(1)}, u32[]{:S(2)}, u32[]{:S(2)}) %collective-permute-start.2) | collective-permute-done | bytes 2080 | tf_op jit(solution)/shard_map/ppermute | solution.py:217
  11.1 0.2 collective-permute-start.3
  11.2 1.0 %collective-permute-done.3.came_ref = f32[1,512]{1,0:T(1,128)S(1)} collective-permute-done((f32[1,512]{1,0:T(1,128)S(1)}, f32[1,512]{1,0:T(1,128)S(1)}, u32[]{:S(2)}, u32[]{:S(2)}) %collective-permute-start.3) | collective-permute-done | bytes 2080 | tf_op jit(solution)/shard_map/ppermute | solution.py:217
  12.4 1.0 %collective-permute-done.4.came_ref = f32[1,512]{1,0:T(1,128)S(1)} collective-permute-done((f32[1,512]{1,0:T(1,128)S(1)}, f32[1,512]{1,0:T(1,128)S(1)}, u32[]{:S(2)}, u32[]{:S(2)}) %collective-permute-start.4) | collective-permute-done | bytes 2080 | tf_op jit(solution)/shard_map/ppermute | solution.py:217
  13.4 0.2 collective-permute-start.5
  13.6 1.0 %collective-permute-done.5.came_ref = f32[1,512]{1,0:T(1,128)S(1)} collective-permute-done((f32[1,512]{1,0:T(1,128)S(1)}, f32[1,512]{1,0:T(1,128)S(1)}, u32[]{:S(2)}, u32[]{:S(2)}) %collective-permute-start.5) | collective-permute-done | bytes 2080 | tf_op jit(solution)/shard_map/ppermute | solution.py:217
  14.6 0.2 collective-permute-start.6
  14.8 1.0 %collective-permute-done.6.came_ref = f32[1,512]{1,0:T(1,128)S(1)} collective-permute-done((f32[1,512]{1,0:T(1,128)S(1)}, f32[1,512]{1,0:T(1,128)S(1)}, u32[]{:S(2)}, u32[]{:S(2)}) %collective-permute-start.6) | collective-permute-done | bytes 2080 | tf_op jit(solution)/shard_map/ppermute | solution.py:217
  15.9 1.0 %collective-permute-done.7.came_ref = f32[1,512]{1,0:T(1,128)S(1)} collective-permute-done((f32[1,512]{1,0:T(1,128)S(1)}, f32[1,512]{1,0:T(1,128)S(1)}, u32[]{:S(2)}, u32[]{:S(2)}) %collective-permute-start.7) | collective-permute-done | bytes 2080 | tf_op jit(solution)/shard_map/ppermute | solution.py:217
  16.9 0.6 forward.13
  17.5 0.9 %turn.1 = (f32[2,512]{1,0:T(2,128)S(1)}, f32[2,512]{1,0:T(2,128)S(1)}, f32[1,512]{1,0:T(1,128)S(1)}) custom-call(f32[2,512]{1,0:T(2,128)S(1)} %get-tuple-element.53.means_ref, bf16[2,512,512]{2,1,0:T(8,128)(2,1)S(1)} %bitcast.17, bf16[512,512]{1,0:T(8,128)(2,1)S(1)} %bitcast.26), custom_call_target="tpu_custom_call" | custom-call | tf_op jit(solution)/shard_map/turn/pallas_call | solution.py:200
  18.4 0.2 collective-permute-start.8
  18.7 1.0 %collective-permute-done.8.came_ref = f32[1,512]{1,0:T(1,128)S(1)} collective-permute-done((f32[1,512]{1,0:T(1,128)S(1)}, f32[1,512]{1,0:T(1,128)S(1)}, u32[]{:S(2)}, u32[]{:S(2)}) %collective-permute-start.8) | collective-permute-done | bytes 2080 | tf_op jit(solution)/shard_map/ppermute | solution.py:217
  19.7 0.2 collective-permute-start.9
  19.8 1.0 %collective-permute-done.9.came_ref = f32[1,512]{1,0:T(1,128)S(1)} collective-permute-done((f32[1,512]{1,0:T(1,128)S(1)}, f32[1,512]{1,0:T(1,128)S(1)}, u32[]{:S(2)}, u32[]{:S(2)}) %collective-permute-start.9) | collective-permute-done | bytes 2080 | tf_op jit(solution)/shard_map/ppermute | solution.py:217
  20.8 0.2 collective-permute-start.10
  21.0 1.0 %collective-permute-done.10.came_ref = f32[1,512]{1,0:T(1,128)S(1)} collective-permute-done((f32[1,512]{1,0:T(1,128)S(1)}, f32[1,512]{1,0:T(1,128)S(1)}, u32[]{:S(2)}, u32[]{:S(2)}) %collective-permute-start.10) | collective-permute-done | bytes 2080 | tf_op jit(solution)/shard_map/ppermute | solution.py:217
  22.2 1.0 %collective-permute-done.11.came_ref = f32[1,512]{1,0:T(1,128)S(1)} collective-permute-done((f32[1,512]{1,0:T(1,128)S(1)}, f32[1,512]{1,0:T(1,128)S(1)}, u32[]{:S(2)}, u32[]{:S(2)}) %collective-permute-start.11) | collective-permute-done | bytes 2080 | tf_op jit(solution)/shard_map/ppermute | solution.py:217
  23.1 0.2 collective-permute-start.12
  23.3 1.0 %collective-permute-done.12.came_ref = f32[1,512]{1,0:T(1,128)S(1)} collective-permute-done((f32[1,512]{1,0:T(1,128)S(1)}, f32[1,512]{1,0:T(1,128)S(1)}, u32[]{:S(2)}, u32[]{:S(2)}) %collective-permute-start.12) | collective-permute-done | bytes 2080 | tf_op jit(solution)/shard_map/ppermute | solution.py:217
  24.5 1.0 %collective-permute-done.13.came_ref = f32[1,512]{1,0:T(1,128)S(1)} collective-permute-done((f32[1,512]{1,0:T(1,128)S(1)}, f32[1,512]{1,0:T(1,128)S(1)}, u32[]{:S(2)}, u32[]{:S(2)}) %collective-permute-start.13) | collective-permute-done | bytes 2080 | tf_op jit(solution)/shard_map/ppermute | solution.py:217
  25.5 30.1 %collective-permute-start.14 = (f32[1,512]{1,0:T(1,128)S(1)}, f32[1,512]{1,0:T(1,128)S(1)}, u32[]{:S(2)}, u32[]{:S(2)}) collective-permute-start(f32[1,512]{1,0:T(1,128)S(1)} %get-tuple-element.67), channel_id=1, source_target_pairs={{2,0},{0,2},{3,1},{1,3},{4,5},{5,4},{6,7},{7,6},{8,9},{9,8},{10,11... | collective-permute-start | bytes 6152 | tf_op jit(solution)/shard_map/ppermute | solution.py:217
  55.5 0.6 %copy.11 = f32[2,1,512]{2,1,0:T(1,128)} copy(f32[2,1,512]{2,0,1:T(2,128)S(1)} %bitcast.27) | data formatting | bytes 8192
  56.1 1.0 %collective-permute-done.14.came_ref = f32[1,512]{1,0:T(1,128)S(1)} collective-permute-done((f32[1,512]{1,0:T(1,128)S(1)}, f32[1,512]{1,0:T(1,128)S(1)}, u32[]{:S(2)}, u32[]{:S(2)}) %collective-permute-start.14) | collective-permute-done | bytes 2080 | tf_op jit(solution)/shard_map/ppermute | solution.py:217
  57.1 1.0 %backward.13 = (f32[2,512]{1,0:T(2,128)S(1)}, f32[1,512]{1,0:T(1,128)}) custom-call(f32[1,512]{1,0:T(1,128)S(1)} %collective-permute-done.14.came_ref, bf16[2,512,512]{2,1,0:T(8,128)(2,1)S(1)} %bitcast.24, f32[2,512]{1,0:T(2,128)S(1)} %get-tuple-element.55.offsets_ref, f32[2,512]{1,0:T(2,128)S(1)} %get-tuple-element.68.kept_ref), custom_call_target="tpu_custom_call" | custom-call | tf_op jit(solution)/shard_map/backward/pallas_call | solution.py:200
  58.2 0.6 %copy.12 = f32[2,1,512]{2,1,0:T(1,128)} copy(f32[2,1,512]{2,0,1:T(2,128)S(1)} %bitcast.28) | data formatting | bytes 8192
  (27 shorter events, 0.8 us)
Async XLA Ops:
  0.6 4.1 %copy-start.4 = (f32[1,512]{1,0:T(1,128)S(1)}, f32[1,512]{1,0:T(1,128)}, u32[]{:S(2)}) copy-start(f32[1,512]{1,0:T(1,128)} %start_ref.1) | copy-start | bytes 6148
  0.6 4.1 %copy-start.2 = (bf16[2,1,512,512]{3,2,1,0:T(8,128)(2,1)S(1)}, bf16[2,1,512,512]{3,2,1,0:T(8,128)(2,1)}, u32[]{:S(2)}) copy-start(bf16[2,1,512,512]{3,2,1,0:T(8,128)(2,1)} %param.14) | copy-start | bytes 3145732
  0.7 4.1 %copy-start = (bf16[2,1,512,512]{3,2,1,0:T(8,128)(2,1)S(1)}, bf16[2,1,512,512]{3,2,1,0:T(8,128)(2,1)}, u32[]{:S(2)}) copy-start(bf16[2,1,512,512]{3,2,1,0:T(8,128)(2,1)} %param.13) | copy-start | bytes 3145732
  3.4 1.3 %collective-permute-start = (f32[2,512]{1,0:T(2,128)S(1)}, f32[2,512]{1,0:T(2,128)S(1)}, u32[]{:S(2)}, u32[]{:S(2)}) collective-permute-start(f32[2,512]{1,0:T(2,128)S(1)} %get-tuple-element.37), channel_id=1, source_target_pairs={{0,1},{1,0},{2,3},{3,2},{4,5},{5,4},{6,7},{7,6},{8,9},{9,8},{10,11... | collective-permute-start | bytes 12296 | tf_op jit(solution)/shard_map/ppermute | solution.py:155
  5.4 4.5 %collective-permute-start.1 = (f32[1,512]{1,0:T(1,128)S(1)}, f32[1,512]{1,0:T(1,128)S(1)}, u32[]{:S(2)}, u32[]{:S(2)}) collective-permute-start(f32[1,512]{1,0:T(1,128)S(1)} %get-tuple-element.38), channel_id=1, source_target_pairs={{0,2},{2,0},{1,3},{3,1},{4,5},{5,4},{6,7},{7,6},{8,9},{9,8},{10,11... | collective-permute-start | bytes 6152 | tf_op jit(solution)/shard_map/ppermute | solution.py:217
  9.9 1.2 %collective-permute-start.2 = (f32[1,512]{1,0:T(1,128)S(1)}, f32[1,512]{1,0:T(1,128)S(1)}, u32[]{:S(2)}, u32[]{:S(2)}) collective-permute-start(f32[1,512]{1,0:T(1,128)S(1)} %get-tuple-element.41), channel_id=1, source_target_pairs={{2,4},{4,2},{3,5},{5,3},{0,1},{1,0},{6,7},{7,6},{8,9},{9,8},{10,11... | collective-permute-start | bytes 6152 | tf_op jit(solution)/shard_map/ppermute | solution.py:217
  11.1 1.2 %collective-permute-start.3 = (f32[1,512]{1,0:T(1,128)S(1)}, f32[1,512]{1,0:T(1,128)S(1)}, u32[]{:S(2)}, u32[]{:S(2)}) collective-permute-start(f32[1,512]{1,0:T(1,128)S(1)} %get-tuple-element.43), channel_id=1, source_target_pairs={{4,6},{6,4},{5,7},{7,5},{0,1},{1,0},{2,3},{3,2},{8,9},{9,8},{10,11... | collective-permute-start | bytes 6152 | tf_op jit(solution)/shard_map/ppermute | solution.py:217
  12.2 1.2 %collective-permute-start.4 = (f32[1,512]{1,0:T(1,128)S(1)}, f32[1,512]{1,0:T(1,128)S(1)}, u32[]{:S(2)}, u32[]{:S(2)}) collective-permute-start(f32[1,512]{1,0:T(1,128)S(1)} %get-tuple-element.45), channel_id=1, source_target_pairs={{6,8},{8,6},{7,9},{9,7},{0,1},{1,0},{2,3},{3,2},{4,5},{5,4},{10,11... | collective-permute-start | bytes 6152 | tf_op jit(solution)/shard_map/ppermute | solution.py:217
  13.4 4.1 %copy-start.1 = (bf16[2,1,512,512]{3,2,1,0:T(8,128)(2,1)S(1)}, bf16[2,1,512,512]{3,2,1,0:T(8,128)(2,1)}, u32[]{:S(2)}) copy-start(bf16[2,1,512,512]{3,2,1,0:T(8,128)(2,1)} %param.15) | copy-start | bytes 3145732
  13.4 4.1 %copy-start.3 = (bf16[1,512,512]{2,1,0:T(8,128)(2,1)S(1)}, bf16[1,512,512]{2,1,0:T(8,128)(2,1)}, u32[]{:S(2)}) copy-start(bf16[1,512,512]{2,1,0:T(8,128)(2,1)} %param.16) | copy-start | bytes 1572868
  13.4 1.2 %collective-permute-start.5 = (f32[1,512]{1,0:T(1,128)S(1)}, f32[1,512]{1,0:T(1,128)S(1)}, u32[]{:S(2)}, u32[]{:S(2)}) collective-permute-start(f32[1,512]{1,0:T(1,128)S(1)} %get-tuple-element.47), channel_id=1, source_target_pairs={{8,10},{10,8},{9,11},{11,9},{0,1},{1,0},{2,3},{3,2},{4,5},{5,4},{6... | collective-permute-start | bytes 6152 | tf_op jit(solution)/shard_map/ppermute | solution.py:217
  14.6 1.2 %collective-permute-start.6 = (f32[1,512]{1,0:T(1,128)S(1)}, f32[1,512]{1,0:T(1,128)S(1)}, u32[]{:S(2)}, u32[]{:S(2)}) collective-permute-start(f32[1,512]{1,0:T(1,128)S(1)} %get-tuple-element.49), channel_id=1, source_target_pairs={{10,12},{12,10},{11,13},{13,11},{0,1},{1,0},{2,3},{3,2},{4,5},{5,4... | collective-permute-start | bytes 6152 | tf_op jit(solution)/shard_map/ppermute | solution.py:217
  15.8 1.2 %collective-permute-start.7 = (f32[1,512]{1,0:T(1,128)S(1)}, f32[1,512]{1,0:T(1,128)S(1)}, u32[]{:S(2)}, u32[]{:S(2)}) collective-permute-start(f32[1,512]{1,0:T(1,128)S(1)} %get-tuple-element.51), channel_id=1, source_target_pairs={{12,14},{14,12},{13,15},{15,13},{0,1},{1,0},{2,3},{3,2},{4,5},{5,4... | collective-permute-start | bytes 6152 | tf_op jit(solution)/shard_map/ppermute | solution.py:217
  18.4 1.2 %collective-permute-start.8 = (f32[1,512]{1,0:T(1,128)S(1)}, f32[1,512]{1,0:T(1,128)S(1)}, u32[]{:S(2)}, u32[]{:S(2)}) collective-permute-start(f32[1,512]{1,0:T(1,128)S(1)} %get-tuple-element.54), channel_id=1, source_target_pairs={{14,12},{12,14},{15,13},{13,15},{0,1},{1,0},{2,3},{3,2},{4,5},{5,4... | collective-permute-start | bytes 6152 | tf_op jit(solution)/shard_map/ppermute | solution.py:217
  19.7 1.2 %collective-permute-start.9 = (f32[1,512]{1,0:T(1,128)S(1)}, f32[1,512]{1,0:T(1,128)S(1)}, u32[]{:S(2)}, u32[]{:S(2)}) collective-permute-start(f32[1,512]{1,0:T(1,128)S(1)} %get-tuple-element.57), channel_id=1, source_target_pairs={{12,10},{10,12},{13,11},{11,13},{0,1},{1,0},{2,3},{3,2},{4,5},{5,4... | collective-permute-start | bytes 6152 | tf_op jit(solution)/shard_map/ppermute | solution.py:217
  20.8 1.2 %collective-permute-start.10 = (f32[1,512]{1,0:T(1,128)S(1)}, f32[1,512]{1,0:T(1,128)S(1)}, u32[]{:S(2)}, u32[]{:S(2)}) collective-permute-start(f32[1,512]{1,0:T(1,128)S(1)} %get-tuple-element.59), channel_id=1, source_target_pairs={{10,8},{8,10},{11,9},{9,11},{0,1},{1,0},{2,3},{3,2},{4,5},{5,4},{6... | collective-permute-start | bytes 6152 | tf_op jit(solution)/shard_map/ppermute | solution.py:217
  22.0 1.2 %collective-permute-start.11 = (f32[1,512]{1,0:T(1,128)S(1)}, f32[1,512]{1,0:T(1,128)S(1)}, u32[]{:S(2)}, u32[]{:S(2)}) collective-permute-start(f32[1,512]{1,0:T(1,128)S(1)} %get-tuple-element.61), channel_id=1, source_target_pairs={{8,6},{6,8},{9,7},{7,9},{0,1},{1,0},{2,3},{3,2},{4,5},{5,4},{10,11... | collective-permute-start | bytes 6152 | tf_op jit(solution)/shard_map/ppermute | solution.py:217
  23.1 1.2 %collective-permute-start.12 = (f32[1,512]{1,0:T(1,128)S(1)}, f32[1,512]{1,0:T(1,128)S(1)}, u32[]{:S(2)}, u32[]{:S(2)}) collective-permute-start(f32[1,512]{1,0:T(1,128)S(1)} %get-tuple-element.63), channel_id=1, source_target_pairs={{6,4},{4,6},{7,5},{5,7},{0,1},{1,0},{2,3},{3,2},{8,9},{9,8},{10,11... | collective-permute-start | bytes 6152 | tf_op jit(solution)/shard_map/ppermute | solution.py:217
  24.3 1.2 %collective-permute-start.13 = (f32[1,512]{1,0:T(1,128)S(1)}, f32[1,512]{1,0:T(1,128)S(1)}, u32[]{:S(2)}, u32[]{:S(2)}) collective-permute-start(f32[1,512]{1,0:T(1,128)S(1)} %get-tuple-element.65), channel_id=1, source_target_pairs={{4,2},{2,4},{5,3},{3,5},{0,1},{1,0},{6,7},{7,6},{8,9},{9,8},{10,11... | collective-permute-start | bytes 6152 | tf_op jit(solution)/shard_map/ppermute | solution.py:217
  25.5 31.6 %collective-permute-start.14 = (f32[1,512]{1,0:T(1,128)S(1)}, f32[1,512]{1,0:T(1,128)S(1)}, u32[]{:S(2)}, u32[]{:S(2)}) collective-permute-start(f32[1,512]{1,0:T(1,128)S(1)} %get-tuple-element.67), channel_id=1, source_target_pairs={{2,0},{0,2},{3,1},{1,3},{4,5},{5,4},{6,7},{7,6},{8,9},{9,8},{10,11... | collective-permute-start | bytes 6152 | tf_op jit(solution)/shard_map/ppermute | solution.py:217

commit v3 on v2

--- a/solution.py
+++ b/solution.py
@@ -165,14 +165,13 @@
     send_ref[...] = state
 
 
-def hop_kernel(turn, reverse, came_ref, matrices_ref, offsets_ref, kept_ref, states_ref, send_ref):
+def hop_kernel(turn, came_ref, matrices_ref, offsets_ref, kept_ref, states_ref, send_ref):
     here = lax.axis_index("tm") == turn
 
     @pl.when(here)
     def _():
         state = came_ref[...]
-        order = range(matrices_ref.shape[0])
-        for t in reversed(order) if reverse else order:
+        for t in range(matrices_ref.shape[0]):
             state = times(matrices_ref[t], state) + offsets_ref[t : t + 1, :]
             states_ref[t : t + 1, :] = state
         send_ref[...] = state
@@ -181,6 +180,37 @@
     def _():
         states_ref[...] = kept_ref[...]
         send_ref[...] = came_ref[...]
+
+
+def compose_kernel(after_ref, gain_ref, composed_ref):
+    del after_ref
+    steps = gain_ref.shape[0]
+    product = gain_ref[0].astype(jnp.float32)
+    for t in range(1, steps):
+        product = sum(
+            jnp.dot(part, gain_ref[t], preferred_element_type=jnp.float32)
+            for part in (halves(product) if t > 1 else [gain_ref[0]])
+        )
+    composed_ref[...] = product
+
+
+def halves(matrix):
+    high = matrix.astype(jnp.bfloat16)
+    return [high, (matrix - high.astype(jnp.float32)).astype(jnp.bfloat16)]
+
+
+def split_kernel(near_ref, far_ref, near_parts_ref, far_parts_ref):
+    for source, target in ((near_ref, near_parts_ref), (far_ref, far_parts_ref)):
+        target[0], target[1] = halves(source[...])
+
+
+def times_parts(parts_ref, row):
+    block = pieces(row)
+    product = sum(
+        lax.dot_general(block, parts_ref[i], (((1,), (1,)), ((), ())), preferred_element_type=jnp.float32)
+        for i in range(2)
+    )
+    return jnp.sum(product, axis=0, keepdims=True)
 
 
 def turn_kernel(last, means_ref, gain_ref, propagator_ref, offsets_ref, states_ref, send_ref):
@@ -188,12 +218,67 @@
     for t in range(steps):
         moved = times(gain_ref[t], times(propagator_ref[...], means_ref[t : t + 1, :]))
         offsets_ref[t : t + 1, :] = means_ref[t : t + 1, :] - moved
-    state = means_ref[steps - 1 : steps, :]
-    states_ref[steps - 1 : steps, :] = state
+    end = slice(steps - 1, steps)
+    state = jnp.where(lax.axis_index("tm") == last, means_ref[end, :], offsets_ref[end, :])
+    states_ref[end, :] = state
     for t in reversed(range(steps - 1)):
         state = times(gain_ref[t], state) + offsets_ref[t : t + 1, :]
         states_ref[t : t + 1, :] = state
     send_ref[...] = state
+
+
+def smooth(state, gain_ref, offsets_ref, states_ref, send_ref):
+    for t in reversed(range(gain_ref.shape[0])):
+        state = times(gain_ref[t], state) + offsets_ref[t : t + 1, :]
+        states_ref[t : t + 1, :] = state
+    send_ref[...] = state
+
+
+def first_back_kernel(
+    places, last_ref, far_ref, near_ref, far_parts_ref, near_parts_ref, gain_ref, offsets_ref, kept_ref,
+    states_ref, send_ref,
+):
+    here = lax.axis_index("tm")
+
+    @pl.when(here == places - 4)
+    def _():
+        state = times_parts(far_parts_ref, last_ref[...]) + far_ref[...]
+        state = times_parts(near_parts_ref, state) + near_ref[...]
+        smooth(state, gain_ref, offsets_ref, states_ref, send_ref)
+
+    @pl.when(here == places - 2)
+    def _():
+        smooth(near_ref[...], gain_ref, offsets_ref, states_ref, send_ref)
+
+    @pl.when((here != places - 4) & (here != places - 2))
+    def _():
+        states_ref[...] = kept_ref[...]
+        send_ref[...] = near_ref[...]
+
+
+def back_kernel(
+    target, stray, two_ref, one_ref, near_ref, near_parts_ref, gain_ref, offsets_ref, kept_ref,
+    states_ref, send_ref,
+):
+    here = lax.axis_index("tm")
+
+    @pl.when(here == target)
+    def _():
+        state = times_parts(near_parts_ref, two_ref[...]) + near_ref[...]
+        smooth(state, gain_ref, offsets_ref, states_ref, send_ref)
+
+    @pl.when(here == target + 1)
+    def _():
+        smooth(one_ref[...], gain_ref, offsets_ref, states_ref, send_ref)
+
+    @pl.when(here == stray)
+    def _():
+        smooth(two_ref[...], gain_ref, offsets_ref, states_ref, send_ref)
+
+    @pl.when((here != target) & (here != target + 1) & (here != stray))
+    def _():
+        states_ref[...] = kept_ref[...]
+        send_ref[...] = two_ref[...]
 
 
 def call(kernel, name, outs, *args):
@@ -207,14 +292,16 @@
     )(*args)
 
 
-def hop(row, source, target, places):
-    pairs = []
-    for core in range(2):
-        pairs += [(source * 2 + core, target * 2 + core), (target * 2 + core, source * 2 + core)]
+def swap(row, pairs, places):
+    route = {}
     for place in range(places):
-        if place not in (source, target):
-            pairs += [(place * 2, place * 2 + 1), (place * 2 + 1, place * 2)]
-    return lax.ppermute(row, ("tm", "block"), pairs)
+        for core in range(2):
+            route[place * 2 + core] = place * 2 + 1 - core
+    for one, two in pairs:
+        for core in range(2):
+            route[one * 2 + core] = two * 2 + core
+            route[two * 2 + core] = one * 2 + core
+    return lax.ppermute(row, ("tm", "block"), sorted(route.items()))
 
 
 def local(
@@ -240,10 +327,13 @@
     inputs, means, send = call(
         inputs_kernel, "inputs", (many, many, one), mine, other, covariance, operator, initial_mean
     )
+    composed = call(compose_kernel, "compose", ((size, size),), mine, gain)[0]
+    near = lax.ppermute(composed, "tm", [(place + 1, place) for place in range(0, places, 2)])
+    far = lax.ppermute(composed, "tm", [(places - 2, places - 4)])
     for place in range(1, places):
-        came = hop(send, place - 1, place, places)
+        came = swap(send, [(place - 1, place)], places)
         means, send = call(
-            functools.partial(hop_kernel, place, False), "forward", (many, one), came, operator, inputs, means
+            functools.partial(hop_kernel, place), "forward", (many, one), came, operator, inputs, means
         )
     offsets, states, send = call(
         functools.partial(turn_kernel, places - 1),
@@ -253,10 +343,45 @@
         gain,
         propagator.reshape(size, size),
     )
-    for place in reversed(range(places - 1)):
-        came = hop(send, place + 1, place, places)
+    last = swap(send, [(places - 1, places - 4)], places)
+    far_offset = swap(send, [(places - 2, places - 4)], places)
+    near_offset = swap(send, [(place, place + 1) for place in range(0, places, 2)], places)
+    near_parts, far_parts = pl.pallas_call(
+        split_kernel,
+        out_shape=[jax.ShapeDtypeStruct((2, size, size), jnp.bfloat16)] * 2,
+        in_specs=[VMEM] * 2,
+        out_specs=[VMEM] * 2,
+        compiler_params=PARAMS,
+        name="split",
+    )(near, far)
+    states, send = call(
+        functools.partial(first_back_kernel, places),
+        "first_back",
+        (many, (1, size)),
+        last,
+        far_offset,
+        near_offset,
+        far_parts,
+        near_parts,
+        gain,
+        offsets,
+        states,
+    )
+    for target in range(places - 6, -1, -2):
+        stray = places - 3 if target == places - 6 else -1
+        two = swap(send, [(target + 2, target)] + ([(stray + 1, stray)] if stray >= 0 else []), places)
+        one = swap(send, [(target + 2, target + 1)], places)
         states, send = call(
-            functools.partial(hop_kernel, place, True), "backward", (many, one), came, gain, offsets, states
+            functools.partial(back_kernel, target, stray),
+            "back",
+            (many, (1, size)),
+            two,
+            one,
+            near_offset,
+            near_parts,
+            gain,
+            offsets,
+            states,
         )
     return (means.reshape(steps, 1, size), states.reshape(steps, 1, size))
 

time: 58.9 us -> 68.8 us (1.17)
  waiting for transfers between devices: 15.3 us -> 30.6 us
  starting transfers between devices: 35.6 us -> 29 us
  Pallas kernels: 5.95 us -> 7.07 us
    ppermute x14 -> x16, waiting for transfers between devices: 14.5 us -> 29.8 us  [the longest x14 29.8 us: swap(): return lax.ppermute(row, ('tm', 'block'), sorted(route.items()))]
    ppermute x14 -> x16, starting transfers between devices: 35 us -> 28.4 us  [the longest x14 26.4 us: swap(): return lax.ppermute(row, ('tm', 'block'), sorted(route.items()))]
    pallas_call x16 -> x13, Pallas kernels: 3.24 us -> 4.09 us  [call(): pl.pallas_call(kernel, out_shape=[jax.ShapeDtypeStruct(shape, jnp.float32...]
  transfers between devices with their start and end apart: 15 -> 17, of which waited for: 15 -> 12; matrix products, arithmetic and copies ran while one was open for 1% -> 1% of each run, Pallas kernels for 0% -> 4%
where the time goes in v3:
time: 68.8 us; the launch traced here: 68.6 us
  waiting for transfers between devices  30.6 us (44%)
  starting transfers between devices  29 us (42%)
  Pallas kernels  7.07 us (10%)
  local copies, waits for them, and re-layouts  1.21 us (2%)
  between operations  0.75 us (1%)
    ppermute x14, waiting for transfers between devices, swap(): return lax.ppermute(row, ('tm', 'block'), sorted(route.items()))  29.8 us
    ppermute x14, starting transfers between devices, swap(): return lax.ppermute(row, ('tm', 'block'), sorted(route.items()))  26.4 us
    pallas_call x13, Pallas kernels, call(): pl.pallas_call(kernel, out_shape=[jax.ShapeDtypeStruct(shape, jnp.float32...  4.09 us
    pallas_call x1, Pallas kernels, sensor_info(): pl.pallas_call(info_kernel, out_shape=[jax.ShapeDtypeStruct((steps, cells...  2.7 us
  transfers between devices with their start and end apart: 17, of which 12 were waited for; matrix products, arithmetic and copies ran while one was open for 1% of the time, Pallas kernels for 4%

profile of v3, /device:TPU:0, one launch (start us, length us, event | category | flops | bytes accessed | tf_op | source)
XLA Modules:
  0.0 68.6 jit_solution(16994531257305231896)
XLA Ops:
  0.7 2.7 %sensor_info.1 = (f32[2,512]{1,0:T(2,128)S(1)}, f32[2,512]{1,0:T(2,128)S(1)}) custom-call(bf16[2,1024,512]{2,1,0:T(8,128)(2,1)} %bitcast.26, bf16[7,7,16]{2,1,0:T(8,128)(2,1)} %bitcast.27, s32[2,64]{1,0:T(2,128)} %observed_hbm.1, s32[1,2]{1,0:T(1,128)} %bitcast.28), custom_call_target="tpu_custom_call" | custom-call | tf_op jit(solution)/shard_map/sensor_info/pallas_call | solution.py:128
  3.4 0.4 compose.1
  3.8 0.7 %collective-permute-start.12 = (f32[512,512]{1,0:T(8,128)S(1)}, f32[512,512]{1,0:T(8,128)S(1)}, u32[]{:S(2)}, u32[]{:S(2)}) collective-permute-start(f32[512,512]{1,0:T(8,128)S(1)} %compose.1), channel_id=1, source_target_pairs={{12,8},{13,9},{28,24},{29,25}} | collective-permute-start | bytes 3145736 | tf_op jit(solution)/shard_map/ppermute | solution.py:332
  4.6 1.3 %collective-permute-start.11 = (f32[512,512]{1,0:T(8,128)S(1)}, f32[512,512]{1,0:T(8,128)S(1)}, u32[]{:S(2)}, u32[]{:S(2)}) collective-permute-start(f32[512,512]{1,0:T(8,128)S(1)} %compose.1), channel_id=1, source_target_pairs={{2,0},{6,4},{10,8},{14,12},{3,1},{7,5},{11,9},{15,13},{18,16},{22,... | collective-permute-start | bytes 3145736 | tf_op jit(solution)/shard_map/ppermute | solution.py:331
  5.9 0.5 collective-permute-start
  6.4 0.8 %collective-permute-done.other_ref = f32[2,512]{1,0:T(2,128)S(1)} collective-permute-done((f32[2,512]{1,0:T(2,128)S(1)}, f32[2,512]{1,0:T(2,128)S(1)}, u32[]{:S(2)}, u32[]{:S(2)}) %collective-permute-start) | collective-permute-done | bytes 4128 | tf_op jit(solution)/shard_map/ppermute | solution.py:155
  7.2 0.7 inputs.1
  7.9 3.0 %collective-permute-start.1 = (f32[1,512]{1,0:T(1,128)S(1)}, f32[1,512]{1,0:T(1,128)S(1)}, u32[]{:S(2)}, u32[]{:S(2)}) collective-permute-start(f32[1,512]{1,0:T(1,128)S(1)} %get-tuple-element.32), channel_id=1, source_target_pairs={{0,2},{1,3},{2,0},{3,1},{4,5},{5,4},{6,7},{7,6},{8,9},{9,8},{10,11... | collective-permute-start | bytes 6152 | tf_op jit(solution)/shard_map/ppermute | solution.py:304
  10.9 21.1 %collective-permute-done.1.came_ref = f32[1,512]{1,0:T(1,128)S(1)} collective-permute-done((f32[1,512]{1,0:T(1,128)S(1)}, f32[1,512]{1,0:T(1,128)S(1)}, u32[]{:S(2)}, u32[]{:S(2)}) %collective-permute-start.1) | collective-permute-done | bytes 2080 | tf_op jit(solution)/shard_map/ppermute | solution.py:304
  32.0 1.2 %collective-permute-done.2.came_ref = f32[1,512]{1,0:T(1,128)S(1)} collective-permute-done((f32[1,512]{1,0:T(1,128)S(1)}, f32[1,512]{1,0:T(1,128)S(1)}, u32[]{:S(2)}, u32[]{:S(2)}) %collective-permute-start.2) | collective-permute-done | bytes 2080 | tf_op jit(solution)/shard_map/ppermute | solution.py:304
  33.4 1.0 %collective-permute-done.3.came_ref = f32[1,512]{1,0:T(1,128)S(1)} collective-permute-done((f32[1,512]{1,0:T(1,128)S(1)}, f32[1,512]{1,0:T(1,128)S(1)}, u32[]{:S(2)}, u32[]{:S(2)}) %collective-permute-start.3) | collective-permute-done | bytes 2080 | tf_op jit(solution)/shard_map/ppermute | solution.py:304
  34.5 1.0 %collective-permute-done.4.came_ref = f32[1,512]{1,0:T(1,128)S(1)} collective-permute-done((f32[1,512]{1,0:T(1,128)S(1)}, f32[1,512]{1,0:T(1,128)S(1)}, u32[]{:S(2)}, u32[]{:S(2)}) %collective-permute-start.4) | collective-permute-done | bytes 2080 | tf_op jit(solution)/shard_map/ppermute | solution.py:304
  35.5 0.2 collective-permute-start.5
  35.7 1.0 %collective-permute-done.5.came_ref = f32[1,512]{1,0:T(1,128)S(1)} collective-permute-done((f32[1,512]{1,0:T(1,128)S(1)}, f32[1,512]{1,0:T(1,128)S(1)}, u32[]{:S(2)}, u32[]{:S(2)}) %collective-permute-start.5) | collective-permute-done | bytes 2080 | tf_op jit(solution)/shard_map/ppermute | solution.py:304
  36.8 1.0 %collective-permute-done.6.came_ref = f32[1,512]{1,0:T(1,128)S(1)} collective-permute-done((f32[1,512]{1,0:T(1,128)S(1)}, f32[1,512]{1,0:T(1,128)S(1)}, u32[]{:S(2)}, u32[]{:S(2)}) %collective-permute-start.6) | collective-permute-done | bytes 2080 | tf_op jit(solution)/shard_map/ppermute | solution.py:304
  37.8 0.2 collective-permute-start.7
  38.0 1.0 %collective-permute-done.7.came_ref = f32[1,512]{1,0:T(1,128)S(1)} collective-permute-done((f32[1,512]{1,0:T(1,128)S(1)}, f32[1,512]{1,0:T(1,128)S(1)}, u32[]{:S(2)}, u32[]{:S(2)}) %collective-permute-start.7) | collective-permute-done | bytes 2080 | tf_op jit(solution)/shard_map/ppermute | solution.py:304
  39.0 0.6 forward.13
  39.6 1.0 %turn.1 = (f32[2,512]{1,0:T(2,128)S(1)}, f32[2,512]{1,0:T(2,128)S(1)}, f32[1,512]{1,0:T(1,128)S(1)}) custom-call(f32[2,512]{1,0:T(2,128)S(1)} %get-tuple-element.47.means_ref, bf16[2,512,512]{2,1,0:T(8,128)(2,1)S(1)} %bitcast.18, bf16[512,512]{1,0:T(8,128)(2,1)S(1)} %bitcast.23), custom_call_target="tpu_custom_call" | custom-call | tf_op jit(solution)/shard_map/turn/pallas_call | solution.py:285
  40.6 3.5 %collective-permute-start.10 = (f32[1,512]{1,0:T(1,128)S(1)}, f32[1,512]{1,0:T(1,128)S(1)}, u32[]{:S(2)}, u32[]{:S(2)}) collective-permute-start(f32[1,512]{1,0:T(1,128)S(1)} %get-tuple-element.48), channel_id=1, source_target_pairs={{0,2},{1,3},{2,0},{3,1},{4,6},{5,7},{6,4},{7,5},{8,10},{9,11},{10,... | collective-permute-start | bytes 6152 | tf_op jit(solution)/shard_map/ppermute | solution.py:304
  44.1 0.5 collective-permute-start.8
  44.6 0.3 split.1
  44.9 0.8 %collective-permute-done.10.near_ref = f32[1,512]{1,0:T(1,128)S(1)} collective-permute-done((f32[1,512]{1,0:T(1,128)S(1)}, f32[1,512]{1,0:T(1,128)S(1)}, u32[]{:S(2)}, u32[]{:S(2)}) %collective-permute-start.10) | collective-permute-done | bytes 2080 | tf_op jit(solution)/shard_map/ppermute | solution.py:304
  45.7 0.5 collective-permute-start.13
  46.2 0.6 collective-permute-done.14.one_ref
  46.9 0.2 collective-permute-done.13.two_ref
  47.0 0.3 collective-permute-start.16
  47.4 17.7 %collective-permute-start.15 = (f32[1,512]{1,0:T(1,128)S(1)}, f32[1,512]{1,0:T(1,128)S(1)}, u32[]{:S(2)}, u32[]{:S(2)}) collective-permute-start(f32[1,512]{1,0:T(1,128)S(1)} %get-tuple-element.55), channel_id=1, source_target_pairs={{0,4},{1,5},{2,3},{3,2},{4,0},{5,1},{6,7},{7,6},{8,9},{9,8},{10,11... | collective-permute-start | bytes 6152 | tf_op jit(solution)/shard_map/ppermute | solution.py:304
  65.0 0.6 copy.11
  65.6 1.0 %collective-permute-done.15.two_ref = f32[1,512]{1,0:T(1,128)S(1)} collective-permute-done((f32[1,512]{1,0:T(1,128)S(1)}, f32[1,512]{1,0:T(1,128)S(1)}, u32[]{:S(2)}, u32[]{:S(2)}) %collective-permute-start.15) | collective-permute-done | bytes 2080 | tf_op jit(solution)/shard_map/ppermute | solution.py:304
  66.6 1.4 %back.3 = (f32[2,512]{1,0:T(2,128)S(1)}, f32[1,512]{1,0:T(1,128)}) custom-call(f32[1,512]{1,0:T(1,128)S(1)} %collective-permute-done.15.two_ref, f32[1,512]{1,0:T(1,128)S(1)} %collective-permute-done.16.one_ref, f32[1,512]{1,0:T(1,128)S(1)} %collective-permute-done.10.near_ref, bf16[2,512,512]{2,1,0:T(8,128)(2,1)S(1)} %get-tuple-element.50.near_parts_ref, ...), custom_call_target="tpu_custom_call" | custom-call | tf_op jit(solution)/shard_map/back/pallas_call | solution.py:285
  68.0 0.6 copy.12
  (29 shorter events, 0.7 us)
Async XLA Ops:
  0.6 2.8 %copy-start.1 = (bf16[2,1,512,512]{3,2,1,0:T(8,128)(2,1)S(1)}, bf16[2,1,512,512]{3,2,1,0:T(8,128)(2,1)}, u32[]{:S(2)}) copy-start(bf16[2,1,512,512]{3,2,1,0:T(8,128)(2,1)} %param.15) | copy-start | bytes 3145732
  0.6 6.6 %copy-start = (bf16[2,1,512,512]{3,2,1,0:T(8,128)(2,1)S(1)}, bf16[2,1,512,512]{3,2,1,0:T(8,128)(2,1)}, u32[]{:S(2)}) copy-start(bf16[2,1,512,512]{3,2,1,0:T(8,128)(2,1)} %param.13) | copy-start | bytes 3145732
  0.7 6.6 %copy-start.2 = (bf16[2,1,512,512]{3,2,1,0:T(8,128)(2,1)S(1)}, bf16[2,1,512,512]{3,2,1,0:T(8,128)(2,1)}, u32[]{:S(2)}) copy-start(bf16[2,1,512,512]{3,2,1,0:T(8,128)(2,1)} %param.14) | copy-start | bytes 3145732
  0.7 6.6 %copy-start.4 = (f32[1,512]{1,0:T(1,128)S(1)}, f32[1,512]{1,0:T(1,128)}, u32[]{:S(2)}) copy-start(f32[1,512]{1,0:T(1,128)} %start_ref.1) | copy-start | bytes 6148
  3.8 40.7 %collective-permute-start.12 = (f32[512,512]{1,0:T(8,128)S(1)}, f32[512,512]{1,0:T(8,128)S(1)}, u32[]{:S(2)}, u32[]{:S(2)}) collective-permute-start(f32[512,512]{1,0:T(8,128)S(1)} %compose.1), channel_id=1, source_target_pairs={{12,8},{13,9},{28,24},{29,25}} | collective-permute-start | bytes 3145736 | tf_op jit(solution)/shard_map/ppermute | solution.py:332
  4.6 40.0 %collective-permute-start.11 = (f32[512,512]{1,0:T(8,128)S(1)}, f32[512,512]{1,0:T(8,128)S(1)}, u32[]{:S(2)}, u32[]{:S(2)}) collective-permute-start(f32[512,512]{1,0:T(8,128)S(1)} %compose.1), channel_id=1, source_target_pairs={{2,0},{6,4},{10,8},{14,12},{3,1},{7,5},{11,9},{15,13},{18,16},{22,... | collective-permute-start | bytes 3145736 | tf_op jit(solution)/shard_map/ppermute | solution.py:331
  5.9 1.3 %collective-permute-start = (f32[2,512]{1,0:T(2,128)S(1)}, f32[2,512]{1,0:T(2,128)S(1)}, u32[]{:S(2)}, u32[]{:S(2)}) collective-permute-start(f32[2,512]{1,0:T(2,128)S(1)} %get-tuple-element.31), channel_id=1, source_target_pairs={{0,1},{1,0},{2,3},{3,2},{4,5},{5,4},{6,7},{7,6},{8,9},{9,8},{10,11... | collective-permute-start | bytes 12296 | tf_op jit(solution)/shard_map/ppermute | solution.py:155
  7.9 24.1 %collective-permute-start.1 = (f32[1,512]{1,0:T(1,128)S(1)}, f32[1,512]{1,0:T(1,128)S(1)}, u32[]{:S(2)}, u32[]{:S(2)}) collective-permute-start(f32[1,512]{1,0:T(1,128)S(1)} %get-tuple-element.32), channel_id=1, source_target_pairs={{0,2},{1,3},{2,0},{3,1},{4,5},{5,4},{6,7},{7,6},{8,9},{9,8},{10,11... | collective-permute-start | bytes 6152 | tf_op jit(solution)/shard_map/ppermute | solution.py:304
  32.0 1.2 %collective-permute-start.2 = (f32[1,512]{1,0:T(1,128)S(1)}, f32[1,512]{1,0:T(1,128)S(1)}, u32[]{:S(2)}, u32[]{:S(2)}) collective-permute-start(f32[1,512]{1,0:T(1,128)S(1)} %get-tuple-element.35), channel_id=1, source_target_pairs={{0,1},{1,0},{2,4},{3,5},{4,2},{5,3},{6,7},{7,6},{8,9},{9,8},{10,11... | collective-permute-start | bytes 6152 | tf_op jit(solution)/shard_map/ppermute | solution.py:304
  33.2 1.2 %collective-permute-start.3 = (f32[1,512]{1,0:T(1,128)S(1)}, f32[1,512]{1,0:T(1,128)S(1)}, u32[]{:S(2)}, u32[]{:S(2)}) collective-permute-start(f32[1,512]{1,0:T(1,128)S(1)} %get-tuple-element.37), channel_id=1, source_target_pairs={{0,1},{1,0},{2,3},{3,2},{4,6},{5,7},{6,4},{7,5},{8,9},{9,8},{10,11... | collective-permute-start | bytes 6152 | tf_op jit(solution)/shard_map/ppermute | solution.py:304
  34.3 1.2 %collective-permute-start.4 = (f32[1,512]{1,0:T(1,128)S(1)}, f32[1,512]{1,0:T(1,128)S(1)}, u32[]{:S(2)}, u32[]{:S(2)}) collective-permute-start(f32[1,512]{1,0:T(1,128)S(1)} %get-tuple-element.39), channel_id=1, source_target_pairs={{0,1},{1,0},{2,3},{3,2},{4,5},{5,4},{6,8},{7,9},{8,6},{9,7},{10,11... | collective-permute-start | bytes 6152 | tf_op jit(solution)/shard_map/ppermute | solution.py:304
  35.5 4.1 %copy-start.3 = (bf16[1,512,512]{2,1,0:T(8,128)(2,1)S(1)}, bf16[1,512,512]{2,1,0:T(8,128)(2,1)}, u32[]{:S(2)}) copy-start(bf16[1,512,512]{2,1,0:T(8,128)(2,1)} %param.16) | copy-start | bytes 1572868
  35.5 1.2 %collective-permute-start.5 = (f32[1,512]{1,0:T(1,128)S(1)}, f32[1,512]{1,0:T(1,128)S(1)}, u32[]{:S(2)}, u32[]{:S(2)}) collective-permute-start(f32[1,512]{1,0:T(1,128)S(1)} %get-tuple-element.41), channel_id=1, source_target_pairs={{0,1},{1,0},{2,3},{3,2},{4,5},{5,4},{6,7},{7,6},{8,10},{9,11},{10,... | collective-permute-start | bytes 6152 | tf_op jit(solution)/shard_map/ppermute | solution.py:304
  36.7 1.2 %collective-permute-start.6 = (f32[1,512]{1,0:T(1,128)S(1)}, f32[1,512]{1,0:T(1,128)S(1)}, u32[]{:S(2)}, u32[]{:S(2)}) collective-permute-start(f32[1,512]{1,0:T(1,128)S(1)} %get-tuple-element.43), channel_id=1, source_target_pairs={{0,1},{1,0},{2,3},{3,2},{4,5},{5,4},{6,7},{7,6},{8,9},{9,8},{10,12... | collective-permute-start | bytes 6152 | tf_op jit(solution)/shard_map/ppermute | solution.py:304
  37.8 1.2 %collective-permute-start.7 = (f32[1,512]{1,0:T(1,128)S(1)}, f32[1,512]{1,0:T(1,128)S(1)}, u32[]{:S(2)}, u32[]{:S(2)}) collective-permute-start(f32[1,512]{1,0:T(1,128)S(1)} %get-tuple-element.45), channel_id=1, source_target_pairs={{0,1},{1,0},{2,3},{3,2},{4,5},{5,4},{6,7},{7,6},{8,9},{9,8},{10,11... | collective-permute-start | bytes 6152 | tf_op jit(solution)/shard_map/ppermute | solution.py:304
  40.6 5.0 %collective-permute-start.10 = (f32[1,512]{1,0:T(1,128)S(1)}, f32[1,512]{1,0:T(1,128)S(1)}, u32[]{:S(2)}, u32[]{:S(2)}) collective-permute-start(f32[1,512]{1,0:T(1,128)S(1)} %get-tuple-element.48), channel_id=1, source_target_pairs={{0,2},{1,3},{2,0},{3,1},{4,6},{5,7},{6,4},{7,5},{8,10},{9,11},{10,... | collective-permute-start | bytes 6152 | tf_op jit(solution)/shard_map/ppermute | solution.py:304
  44.1 1.6 %collective-permute-start.9 = (f32[1,512]{1,0:T(1,128)S(1)}, f32[1,512]{1,0:T(1,128)S(1)}, u32[]{:S(2)}, u32[]{:S(2)}) collective-permute-start(f32[1,512]{1,0:T(1,128)S(1)} %get-tuple-element.48), channel_id=1, source_target_pairs={{0,1},{1,0},{2,3},{3,2},{4,5},{5,4},{6,7},{7,6},{8,12},{9,13},{10,... | collective-permute-start | bytes 6152 | tf_op jit(solution)/shard_map/ppermute | solution.py:304
  44.1 1.6 %collective-permute-start.8 = (f32[1,512]{1,0:T(1,128)S(1)}, f32[1,512]{1,0:T(1,128)S(1)}, u32[]{:S(2)}, u32[]{:S(2)}) collective-permute-start(f32[1,512]{1,0:T(1,128)S(1)} %get-tuple-element.48), channel_id=1, source_target_pairs={{0,1},{1,0},{2,3},{3,2},{4,5},{5,4},{6,7},{7,6},{8,14},{9,15},{10,... | collective-permute-start | bytes 6152 | tf_op jit(solution)/shard_map/ppermute | solution.py:304
  45.6 1.2 %collective-permute-start.14 = (f32[1,512]{1,0:T(1,128)S(1)}, f32[1,512]{1,0:T(1,128)S(1)}, u32[]{:S(2)}, u32[]{:S(2)}) collective-permute-start(f32[1,512]{1,0:T(1,128)S(1)} %get-tuple-element.53), channel_id=1, source_target_pairs={{0,1},{1,0},{2,3},{3,2},{4,5},{5,4},{6,8},{7,9},{8,6},{9,7},{10,11... | collective-permute-start | bytes 6152 | tf_op jit(solution)/shard_map/ppermute | solution.py:304
  45.7 1.3 %collective-permute-start.13 = (f32[1,512]{1,0:T(1,128)S(1)}, f32[1,512]{1,0:T(1,128)S(1)}, u32[]{:S(2)}, u32[]{:S(2)}) collective-permute-start(f32[1,512]{1,0:T(1,128)S(1)} %get-tuple-element.53), channel_id=1, source_target_pairs={{0,1},{1,0},{2,3},{3,2},{4,8},{5,9},{6,7},{7,6},{8,4},{9,5},{10,12... | collective-permute-start | bytes 6152 | tf_op jit(solution)/shard_map/ppermute | solution.py:304
  47.0 18.6 %collective-permute-start.16 = (f32[1,512]{1,0:T(1,128)S(1)}, f32[1,512]{1,0:T(1,128)S(1)}, u32[]{:S(2)}, u32[]{:S(2)}) collective-permute-start(f32[1,512]{1,0:T(1,128)S(1)} %get-tuple-element.55), channel_id=1, source_target_pairs={{0,1},{1,0},{2,4},{3,5},{4,2},{5,3},{6,7},{7,6},{8,9},{9,8},{10,11... | collective-permute-start | bytes 6152 | tf_op jit(solution)/shard_map/ppermute | solution.py:304
  47.4 19.2 %collective-permute-start.15 = (f32[1,512]{1,0:T(1,128)S(1)}, f32[1,512]{1,0:T(1,128)S(1)}, u32[]{:S(2)}, u32[]{:S(2)}) collective-permute-start(f32[1,512]{1,0:T(1,128)S(1)} %get-tuple-element.55), channel_id=1, source_target_pairs={{0,4},{1,5},{2,3},{3,2},{4,0},{5,1},{6,7},{7,6},{8,9},{9,8},{10,11... | collective-permute-start | bytes 6152 | tf_op jit(solution)/shard_map/ppermute | solution.py:304

commit v4 on v3

--- a/solution.py
+++ b/solution.py
@@ -292,16 +292,22 @@
     )(*args)
 
 
-def swap(row, pairs, places):
+def pass_row(row, rings, places):
     route = {}
     for place in range(places):
         for core in range(2):
             route[place * 2 + core] = place * 2 + 1 - core
-    for one, two in pairs:
-        for core in range(2):
-            route[one * 2 + core] = two * 2 + core
-            route[two * 2 + core] = one * 2 + core
+    for ring in rings:
+        for i, place in enumerate(ring):
+            for core in range(2):
+                route[place * 2 + core] = ring[(i + 1) % len(ring)] * 2 + core
     return lax.ppermute(row, ("tm", "block"), sorted(route.items()))
+
+
+def ring_up(place, places):
+    if place % 2 or place == places - 2:
+        return (place, place + 1)
+    return (place, place + 1, place - 2 if place else 2)
 
 
 def local(
@@ -327,11 +333,11 @@
     inputs, means, send = call(
         inputs_kernel, "inputs", (many, many, one), mine, other, covariance, operator, initial_mean
     )
-    composed = call(compose_kernel, "compose", ((size, size),), mine, gain)[0]
-    near = lax.ppermute(composed, "tm", [(place + 1, place) for place in range(0, places, 2)])
+    composed = call(compose_kernel, "compose", ((size, size),), send, gain)[0]
+    near = lax.ppermute(composed, "tm", [(place + 1, place) for place in range(0, places - 2, 2)])
     far = lax.ppermute(composed, "tm", [(places - 2, places - 4)])
     for place in range(1, places):
-        came = swap(send, [(place - 1, place)], places)
+        came = pass_row(send, [ring_up(place - 1, places)], places)
         means, send = call(
             functools.partial(hop_kernel, place), "forward", (many, one), came, operator, inputs, means
         )
@@ -343,9 +349,9 @@
         gain,
         propagator.reshape(size, size),
     )
-    last = swap(send, [(places - 1, places - 4)], places)
-    far_offset = swap(send, [(places - 2, places - 4)], places)
-    near_offset = swap(send, [(place, place + 1) for place in range(0, places, 2)], places)
+    last = pass_row(send, [(places - 1, places - 4)], places)
+    far_offset = pass_row(send, [(places - 2, places - 4)], places)
+    near_offset = pass_row(send, [(place, place + 1) for place in range(0, places, 2)], places)
     near_parts, far_parts = pl.pallas_call(
         split_kernel,
         out_shape=[jax.ShapeDtypeStruct((2, size, size), jnp.bfloat16)] * 2,
@@ -369,8 +375,8 @@
     )
     for target in range(places - 6, -1, -2):
         stray = places - 3 if target == places - 6 else -1
-        two = swap(send, [(target + 2, target)] + ([(stray + 1, stray)] if stray >= 0 else []), places)
-        one = swap(send, [(target + 2, target + 1)], places)
+        two = pass_row(send, [(target + 2, target)] + ([(stray + 1, stray)] if stray >= 0 else []), places)
+        one = pass_row(send, [(target + 2, target + 1)], places)
         states, send = call(
             functools.partial(back_kernel, target, stray),
             "back",

time: 68.8 us -> 55.3 us (0.80)
  waiting for transfers between devices: 30.6 us -> 16.2 us
  starting transfers between devices: 29 us -> 29.8 us
    ppermute x14, waiting for transfers between devices: 29.8 us -> 9.91 us  [pass_row(): return lax.ppermute(row, ('tm', 'block'), sorted(route.items()))]
    ppermute x1, waiting for transfers between devices: 0.01 us -> 5.47 us  [local(): lax.ppermute(composed, 'tm', [(place + 1, place) for place in range(0, pl...]
    ppermute x14, starting transfers between devices: 26.4 us -> 27.3 us  [pass_row(): return lax.ppermute(row, ('tm', 'block'), sorted(route.items()))]
  transfers between devices with their start and end apart: 17 -> 17, of which waited for: 12 -> 12; matrix products, arithmetic and copies ran while one was open for 1% -> 1% of each run, Pallas kernels for 4% -> 3%
where the time goes in v4:
time: 55.3 us; the launch traced here: 55.1 us
  starting transfers between devices  29.8 us (54%)
  waiting for transfers between devices  16.2 us (29%)
  Pallas kernels  7.1 us (13%)
  local copies, waits for them, and re-layouts  1.21 us (2%)
  between operations  0.79 us (1%)
    ppermute x14, starting transfers between devices, pass_row(): return lax.ppermute(row, ('tm', 'block'), sorted(route.items()))  27.3 us
    ppermute x14, waiting for transfers between devices, pass_row(): return lax.ppermute(row, ('tm', 'block'), sorted(route.items()))  9.91 us
    ppermute x1, waiting for transfers between devices, local(): lax.ppermute(composed, 'tm', [(place + 1, place) for place in range(0, pl...  5.47 us
    pallas_call x13, Pallas kernels, call(): pl.pallas_call(kernel, out_shape=[jax.ShapeDtypeStruct(shape, jnp.float32...  4.12 us
    pallas_call x1, Pallas kernels, sensor_info(): pl.pallas_call(info_kernel, out_shape=[jax.ShapeDtypeStruct((steps, cells...  2.71 us
    ppermute x1, starting transfers between devices, local(): lax.ppermute(composed, 'tm', [(place + 1, place) for place in range(0, pl...  1.29 us
    unnamed x12, local copies, waits for them, and re-layouts  1.21 us
  transfers between devices with their start and end apart: 17, of which 12 were waited for; matrix products, arithmetic and copies ran while one was open for 1% of the time, Pallas kernels for 3%

profile of v4, /device:TPU:0, one launch (start us, length us, event | category | flops | bytes accessed | tf_op | source)
XLA Modules:
  0.0 55.1 jit_solution(16981384645172201045)
XLA Ops:
  0.7 2.7 %sensor_info.1 = (f32[2,512]{1,0:T(2,128)S(1)}, f32[2,512]{1,0:T(2,128)S(1)}) custom-call(bf16[2,1024,512]{2,1,0:T(8,128)(2,1)} %bitcast.26, bf16[7,7,16]{2,1,0:T(8,128)(2,1)} %bitcast.27, s32[2,64]{1,0:T(2,128)} %observed_hbm.1, s32[1,2]{1,0:T(1,128)} %bitcast.28), custom_call_target="tpu_custom_call" | custom-call | tf_op jit(solution)/shard_map/sensor_info/pallas_call | solution.py:128
  3.4 0.5 collective-permute-start
  3.9 0.8 %collective-permute-done.other_ref = f32[2,512]{1,0:T(2,128)S(1)} collective-permute-done((f32[2,512]{1,0:T(2,128)S(1)}, f32[2,512]{1,0:T(2,128)S(1)}, u32[]{:S(2)}, u32[]{:S(2)}) %collective-permute-start) | collective-permute-done | bytes 4128 | tf_op jit(solution)/shard_map/ppermute | solution.py:155
  4.7 0.7 %inputs.1 = (f32[2,512]{1,0:T(2,128)S(1)}, f32[2,512]{1,0:T(2,128)S(1)}, f32[1,512]{1,0:T(1,128)S(1)}) custom-call(f32[2,512]{1,0:T(2,128)S(1)} %get-tuple-element.30.mine_ref, f32[2,512]{1,0:T(2,128)S(1)} %collective-permute-done.other_ref, bf16[2,512,512]{2,1,0:T(8,128)(2,1)S(1)} %bitcast.22, bf16[2,512,512]{2,1,0:T(8,128)(2,1)S(1)} %bitcast.9, ...), custom_call_target="tpu_custom_call" | custom-call | tf_op jit(solution)/shard_map/inputs/pallas_call | solution.py:285
  5.4 0.4 compose.1
  5.9 0.7 %collective-permute-start.12 = (f32[512,512]{1,0:T(8,128)S(1)}, f32[512,512]{1,0:T(8,128)S(1)}, u32[]{:S(2)}, u32[]{:S(2)}) collective-permute-start(f32[512,512]{1,0:T(8,128)S(1)} %compose.1), channel_id=1, source_target_pairs={{12,8},{13,9},{28,24},{29,25}} | collective-permute-start | bytes 3145736 | tf_op jit(solution)/shard_map/ppermute | solution.py:338
  6.6 1.3 %collective-permute-start.11 = (f32[512,512]{1,0:T(8,128)S(1)}, f32[512,512]{1,0:T(8,128)S(1)}, u32[]{:S(2)}, u32[]{:S(2)}) collective-permute-start(f32[512,512]{1,0:T(8,128)S(1)} %compose.1), channel_id=1, source_target_pairs={{2,0},{6,4},{10,8},{3,1},{7,5},{11,9},{18,16},{22,20},{26,24},{19,... | collective-permute-start | bytes 3145736 | tf_op jit(solution)/shard_map/ppermute | solution.py:337
  7.9 3.0 %collective-permute-start.1 = (f32[1,512]{1,0:T(1,128)S(1)}, f32[1,512]{1,0:T(1,128)S(1)}, u32[]{:S(2)}, u32[]{:S(2)}) collective-permute-start(f32[1,512]{1,0:T(1,128)S(1)} %get-tuple-element.32.after_ref), channel_id=1, source_target_pairs={{0,2},{1,3},{2,4},{3,5},{4,0},{5,1},{6,7},{7,6},{8,9},{9,8},{10,11... | collective-permute-start | bytes 6152 | tf_op jit(solution)/shard_map/ppermute | solution.py:304
  10.9 1.6 %collective-permute-done.1.came_ref = f32[1,512]{1,0:T(1,128)S(1)} collective-permute-done((f32[1,512]{1,0:T(1,128)S(1)}, f32[1,512]{1,0:T(1,128)S(1)}, u32[]{:S(2)}, u32[]{:S(2)}) %collective-permute-start.1) | collective-permute-done | bytes 2080 | tf_op jit(solution)/shard_map/ppermute | solution.py:304
  12.5 1.2 %collective-permute-done.2.came_ref = f32[1,512]{1,0:T(1,128)S(1)} collective-permute-done((f32[1,512]{1,0:T(1,128)S(1)}, f32[1,512]{1,0:T(1,128)S(1)}, u32[]{:S(2)}, u32[]{:S(2)}) %collective-permute-start.2) | collective-permute-done | bytes 2080 | tf_op jit(solution)/shard_map/ppermute | solution.py:304
  13.6 7.0 %collective-permute-start.3 = (f32[1,512]{1,0:T(1,128)S(1)}, f32[1,512]{1,0:T(1,128)S(1)}, u32[]{:S(2)}, u32[]{:S(2)}) collective-permute-start(f32[1,512]{1,0:T(1,128)S(1)} %get-tuple-element.37), channel_id=1, source_target_pairs={{0,4},{1,5},{2,3},{3,2},{4,6},{5,7},{6,0},{7,1},{8,9},{9,8},{10,11... | collective-permute-start | bytes 6152 | tf_op jit(solution)/shard_map/ppermute | solution.py:304
  20.6 1.3 %collective-permute-done.3.came_ref = f32[1,512]{1,0:T(1,128)S(1)} collective-permute-done((f32[1,512]{1,0:T(1,128)S(1)}, f32[1,512]{1,0:T(1,128)S(1)}, u32[]{:S(2)}, u32[]{:S(2)}) %collective-permute-start.3) | collective-permute-done | bytes 2080 | tf_op jit(solution)/shard_map/ppermute | solution.py:304
  21.9 1.2 %collective-permute-done.4.came_ref = f32[1,512]{1,0:T(1,128)S(1)} collective-permute-done((f32[1,512]{1,0:T(1,128)S(1)}, f32[1,512]{1,0:T(1,128)S(1)}, u32[]{:S(2)}, u32[]{:S(2)}) %collective-permute-start.4) | collective-permute-done | bytes 2080 | tf_op jit(solution)/shard_map/ppermute | solution.py:304
  23.1 0.2 collective-permute-start.5
  23.3 1.0 %collective-permute-done.5.came_ref = f32[1,512]{1,0:T(1,128)S(1)} collective-permute-done((f32[1,512]{1,0:T(1,128)S(1)}, f32[1,512]{1,0:T(1,128)S(1)}, u32[]{:S(2)}, u32[]{:S(2)}) %collective-permute-start.5) | collective-permute-done | bytes 2080 | tf_op jit(solution)/shard_map/ppermute | solution.py:304
  24.2 0.2 collective-permute-start.6
  24.4 1.0 %collective-permute-done.6.came_ref = f32[1,512]{1,0:T(1,128)S(1)} collective-permute-done((f32[1,512]{1,0:T(1,128)S(1)}, f32[1,512]{1,0:T(1,128)S(1)}, u32[]{:S(2)}, u32[]{:S(2)}) %collective-permute-start.6) | collective-permute-done | bytes 2080 | tf_op jit(solution)/shard_map/ppermute | solution.py:304
  25.6 1.0 %collective-permute-done.7.came_ref = f32[1,512]{1,0:T(1,128)S(1)} collective-permute-done((f32[1,512]{1,0:T(1,128)S(1)}, f32[1,512]{1,0:T(1,128)S(1)}, u32[]{:S(2)}, u32[]{:S(2)}) %collective-permute-start.7) | collective-permute-done | bytes 2080 | tf_op jit(solution)/shard_map/ppermute | solution.py:304
  26.6 0.6 %forward.13 = (f32[2,512]{1,0:T(2,128)S(1)}, f32[1,512]{1,0:T(1,128)}) custom-call(f32[1,512]{1,0:T(1,128)S(1)} %collective-permute-done.7.came_ref, bf16[2,512,512]{2,1,0:T(8,128)(2,1)S(1)} %bitcast.16, f32[2,512]{1,0:T(2,128)S(1)} %get-tuple-element.33.offsets_ref, f32[2,512]{1,0:T(2,128)S(1)} %get-tuple-element.46.kept_ref), custom_call_target="tpu_custom_call" | custom-call | tf_op jit(solution)/shard_map/forward/pallas_call | solution.py:285
  27.1 1.0 %turn.1 = (f32[2,512]{1,0:T(2,128)S(1)}, f32[2,512]{1,0:T(2,128)S(1)}, f32[1,512]{1,0:T(1,128)S(1)}) custom-call(f32[2,512]{1,0:T(2,128)S(1)} %get-tuple-element.47.means_ref, bf16[2,512,512]{2,1,0:T(8,128)(2,1)S(1)} %bitcast.18, bf16[512,512]{1,0:T(8,128)(2,1)S(1)} %bitcast.23), custom_call_target="tpu_custom_call" | custom-call | tf_op jit(solution)/shard_map/turn/pallas_call | solution.py:285
  28.2 0.2 collective-permute-start.9
  28.5 0.3 collective-permute-start.8
  28.8 5.5 %collective-permute-done.11.near_ref = f32[512,512]{1,0:T(8,128)S(1)} collective-permute-done((f32[512,512]{1,0:T(8,128)S(1)}, f32[512,512]{1,0:T(8,128)S(1)}, u32[]{:S(2)}, u32[]{:S(2)}) %collective-permute-start.11) | collective-permute-done | bytes 1048608 | tf_op jit(solution)/shard_map/ppermute | solution.py:337
  34.3 0.3 split.1
  34.7 0.5 collective-permute-start.13
  35.2 0.6 %collective-permute-done.14.one_ref = f32[1,512]{1,0:T(1,128)S(1)} collective-permute-done((f32[1,512]{1,0:T(1,128)S(1)}, f32[1,512]{1,0:T(1,128)S(1)}, u32[]{:S(2)}, u32[]{:S(2)}) %collective-permute-start.14) | collective-permute-done | bytes 2080 | tf_op jit(solution)/shard_map/ppermute | solution.py:304
  36.0 0.3 collective-permute-start.16
  36.4 15.2 %collective-permute-start.15 = (f32[1,512]{1,0:T(1,128)S(1)}, f32[1,512]{1,0:T(1,128)S(1)}, u32[]{:S(2)}, u32[]{:S(2)}) collective-permute-start(f32[1,512]{1,0:T(1,128)S(1)} %get-tuple-element.55), channel_id=1, source_target_pairs={{0,4},{1,5},{2,3},{3,2},{4,0},{5,1},{6,7},{7,6},{8,9},{9,8},{10,11... | collective-permute-start | bytes 6152 | tf_op jit(solution)/shard_map/ppermute | solution.py:304
  51.6 0.6 %copy.11 = f32[2,1,512]{2,1,0:T(1,128)} copy(f32[2,1,512]{2,0,1:T(2,128)S(1)} %bitcast.24) | data formatting | bytes 8192
  52.2 1.0 %collective-permute-done.15.two_ref = f32[1,512]{1,0:T(1,128)S(1)} collective-permute-done((f32[1,512]{1,0:T(1,128)S(1)}, f32[1,512]{1,0:T(1,128)S(1)}, u32[]{:S(2)}, u32[]{:S(2)}) %collective-permute-start.15) | collective-permute-done | bytes 2080 | tf_op jit(solution)/shard_map/ppermute | solution.py:304
  53.2 1.4 %back.3 = (f32[2,512]{1,0:T(2,128)S(1)}, f32[1,512]{1,0:T(1,128)}) custom-call(f32[1,512]{1,0:T(1,128)S(1)} %collective-permute-done.15.two_ref, f32[1,512]{1,0:T(1,128)S(1)} %collective-permute-done.16.one_ref, f32[1,512]{1,0:T(1,128)S(1)} %collective-permute-done.10.near_ref, bf16[2,512,512]{2,1,0:T(8,128)(2,1)S(1)} %get-tuple-element.50.near_parts_ref, ...), custom_call_target="tpu_custom_call" | custom-call | tf_op jit(solution)/shard_map/back/pallas_call | solution.py:285
  54.6 0.6 %copy.12 = f32[2,1,512]{2,1,0:T(1,128)} copy(f32[2,1,512]{2,0,1:T(2,128)S(1)} %bitcast.25) | data formatting | bytes 8192
  (29 shorter events, 0.6 us)
Async XLA Ops:
  0.6 4.1 %copy-start.4 = (f32[1,512]{1,0:T(1,128)S(1)}, f32[1,512]{1,0:T(1,128)}, u32[]{:S(2)}) copy-start(f32[1,512]{1,0:T(1,128)} %start_ref.1) | copy-start | bytes 6148
  0.6 4.1 %copy-start.2 = (bf16[2,1,512,512]{3,2,1,0:T(8,128)(2,1)S(1)}, bf16[2,1,512,512]{3,2,1,0:T(8,128)(2,1)}, u32[]{:S(2)}) copy-start(bf16[2,1,512,512]{3,2,1,0:T(8,128)(2,1)} %param.14) | copy-start | bytes 3145732
  0.7 4.1 %copy-start = (bf16[2,1,512,512]{3,2,1,0:T(8,128)(2,1)S(1)}, bf16[2,1,512,512]{3,2,1,0:T(8,128)(2,1)}, u32[]{:S(2)}) copy-start(bf16[2,1,512,512]{3,2,1,0:T(8,128)(2,1)} %param.13) | copy-start | bytes 3145732
  0.7 4.7 %copy-start.1 = (bf16[2,1,512,512]{3,2,1,0:T(8,128)(2,1)S(1)}, bf16[2,1,512,512]{3,2,1,0:T(8,128)(2,1)}, u32[]{:S(2)}) copy-start(bf16[2,1,512,512]{3,2,1,0:T(8,128)(2,1)} %param.15) | copy-start | bytes 3145732
  3.4 1.3 %collective-permute-start = (f32[2,512]{1,0:T(2,128)S(1)}, f32[2,512]{1,0:T(2,128)S(1)}, u32[]{:S(2)}, u32[]{:S(2)}) collective-permute-start(f32[2,512]{1,0:T(2,128)S(1)} %get-tuple-element.31), channel_id=1, source_target_pairs={{0,1},{1,0},{2,3},{3,2},{4,5},{5,4},{6,7},{7,6},{8,9},{9,8},{10,11... | collective-permute-start | bytes 12296 | tf_op jit(solution)/shard_map/ppermute | solution.py:155
  5.9 23.0 %collective-permute-start.12 = (f32[512,512]{1,0:T(8,128)S(1)}, f32[512,512]{1,0:T(8,128)S(1)}, u32[]{:S(2)}, u32[]{:S(2)}) collective-permute-start(f32[512,512]{1,0:T(8,128)S(1)} %compose.1), channel_id=1, source_target_pairs={{12,8},{13,9},{28,24},{29,25}} | collective-permute-start | bytes 3145736 | tf_op jit(solution)/shard_map/ppermute | solution.py:338
  6.6 27.7 %collective-permute-start.11 = (f32[512,512]{1,0:T(8,128)S(1)}, f32[512,512]{1,0:T(8,128)S(1)}, u32[]{:S(2)}, u32[]{:S(2)}) collective-permute-start(f32[512,512]{1,0:T(8,128)S(1)} %compose.1), channel_id=1, source_target_pairs={{2,0},{6,4},{10,8},{3,1},{7,5},{11,9},{18,16},{22,20},{26,24},{19,... | collective-permute-start | bytes 3145736 | tf_op jit(solution)/shard_map/ppermute | solution.py:337
  7.9 4.6 %collective-permute-start.1 = (f32[1,512]{1,0:T(1,128)S(1)}, f32[1,512]{1,0:T(1,128)S(1)}, u32[]{:S(2)}, u32[]{:S(2)}) collective-permute-start(f32[1,512]{1,0:T(1,128)S(1)} %get-tuple-element.32.after_ref), channel_id=1, source_target_pairs={{0,2},{1,3},{2,4},{3,5},{4,0},{5,1},{6,7},{7,6},{8,9},{9,8},{10,11... | collective-permute-start | bytes 6152 | tf_op jit(solution)/shard_map/ppermute | solution.py:304
  12.5 1.2 %collective-permute-start.2 = (f32[1,512]{1,0:T(1,128)S(1)}, f32[1,512]{1,0:T(1,128)S(1)}, u32[]{:S(2)}, u32[]{:S(2)}) collective-permute-start(f32[1,512]{1,0:T(1,128)S(1)} %get-tuple-element.35), channel_id=1, source_target_pairs={{0,1},{1,0},{2,4},{3,5},{4,2},{5,3},{6,7},{7,6},{8,9},{9,8},{10,11... | collective-permute-start | bytes 6152 | tf_op jit(solution)/shard_map/ppermute | solution.py:304
  13.6 8.3 %collective-permute-start.3 = (f32[1,512]{1,0:T(1,128)S(1)}, f32[1,512]{1,0:T(1,128)S(1)}, u32[]{:S(2)}, u32[]{:S(2)}) collective-permute-start(f32[1,512]{1,0:T(1,128)S(1)} %get-tuple-element.37), channel_id=1, source_target_pairs={{0,4},{1,5},{2,3},{3,2},{4,6},{5,7},{6,0},{7,1},{8,9},{9,8},{10,11... | collective-permute-start | bytes 6152 | tf_op jit(solution)/shard_map/ppermute | solution.py:304
  21.9 1.2 %collective-permute-start.4 = (f32[1,512]{1,0:T(1,128)S(1)}, f32[1,512]{1,0:T(1,128)S(1)}, u32[]{:S(2)}, u32[]{:S(2)}) collective-permute-start(f32[1,512]{1,0:T(1,128)S(1)} %get-tuple-element.39), channel_id=1, source_target_pairs={{0,1},{1,0},{2,3},{3,2},{4,5},{5,4},{6,8},{7,9},{8,6},{9,7},{10,11... | collective-permute-start | bytes 6152 | tf_op jit(solution)/shard_map/ppermute | solution.py:304
  23.1 4.1 %copy-start.3 = (bf16[1,512,512]{2,1,0:T(8,128)(2,1)S(1)}, bf16[1,512,512]{2,1,0:T(8,128)(2,1)}, u32[]{:S(2)}) copy-start(bf16[1,512,512]{2,1,0:T(8,128)(2,1)} %param.16) | copy-start | bytes 1572868
  23.1 1.2 %collective-permute-start.5 = (f32[1,512]{1,0:T(1,128)S(1)}, f32[1,512]{1,0:T(1,128)S(1)}, u32[]{:S(2)}, u32[]{:S(2)}) collective-permute-start(f32[1,512]{1,0:T(1,128)S(1)} %get-tuple-element.41), channel_id=1, source_target_pairs={{0,1},{1,0},{2,3},{3,2},{4,8},{5,9},{6,7},{7,6},{8,10},{9,11},{10,... | collective-permute-start | bytes 6152 | tf_op jit(solution)/shard_map/ppermute | solution.py:304
  24.2 1.2 %collective-permute-start.6 = (f32[1,512]{1,0:T(1,128)S(1)}, f32[1,512]{1,0:T(1,128)S(1)}, u32[]{:S(2)}, u32[]{:S(2)}) collective-permute-start(f32[1,512]{1,0:T(1,128)S(1)} %get-tuple-element.43), channel_id=1, source_target_pairs={{0,1},{1,0},{2,3},{3,2},{4,5},{5,4},{6,7},{7,6},{8,9},{9,8},{10,12... | collective-permute-start | bytes 6152 | tf_op jit(solution)/shard_map/ppermute | solution.py:304
  25.4 1.2 %collective-permute-start.7 = (f32[1,512]{1,0:T(1,128)S(1)}, f32[1,512]{1,0:T(1,128)S(1)}, u32[]{:S(2)}, u32[]{:S(2)}) collective-permute-start(f32[1,512]{1,0:T(1,128)S(1)} %get-tuple-element.45), channel_id=1, source_target_pairs={{0,1},{1,0},{2,3},{3,2},{4,5},{5,4},{6,7},{7,6},{8,9},{9,8},{10,11... | collective-permute-start | bytes 6152 | tf_op jit(solution)/shard_map/ppermute | solution.py:304
  28.2 6.4 %collective-permute-start.10 = (f32[1,512]{1,0:T(1,128)S(1)}, f32[1,512]{1,0:T(1,128)S(1)}, u32[]{:S(2)}, u32[]{:S(2)}) collective-permute-start(f32[1,512]{1,0:T(1,128)S(1)} %get-tuple-element.48), channel_id=1, source_target_pairs={{0,2},{1,3},{2,0},{3,1},{4,6},{5,7},{6,4},{7,5},{8,10},{9,11},{10,... | collective-permute-start | bytes 6152 | tf_op jit(solution)/shard_map/ppermute | solution.py:304
  28.2 6.3 %collective-permute-start.9 = (f32[1,512]{1,0:T(1,128)S(1)}, f32[1,512]{1,0:T(1,128)S(1)}, u32[]{:S(2)}, u32[]{:S(2)}) collective-permute-start(f32[1,512]{1,0:T(1,128)S(1)} %get-tuple-element.48), channel_id=1, source_target_pairs={{0,1},{1,0},{2,3},{3,2},{4,5},{5,4},{6,7},{7,6},{8,12},{9,13},{10,... | collective-permute-start | bytes 6152 | tf_op jit(solution)/shard_map/ppermute | solution.py:304
  28.5 6.1 %collective-permute-start.8 = (f32[1,512]{1,0:T(1,128)S(1)}, f32[1,512]{1,0:T(1,128)S(1)}, u32[]{:S(2)}, u32[]{:S(2)}) collective-permute-start(f32[1,512]{1,0:T(1,128)S(1)} %get-tuple-element.48), channel_id=1, source_target_pairs={{0,1},{1,0},{2,3},{3,2},{4,5},{5,4},{6,7},{7,6},{8,14},{9,15},{10,... | collective-permute-start | bytes 6152 | tf_op jit(solution)/shard_map/ppermute | solution.py:304
  34.6 1.2 %collective-permute-start.14 = (f32[1,512]{1,0:T(1,128)S(1)}, f32[1,512]{1,0:T(1,128)S(1)}, u32[]{:S(2)}, u32[]{:S(2)}) collective-permute-start(f32[1,512]{1,0:T(1,128)S(1)} %get-tuple-element.53), channel_id=1, source_target_pairs={{0,1},{1,0},{2,3},{3,2},{4,5},{5,4},{6,8},{7,9},{8,6},{9,7},{10,11... | collective-permute-start | bytes 6152 | tf_op jit(solution)/shard_map/ppermute | solution.py:304
  34.7 1.3 %collective-permute-start.13 = (f32[1,512]{1,0:T(1,128)S(1)}, f32[1,512]{1,0:T(1,128)S(1)}, u32[]{:S(2)}, u32[]{:S(2)}) collective-permute-start(f32[1,512]{1,0:T(1,128)S(1)} %get-tuple-element.53), channel_id=1, source_target_pairs={{0,1},{1,0},{2,3},{3,2},{4,8},{5,9},{6,7},{7,6},{8,4},{9,5},{10,12... | collective-permute-start | bytes 6152 | tf_op jit(solution)/shard_map/ppermute | solution.py:304
  36.0 16.2 %collective-permute-start.16 = (f32[1,512]{1,0:T(1,128)S(1)}, f32[1,512]{1,0:T(1,128)S(1)}, u32[]{:S(2)}, u32[]{:S(2)}) collective-permute-start(f32[1,512]{1,0:T(1,128)S(1)} %get-tuple-element.55), channel_id=1, source_target_pairs={{0,1},{1,0},{2,4},{3,5},{4,2},{5,3},{6,7},{7,6},{8,9},{9,8},{10,11... | collective-permute-start | bytes 6152 | tf_op jit(solution)/shard_map/ppermute | solution.py:304
  36.4 16.8 %collective-permute-start.15 = (f32[1,512]{1,0:T(1,128)S(1)}, f32[1,512]{1,0:T(1,128)S(1)}, u32[]{:S(2)}, u32[]{:S(2)}) collective-permute-start(f32[1,512]{1,0:T(1,128)S(1)} %get-tuple-element.55), channel_id=1, source_target_pairs={{0,4},{1,5},{2,3},{3,2},{4,0},{5,1},{6,7},{7,6},{8,9},{9,8},{10,11... | collective-permute-start | bytes 6152 | tf_op jit(solution)/shard_map/ppermute | solution.py:304

commit v5 on v4

--- a/solution.py
+++ b/solution.py
@@ -9,26 +9,31 @@
 
 GH = 16
 MAP_COPIES = 4
+MATRIX_COST = 60.0
 VMEM = pl.BlockSpec(memory_space=pltpu.VMEM)
 PARAMS = pltpu.CompilerParams(vmem_limit_bytes=16 * 2**20)
 
 
-def pieces(row, rows=8, count=3):
-    at = lax.broadcasted_iota(jnp.int32, (rows, row.shape[1]), 0)
-    block = jnp.zeros((rows, row.shape[1]), jnp.float32)
-    rest = row
-    for i in range(count):
-        piece = rest.astype(jnp.bfloat16).astype(jnp.float32)
-        block = jnp.where(at == i, piece, block)
-        rest = rest - piece
+def pieces(rows, count=3):
+    height = -(-len(rows) * count // 8) * 8
+    at = lax.broadcasted_iota(jnp.int32, (height, rows[0].shape[1]), 0)
+    block = jnp.zeros(at.shape, jnp.float32)
+    for k, rest in enumerate(rows):
+        for i in range(count):
+            piece = rest.astype(jnp.bfloat16).astype(jnp.float32)
+            block = jnp.where(at == k * count + i, piece, block)
+            rest = rest - piece
     return block.astype(jnp.bfloat16)
 
 
-def times(matrix, row):
-    product = lax.dot_general(
-        pieces(row), matrix, (((1,), (1,)), ((), ())), preferred_element_type=jnp.float32
-    )
-    return jnp.sum(product, axis=0, keepdims=True)
+def times(matrices, *rows):
+    block = pieces(rows)
+    product = sum(
+        lax.dot_general(block, matrix, (((1,), (1,)), ((), ())), preferred_element_type=jnp.float32)
+        for matrix in matrices
+    )
+    found = [jnp.sum(product[3 * k : 3 * k + 3, :], axis=0, keepdims=True) for k in range(len(rows))]
+    return found if len(rows) > 1 else found[0]
 
 
 def info_kernel(
@@ -158,9 +163,9 @@
 def inputs_kernel(mine_ref, other_ref, covariance_ref, operator_ref, start_ref, inputs_ref, states_ref, send_ref):
     state = start_ref[...]
     for t in range(mine_ref.shape[0]):
-        drive = times(covariance_ref[t], mine_ref[t : t + 1, :] + other_ref[t : t + 1, :])
+        drive = times([covariance_ref[t]], mine_ref[t : t + 1, :] + other_ref[t : t + 1, :])
         inputs_ref[t : t + 1, :] = drive
-        state = times(operator_ref[t], state) + drive
+        state = times([operator_ref[t]], state) + drive
         states_ref[t : t + 1, :] = state
     send_ref[...] = state
 
@@ -172,7 +177,7 @@
     def _():
         state = came_ref[...]
         for t in range(matrices_ref.shape[0]):
-            state = times(matrices_ref[t], state) + offsets_ref[t : t + 1, :]
+            state = times([matrices_ref[t]], state) + offsets_ref[t : t + 1, :]
             states_ref[t : t + 1, :] = state
         send_ref[...] = state
 
@@ -199,95 +204,118 @@
     return [high, (matrix - high.astype(jnp.float32)).astype(jnp.bfloat16)]
 
 
-def split_kernel(near_ref, far_ref, near_parts_ref, far_parts_ref):
+def split_kernel(near_ref, far_ref, means_ref, near_parts_ref, far_parts_ref, result_ref):
     for source, target in ((near_ref, near_parts_ref), (far_ref, far_parts_ref)):
         target[0], target[1] = halves(source[...])
-
-
-def times_parts(parts_ref, row):
-    block = pieces(row)
-    product = sum(
-        lax.dot_general(block, parts_ref[i], (((1,), (1,)), ((), ())), preferred_element_type=jnp.float32)
-        for i in range(2)
-    )
-    return jnp.sum(product, axis=0, keepdims=True)
-
-
-def turn_kernel(last, means_ref, gain_ref, propagator_ref, offsets_ref, states_ref, send_ref):
-    steps = means_ref.shape[0]
-    for t in range(steps):
-        moved = times(gain_ref[t], times(propagator_ref[...], means_ref[t : t + 1, :]))
-        offsets_ref[t : t + 1, :] = means_ref[t : t + 1, :] - moved
-    end = slice(steps - 1, steps)
-    state = jnp.where(lax.axis_index("tm") == last, means_ref[end, :], offsets_ref[end, :])
-    states_ref[end, :] = state
-    for t in reversed(range(steps - 1)):
-        state = times(gain_ref[t], state) + offsets_ref[t : t + 1, :]
-        states_ref[t : t + 1, :] = state
-    send_ref[...] = state
+    for t in range(means_ref.shape[0]):
+        result_ref[t] = means_ref[t : t + 1, :]
+
+
+def offsets_kernel(last, means_ref, gain_ref, propagator_ref, offsets_ref, send_ref):
+    @pl.when(lax.axis_index("tm") != last)
+    def _():
+        steps = means_ref.shape[0]
+        means = [means_ref[t : t + 1, :] for t in range(steps)]
+        moved = times([propagator_ref[...]], *means)
+        state = jnp.zeros_like(means[0])
+        for t in reversed(range(steps)):
+            left, state = times([gain_ref[t]], moved[t], state)
+            offsets_ref[t : t + 1, :] = means[t] - left
+            state = state + offsets_ref[t : t + 1, :]
+        send_ref[...] = state
+
+    @pl.when(lax.axis_index("tm") == last)
+    def _():
+        offsets_ref[...] = means_ref[...]
+        send_ref[...] = means_ref[0:1, :]
+
+
+def turn_kernel(last, means_ref, gain_ref, propagator_ref, states_ref, send_ref):
+    @pl.when(lax.axis_index("tm") == last)
+    def _():
+        steps = means_ref.shape[0]
+        means = [means_ref[t : t + 1, :] for t in range(steps)]
+        moved = times([propagator_ref[...]], *means)
+        state = means[-1]
+        states_ref[steps - 1 : steps, :] = state
+        for t in reversed(range(steps - 1)):
+            left, state = times([gain_ref[t]], moved[t], state)
+            state = state + (means[t] - left)
+            states_ref[t : t + 1, :] = state
+        send_ref[...] = state
+
+    @pl.when(lax.axis_index("tm") != last)
+    def _():
+        states_ref[...] = means_ref[...]
+        send_ref[...] = means_ref[0:1, :]
 
 
 def smooth(state, gain_ref, offsets_ref, states_ref, send_ref):
-    for t in reversed(range(gain_ref.shape[0])):
-        state = times(gain_ref[t], state) + offsets_ref[t : t + 1, :]
-        states_ref[t : t + 1, :] = state
+    steps = gain_ref.shape[0]
+    for t in reversed(range(steps)):
+        state = times([gain_ref[t]], state) + offsets_ref[t : t + 1, :]
+        if len(states_ref.shape) == 3:
+            states_ref[t] = state
+        else:
+            states_ref[t : t + 1, :] = state
     send_ref[...] = state
 
 
 def first_back_kernel(
     places, last_ref, far_ref, near_ref, far_parts_ref, near_parts_ref, gain_ref, offsets_ref, kept_ref,
-    states_ref, send_ref,
+    came_ref, states_ref, send_ref,
+):
+    here = lax.axis_index("tm") == places - 4
+
+    @pl.when(here)
+    def _():
+        state = times([far_parts_ref[0], far_parts_ref[1]], last_ref[...]) + far_ref[...]
+        state = times([near_parts_ref[0], near_parts_ref[1]], state) + near_ref[...]
+        smooth(state, gain_ref, offsets_ref, states_ref, send_ref)
+
+    @pl.when(jnp.logical_not(here))
+    def _():
+        states_ref[...] = kept_ref[...]
+        send_ref[...] = came_ref[...]
+
+
+def back_kernel(
+    target, stray, two_ref, one_ref, near_ref, near_parts_ref, gain_ref, offsets_ref, kept_ref,
+    came_ref, states_ref, send_ref,
 ):
     here = lax.axis_index("tm")
 
-    @pl.when(here == places - 4)
-    def _():
-        state = times_parts(far_parts_ref, last_ref[...]) + far_ref[...]
-        state = times_parts(near_parts_ref, state) + near_ref[...]
+    @pl.when(here == target)
+    def _():
+        state = times([near_parts_ref[0], near_parts_ref[1]], two_ref[...]) + near_ref[...]
         smooth(state, gain_ref, offsets_ref, states_ref, send_ref)
 
-    @pl.when(here == places - 2)
-    def _():
-        smooth(near_ref[...], gain_ref, offsets_ref, states_ref, send_ref)
-
-    @pl.when((here != places - 4) & (here != places - 2))
-    def _():
-        states_ref[...] = kept_ref[...]
-        send_ref[...] = near_ref[...]
-
-
-def back_kernel(
-    target, stray, two_ref, one_ref, near_ref, near_parts_ref, gain_ref, offsets_ref, kept_ref,
-    states_ref, send_ref,
-):
-    here = lax.axis_index("tm")
-
-    @pl.when(here == target)
-    def _():
-        state = times_parts(near_parts_ref, two_ref[...]) + near_ref[...]
+    @pl.when((here == target + 1) | (here == stray))
+    def _():
+        state = jnp.where(here == stray, two_ref[...], one_ref[...])
         smooth(state, gain_ref, offsets_ref, states_ref, send_ref)
 
-    @pl.when(here == target + 1)
-    def _():
-        smooth(one_ref[...], gain_ref, offsets_ref, states_ref, send_ref)
-
-    @pl.when(here == stray)
-    def _():
-        smooth(two_ref[...], gain_ref, offsets_ref, states_ref, send_ref)
-
     @pl.when((here != target) & (here != target + 1) & (here != stray))
     def _():
-        states_ref[...] = kept_ref[...]
-        send_ref[...] = two_ref[...]
-
-
-def call(kernel, name, outs, *args):
+        for t in range(kept_ref.shape[0]):
+            if len(states_ref.shape) == 3:
+                states_ref[t] = kept_ref[t : t + 1, :]
+            else:
+                states_ref[t : t + 1, :] = kept_ref[t : t + 1, :]
+        send_ref[...] = came_ref[...]
+
+
+def call(kernel, name, outs, *args, cost=1.0):
     return pl.pallas_call(
         kernel,
-        out_shape=[jax.ShapeDtypeStruct(shape, jnp.float32) for shape in outs],
+        out_shape=[
+            jax.ShapeDtypeStruct(shape, jnp.bfloat16 if len(shape) == 3 and shape[1] > 1 else jnp.float32)
+            for shape in outs
+        ],
         in_specs=[VMEM] * len(args),
         out_specs=[VMEM] * len(outs),
         compiler_params=PARAMS,
+        cost_estimate=pl.CostEstimate(flops=int(cost * 1e9), bytes_accessed=2**20, transcendentals=0),
         name=name,
     )(*args)
 
@@ -305,9 +333,13 @@
 
 
 def ring_up(place, places):
+    if place == 0:
+        return (0, 1, 3)
+    if place == places - 3:
+        return (place, place + 1, place + 2)
     if place % 2 or place == places - 2:
         return (place, place + 1)
-    return (place, place + 1, place - 2 if place else 2)
+    return (place, place + 1, place - 2)
 
 
 def local(
@@ -336,34 +368,30 @@
     composed = call(compose_kernel, "compose", ((size, size),), send, gain)[0]
     near = lax.ppermute(composed, "tm", [(place + 1, place) for place in range(0, places - 2, 2)])
     far = lax.ppermute(composed, "tm", [(places - 2, places - 4)])
+    matrix = propagator.reshape(size, size)
     for place in range(1, places):
         came = pass_row(send, [ring_up(place - 1, places)], places)
+        if place == places - 1:
+            offsets, left = call(
+                functools.partial(offsets_kernel, places - 1), "offsets", (many, one), means, gain, matrix
+            )
+            far_offset = pass_row(left, [(places - 2, places - 4)], places)
+            near_offset = pass_row(left, [(at, at + 1) for at in range(0, places - 2, 2)], places)
         means, send = call(
-            functools.partial(hop_kernel, place), "forward", (many, one), came, operator, inputs, means
-        )
-    offsets, states, send = call(
-        functools.partial(turn_kernel, places - 1),
-        "turn",
-        (many, many, one),
-        means,
-        gain,
-        propagator.reshape(size, size),
+            functools.partial(hop_kernel, place), "forward", (many, one), came, operator, inputs, means,
+            cost=MATRIX_COST if place == 1 else 0.5,
+        )
+    states, send = call(
+        functools.partial(turn_kernel, places - 1), "turn", (many, one), means, gain, matrix
     )
     last = pass_row(send, [(places - 1, places - 4)], places)
-    far_offset = pass_row(send, [(places - 2, places - 4)], places)
-    near_offset = pass_row(send, [(place, place + 1) for place in range(0, places, 2)], places)
-    near_parts, far_parts = pl.pallas_call(
-        split_kernel,
-        out_shape=[jax.ShapeDtypeStruct((2, size, size), jnp.bfloat16)] * 2,
-        in_specs=[VMEM] * 2,
-        out_specs=[VMEM] * 2,
-        compiler_params=PARAMS,
-        name="split",
-    )(near, far)
+    parts = (2, size, size)
+    result = (steps, 1, size)
+    near_parts, far_parts, means = call(split_kernel, "split", (parts, parts, result), near, far, means)
     states, send = call(
         functools.partial(first_back_kernel, places),
         "first_back",
-        (many, (1, size)),
+        (many, one),
         last,
         far_offset,
         near_offset,
@@ -372,24 +400,28 @@
         gain,
         offsets,
         states,
-    )
+        send,
+    )
+    stray = places - 2
     for target in range(places - 6, -1, -2):
-        stray = places - 3 if target == places - 6 else -1
-        two = pass_row(send, [(target + 2, target)] + ([(stray + 1, stray)] if stray >= 0 else []), places)
-        one = pass_row(send, [(target + 2, target + 1)], places)
+        rings = [(target + 2, target)] + ([(stray + 1, stray)] if stray > target + 2 else [])
+        two = pass_row(send, rings, places)
+        one_up = pass_row(send, [(target + 2, target + 1)], places)
         states, send = call(
             functools.partial(back_kernel, target, stray),
             "back",
-            (many, (1, size)),
+            (many if target else result, one),
             two,
-            one,
+            one_up,
             near_offset,
             near_parts,
             gain,
             offsets,
             states,
-        )
-    return (means.reshape(steps, 1, size), states.reshape(steps, 1, size))
+            send,
+        )
+        stray = stray - 1 if stray == places - 2 else -1
+    return means, states
 
 
 def solution(mesh):

time: 55.3 us -> 46.8 us (0.85)
  starting transfers between devices: 29.8 us -> 19 us
  waiting for transfers between devices: 16.2 us -> 19.5 us
  local copies, waits for them, and re-layouts: 1.21 us -> 0.02 us
    ppermute x14, starting transfers between devices: 27.3 us -> 16.5 us  [pass_row(): return lax.ppermute(row, ('tm', 'block'), sorted(route.items()))]
    ppermute x1, waiting for transfers between devices: 5.47 us -> 10.6 us  [local(): lax.ppermute(composed, 'tm', [(place + 1, place) for place in range(0, pl...]
    ppermute x14, waiting for transfers between devices: 9.91 us -> 8.07 us  [pass_row(): return lax.ppermute(row, ('tm', 'block'), sorted(route.items()))]
    unnamed x12 -> x10, local copies, waits for them, and re-layouts: 1.21 us -> 0.02 us
    pallas_call x14 -> x15, Pallas kernels: 4.4 us -> 4.62 us  [call(): pl.pallas_call(kernel, out_shape=[jax.ShapeDtypeStruct(shape, jnp.bfloat1...]
  transfers between devices with their start and end apart: 17 -> 17, of which waited for: 12 -> 11; matrix products, arithmetic and copies ran while one was open for 1% -> 0% of each run, Pallas kernels for 3% -> 5%
where the time goes in v5:
time: 46.8 us; the launch traced here: 46.6 us
  waiting for transfers between devices  19.5 us (42%)
  starting transfers between devices  19 us (41%)
  Pallas kernels  7.32 us (16%)
  between operations  0.76 us (2%)
    ppermute x14, starting transfers between devices, pass_row(): return lax.ppermute(row, ('tm', 'block'), sorted(route.items()))  16.5 us
    ppermute x1, waiting for transfers between devices, local(): lax.ppermute(composed, 'tm', [(place + 1, place) for place in range(0, pl...  10.6 us
    ppermute x14, waiting for transfers between devices, pass_row(): return lax.ppermute(row, ('tm', 'block'), sorted(route.items()))  8.07 us
    pallas_call x15, Pallas kernels, call(): pl.pallas_call(kernel, out_shape=[jax.ShapeDtypeStruct(shape, jnp.bfloat1...  4.62 us
    pallas_call x1, Pallas kernels, sensor_info(): pl.pallas_call(info_kernel, out_shape=[jax.ShapeDtypeStruct((steps, cells...  2.7 us
    ppermute x1, starting transfers between devices, local(): lax.ppermute(composed, 'tm', [(place + 1, place) for place in range(0, pl...  1.29 us
  transfers between devices with their start and end apart: 17, of which 11 were waited for; matrix products, arithmetic and copies ran while one was open for 0% of the time, Pallas kernels for 5%

profile of v5, /device:TPU:0, one launch (start us, length us, event | category | flops | bytes accessed | tf_op | source)
XLA Modules:
  0.0 46.6 jit_solution(14699113887082717127)
XLA Ops:
  0.7 2.7 %sensor_info.1 = (f32[2,512]{1,0:T(2,128)S(1)}, f32[2,512]{1,0:T(2,128)S(1)}) custom-call(bf16[2,1024,512]{2,1,0:T(8,128)(2,1)} %bitcast.24, bf16[7,7,16]{2,1,0:T(8,128)(2,1)} %bitcast.25, s32[2,64]{1,0:T(2,128)} %observed_hbm.1, s32[1,2]{1,0:T(1,128)} %bitcast.26), custom_call_target="tpu_custom_call" | custom-call | tf_op jit(solution)/shard_map/sensor_info/pallas_call | solution.py:133
  3.4 0.0 copy-start.2
  3.4 0.5 %collective-permute-start = (f32[2,512]{1,0:T(2,128)S(1)}, f32[2,512]{1,0:T(2,128)S(1)}, u32[]{:S(2)}, u32[]{:S(2)}) collective-permute-start(f32[2,512]{1,0:T(2,128)S(1)} %get-tuple-element.33), channel_id=1, source_target_pairs={{0,1},{1,0},{2,3},{3,2},{4,5},{5,4},{6,7},{7,6},{8,9},{9,8},{10,11... | collective-permute-start | bytes 12296 | tf_op jit(solution)/shard_map/ppermute | solution.py:160
  3.9 0.8 %collective-permute-done.other_ref = f32[2,512]{1,0:T(2,128)S(1)} collective-permute-done((f32[2,512]{1,0:T(2,128)S(1)}, f32[2,512]{1,0:T(2,128)S(1)}, u32[]{:S(2)}, u32[]{:S(2)}) %collective-permute-start) | collective-permute-done | bytes 4128 | tf_op jit(solution)/shard_map/ppermute | solution.py:160
  4.7 0.7 %inputs.1 = (f32[2,512]{1,0:T(2,128)S(1)}, f32[2,512]{1,0:T(2,128)S(1)}, f32[1,512]{1,0:T(1,128)S(1)}) custom-call(f32[2,512]{1,0:T(2,128)S(1)} %get-tuple-element.32.mine_ref, f32[2,512]{1,0:T(2,128)S(1)} %collective-permute-done.other_ref, bf16[2,512,512]{2,1,0:T(8,128)(2,1)S(1)} %bitcast.7, bf16[2,512,512]{2,1,0:T(8,128)(2,1)S(1)} %bitcast.8, ...), custom_call_target="tpu_custom_call" | custom-call | flops 1000000000 | bytes 1048576 | tf_op jit(solution)/shard_map/inputs/pallas_call | solution.py:309
  5.4 2.9 %collective-permute-start.3 = (f32[1,512]{1,0:T(1,128)S(1)}, f32[1,512]{1,0:T(1,128)S(1)}, u32[]{:S(2)}, u32[]{:S(2)}) collective-permute-start(f32[1,512]{1,0:T(1,128)S(1)} %get-tuple-element.34.after_ref), channel_id=1, source_target_pairs={{0,2},{1,3},{2,6},{3,7},{4,5},{5,4},{6,0},{7,1},{8,9},{9,8},{10,11... | collective-permute-start | bytes 6152 | tf_op jit(solution)/shard_map/ppermute | solution.py:332
  8.3 0.4 compose.1
  8.8 1.3 %collective-permute-start.1 = (f32[512,512]{1,0:T(8,128)S(1)}, f32[512,512]{1,0:T(8,128)S(1)}, u32[]{:S(2)}, u32[]{:S(2)}) collective-permute-start(f32[512,512]{1,0:T(8,128)S(1)} %compose.1), channel_id=1, source_target_pairs={{2,0},{6,4},{10,8},{3,1},{7,5},{11,9},{18,16},{22,20},{26,24},{19,... | collective-permute-start | bytes 3145736 | tf_op jit(solution)/shard_map/ppermute | solution.py:369
  10.1 0.7 %collective-permute-start.2 = (f32[512,512]{1,0:T(8,128)S(1)}, f32[512,512]{1,0:T(8,128)S(1)}, u32[]{:S(2)}, u32[]{:S(2)}) collective-permute-start(f32[512,512]{1,0:T(8,128)S(1)} %compose.1), channel_id=1, source_target_pairs={{12,8},{13,9},{28,24},{29,25}} | collective-permute-start | bytes 3145736 | tf_op jit(solution)/shard_map/ppermute | solution.py:370
  10.8 0.1 collective-permute-done.3.came_ref
  10.9 1.1 %collective-permute-done.4.came_ref = f32[1,512]{1,0:T(1,128)S(1)} collective-permute-done((f32[1,512]{1,0:T(1,128)S(1)}, f32[1,512]{1,0:T(1,128)S(1)}, u32[]{:S(2)}, u32[]{:S(2)}) %collective-permute-start.4) | collective-permute-done | bytes 2080 | tf_op jit(solution)/shard_map/ppermute | solution.py:332
  12.1 5.7 %collective-permute-start.5 = (f32[1,512]{1,0:T(1,128)S(1)}, f32[1,512]{1,0:T(1,128)S(1)}, u32[]{:S(2)}, u32[]{:S(2)}) collective-permute-start(f32[1,512]{1,0:T(1,128)S(1)} %get-tuple-element.39), channel_id=1, source_target_pairs={{0,4},{1,5},{2,3},{3,2},{4,6},{5,7},{6,0},{7,1},{8,9},{9,8},{10,11... | collective-permute-start | bytes 6152 | tf_op jit(solution)/shard_map/ppermute | solution.py:332
  17.7 1.3 %collective-permute-done.5.came_ref = f32[1,512]{1,0:T(1,128)S(1)} collective-permute-done((f32[1,512]{1,0:T(1,128)S(1)}, f32[1,512]{1,0:T(1,128)S(1)}, u32[]{:S(2)}, u32[]{:S(2)}) %collective-permute-start.5) | collective-permute-done | bytes 2080 | tf_op jit(solution)/shard_map/ppermute | solution.py:332
  19.1 1.2 %collective-permute-done.6.came_ref = f32[1,512]{1,0:T(1,128)S(1)} collective-permute-done((f32[1,512]{1,0:T(1,128)S(1)}, f32[1,512]{1,0:T(1,128)S(1)}, u32[]{:S(2)}, u32[]{:S(2)}) %collective-permute-start.6) | collective-permute-done | bytes 2080 | tf_op jit(solution)/shard_map/ppermute | solution.py:332
  20.2 0.2 collective-permute-start.7
  20.4 1.0 %collective-permute-done.7.came_ref = f32[1,512]{1,0:T(1,128)S(1)} collective-permute-done((f32[1,512]{1,0:T(1,128)S(1)}, f32[1,512]{1,0:T(1,128)S(1)}, u32[]{:S(2)}, u32[]{:S(2)}) %collective-permute-start.7) | collective-permute-done | bytes 2080 | tf_op jit(solution)/shard_map/ppermute | solution.py:332
  21.4 0.2 collective-permute-start.8
  21.6 1.0 %collective-permute-done.8.came_ref = f32[1,512]{1,0:T(1,128)S(1)} collective-permute-done((f32[1,512]{1,0:T(1,128)S(1)}, f32[1,512]{1,0:T(1,128)S(1)}, u32[]{:S(2)}, u32[]{:S(2)}) %collective-permute-start.8) | collective-permute-done | bytes 2080 | tf_op jit(solution)/shard_map/ppermute | solution.py:332
  22.5 0.2 collective-permute-start.9
  22.7 0.7 %offsets.1 = (f32[2,512]{1,0:T(2,128)S(1)}, f32[1,512]{1,0:T(1,128)S(1)}) custom-call(f32[2,512]{1,0:T(2,128)S(1)} %get-tuple-element.48.kept_ref.means_ref, bf16[2,512,512]{2,1,0:T(8,128)(2,1)S(1)} %bitcast.17, bf16[512,512]{1,0:T(8,128)(2,1)S(1)} %bitcast.22), custom_call_target="tpu_custom_call" | custom-call | flops 1000000000 | bytes 1048576 | tf_op jit(solution)/shard_map/offsets/pallas_call | solution.py:309
  23.4 0.4 collective-permute-start.11
  23.8 0.7 %collective-permute-start.12 = (f32[1,512]{1,0:T(1,128)S(1)}, f32[1,512]{1,0:T(1,128)S(1)}, u32[]{:S(2)}, u32[]{:S(2)}) collective-permute-start(f32[1,512]{1,0:T(1,128)S(1)} %get-tuple-element.52), channel_id=1, source_target_pairs={{0,2},{1,3},{2,0},{3,1},{4,6},{5,7},{6,4},{7,5},{8,10},{9,11},{10,... | collective-permute-start | bytes 6152 | tf_op jit(solution)/shard_map/ppermute | solution.py:332
  24.5 0.6 %forward.13 = (f32[2,512]{1,0:T(2,128)S(1)}, f32[1,512]{1,0:T(1,128)}) custom-call(f32[1,512]{1,0:T(1,128)S(1)} %collective-permute-done.9.came_ref, bf16[2,512,512]{2,1,0:T(8,128)(2,1)S(1)} %bitcast.15, f32[2,512]{1,0:T(2,128)S(1)} %get-tuple-element.35.offsets_ref, f32[2,512]{1,0:T(2,128)S(1)} %get-tuple-element.48.kept_ref.means_ref), custom_call_target="tpu_custom_call" | custom-call | flops 500000000 | bytes 1048576 | tf_op jit(solution)/shard_map/forward/pallas_call | solution.py:309
  25.1 10.6 %collective-permute-done.1.near_ref = f32[512,512]{1,0:T(8,128)S(1)} collective-permute-done((f32[512,512]{1,0:T(8,128)S(1)}, f32[512,512]{1,0:T(8,128)S(1)}, u32[]{:S(2)}, u32[]{:S(2)}) %collective-permute-start.1) | collective-permute-done | bytes 1048608 | tf_op jit(solution)/shard_map/ppermute | solution.py:369
  35.7 0.8 %split.1 = (bf16[2,512,512]{2,1,0:T(8,128)(2,1)S(1)}, bf16[2,512,512]{2,1,0:T(8,128)(2,1)S(1)}, f32[2,1,512]{2,1,0:T(1,128)}) custom-call(f32[512,512]{1,0:T(8,128)S(1)} %collective-permute-done.1.near_ref, f32[512,512]{1,0:T(8,128)S(1)} %collective-permute-done.2.far_ref, f32[2,512]{1,0:T(2,128)S(1)} %get-tuple-element.49.means_ref), custom_call_target="tpu_custom_call" | custom-call | flops 1000000000 | bytes 1048576 | tf_op jit(solution)/shard_map/split/pallas_call | solution.py:309
  36.6 0.1 collective-permute-start.13
  36.6 0.5 %collective-permute-start.14 = (f32[1,512]{1,0:T(1,128)S(1)}, f32[1,512]{1,0:T(1,128)S(1)}, u32[]{:S(2)}, u32[]{:S(2)}) collective-permute-start(f32[1,512]{1,0:T(1,128)S(1)} %get-tuple-element.57.came_ref), channel_id=1, source_target_pairs={{0,1},{1,0},{2,3},{3,2},{4,5},{5,4},{6,8},{7,9},{8,6},{9,7},{10,11... | collective-permute-start | bytes 6152 | tf_op jit(solution)/shard_map/ppermute | solution.py:332
  37.1 0.6 %collective-permute-done.13.two_ref = f32[1,512]{1,0:T(1,128)S(1)} collective-permute-done((f32[1,512]{1,0:T(1,128)S(1)}, f32[1,512]{1,0:T(1,128)S(1)}, u32[]{:S(2)}, u32[]{:S(2)}) %collective-permute-start.13) | collective-permute-done | bytes 2080 | tf_op jit(solution)/shard_map/ppermute | solution.py:332
  37.8 0.2 collective-permute-done.14.one_ref
  38.0 5.7 %collective-permute-start.15 = (f32[1,512]{1,0:T(1,128)S(1)}, f32[1,512]{1,0:T(1,128)S(1)}, u32[]{:S(2)}, u32[]{:S(2)}) collective-permute-start(f32[1,512]{1,0:T(1,128)S(1)} %get-tuple-element.59.came_ref), channel_id=1, source_target_pairs={{0,4},{1,5},{2,3},{3,2},{4,0},{5,1},{6,7},{7,6},{8,9},{9,8},{10,12... | collective-permute-start | bytes 6152 | tf_op jit(solution)/shard_map/ppermute | solution.py:332
  43.7 1.6 %collective-permute-done.15.two_ref = f32[1,512]{1,0:T(1,128)S(1)} collective-permute-done((f32[1,512]{1,0:T(1,128)S(1)}, f32[1,512]{1,0:T(1,128)S(1)}, u32[]{:S(2)}, u32[]{:S(2)}) %collective-permute-start.15) | collective-permute-done | bytes 2080 | tf_op jit(solution)/shard_map/ppermute | solution.py:332
  45.2 1.4 %back.3 = (f32[2,1,512]{2,1,0:T(1,128)}, f32[1,512]{1,0:T(1,128)}) custom-call(f32[1,512]{1,0:T(1,128)S(1)} %collective-permute-done.15.two_ref, f32[1,512]{1,0:T(1,128)S(1)} %collective-permute-done.16.one_ref, f32[1,512]{1,0:T(1,128)S(1)} %collective-permute-done.12.near_ref, bf16[2,512,512]{2,1,0:T(8,128)(2,1)S(1)} %get-tuple-element.54.near_parts_ref, ...), custom_call_target="tpu_custom_call" | custom-call | flops 1000000000 | bytes 1048576 | tf_op jit(solution)/shard_map/back/pallas_call | solution.py:309
  (28 shorter events, 0.1 us)
Async XLA Ops:
  0.6 4.1 %copy-start.1 = (bf16[2,1,512,512]{3,2,1,0:T(8,128)(2,1)S(1)}, bf16[2,1,512,512]{3,2,1,0:T(8,128)(2,1)}, u32[]{:S(2)}) copy-start(bf16[2,1,512,512]{3,2,1,0:T(8,128)(2,1)} %param.13) | copy-start | bytes 3145732
  0.6 4.1 %copy-start = (bf16[2,1,512,512]{3,2,1,0:T(8,128)(2,1)S(1)}, bf16[2,1,512,512]{3,2,1,0:T(8,128)(2,1)}, u32[]{:S(2)}) copy-start(bf16[2,1,512,512]{3,2,1,0:T(8,128)(2,1)} %param.14) | copy-start | bytes 3145732
  0.7 4.1 %copy-start.4 = (f32[1,512]{1,0:T(1,128)S(1)}, f32[1,512]{1,0:T(1,128)}, u32[]{:S(2)}) copy-start(f32[1,512]{1,0:T(1,128)} %start_ref.1) | copy-start | bytes 6148
  3.4 5.0 %copy-start.2 = (bf16[2,1,512,512]{3,2,1,0:T(8,128)(2,1)S(1)}, bf16[2,1,512,512]{3,2,1,0:T(8,128)(2,1)}, u32[]{:S(2)}) copy-start(bf16[2,1,512,512]{3,2,1,0:T(8,128)(2,1)} %param.15) | copy-start | bytes 3145732
  3.4 1.3 %collective-permute-start = (f32[2,512]{1,0:T(2,128)S(1)}, f32[2,512]{1,0:T(2,128)S(1)}, u32[]{:S(2)}, u32[]{:S(2)}) collective-permute-start(f32[2,512]{1,0:T(2,128)S(1)} %get-tuple-element.33), channel_id=1, source_target_pairs={{0,1},{1,0},{2,3},{3,2},{4,5},{5,4},{6,7},{7,6},{8,9},{9,8},{10,11... | collective-permute-start | bytes 12296 | tf_op jit(solution)/shard_map/ppermute | solution.py:160
  5.4 5.5 %collective-permute-start.3 = (f32[1,512]{1,0:T(1,128)S(1)}, f32[1,512]{1,0:T(1,128)S(1)}, u32[]{:S(2)}, u32[]{:S(2)}) collective-permute-start(f32[1,512]{1,0:T(1,128)S(1)} %get-tuple-element.34.after_ref), channel_id=1, source_target_pairs={{0,2},{1,3},{2,6},{3,7},{4,5},{5,4},{6,0},{7,1},{8,9},{9,8},{10,11... | collective-permute-start | bytes 6152 | tf_op jit(solution)/shard_map/ppermute | solution.py:332
  8.8 26.9 %collective-permute-start.1 = (f32[512,512]{1,0:T(8,128)S(1)}, f32[512,512]{1,0:T(8,128)S(1)}, u32[]{:S(2)}, u32[]{:S(2)}) collective-permute-start(f32[512,512]{1,0:T(8,128)S(1)} %compose.1), channel_id=1, source_target_pairs={{2,0},{6,4},{10,8},{3,1},{7,5},{11,9},{18,16},{22,20},{26,24},{19,... | collective-permute-start | bytes 3145736 | tf_op jit(solution)/shard_map/ppermute | solution.py:369
  10.1 25.6 %collective-permute-start.2 = (f32[512,512]{1,0:T(8,128)S(1)}, f32[512,512]{1,0:T(8,128)S(1)}, u32[]{:S(2)}, u32[]{:S(2)}) collective-permute-start(f32[512,512]{1,0:T(8,128)S(1)} %compose.1), channel_id=1, source_target_pairs={{12,8},{13,9},{28,24},{29,25}} | collective-permute-start | bytes 3145736 | tf_op jit(solution)/shard_map/ppermute | solution.py:370
  10.9 1.2 %collective-permute-start.4 = (f32[1,512]{1,0:T(1,128)S(1)}, f32[1,512]{1,0:T(1,128)S(1)}, u32[]{:S(2)}, u32[]{:S(2)}) collective-permute-start(f32[1,512]{1,0:T(1,128)S(1)} %get-tuple-element.37), channel_id=1, source_target_pairs={{0,1},{1,0},{2,4},{3,5},{4,2},{5,3},{6,7},{7,6},{8,9},{9,8},{10,11... | collective-permute-start | bytes 6152 | tf_op jit(solution)/shard_map/ppermute | solution.py:332
  12.1 7.0 %collective-permute-start.5 = (f32[1,512]{1,0:T(1,128)S(1)}, f32[1,512]{1,0:T(1,128)S(1)}, u32[]{:S(2)}, u32[]{:S(2)}) collective-permute-start(f32[1,512]{1,0:T(1,128)S(1)} %get-tuple-element.39), channel_id=1, source_target_pairs={{0,4},{1,5},{2,3},{3,2},{4,6},{5,7},{6,0},{7,1},{8,9},{9,8},{10,11... | collective-permute-start | bytes 6152 | tf_op jit(solution)/shard_map/ppermute | solution.py:332
  19.1 1.2 %collective-permute-start.6 = (f32[1,512]{1,0:T(1,128)S(1)}, f32[1,512]{1,0:T(1,128)S(1)}, u32[]{:S(2)}, u32[]{:S(2)}) collective-permute-start(f32[1,512]{1,0:T(1,128)S(1)} %get-tuple-element.41), channel_id=1, source_target_pairs={{0,1},{1,0},{2,3},{3,2},{4,5},{5,4},{6,8},{7,9},{8,6},{9,7},{10,11... | collective-permute-start | bytes 6152 | tf_op jit(solution)/shard_map/ppermute | solution.py:332
  20.2 2.5 %copy-start.3 = (bf16[1,512,512]{2,1,0:T(8,128)(2,1)S(1)}, bf16[1,512,512]{2,1,0:T(8,128)(2,1)}, u32[]{:S(2)}) copy-start(bf16[1,512,512]{2,1,0:T(8,128)(2,1)} %param.16) | copy-start | bytes 1572868
  20.2 1.2 %collective-permute-start.7 = (f32[1,512]{1,0:T(1,128)S(1)}, f32[1,512]{1,0:T(1,128)S(1)}, u32[]{:S(2)}, u32[]{:S(2)}) collective-permute-start(f32[1,512]{1,0:T(1,128)S(1)} %get-tuple-element.43), channel_id=1, source_target_pairs={{0,1},{1,0},{2,3},{3,2},{4,8},{5,9},{6,7},{7,6},{8,10},{9,11},{10,... | collective-permute-start | bytes 6152 | tf_op jit(solution)/shard_map/ppermute | solution.py:332
  21.4 1.2 %collective-permute-start.8 = (f32[1,512]{1,0:T(1,128)S(1)}, f32[1,512]{1,0:T(1,128)S(1)}, u32[]{:S(2)}, u32[]{:S(2)}) collective-permute-start(f32[1,512]{1,0:T(1,128)S(1)} %get-tuple-element.45), channel_id=1, source_target_pairs={{0,1},{1,0},{2,3},{3,2},{4,5},{5,4},{6,7},{7,6},{8,9},{9,8},{10,12... | collective-permute-start | bytes 6152 | tf_op jit(solution)/shard_map/ppermute | solution.py:332
  22.5 1.9 %collective-permute-start.9 = (f32[1,512]{1,0:T(1,128)S(1)}, f32[1,512]{1,0:T(1,128)S(1)}, u32[]{:S(2)}, u32[]{:S(2)}) collective-permute-start(f32[1,512]{1,0:T(1,128)S(1)} %get-tuple-element.47), channel_id=1, source_target_pairs={{0,1},{1,0},{2,3},{3,2},{4,5},{5,4},{6,7},{7,6},{8,9},{9,8},{10,11... | collective-permute-start | bytes 6152 | tf_op jit(solution)/shard_map/ppermute | solution.py:332
  23.4 13.1 %collective-permute-start.11 = (f32[1,512]{1,0:T(1,128)S(1)}, f32[1,512]{1,0:T(1,128)S(1)}, u32[]{:S(2)}, u32[]{:S(2)}) collective-permute-start(f32[1,512]{1,0:T(1,128)S(1)} %get-tuple-element.52), channel_id=1, source_target_pairs={{0,1},{1,0},{2,3},{3,2},{4,5},{5,4},{6,7},{7,6},{8,12},{9,13},{10,... | collective-permute-start | bytes 6152 | tf_op jit(solution)/shard_map/ppermute | solution.py:332
  23.8 12.7 %collective-permute-start.12 = (f32[1,512]{1,0:T(1,128)S(1)}, f32[1,512]{1,0:T(1,128)S(1)}, u32[]{:S(2)}, u32[]{:S(2)}) collective-permute-start(f32[1,512]{1,0:T(1,128)S(1)} %get-tuple-element.52), channel_id=1, source_target_pairs={{0,2},{1,3},{2,0},{3,1},{4,6},{5,7},{6,4},{7,5},{8,10},{9,11},{10,... | collective-permute-start | bytes 6152 | tf_op jit(solution)/shard_map/ppermute | solution.py:332
  25.1 11.5 %collective-permute-start.10 = (f32[1,512]{1,0:T(1,128)S(1)}, f32[1,512]{1,0:T(1,128)S(1)}, u32[]{:S(2)}, u32[]{:S(2)}) collective-permute-start(f32[1,512]{1,0:T(1,128)S(1)} %get-tuple-element.51.came_ref), channel_id=1, source_target_pairs={{0,1},{1,0},{2,3},{3,2},{4,5},{5,4},{6,7},{7,6},{8,14},{9,15},{10,... | collective-permute-start | bytes 6152 | tf_op jit(solution)/shard_map/ppermute | solution.py:332
  36.6 1.2 %collective-permute-start.13 = (f32[1,512]{1,0:T(1,128)S(1)}, f32[1,512]{1,0:T(1,128)S(1)}, u32[]{:S(2)}, u32[]{:S(2)}) collective-permute-start(f32[1,512]{1,0:T(1,128)S(1)} %get-tuple-element.57.came_ref), channel_id=1, source_target_pairs={{0,1},{1,0},{2,3},{3,2},{4,8},{5,9},{6,7},{7,6},{8,4},{9,5},{10,11... | collective-permute-start | bytes 6152 | tf_op jit(solution)/shard_map/ppermute | solution.py:332
  36.6 1.3 %collective-permute-start.14 = (f32[1,512]{1,0:T(1,128)S(1)}, f32[1,512]{1,0:T(1,128)S(1)}, u32[]{:S(2)}, u32[]{:S(2)}) collective-permute-start(f32[1,512]{1,0:T(1,128)S(1)} %get-tuple-element.57.came_ref), channel_id=1, source_target_pairs={{0,1},{1,0},{2,3},{3,2},{4,5},{5,4},{6,8},{7,9},{8,6},{9,7},{10,11... | collective-permute-start | bytes 6152 | tf_op jit(solution)/shard_map/ppermute | solution.py:332
  38.0 7.3 %collective-permute-start.15 = (f32[1,512]{1,0:T(1,128)S(1)}, f32[1,512]{1,0:T(1,128)S(1)}, u32[]{:S(2)}, u32[]{:S(2)}) collective-permute-start(f32[1,512]{1,0:T(1,128)S(1)} %get-tuple-element.59.came_ref), channel_id=1, source_target_pairs={{0,4},{1,5},{2,3},{3,2},{4,0},{5,1},{6,7},{7,6},{8,9},{9,8},{10,12... | collective-permute-start | bytes 6152 | tf_op jit(solution)/shard_map/ppermute | solution.py:332
  43.7 1.6 %collective-permute-start.16 = (f32[1,512]{1,0:T(1,128)S(1)}, f32[1,512]{1,0:T(1,128)S(1)}, u32[]{:S(2)}, u32[]{:S(2)}) collective-permute-start(f32[1,512]{1,0:T(1,128)S(1)} %get-tuple-element.59.came_ref), channel_id=1, source_target_pairs={{0,1},{1,0},{2,4},{3,5},{4,2},{5,3},{6,7},{7,6},{8,9},{9,8},{10,11... | collective-permute-start | bytes 6152 | tf_op jit(solution)/shard_map/ppermute | solution.py:332

commit v6 on v5

--- a/solution.py
+++ b/solution.py
@@ -9,7 +9,7 @@
 
 GH = 16
 MAP_COPIES = 4
-MATRIX_COST = 60.0
+COSTS = (60.0, 2.5, 2.5, 6.0, 0.5)
 VMEM = pl.BlockSpec(memory_space=pltpu.VMEM)
 PARAMS = pltpu.CompilerParams(vmem_limit_bytes=16 * 2**20)
 
@@ -187,56 +187,140 @@
         send_ref[...] = came_ref[...]
 
 
-def compose_kernel(after_ref, gain_ref, composed_ref):
-    del after_ref
-    steps = gain_ref.shape[0]
-    product = gain_ref[0].astype(jnp.float32)
-    for t in range(1, steps):
-        product = sum(
-            jnp.dot(part, gain_ref[t], preferred_element_type=jnp.float32)
-            for part in (halves(product) if t > 1 else [gain_ref[0]])
-        )
-    composed_ref[...] = product
-
-
 def halves(matrix):
     high = matrix.astype(jnp.bfloat16)
     return [high, (matrix - high.astype(jnp.float32)).astype(jnp.bfloat16)]
 
 
-def split_kernel(near_ref, far_ref, means_ref, near_parts_ref, far_parts_ref, result_ref):
-    for source, target in ((near_ref, near_parts_ref), (far_ref, far_parts_ref)):
-        target[0], target[1] = halves(source[...])
-    for t in range(means_ref.shape[0]):
-        result_ref[t] = means_ref[t : t + 1, :]
-
-
-def offsets_kernel(last, means_ref, gain_ref, propagator_ref, offsets_ref, send_ref):
-    @pl.when(lax.axis_index("tm") != last)
-    def _():
-        steps = means_ref.shape[0]
-        means = [means_ref[t : t + 1, :] for t in range(steps)]
-        moved = times([propagator_ref[...]], *means)
-        state = jnp.zeros_like(means[0])
-        for t in reversed(range(steps)):
-            left, state = times([gain_ref[t]], moved[t], state)
-            offsets_ref[t : t + 1, :] = means[t] - left
-            state = state + offsets_ref[t : t + 1, :]
-        send_ref[...] = state
-
-    @pl.when(lax.axis_index("tm") == last)
+def composed(gain_ref):
+    product = gain_ref[0]
+    for t in range(1, gain_ref.shape[0]):
+        product = sum(
+            jnp.dot(part, gain_ref[t], preferred_element_type=jnp.float32)
+            for part in (halves(product) if t > 1 else [product])
+        )
+    return product.astype(jnp.float32)
+
+
+def compose_kernel(senders, after_ref, gain_ref, composed_ref):
+    del after_ref
+    here = lax.axis_index("tm")
+    sends = functools.reduce(jnp.logical_or, [here == place for place in senders])
+
+    @pl.when(sends)
+    def _():
+        composed_ref[...] = composed(gain_ref)
+
+
+def late_kernel(senders, means_ref, gain_ref, propagator_ref, composed_ref):
+    size = gain_ref.shape[1]
+    here = lax.axis_index("tm")
+    sends = functools.reduce(jnp.logical_or, [here == place for place in senders])
+
+    @pl.when(sends)
+    def _():
+        composed_ref[:size, :] = composed(gain_ref)
+        composed_ref[size:, :] = jnp.zeros((composed_ref.shape[0] - size, size), jnp.float32)
+        composed_ref[size : size + 1, :] = offsets(means_ref, gain_ref, propagator_ref)[0]
+
+
+def offsets(means_ref, gain_ref, propagator_ref):
+    steps = means_ref.shape[0]
+    means = [means_ref[t : t + 1, :] for t in range(steps)]
+    moved = times([propagator_ref[...]], *means)
+    state = jnp.zeros_like(means[0])
+    found = [None] * steps
+    for t in reversed(range(steps)):
+        left, state = times([gain_ref[t]], moved[t], state)
+        found[t] = means[t] - left
+        state = state + found[t]
+    return state, found
+
+
+def pair_kernel(
+    places,
+    skip_place,
+    near_ref,
+    skip_ref,
+    gain_ref,
+    left_ref,
+    near_offset_ref,
+    near_parts_ref,
+    pair_parts_ref,
+    pair_offset_ref,
+    skip_parts_ref,
+):
+    here = lax.axis_index("tm")
+
+    @pl.when(functools.reduce(jnp.logical_or, [here == place for place in places]))
+    def _():
+        near = halves(near_ref[...])
+        own = halves(composed(gain_ref))
+        near_parts_ref[0], near_parts_ref[1] = near
+        pair_parts_ref[0], pair_parts_ref[1] = halves(
+            jnp.dot(own[0], near[0], preferred_element_type=jnp.float32)
+            + jnp.dot(own[0], near[1], preferred_element_type=jnp.float32)
+            + jnp.dot(own[1], near[0], preferred_element_type=jnp.float32)
+        )
+        pair_offset_ref[...] = times(own, near_offset_ref[...]) + left_ref[...]
+
+    @pl.when(here == skip_place)
+    def _():
+        skip_parts_ref[0], skip_parts_ref[1] = halves(skip_ref[...])
+
+
+def late_split_kernel(place, late_ref, after_ref, parts_ref, offset_ref):
+    del after_ref
+    size = late_ref.shape[1]
+
+    @pl.when(lax.axis_index("tm") == place)
+    def _():
+        parts_ref[0], parts_ref[1] = halves(late_ref[:size, :])
+        offset_ref[...] = late_ref[size : size + 1, :]
+
+
+def split_kernel(place, matrix_ref, left_ref, parts_ref, again_ref):
+    again_ref[...] = left_ref[...]
+
+    @pl.when(lax.axis_index("tm") == place)
+    def _():
+        parts_ref[0], parts_ref[1] = halves(matrix_ref[...])
+
+
+def offsets_kernel(last, means_ref, gain_ref, propagator_ref, offsets_ref, send_ref, own_parts_ref):
+    here = lax.axis_index("tm") == last
+
+    @pl.when(lax.axis_index("tm") == last - 2)
+    def _():
+        own_parts_ref[0], own_parts_ref[1] = halves(composed(gain_ref))
+
+    @pl.when(jnp.logical_not(here))
+    def _():
+        send_ref[...], found = offsets(means_ref, gain_ref, propagator_ref)
+        for t, row in enumerate(found):
+            offsets_ref[t : t + 1, :] = row
+
+    @pl.when(here)
     def _():
         offsets_ref[...] = means_ref[...]
         send_ref[...] = means_ref[0:1, :]
 
 
-def turn_kernel(last, means_ref, gain_ref, propagator_ref, states_ref, send_ref):
+def last_kernel(
+    last, came_ref, operator_ref, inputs_ref, kept_ref, gain_ref, propagator_ref,
+    means_ref, states_ref, send_ref,
+):
     @pl.when(lax.axis_index("tm") == last)
     def _():
-        steps = means_ref.shape[0]
-        means = [means_ref[t : t + 1, :] for t in range(steps)]
-        moved = times([propagator_ref[...]], *means)
-        state = means[-1]
+        steps = operator_ref.shape[0]
+        state = came_ref[...]
+        means, moved = [], []
+        for t in range(steps):
+            state = times([operator_ref[t]], state) + inputs_ref[t : t + 1, :]
+            means_ref[t : t + 1, :] = state
+            means.append(state)
+            if t < steps - 1:
+                moved.append(times([propagator_ref[...]], state))
         states_ref[steps - 1 : steps, :] = state
         for t in reversed(range(steps - 1)):
             left, state = times([gain_ref[t]], moved[t], state)
@@ -246,63 +330,174 @@
 
     @pl.when(lax.axis_index("tm") != last)
     def _():
-        states_ref[...] = means_ref[...]
-        send_ref[...] = means_ref[0:1, :]
-
-
-def smooth(state, gain_ref, offsets_ref, states_ref, send_ref):
-    steps = gain_ref.shape[0]
-    for t in reversed(range(steps)):
-        state = times([gain_ref[t]], state) + offsets_ref[t : t + 1, :]
-        if len(states_ref.shape) == 3:
-            states_ref[t] = state
-        else:
-            states_ref[t : t + 1, :] = state
-    send_ref[...] = state
-
-
-def first_back_kernel(
-    places, last_ref, far_ref, near_ref, far_parts_ref, near_parts_ref, gain_ref, offsets_ref, kept_ref,
-    came_ref, states_ref, send_ref,
-):
-    here = lax.axis_index("tm") == places - 4
-
-    @pl.when(here)
-    def _():
-        state = times([far_parts_ref[0], far_parts_ref[1]], last_ref[...]) + far_ref[...]
-        state = times([near_parts_ref[0], near_parts_ref[1]], state) + near_ref[...]
-        smooth(state, gain_ref, offsets_ref, states_ref, send_ref)
-
-    @pl.when(jnp.logical_not(here))
-    def _():
+        means_ref[...] = kept_ref[...]
         states_ref[...] = kept_ref[...]
         send_ref[...] = came_ref[...]
 
 
+def smooth(state, gain_ref, offsets_ref, put):
+    for t in reversed(range(gain_ref.shape[0])):
+        state = times([gain_ref[t]], state) + offsets_ref[t : t + 1, :]
+        put(t, state)
+
+
+def parts_times(parts_ref, row_ref):
+    return times([parts_ref[0], parts_ref[1]], row_ref[...])
+
+
+def first_back_kernel(
+    place, last_ref, far_offset_ref, far_parts_ref, own_parts_ref, left_ref, came_ref, entry_ref, send_ref
+):
+    here = lax.axis_index("tm") == place
+
+    @pl.when(here)
+    def _():
+        entry_ref[...] = parts_times(far_parts_ref, last_ref) + far_offset_ref[...]
+        send_ref[...] = parts_times(own_parts_ref, entry_ref) + left_ref[...]
+
+    @pl.when(jnp.logical_not(here))
+    def _():
+        entry_ref[...] = last_ref[...]
+        send_ref[...] = came_ref[...]
+
+
+def second_back_kernel(
+    last,
+    three_ref,
+    one_ref,
+    entry_ref,
+    skip_offset_ref,
+    skip_parts_ref,
+    pair_parts_ref,
+    pair_offset_ref,
+    gain_ref,
+    offsets_ref,
+    kept_ref,
+    came_ref,
+    states_ref,
+    next_ref,
+    send_ref,
+):
+    here = lax.axis_index("tm")
+
+    def put(t, state):
+        states_ref[t : t + 1, :] = state
+
+    @pl.when(here == last - 5)
+    def _():
+        state = parts_times(skip_parts_ref, three_ref) + skip_offset_ref[...]
+        next_ref[...] = state
+        send_ref[...] = times([pair_parts_ref[0], pair_parts_ref[1]], state) + pair_offset_ref[...]
+        states_ref[...] = kept_ref[...]
+
+    @pl.when(here != last - 5)
+    def _():
+        send_ref[...] = came_ref[...]
+        next_ref[...] = entry_ref[...]
+
+    @pl.when(here == last - 2)
+    def _():
+        smooth(entry_ref[...], gain_ref, offsets_ref, put)
+
+    @pl.when((here == last - 3) | (here == last - 1))
+    def _():
+        smooth(jnp.where(here == last - 1, three_ref[...], one_ref[...]), gain_ref, offsets_ref, put)
+        send_ref[...] = states_ref[0:1, :]
+
+    @pl.when((here == last) | (here == last - 4) | (here < last - 5))
+    def _():
+        states_ref[...] = kept_ref[...]
+
+
 def back_kernel(
-    target, stray, two_ref, one_ref, near_ref, near_parts_ref, gain_ref, offsets_ref, kept_ref,
-    came_ref, states_ref, send_ref,
+    target,
+    stray,
+    two_ref,
+    one_ref,
+    entry_ref,
+    near_offset_ref,
+    near_parts_ref,
+    pair_parts_ref,
+    pair_offset_ref,
+    gain_ref,
+    offsets_ref,
+    kept_ref,
+    came_ref,
+    states_ref,
+    next_ref,
+    send_ref,
 ):
     here = lax.axis_index("tm")
 
+    def put(t, state):
+        states_ref[t : t + 1, :] = state
+
     @pl.when(here == target)
     def _():
-        state = times([near_parts_ref[0], near_parts_ref[1]], two_ref[...]) + near_ref[...]
-        smooth(state, gain_ref, offsets_ref, states_ref, send_ref)
+        send_ref[...] = times([pair_parts_ref[0], pair_parts_ref[1]], two_ref[...]) + pair_offset_ref[...]
+        next_ref[...] = two_ref[...]
+        states_ref[...] = kept_ref[...]
+
+    @pl.when(here != target)
+    def _():
+        send_ref[...] = came_ref[...]
+        next_ref[...] = entry_ref[...]
+
+    @pl.when(here == target + 2)
+    def _():
+        state = times([near_parts_ref[0], near_parts_ref[1]], entry_ref[...]) + near_offset_ref[...]
+        smooth(state, gain_ref, offsets_ref, put)
 
     @pl.when((here == target + 1) | (here == stray))
     def _():
-        state = jnp.where(here == stray, two_ref[...], one_ref[...])
-        smooth(state, gain_ref, offsets_ref, states_ref, send_ref)
-
-    @pl.when((here != target) & (here != target + 1) & (here != stray))
+        smooth(jnp.where(here == stray, two_ref[...], one_ref[...]), gain_ref, offsets_ref, put)
+        send_ref[...] = states_ref[0:1, :]
+
+    @pl.when((here > target + 2) & (here != stray) | (here < target))
+    def _():
+        states_ref[...] = kept_ref[...]
+
+
+def final_kernel(
+    stray,
+    two_ref,
+    one_ref,
+    entry_ref,
+    near_offset_ref,
+    near_parts_ref,
+    late_offset_ref,
+    late_parts_ref,
+    gain_ref,
+    offsets_ref,
+    kept_ref,
+    means_ref,
+    result_ref,
+    states_ref,
+):
+    here = lax.axis_index("tm")
+    for t in range(means_ref.shape[0]):
+        result_ref[t] = means_ref[t : t + 1, :]
+
+    def put(t, state):
+        states_ref[t] = state
+
+    @pl.when(here == 0)
+    def _():
+        smooth(parts_times(late_parts_ref, two_ref) + late_offset_ref[...], gain_ref, offsets_ref, put)
+
+    @pl.when(here == 2)
+    def _():
+        state = times([near_parts_ref[0], near_parts_ref[1]], entry_ref[...]) + near_offset_ref[...]
+        smooth(state, gain_ref, offsets_ref, put)
+
+    @pl.when((here == 1) | (here == stray))
+    def _():
+        smooth(jnp.where(here == stray, two_ref[...], one_ref[...]), gain_ref, offsets_ref, put)
+
+    @pl.when((here > 2) & (here != stray))
     def _():
         for t in range(kept_ref.shape[0]):
-            if len(states_ref.shape) == 3:
-                states_ref[t] = kept_ref[t : t + 1, :]
-            else:
-                states_ref[t : t + 1, :] = kept_ref[t : t + 1, :]
-        send_ref[...] = came_ref[...]
+            states_ref[t] = kept_ref[t : t + 1, :]
 
 
 def call(kernel, name, outs, *args, cost=1.0):
@@ -335,7 +530,7 @@
 def ring_up(place, places):
     if place == 0:
         return (0, 1, 3)
-    if place == places - 3:
+    if place % 2 and place >= places - 5 and place < places - 1:
         return (place, place + 1, place + 2)
     if place % 2 or place == places - 2:
         return (place, place + 1)
@@ -359,68 +554,115 @@
     operator = filtering_operator.reshape(steps, size, size)
     covariance = updated_covariance.reshape(steps, size, size)
     gain = backward_factor.reshape(steps, size, size)
+    last = places - 1
+    matrix = propagator.reshape(size, size)
+    square, parts, result = (size, size), (2, size, size), (steps, 1, size)
     mine, other = sensor_info(
         scaled_residual_maps, measurement_stencil, observed_partition, active_probe_total
     )
+
+    def compose(after, *senders):
+        return call(functools.partial(compose_kernel, senders), "compose", (square,), after, gain, cost=0.5)[0]
+
+    near_senders = range(3, last - 3, 2)
+    first = lax.ppermute(
+        compose(mine, last - 1, *near_senders), "tm", [(place, place - 1) for place in (*near_senders, last - 1)]
+    )
     inputs, means, send = call(
-        inputs_kernel, "inputs", (many, many, one), mine, other, covariance, operator, initial_mean
-    )
-    composed = call(compose_kernel, "compose", ((size, size),), send, gain)[0]
-    near = lax.ppermute(composed, "tm", [(place + 1, place) for place in range(0, places - 2, 2)])
-    far = lax.ppermute(composed, "tm", [(places - 2, places - 4)])
-    matrix = propagator.reshape(size, size)
+        inputs_kernel, "inputs", (many, many, one), mine, other, covariance, operator, initial_mean,
+        cost=COSTS[0],
+    )
+    skip = lax.ppermute(compose(send, last - 3), "tm", [(last - 3, last - 5)])
     for place in range(1, places):
         came = pass_row(send, [ring_up(place - 1, places)], places)
-        if place == places - 1:
-            offsets, left = call(
-                functools.partial(offsets_kernel, places - 1), "offsets", (many, one), means, gain, matrix
+        if place == 2:
+            late = call(
+                functools.partial(late_kernel, (1,)), "late", ((size + 8, size),), means, gain, matrix,
+                cost=0.5,
+            )[0]
+            late = lax.ppermute(late, "tm", [(1, 0)])
+        if place < last:
+            means, send = call(
+                functools.partial(hop_kernel, place), "forward", (many, one), came, operator, inputs, means,
+                cost={1: COSTS[1], 2: COSTS[2]}.get(place, 0.5),
             )
-            far_offset = pass_row(left, [(places - 2, places - 4)], places)
-            near_offset = pass_row(left, [(at, at + 1) for at in range(0, places - 2, 2)], places)
-        means, send = call(
-            functools.partial(hop_kernel, place), "forward", (many, one), came, operator, inputs, means,
-            cost=MATRIX_COST if place == 1 else 0.5,
-        )
-    states, send = call(
-        functools.partial(turn_kernel, places - 1), "turn", (many, one), means, gain, matrix
-    )
-    last = pass_row(send, [(places - 1, places - 4)], places)
-    parts = (2, size, size)
-    result = (steps, 1, size)
-    near_parts, far_parts, means = call(split_kernel, "split", (parts, parts, result), near, far, means)
-    states, send = call(
-        functools.partial(first_back_kernel, places),
-        "first_back",
-        (many, one),
-        last,
-        far_offset,
+    offset_rows, left, own_parts = call(
+        functools.partial(offsets_kernel, last), "offsets", (many, one, parts), means, gain, matrix
+    )
+    other_offset = pass_row(left, [(last - 1, last - 2), (last - 3, last - 5)], places)
+    means, states, send = call(
+        functools.partial(last_kernel, last),
+        "last",
+        (many, many, one),
+        came,
+        operator,
+        inputs,
+        means,
+        gain,
+        matrix,
+        cost=0.5,
+    )
+    came = pass_row(send, [(last, last - 2)], places)
+
+    far_parts, again = call(
+        functools.partial(split_kernel, last - 2), "split", (parts, one), first, left, cost=0.05
+    )
+    near_offset = pass_row(again, [(place - 1, place) for place in near_senders], places)
+    entry, send = call(
+        functools.partial(first_back_kernel, last - 2), "first_back", (one, one),
+        came, other_offset, far_parts, own_parts, left, send,
+        cost=COSTS[3],
+    )
+    one_up = pass_row(send, [(last - 2, last - 3)], places)
+    three = pass_row(send, [(last - 2, last - 5), (last, last - 1)], places)
+    near_parts, pair_parts, pair_offset, skip_parts = call(
+        functools.partial(pair_kernel, tuple(place - 1 for place in near_senders), last - 5),
+        "pair",
+        (parts, parts, one, parts),
+        first,
+        skip,
+        gain,
+        left,
         near_offset,
-        far_parts,
-        near_parts,
+        cost=0.05,
+    )
+    states, entry, send = call(
+        functools.partial(second_back_kernel, last),
+        "second_back",
+        (many, one, one),
+        three,
+        one_up,
+        entry,
+        other_offset,
+        skip_parts,
+        pair_parts,
+        pair_offset,
         gain,
-        offsets,
+        offset_rows,
         states,
         send,
-    )
-    stray = places - 2
-    for target in range(places - 6, -1, -2):
-        rings = [(target + 2, target)] + ([(stray + 1, stray)] if stray > target + 2 else [])
+        cost=COSTS[4],
+    )
+    stray = last - 4
+    for target in range(last - 7, -1, -2):
+        rings = [(target + 2, target)] + ([(stray + 1, stray)] if stray > 0 else [])
+        one_up = pass_row(send, [(target + 2, target + 1)], places)
         two = pass_row(send, rings, places)
-        one_up = pass_row(send, [(target + 2, target + 1)], places)
-        states, send = call(
-            functools.partial(back_kernel, target, stray),
-            "back",
-            (many if target else result, one),
-            two,
-            one_up,
-            near_offset,
-            near_parts,
-            gain,
-            offsets,
-            states,
-            send,
-        )
-        stray = stray - 1 if stray == places - 2 else -1
+        if target:
+            states, entry, send = call(
+                functools.partial(back_kernel, target, stray), "back", (many, one, one),
+                two, one_up, entry, near_offset, near_parts, pair_parts, pair_offset, gain, offset_rows, states,
+                send,
+            )
+        else:
+            late_parts, late_offset = call(
+                functools.partial(late_split_kernel, 0), "late_split", (parts, one), late, send, cost=0.05
+            )
+            means, states = call(
+                functools.partial(final_kernel, stray), "final", (result, result),
+                two, one_up, entry, near_offset, near_parts, late_offset, late_parts, gain, offset_rows, states, means,
+            )
+        stray = -1
     return means, states
 
 

time: 46.8 us -> 44.9 us (0.959)
  waiting for transfers between devices: 19.5 us -> 11.6 us
  starting transfers between devices: 19 us -> 25.5 us
  Pallas kernels: 7.32 us -> 5.6 us
  local copies, waits for them, and re-layouts: 0.02 us -> 1.17 us
    ppermute x2 -> x3, waiting for transfers between devices: 10.6 us -> 0.01 us  [the longest x1 0.01 us: local(): late = lax.ppermute(late, 'tm', [(1, 0)])]
    ppermute x14, starting transfers between devices: 16.5 us -> 22.1 us  [pass_row(): return lax.ppermute(row, ('tm', 'block'), sorted(route.items()))]
    ppermute x14, waiting for transfers between devices: 8.07 us -> 11.6 us  [pass_row(): return lax.ppermute(row, ('tm', 'block'), sorted(route.items()))]
    pallas_call x15 -> x18, Pallas kernels: 4.62 us -> 2.94 us  [call(): pl.pallas_call(kernel, out_shape=[jax.ShapeDtypeStruct(shape, jnp.bfloat1...]
    unnamed x10, local copies, waits for them, and re-layouts: 0.02 us -> 1.17 us
    ppermute x2 -> x3, starting transfers between devices: 2.02 us -> 2.84 us  [the longest x1 1.28 us: local(): late = lax.ppermute(late, 'tm', [(1, 0)])]
    ppermute x1, waiting for transfers between devices: 0.82 us -> 0.01 us  [sensor_info(): return (mine, lax.ppermute(theirs, 'block', [(0, 1), (1, 0)]))]
  transfers between devices with their start and end apart: 17 -> 18, of which waited for: 11 -> 10; matrix products, arithmetic and copies ran while one was open for 0% -> 0% of each run, Pallas kernels for 5% -> 3%
where the time goes in v6:
time: 44.9 us; the launch traced here: 44.6 us
  starting transfers between devices  25.5 us (57%)
  waiting for transfers between devices  11.6 us (26%)
  Pallas kernels  5.6 us (12%)
  local copies, waits for them, and re-layouts  1.17 us (3%)
  between operations  0.78 us (2%)
    ppermute x14, starting transfers between devices, pass_row(): return lax.ppermute(row, ('tm', 'block'), sorted(route.items()))  22.1 us
    ppermute x14, waiting for transfers between devices, pass_row(): return lax.ppermute(row, ('tm', 'block'), sorted(route.items()))  11.6 us
    pallas_call x18, Pallas kernels, call(): pl.pallas_call(kernel, out_shape=[jax.ShapeDtypeStruct(shape, jnp.bfloat1...  2.94 us
    pallas_call x1, Pallas kernels, sensor_info(): pl.pallas_call(info_kernel, out_shape=[jax.ShapeDtypeStruct((steps, cells...  2.66 us
    ppermute x1, starting transfers between devices, local(): late = lax.ppermute(late, 'tm', [(1, 0)])  1.28 us
    unnamed x10, local copies, waits for them, and re-layouts  1.17 us
  transfers between devices with their start and end apart: 18, of which 10 were waited for; matrix products, arithmetic and copies ran while one was open for 0% of the time, Pallas kernels for 3%

profile of v6, /device:TPU:0, one launch (start us, length us, event | category | flops | bytes accessed | tf_op | source)
XLA Modules:
  0.0 44.6 jit_solution(33954210454774054)
XLA Ops:
  0.6 2.7 %sensor_info.1 = (f32[2,512]{1,0:T(2,128)S(1)}, f32[2,512]{1,0:T(2,128)S(1)}) custom-call(bf16[2,1024,512]{2,1,0:T(8,128)(2,1)} %bitcast.27, bf16[7,7,16]{2,1,0:T(8,128)(2,1)} %bitcast.28, s32[2,64]{1,0:T(2,128)} %observed_hbm.1, s32[1,2]{1,0:T(1,128)} %bitcast.29), custom_call_target="tpu_custom_call" | custom-call | tf_op jit(solution)/shard_map/sensor_info/pallas_call | solution.py:133
  3.3 0.5 %collective-permute-start = (f32[2,512]{1,0:T(2,128)S(1)}, f32[2,512]{1,0:T(2,128)S(1)}, u32[]{:S(2)}, u32[]{:S(2)}) collective-permute-start(f32[2,512]{1,0:T(2,128)S(1)} %get-tuple-element.39), channel_id=1, source_target_pairs={{0,1},{1,0},{2,3},{3,2},{4,5},{5,4},{6,7},{7,6},{8,9},{9,8},{10,11... | collective-permute-start | bytes 12296 | tf_op jit(solution)/shard_map/ppermute | solution.py:160
  3.9 0.8 %collective-permute-start.10 = (f32[512,512]{1,0:T(8,128)S(1)}, f32[512,512]{1,0:T(8,128)S(1)}, u32[]{:S(2)}, u32[]{:S(2)}) collective-permute-start(f32[512,512]{1,0:T(8,128)S(1)} %compose.2), channel_id=1, source_target_pairs={{6,4},{12,10},{7,5},{13,11},{22,20},{28,26},{23,21},{29,27}} | collective-permute-start | bytes 3145736 | tf_op jit(solution)/shard_map/ppermute | solution.py:568
  4.9 0.7 %inputs.1 = (f32[2,512]{1,0:T(2,128)S(1)}, f32[2,512]{1,0:T(2,128)S(1)}, f32[1,512]{1,0:T(1,128)S(1)}) custom-call(f32[2,512]{1,0:T(2,128)S(1)} %get-tuple-element.38.mine_ref.after_ref, f32[2,512]{1,0:T(2,128)S(1)} %collective-permute-done.other_ref, bf16[2,512,512]{2,1,0:T(8,128)(2,1)S(1)} %bitcast.26, bf16[2,512,512]{2,1,0:T(8,128)(2,1)S(1)} %bitcast.18, ...), custom_call_target="tpu_custom_call" | custom-call | flops 60000002048 | bytes 1048576 | tf_op jit(solution)/shard_map/inputs/pallas_call | solution.py:504
  5.5 3.0 %collective-permute-start.1 = (f32[1,512]{1,0:T(1,128)S(1)}, f32[1,512]{1,0:T(1,128)S(1)}, u32[]{:S(2)}, u32[]{:S(2)}) collective-permute-start(f32[1,512]{1,0:T(1,128)S(1)} %get-tuple-element.40.after_ref), channel_id=1, source_target_pairs={{0,2},{1,3},{2,6},{3,7},{4,5},{5,4},{6,0},{7,1},{8,9},{9,8},{10,11... | collective-permute-start | bytes 6152 | tf_op jit(solution)/shard_map/ppermute | solution.py:527
  8.6 0.7 %collective-permute-start.13 = (f32[512,512]{1,0:T(8,128)S(1)}, f32[512,512]{1,0:T(8,128)S(1)}, u32[]{:S(2)}, u32[]{:S(2)}) collective-permute-start(f32[512,512]{1,0:T(8,128)S(1)} %compose.3), channel_id=1, source_target_pairs={{8,4},{9,5},{24,20},{25,21}} | collective-permute-start | bytes 3145736 | tf_op jit(solution)/shard_map/ppermute | solution.py:575
  9.3 3.1 %collective-permute-done.1.came_ref = f32[1,512]{1,0:T(1,128)S(1)} collective-permute-done((f32[1,512]{1,0:T(1,128)S(1)}, f32[1,512]{1,0:T(1,128)S(1)}, u32[]{:S(2)}, u32[]{:S(2)}) %collective-permute-start.1) | collective-permute-done | bytes 2080 | tf_op jit(solution)/shard_map/ppermute | solution.py:527
  12.4 1.0 %copy-done.1 = bf16[1,512,512]{2,1,0:T(8,128)(2,1)S(1)} copy-done((bf16[1,512,512]{2,1,0:T(8,128)(2,1)S(1)}, bf16[1,512,512]{2,1,0:T(8,128)(2,1)}, u32[]{:S(2)}) %copy-start.1) | copy-done | bytes 524312
  13.5 1.3 %collective-permute-start.17 = (f32[520,512]{1,0:T(8,128)S(1)}, f32[520,512]{1,0:T(8,128)S(1)}, u32[]{:S(2)}, u32[]{:S(2)}) collective-permute-start(f32[520,512]{1,0:T(8,128)S(1)} %late.1), channel_id=1, source_target_pairs={{2,0},{3,1},{18,16},{19,17}} | collective-permute-start | bytes 3194888 | tf_op jit(solution)/shard_map/ppermute | solution.py:583
  14.8 2.1 %collective-permute-start.3 = (f32[1,512]{1,0:T(1,128)S(1)}, f32[1,512]{1,0:T(1,128)S(1)}, u32[]{:S(2)}, u32[]{:S(2)}) collective-permute-start(f32[1,512]{1,0:T(1,128)S(1)} %get-tuple-element.45), channel_id=1, source_target_pairs={{0,4},{1,5},{2,3},{3,2},{4,6},{5,7},{6,0},{7,1},{8,9},{9,8},{10,11... | collective-permute-start | bytes 6152 | tf_op jit(solution)/shard_map/ppermute | solution.py:527
  16.9 2.5 %collective-permute-done.3.came_ref = f32[1,512]{1,0:T(1,128)S(1)} collective-permute-done((f32[1,512]{1,0:T(1,128)S(1)}, f32[1,512]{1,0:T(1,128)S(1)}, u32[]{:S(2)}, u32[]{:S(2)}) %collective-permute-start.3) | collective-permute-done | bytes 2080 | tf_op jit(solution)/shard_map/ppermute | solution.py:527
  19.5 1.2 %collective-permute-done.4.came_ref = f32[1,512]{1,0:T(1,128)S(1)} collective-permute-done((f32[1,512]{1,0:T(1,128)S(1)}, f32[1,512]{1,0:T(1,128)S(1)}, u32[]{:S(2)}, u32[]{:S(2)}) %collective-permute-start.4) | collective-permute-done | bytes 2080 | tf_op jit(solution)/shard_map/ppermute | solution.py:527
  20.6 0.2 collective-permute-start.5
  20.8 1.0 %collective-permute-done.5.came_ref = f32[1,512]{1,0:T(1,128)S(1)} collective-permute-done((f32[1,512]{1,0:T(1,128)S(1)}, f32[1,512]{1,0:T(1,128)S(1)}, u32[]{:S(2)}, u32[]{:S(2)}) %collective-permute-start.5) | collective-permute-done | bytes 2080 | tf_op jit(solution)/shard_map/ppermute | solution.py:527
  21.8 0.2 collective-permute-start.6
  21.9 1.0 %collective-permute-done.6.came_ref = f32[1,512]{1,0:T(1,128)S(1)} collective-permute-done((f32[1,512]{1,0:T(1,128)S(1)}, f32[1,512]{1,0:T(1,128)S(1)}, u32[]{:S(2)}, u32[]{:S(2)}) %collective-permute-start.6) | collective-permute-done | bytes 2080 | tf_op jit(solution)/shard_map/ppermute | solution.py:527
  22.9 0.2 collective-permute-start.7
  23.1 0.7 %offsets.1 = (f32[2,512]{1,0:T(2,128)S(1)}, f32[1,512]{1,0:T(1,128)S(1)}, bf16[2,512,512]{2,1,0:T(8,128)(2,1)S(1)}) custom-call(f32[2,512]{1,0:T(2,128)S(1)} %get-tuple-element.54.kept_ref.means_ref, bf16[2,512,512]{2,1,0:T(8,128)(2,1)S(1)} %bitcast.10, bf16[512,512]{1,0:T(8,128)(2,1)S(1)} %bitcast.16), custom_call_target="tpu_custom_call" | custom-call | flops 1000000000 | bytes 1048576 | tf_op jit(solution)/shard_map/offsets/pallas_call | solution.py:504
  23.8 0.4 collective-permute-start.9
  24.2 0.2 collective-permute-start.8
  24.4 0.3 collective-permute-start.14
  24.7 0.3 collective-permute-done.9.far_offset_ref.skip_offset_ref
  25.0 0.3 collective-permute-done.8.last_ref
  25.4 0.2 collective-permute-start.12
  25.5 0.3 collective-permute-start.11
  25.9 0.6 %collective-permute-done.12.one_ref = f32[1,512]{1,0:T(1,128)S(1)} collective-permute-done((f32[1,512]{1,0:T(1,128)S(1)}, f32[1,512]{1,0:T(1,128)S(1)}, u32[]{:S(2)}, u32[]{:S(2)}) %collective-permute-start.12) | collective-permute-done | bytes 2080 | tf_op jit(solution)/shard_map/ppermute | solution.py:527
  26.5 0.2 collective-permute-done.11.three_ref
  26.7 0.3 collective-permute-start.16
  27.0 14.6 %collective-permute-start.15 = (f32[1,512]{1,0:T(1,128)S(1)}, f32[1,512]{1,0:T(1,128)S(1)}, u32[]{:S(2)}, u32[]{:S(2)}) collective-permute-start(f32[1,512]{1,0:T(1,128)S(1)} %get-tuple-element.67.after_ref), channel_id=1, source_target_pairs={{0,4},{1,5},{2,3},{3,2},{4,0},{5,1},{6,8},{7,9},{8,6},{9,7},{10,11... | collective-permute-start | bytes 6152 | tf_op jit(solution)/shard_map/ppermute | solution.py:527
  41.7 0.1 late_split.1
  41.8 1.4 %collective-permute-done.15.two_ref = f32[1,512]{1,0:T(1,128)S(1)} collective-permute-done((f32[1,512]{1,0:T(1,128)S(1)}, f32[1,512]{1,0:T(1,128)S(1)}, u32[]{:S(2)}, u32[]{:S(2)}) %collective-permute-start.15) | collective-permute-done | bytes 2080 | tf_op jit(solution)/shard_map/ppermute | solution.py:527
  43.2 1.4 %final.1 = (f32[2,1,512]{2,1,0:T(1,128)}, f32[2,1,512]{2,1,0:T(1,128)}) custom-call(f32[1,512]{1,0:T(1,128)S(1)} %collective-permute-done.15.two_ref, f32[1,512]{1,0:T(1,128)S(1)} %collective-permute-done.16.one_ref, f32[1,512]{1,0:T(1,128)S(1)} %get-tuple-element.68.entry_ref, f32[1,512]{1,0:T(1,128)S(1)} %collective-permute-done.14.near_offset_ref, ...), custom_call_target="tpu_custom_call" | custom-call | flops 1000000000 | bytes 1048576 | tf_op jit(solution)/shard_map/final/pallas_call | solution.py:504
  (33 shorter events, 0.2 us)
Async XLA Ops:
  0.6 3.2 %copy-start = (bf16[2,1,512,512]{3,2,1,0:T(8,128)(2,1)S(1)}, bf16[2,1,512,512]{3,2,1,0:T(8,128)(2,1)}, u32[]{:S(2)}) copy-start(bf16[2,1,512,512]{3,2,1,0:T(8,128)(2,1)} %param.15) | copy-start | bytes 3145732
  3.3 1.4 %copy-start.2 = (bf16[2,1,512,512]{3,2,1,0:T(8,128)(2,1)S(1)}, bf16[2,1,512,512]{3,2,1,0:T(8,128)(2,1)}, u32[]{:S(2)}) copy-start(bf16[2,1,512,512]{3,2,1,0:T(8,128)(2,1)} %param.13) | copy-start | bytes 3145732
  3.3 1.5 %copy-start.3 = (bf16[2,1,512,512]{3,2,1,0:T(8,128)(2,1)S(1)}, bf16[2,1,512,512]{3,2,1,0:T(8,128)(2,1)}, u32[]{:S(2)}) copy-start(bf16[2,1,512,512]{3,2,1,0:T(8,128)(2,1)} %param.14) | copy-start | bytes 3145732
  3.3 1.5 %copy-start.4 = (f32[1,512]{1,0:T(1,128)S(1)}, f32[1,512]{1,0:T(1,128)}, u32[]{:S(2)}) copy-start(f32[1,512]{1,0:T(1,128)} %start_ref.1) | copy-start | bytes 6148
  3.3 1.4 %collective-permute-start = (f32[2,512]{1,0:T(2,128)S(1)}, f32[2,512]{1,0:T(2,128)S(1)}, u32[]{:S(2)}, u32[]{:S(2)}) collective-permute-start(f32[2,512]{1,0:T(2,128)S(1)} %get-tuple-element.39), channel_id=1, source_target_pairs={{0,1},{1,0},{2,3},{3,2},{4,5},{5,4},{6,7},{7,6},{8,9},{9,8},{10,11... | collective-permute-start | bytes 12296 | tf_op jit(solution)/shard_map/ppermute | solution.py:160
  3.9 20.5 %collective-permute-start.10 = (f32[512,512]{1,0:T(8,128)S(1)}, f32[512,512]{1,0:T(8,128)S(1)}, u32[]{:S(2)}, u32[]{:S(2)}) collective-permute-start(f32[512,512]{1,0:T(8,128)S(1)} %compose.2), channel_id=1, source_target_pairs={{6,4},{12,10},{7,5},{13,11},{22,20},{28,26},{23,21},{29,27}} | collective-permute-start | bytes 3145736 | tf_op jit(solution)/shard_map/ppermute | solution.py:568
  5.5 6.9 %collective-permute-start.1 = (f32[1,512]{1,0:T(1,128)S(1)}, f32[1,512]{1,0:T(1,128)S(1)}, u32[]{:S(2)}, u32[]{:S(2)}) collective-permute-start(f32[1,512]{1,0:T(1,128)S(1)} %get-tuple-element.40.after_ref), channel_id=1, source_target_pairs={{0,2},{1,3},{2,6},{3,7},{4,5},{5,4},{6,0},{7,1},{8,9},{9,8},{10,11... | collective-permute-start | bytes 6152 | tf_op jit(solution)/shard_map/ppermute | solution.py:527
  8.6 17.3 %collective-permute-start.13 = (f32[512,512]{1,0:T(8,128)S(1)}, f32[512,512]{1,0:T(8,128)S(1)}, u32[]{:S(2)}, u32[]{:S(2)}) collective-permute-start(f32[512,512]{1,0:T(8,128)S(1)} %compose.3), channel_id=1, source_target_pairs={{8,4},{9,5},{24,20},{25,21}} | collective-permute-start | bytes 3145736 | tf_op jit(solution)/shard_map/ppermute | solution.py:575
  12.4 1.0 %copy-start.1 = (bf16[1,512,512]{2,1,0:T(8,128)(2,1)S(1)}, bf16[1,512,512]{2,1,0:T(8,128)(2,1)}, u32[]{:S(2)}) copy-start(bf16[1,512,512]{2,1,0:T(8,128)(2,1)} %param.16) | copy-start | bytes 1572868
  12.4 2.3 %collective-permute-start.2 = (f32[1,512]{1,0:T(1,128)S(1)}, f32[1,512]{1,0:T(1,128)S(1)}, u32[]{:S(2)}, u32[]{:S(2)}) collective-permute-start(f32[1,512]{1,0:T(1,128)S(1)} %get-tuple-element.43), channel_id=1, source_target_pairs={{0,1},{1,0},{2,4},{3,5},{4,2},{5,3},{6,7},{7,6},{8,9},{9,8},{10,11... | collective-permute-start | bytes 6152 | tf_op jit(solution)/shard_map/ppermute | solution.py:527
  13.5 28.2 %collective-permute-start.17 = (f32[520,512]{1,0:T(8,128)S(1)}, f32[520,512]{1,0:T(8,128)S(1)}, u32[]{:S(2)}, u32[]{:S(2)}) collective-permute-start(f32[520,512]{1,0:T(8,128)S(1)} %late.1), channel_id=1, source_target_pairs={{2,0},{3,1},{18,16},{19,17}} | collective-permute-start | bytes 3194888 | tf_op jit(solution)/shard_map/ppermute | solution.py:583
  14.8 4.7 %collective-permute-start.3 = (f32[1,512]{1,0:T(1,128)S(1)}, f32[1,512]{1,0:T(1,128)S(1)}, u32[]{:S(2)}, u32[]{:S(2)}) collective-permute-start(f32[1,512]{1,0:T(1,128)S(1)} %get-tuple-element.45), channel_id=1, source_target_pairs={{0,4},{1,5},{2,3},{3,2},{4,6},{5,7},{6,0},{7,1},{8,9},{9,8},{10,11... | collective-permute-start | bytes 6152 | tf_op jit(solution)/shard_map/ppermute | solution.py:527
  19.4 1.2 %collective-permute-start.4 = (f32[1,512]{1,0:T(1,128)S(1)}, f32[1,512]{1,0:T(1,128)S(1)}, u32[]{:S(2)}, u32[]{:S(2)}) collective-permute-start(f32[1,512]{1,0:T(1,128)S(1)} %get-tuple-element.47), channel_id=1, source_target_pairs={{0,1},{1,0},{2,3},{3,2},{4,5},{5,4},{6,8},{7,9},{8,10},{9,11},{10,... | collective-permute-start | bytes 6152 | tf_op jit(solution)/shard_map/ppermute | solution.py:527
  20.6 1.2 %collective-permute-start.5 = (f32[1,512]{1,0:T(1,128)S(1)}, f32[1,512]{1,0:T(1,128)S(1)}, u32[]{:S(2)}, u32[]{:S(2)}) collective-permute-start(f32[1,512]{1,0:T(1,128)S(1)} %get-tuple-element.49), channel_id=1, source_target_pairs={{0,1},{1,0},{2,3},{3,2},{4,8},{5,9},{6,7},{7,6},{8,10},{9,11},{10,... | collective-permute-start | bytes 6152 | tf_op jit(solution)/shard_map/ppermute | solution.py:527
  21.8 1.2 %collective-permute-start.6 = (f32[1,512]{1,0:T(1,128)S(1)}, f32[1,512]{1,0:T(1,128)S(1)}, u32[]{:S(2)}, u32[]{:S(2)}) collective-permute-start(f32[1,512]{1,0:T(1,128)S(1)} %get-tuple-element.51), channel_id=1, source_target_pairs={{0,1},{1,0},{2,3},{3,2},{4,5},{5,4},{6,7},{7,6},{8,9},{9,8},{10,12... | collective-permute-start | bytes 6152 | tf_op jit(solution)/shard_map/ppermute | solution.py:527
  22.9 1.3 %collective-permute-start.7 = (f32[1,512]{1,0:T(1,128)S(1)}, f32[1,512]{1,0:T(1,128)S(1)}, u32[]{:S(2)}, u32[]{:S(2)}) collective-permute-start(f32[1,512]{1,0:T(1,128)S(1)} %get-tuple-element.53), channel_id=1, source_target_pairs={{0,1},{1,0},{2,3},{3,2},{4,5},{5,4},{6,7},{7,6},{8,9},{9,8},{10,11... | collective-permute-start | bytes 6152 | tf_op jit(solution)/shard_map/ppermute | solution.py:527
  23.8 1.2 %collective-permute-start.9 = (f32[1,512]{1,0:T(1,128)S(1)}, f32[1,512]{1,0:T(1,128)S(1)}, u32[]{:S(2)}, u32[]{:S(2)}) collective-permute-start(f32[1,512]{1,0:T(1,128)S(1)} %get-tuple-element.56.left_ref), channel_id=1, source_target_pairs={{0,1},{1,0},{2,3},{3,2},{4,8},{5,9},{6,7},{7,6},{8,4},{9,5},{10,12... | collective-permute-start | bytes 6152 | tf_op jit(solution)/shard_map/ppermute | solution.py:527
  24.2 1.2 %collective-permute-start.8 = (f32[1,512]{1,0:T(1,128)S(1)}, f32[1,512]{1,0:T(1,128)S(1)}, u32[]{:S(2)}, u32[]{:S(2)}) collective-permute-start(f32[1,512]{1,0:T(1,128)S(1)} %get-tuple-element.55.came_ref), channel_id=1, source_target_pairs={{0,1},{1,0},{2,3},{3,2},{4,5},{5,4},{6,7},{7,6},{8,9},{9,8},{10,14... | collective-permute-start | bytes 6152 | tf_op jit(solution)/shard_map/ppermute | solution.py:527
  24.4 1.5 %collective-permute-start.14 = (f32[1,512]{1,0:T(1,128)S(1)}, f32[1,512]{1,0:T(1,128)S(1)}, u32[]{:S(2)}, u32[]{:S(2)}) collective-permute-start(f32[1,512]{1,0:T(1,128)S(1)} %get-tuple-element.61), channel_id=1, source_target_pairs={{0,1},{1,0},{2,3},{3,2},{4,6},{5,7},{6,4},{7,5},{8,9},{9,8},{10,11... | collective-permute-start | bytes 6152 | tf_op jit(solution)/shard_map/ppermute | solution.py:527
  25.4 1.2 %collective-permute-start.12 = (f32[1,512]{1,0:T(1,128)S(1)}, f32[1,512]{1,0:T(1,128)S(1)}, u32[]{:S(2)}, u32[]{:S(2)}) collective-permute-start(f32[1,512]{1,0:T(1,128)S(1)} %get-tuple-element.59.came_ref), channel_id=1, source_target_pairs={{0,1},{1,0},{2,3},{3,2},{4,5},{5,4},{6,7},{7,6},{8,10},{9,11},{10,... | collective-permute-start | bytes 6152 | tf_op jit(solution)/shard_map/ppermute | solution.py:527
  25.5 1.2 %collective-permute-start.11 = (f32[1,512]{1,0:T(1,128)S(1)}, f32[1,512]{1,0:T(1,128)S(1)}, u32[]{:S(2)}, u32[]{:S(2)}) collective-permute-start(f32[1,512]{1,0:T(1,128)S(1)} %get-tuple-element.59.came_ref), channel_id=1, source_target_pairs={{0,1},{1,0},{2,3},{3,2},{4,10},{5,11},{6,7},{7,6},{8,9},{9,8},{10,... | collective-permute-start | bytes 6152 | tf_op jit(solution)/shard_map/ppermute | solution.py:527
  26.7 15.1 %collective-permute-start.16 = (f32[1,512]{1,0:T(1,128)S(1)}, f32[1,512]{1,0:T(1,128)S(1)}, u32[]{:S(2)}, u32[]{:S(2)}) collective-permute-start(f32[1,512]{1,0:T(1,128)S(1)} %get-tuple-element.67.after_ref), channel_id=1, source_target_pairs={{0,1},{1,0},{2,4},{3,5},{4,2},{5,3},{6,7},{7,6},{8,9},{9,8},{10,11... | collective-permute-start | bytes 6152 | tf_op jit(solution)/shard_map/ppermute | solution.py:527
  27.0 16.2 %collective-permute-start.15 = (f32[1,512]{1,0:T(1,128)S(1)}, f32[1,512]{1,0:T(1,128)S(1)}, u32[]{:S(2)}, u32[]{:S(2)}) collective-permute-start(f32[1,512]{1,0:T(1,128)S(1)} %get-tuple-element.67.after_ref), channel_id=1, source_target_pairs={{0,4},{1,5},{2,3},{3,2},{4,0},{5,1},{6,8},{7,9},{8,6},{9,7},{10,11... | collective-permute-start | bytes 6152 | tf_op jit(solution)/shard_map/ppermute | solution.py:527

commit v7 on v6

--- a/solution.py
+++ b/solution.py
@@ -36,7 +36,13 @@
     return found if len(rows) > 1 else found[0]
 
 
-def info_kernel(
+def info_kernel(zero, *refs):
+    @pl.when((lax.axis_index("tm") == 0) == zero)
+    def _():
+        place_info(*(refs if zero else refs[1:]))
+
+
+def place_info(
     maps_hbm,
     stencil_hbm,
     observed_hbm,
@@ -127,13 +133,14 @@
         theirs_ref[t : t + 1, :] = jnp.where(me == 0, found[1], found[0])
 
 
-def sensor_info(scaled_residual_maps, measurement_stencil, observed_partition, active_probe_total):
+def sensor_info(after, scaled_residual_maps, measurement_stencil, observed_partition, active_probe_total):
+    zero = not after
     steps, slots, channels, cells = scaled_residual_maps.shape
     side = measurement_stencil.shape[1]
     mine, theirs = pl.pallas_call(
-        info_kernel,
+        functools.partial(info_kernel, zero),
         out_shape=[jax.ShapeDtypeStruct((steps, cells), jnp.float32)] * 2,
-        in_specs=[pl.BlockSpec(memory_space=pltpu.HBM)] * 4,
+        in_specs=[VMEM] * len(after) + [pl.BlockSpec(memory_space=pltpu.HBM)] * 4,
         out_specs=[VMEM] * 2,
         scratch_shapes=[
             pltpu.VMEM((steps, slots * channels, cells), jnp.bfloat16),
@@ -145,8 +152,10 @@
             pltpu.SemaphoreType.DMA((3,)),
         ],
         compiler_params=PARAMS,
+        cost_estimate=pl.CostEstimate(flops=10**6 if zero else int(COSTS[0] * 1e9), bytes_accessed=2**12, transcendentals=0),
         name="sensor_info",
     )(
+        *after,
         *(
             pltpu.with_memory_space_constraint(array, pltpu.HBM)
             for array in (
@@ -160,14 +169,54 @@
     return mine, lax.ppermute(theirs, "block", [(0, 1), (1, 0)])
 
 
-def inputs_kernel(mine_ref, other_ref, covariance_ref, operator_ref, start_ref, inputs_ref, states_ref, send_ref):
-    state = start_ref[...]
-    for t in range(mine_ref.shape[0]):
-        drive = times([covariance_ref[t]], mine_ref[t : t + 1, :] + other_ref[t : t + 1, :])
-        inputs_ref[t : t + 1, :] = drive
-        state = times([operator_ref[t]], state) + drive
-        states_ref[t : t + 1, :] = state
-    send_ref[...] = state
+def start_kernel(mine_ref, other_ref, covariance_ref, operator_ref, start_ref, inputs_ref, states_ref, send_ref):
+    here = lax.axis_index("tm") == 0
+
+    @pl.when(here)
+    def _():
+        state = start_ref[...]
+        for t in range(mine_ref.shape[0]):
+            drive = times([covariance_ref[t]], mine_ref[t : t + 1, :] + other_ref[t : t + 1, :])
+            inputs_ref[t : t + 1, :] = drive
+            state = times([operator_ref[t]], state) + drive
+            states_ref[t : t + 1, :] = state
+        send_ref[...] = jnp.broadcast_to(state, send_ref.shape)
+
+    @pl.when(jnp.logical_not(here))
+    def _():
+        inputs_ref[...] = jnp.zeros_like(inputs_ref)
+        states_ref[...] = jnp.zeros_like(states_ref)
+        send_ref[...] = jnp.zeros_like(send_ref)
+
+
+def first_hop_kernel(
+    came_ref, mine_ref, other_ref, covariance_ref, operator_ref, kept_inputs_ref, kept_ref,
+    inputs_ref, states_ref, send_ref,
+):
+    here = lax.axis_index("tm")
+
+    @pl.when(here == 0)
+    def _():
+        inputs_ref[...] = kept_inputs_ref[...]
+
+    @pl.when(here != 0)
+    def _():
+        for t in range(mine_ref.shape[0]):
+            info = mine_ref[t : t + 1, :] + other_ref[t : t + 1, :]
+            inputs_ref[t : t + 1, :] = times([covariance_ref[t]], info)
+
+    @pl.when(here == 1)
+    def _():
+        state = came_ref[0:1, :]
+        for t in range(operator_ref.shape[0]):
+            state = times([operator_ref[t]], state) + inputs_ref[t : t + 1, :]
+            states_ref[t : t + 1, :] = state
+        send_ref[...] = state
+
+    @pl.when(here != 1)
+    def _():
+        states_ref[...] = kept_ref[...]
+        send_ref[...] = came_ref[0:1, :]
 
 
 def hop_kernel(turn, came_ref, matrices_ref, offsets_ref, kept_ref, states_ref, send_ref):
@@ -510,7 +559,7 @@
         in_specs=[VMEM] * len(args),
         out_specs=[VMEM] * len(outs),
         compiler_params=PARAMS,
-        cost_estimate=pl.CostEstimate(flops=int(cost * 1e9), bytes_accessed=2**20, transcendentals=0),
+        cost_estimate=pl.CostEstimate(flops=int(cost * 1e9), bytes_accessed=2**12, transcendentals=0),
         name=name,
     )(*args)
 
@@ -557,24 +606,29 @@
     last = places - 1
     matrix = propagator.reshape(size, size)
     square, parts, result = (size, size), (2, size, size), (steps, 1, size)
-    mine, other = sensor_info(
-        scaled_residual_maps, measurement_stencil, observed_partition, active_probe_total
-    )
+    sensors = (scaled_residual_maps, measurement_stencil, observed_partition, active_probe_total)
+    mine, other = sensor_info((), *sensors)
 
     def compose(after, *senders):
-        return call(functools.partial(compose_kernel, senders), "compose", (square,), after, gain, cost=0.5)[0]
+        return call(functools.partial(compose_kernel, senders), "compose", (square,), after, gain, cost=0.01)[0]
 
     near_senders = range(3, last - 3, 2)
+    inputs, means, send = call(
+        start_kernel, "start", (many, many, (8, size)), mine, other, covariance, operator, initial_mean, cost=0.5
+    )
     first = lax.ppermute(
-        compose(mine, last - 1, *near_senders), "tm", [(place, place - 1) for place in (*near_senders, last - 1)]
-    )
-    inputs, means, send = call(
-        inputs_kernel, "inputs", (many, many, one), mine, other, covariance, operator, initial_mean,
-        cost=COSTS[0],
+        compose(send, last - 1, *near_senders), "tm", [(place, place - 1) for place in (*near_senders, last - 1)]
     )
     skip = lax.ppermute(compose(send, last - 3), "tm", [(last - 3, last - 5)])
     for place in range(1, places):
         came = pass_row(send, [ring_up(place - 1, places)], places)
+        if place == 1:
+            mine, other = sensor_info((send,), *sensors)
+            inputs, means, send = call(
+                first_hop_kernel, "forward", (many, many, one),
+                came, mine, other, covariance, operator, inputs, means, cost=COSTS[1],
+            )
+            continue
         if place == 2:
             late = call(
                 functools.partial(late_kernel, (1,)), "late", ((size + 8, size),), means, gain, matrix,
@@ -584,12 +638,12 @@
         if place < last:
             means, send = call(
                 functools.partial(hop_kernel, place), "forward", (many, one), came, operator, inputs, means,
-                cost={1: COSTS[1], 2: COSTS[2]}.get(place, 0.5),
+                cost=COSTS[2] if place == 2 else 0.5,
             )
     offset_rows, left, own_parts = call(
         functools.partial(offsets_kernel, last), "offsets", (many, one, parts), means, gain, matrix
     )
-    other_offset = pass_row(left, [(last - 1, last - 2), (last - 3, last - 5)], places)
+    first_offset = pass_row(left, [(place - 1, place) for place in (*near_senders, last - 1)], places)
     means, states, send = call(
         functools.partial(last_kernel, last),
         "last",
@@ -607,10 +661,10 @@
     far_parts, again = call(
         functools.partial(split_kernel, last - 2), "split", (parts, one), first, left, cost=0.05
     )
-    near_offset = pass_row(again, [(place - 1, place) for place in near_senders], places)
+    skip_offset = pass_row(again, [(last - 3, last - 5)], places)
     entry, send = call(
         functools.partial(first_back_kernel, last - 2), "first_back", (one, one),
-        came, other_offset, far_parts, own_parts, left, send,
+        came, first_offset, far_parts, own_parts, left, send,
         cost=COSTS[3],
     )
     one_up = pass_row(send, [(last - 2, last - 3)], places)
@@ -623,7 +677,7 @@
         skip,
         gain,
         left,
-        near_offset,
+        first_offset,
         cost=0.05,
     )
     states, entry, send = call(
@@ -633,7 +687,7 @@
         three,
         one_up,
         entry,
-        other_offset,
+        skip_offset,
         skip_parts,
         pair_parts,
         pair_offset,
@@ -651,7 +705,7 @@
         if target:
             states, entry, send = call(
                 functools.partial(back_kernel, target, stray), "back", (many, one, one),
-                two, one_up, entry, near_offset, near_parts, pair_parts, pair_offset, gain, offset_rows, states,
+                two, one_up, entry, first_offset, near_parts, pair_parts, pair_offset, gain, offset_rows, states,
                 send,
             )
         else:
@@ -660,7 +714,7 @@
             )
             means, states = call(
                 functools.partial(final_kernel, stray), "final", (result, result),
-                two, one_up, entry, near_offset, near_parts, late_offset, late_parts, gain, offset_rows, states, means,
+                two, one_up, entry, first_offset, near_parts, late_offset, late_parts, gain, offset_rows, states, means,
             )
         stray = -1
     return means, states

time: 44.9 us -> 47.2 us (1.051)
  the two profiles are of different devices: /device:TPU:0 before, /device:TPU:10 now
where the time goes in v7:
time: 47.2 us; the launch traced here: 47 us
  waiting for transfers between devices  20.8 us (44%)
  starting transfers between devices  16.8 us (36%)
  Pallas kernels  8.14 us (17%)
  between operations  0.86 us (2%)
    ppermute x14, waiting for transfers between devices, pass_row(): return lax.ppermute(row, ('tm', 'block'), sorted(route.items()))  13.6 us
    ppermute x14, starting transfers between devices, pass_row(): return lax.ppermute(row, ('tm', 'block'), sorted(route.items()))  13.2 us
    ppermute x1, waiting for transfers between devices, local(): lax.ppermute(compose(send, last - 1, *near_senders), 'tm', [(place, place...  6 us
    pallas_call x18, Pallas kernels, call(): pl.pallas_call(kernel, out_shape=[jax.ShapeDtypeStruct(shape, jnp.bfloat1...  5.43 us
    pallas_call x2, Pallas kernels, sensor_info(): pl.pallas_call(functools.partial(info_kernel, zero), out_shape=[jax.Shape...  2.71 us
    ppermute x1, starting transfers between devices, local(): lax.ppermute(compose(send, last - 1, *near_senders), 'tm', [(place, place...  1.28 us
    ppermute x1, starting transfers between devices, local(): skip = lax.ppermute(compose(send, last - 3), 'tm', [(last - 3, last - 5)])  1.28 us
    ppermute x2, waiting for transfers between devices, sensor_info(): return (mine, lax.ppermute(theirs, 'block', [(0, 1), (1, 0)]))  1.16 us
  transfers between devices with their start and end apart: 19, of which 10 were waited for; matrix products, arithmetic and copies ran while one was open for 0% of the time, Pallas kernels for 14%

profile of v7, /device:TPU:10, one launch (start us, length us, event | category | flops | bytes accessed | tf_op | source)
XLA Modules:
  0.0 47.0 jit_solution(15495906364747025227)
XLA Ops:
  0.7 0.1 sensor_info.2
  0.9 1.2 %collective-permute-done.other_ref = f32[2,512]{1,0:T(2,128)S(1)} collective-permute-done((f32[2,512]{1,0:T(2,128)S(1)}, f32[2,512]{1,0:T(2,128)S(1)}, u32[]{:S(2)}, u32[]{:S(2)}) %collective-permute-start) | collective-permute-done | bytes 4128 | tf_op jit(solution)/shard_map/ppermute | solution.py:169
  2.0 0.2 copy-done.1
  2.2 0.1 collective-permute-start.1
  2.3 0.2 copy-done
  2.5 1.3 %collective-permute-start.11 = (f32[512,512]{1,0:T(8,128)S(1)}, f32[512,512]{1,0:T(8,128)S(1)}, u32[]{:S(2)}, u32[]{:S(2)}) collective-permute-start(f32[512,512]{1,0:T(8,128)S(1)} %compose.2), channel_id=1, source_target_pairs={{6,4},{12,10},{7,5},{13,11},{22,20},{28,26},{23,21},{29,27}} | collective-permute-start | bytes 3145736 | tf_op jit(solution)/shard_map/ppermute | solution.py:619
  3.8 2.6 %sensor_info.3 = (f32[2,512]{1,0:T(2,128)S(1)}, f32[2,512]{1,0:T(2,128)S(1)}) custom-call(f32[8,512]{1,0:T(8,128)S(1)} %get-tuple-element.43.refs_0_.after_ref, bf16[2,1024,512]{2,1,0:T(8,128)(2,1)} %bitcast.29, bf16[7,7,16]{2,1,0:T(8,128)(2,1)} %bitcast.31, s32[2,64]{1,0:T(2,128)} %refs_3_.1, s32[1,2]{1,0:T(1,128)} %bitcast.33), custom_call_target="tpu_custom_call" | custom-call | flops 60000002048 | bytes 4096 | tf_op jit(solution)/shard_map/sensor_info/pallas_call | solution.py:140
  6.4 0.2 collective-permute-start.2
  6.7 1.3 %collective-permute-start.15 = (f32[512,512]{1,0:T(8,128)S(1)}, f32[512,512]{1,0:T(8,128)S(1)}, u32[]{:S(2)}, u32[]{:S(2)}) collective-permute-start(f32[512,512]{1,0:T(8,128)S(1)} %compose.3), channel_id=1, source_target_pairs={{8,4},{9,5},{24,20},{25,21}} | collective-permute-start | bytes 3145736 | tf_op jit(solution)/shard_map/ppermute | solution.py:622
  8.0 0.4 forward.6
  8.4 2.3 %collective-permute-start.3 = (f32[1,512]{1,0:T(1,128)S(1)}, f32[1,512]{1,0:T(1,128)S(1)}, u32[]{:S(2)}, u32[]{:S(2)}) collective-permute-start(f32[1,512]{1,0:T(1,128)S(1)} %get-tuple-element.48), channel_id=1, source_target_pairs={{0,1},{1,0},{2,4},{3,5},{4,2},{5,3},{6,7},{7,6},{8,9},{9,8},{10,11... | collective-permute-start | bytes 6152 | tf_op jit(solution)/shard_map/ppermute | solution.py:576
  10.7 0.7 %collective-permute-start.18 = (f32[520,512]{1,0:T(8,128)S(1)}, f32[520,512]{1,0:T(8,128)S(1)}, u32[]{:S(2)}, u32[]{:S(2)}) collective-permute-start(f32[520,512]{1,0:T(8,128)S(1)} %late.1), channel_id=1, source_target_pairs={{2,0},{3,1},{18,16},{19,17}} | collective-permute-start | bytes 3194888 | tf_op jit(solution)/shard_map/ppermute | solution.py:637
  11.4 1.7 %collective-permute-done.3.came_ref = f32[1,512]{1,0:T(1,128)S(1)} collective-permute-done((f32[1,512]{1,0:T(1,128)S(1)}, f32[1,512]{1,0:T(1,128)S(1)}, u32[]{:S(2)}, u32[]{:S(2)}) %collective-permute-start.3) | collective-permute-done | bytes 2080 | tf_op jit(solution)/shard_map/ppermute | solution.py:576
  13.1 0.5 forward.7
  13.5 1.3 %collective-permute-start.4 = (f32[1,512]{1,0:T(1,128)S(1)}, f32[1,512]{1,0:T(1,128)S(1)}, u32[]{:S(2)}, u32[]{:S(2)}) collective-permute-start(f32[1,512]{1,0:T(1,128)S(1)} %get-tuple-element.51), channel_id=1, source_target_pairs={{0,4},{1,5},{2,3},{3,2},{4,6},{5,7},{6,0},{7,1},{8,9},{9,8},{10,11... | collective-permute-start | bytes 6152 | tf_op jit(solution)/shard_map/ppermute | solution.py:576
  14.9 2.3 %collective-permute-done.4.came_ref = f32[1,512]{1,0:T(1,128)S(1)} collective-permute-done((f32[1,512]{1,0:T(1,128)S(1)}, f32[1,512]{1,0:T(1,128)S(1)}, u32[]{:S(2)}, u32[]{:S(2)}) %collective-permute-start.4) | collective-permute-done | bytes 2080 | tf_op jit(solution)/shard_map/ppermute | solution.py:576
  17.2 1.2 %collective-permute-done.5.came_ref = f32[1,512]{1,0:T(1,128)S(1)} collective-permute-done((f32[1,512]{1,0:T(1,128)S(1)}, f32[1,512]{1,0:T(1,128)S(1)}, u32[]{:S(2)}, u32[]{:S(2)}) %collective-permute-start.5) | collective-permute-done | bytes 2080 | tf_op jit(solution)/shard_map/ppermute | solution.py:576
  18.4 4.1 %collective-permute-start.6 = (f32[1,512]{1,0:T(1,128)S(1)}, f32[1,512]{1,0:T(1,128)S(1)}, u32[]{:S(2)}, u32[]{:S(2)}) collective-permute-start(f32[1,512]{1,0:T(1,128)S(1)} %get-tuple-element.55), channel_id=1, source_target_pairs={{0,1},{1,0},{2,3},{3,2},{4,8},{5,9},{6,7},{7,6},{8,10},{9,11},{10,... | collective-permute-start | bytes 6152 | tf_op jit(solution)/shard_map/ppermute | solution.py:576
  22.5 1.3 %collective-permute-done.6.came_ref = f32[1,512]{1,0:T(1,128)S(1)} collective-permute-done((f32[1,512]{1,0:T(1,128)S(1)}, f32[1,512]{1,0:T(1,128)S(1)}, u32[]{:S(2)}, u32[]{:S(2)}) %collective-permute-start.6) | collective-permute-done | bytes 2080 | tf_op jit(solution)/shard_map/ppermute | solution.py:576
  23.8 1.2 %collective-permute-done.7.came_ref = f32[1,512]{1,0:T(1,128)S(1)} collective-permute-done((f32[1,512]{1,0:T(1,128)S(1)}, f32[1,512]{1,0:T(1,128)S(1)}, u32[]{:S(2)}, u32[]{:S(2)}) %collective-permute-start.7) | collective-permute-done | bytes 2080 | tf_op jit(solution)/shard_map/ppermute | solution.py:576
  25.0 0.2 collective-permute-start.8
  25.1 0.7 %offsets.1 = (f32[2,512]{1,0:T(2,128)S(1)}, f32[1,512]{1,0:T(1,128)S(1)}, bf16[2,512,512]{2,1,0:T(8,128)(2,1)S(1)}) custom-call(f32[2,512]{1,0:T(2,128)S(1)} %get-tuple-element.60.kept_ref.means_ref, bf16[2,512,512]{2,1,0:T(8,128)(2,1)S(1)} %bitcast.10, bf16[512,512]{1,0:T(8,128)(2,1)S(1)} %bitcast.24), custom_call_target="tpu_custom_call" | custom-call | flops 1000000000 | bytes 4096 | tf_op jit(solution)/shard_map/offsets/pallas_call | solution.py:553
  25.9 0.2 collective-permute-done.8.came_ref
  26.1 0.2 collective-permute-start.9
  26.3 6.0 %collective-permute-done.11.matrix_ref.near_ref = f32[512,512]{1,0:T(8,128)S(1)} collective-permute-done((f32[512,512]{1,0:T(8,128)S(1)}, f32[512,512]{1,0:T(8,128)S(1)}, u32[]{:S(2)}, u32[]{:S(2)}) %collective-permute-start.11) | collective-permute-done | bytes 1048608 | tf_op jit(solution)/shard_map/ppermute | solution.py:619
  32.5 4.2 %collective-permute-start.12 = (f32[1,512]{1,0:T(1,128)S(1)}, f32[1,512]{1,0:T(1,128)S(1)}, u32[]{:S(2)}, u32[]{:S(2)}) collective-permute-start(f32[1,512]{1,0:T(1,128)S(1)} %get-tuple-element.65.came_ref), channel_id=1, source_target_pairs={{0,1},{1,0},{2,3},{3,2},{4,10},{5,11},{6,7},{7,6},{8,9},{9,8},{10,... | collective-permute-start | bytes 6152 | tf_op jit(solution)/shard_map/ppermute | solution.py:576
  36.7 0.5 %collective-permute-start.14 = (f32[1,512]{1,0:T(1,128)S(1)}, f32[1,512]{1,0:T(1,128)S(1)}, u32[]{:S(2)}, u32[]{:S(2)}) collective-permute-start(f32[1,512]{1,0:T(1,128)S(1)} %get-tuple-element.67), channel_id=1, source_target_pairs={{0,1},{1,0},{2,3},{3,2},{4,8},{5,9},{6,7},{7,6},{8,4},{9,5},{10,11... | collective-permute-start | bytes 6152 | tf_op jit(solution)/shard_map/ppermute | solution.py:576
  37.2 1.7 %pair.1 = (bf16[2,512,512]{2,1,0:T(8,128)(2,1)S(1)}, bf16[2,512,512]{2,1,0:T(8,128)(2,1)S(1)}, f32[1,512]{1,0:T(1,128)S(1)}, bf16[2,512,512]{2,1,0:T(8,128)(2,1)S(1)}) custom-call(f32[512,512]{1,0:T(8,128)S(1)} %collective-permute-done.11.matrix_ref.near_ref, f32[512,512]{1,0:T(8,128)S(1)} %collective-permute-done.15.skip_ref, ...), custom_call_target="tpu_custom_call" | custom-call | flops 50000000 | bytes 4096 | tf_op jit(solution)/shard_map/pair/pallas_call | solution.py:553
  38.9 1.4 %collective-permute-done.14.skip_offset_ref = f32[1,512]{1,0:T(1,128)S(1)} collective-permute-done((f32[1,512]{1,0:T(1,128)S(1)}, f32[1,512]{1,0:T(1,128)S(1)}, u32[]{:S(2)}, u32[]{:S(2)}) %collective-permute-start.14) | collective-permute-done | bytes 2080 | tf_op jit(solution)/shard_map/ppermute | solution.py:576
  40.3 0.7 %second_back.1 = (f32[2,512]{1,0:T(2,128)S(1)}, f32[1,512]{1,0:T(1,128)S(1)}, f32[1,512]{1,0:T(1,128)S(1)}) custom-call(f32[1,512]{1,0:T(1,128)S(1)} %collective-permute-done.12.three_ref, f32[1,512]{1,0:T(1,128)S(1)} %collective-permute-done.13.one_ref, f32[1,512]{1,0:T(1,128)S(1)} %get-tuple-element.66.entry_ref, ...), custom_call_target="tpu_custom_call" | custom-call | flops 500000000 | bytes 4096 | tf_op jit(solution)/shard_map/second_back/pallas_call | solution.py:553
  41.2 4.4 %collective-permute-done.17.one_ref = f32[1,512]{1,0:T(1,128)S(1)} collective-permute-done((f32[1,512]{1,0:T(1,128)S(1)}, f32[1,512]{1,0:T(1,128)S(1)}, u32[]{:S(2)}, u32[]{:S(2)}) %collective-permute-start.17) | collective-permute-done | bytes 2080 | tf_op jit(solution)/shard_map/ppermute | solution.py:576
  45.6 1.4 %final.1 = (f32[2,1,512]{2,1,0:T(1,128)}, f32[2,1,512]{2,1,0:T(1,128)}) custom-call(f32[1,512]{1,0:T(1,128)S(1)} %collective-permute-done.16.two_ref, f32[1,512]{1,0:T(1,128)S(1)} %collective-permute-done.17.one_ref, f32[1,512]{1,0:T(1,128)S(1)} %get-tuple-element.74.entry_ref, f32[1,512]{1,0:T(1,128)S(1)} %collective-permute-done.10.far_offset_ref.near_offset_ref, ...), custom_call_target="tpu_custom_call" | custom-call | flops 1000000000 | bytes 4096 | tf_op jit(solution)/shard_map/final/pallas_call | solution.py:553
  (36 shorter events, 0.5 us)
Async XLA Ops:
  0.6 1.4 %copy-start.4 = (f32[1,512]{1,0:T(1,128)S(1)}, f32[1,512]{1,0:T(1,128)}, u32[]{:S(2)}) copy-start(f32[1,512]{1,0:T(1,128)} %start_ref.1) | copy-start | bytes 6148
  0.6 1.4 %copy-start.3 = (bf16[2,1,512,512]{3,2,1,0:T(8,128)(2,1)S(1)}, bf16[2,1,512,512]{3,2,1,0:T(8,128)(2,1)}, u32[]{:S(2)}) copy-start(bf16[2,1,512,512]{3,2,1,0:T(8,128)(2,1)} %param.14) | copy-start | bytes 3145732
  0.7 1.5 %copy-start.1 = (bf16[2,1,512,512]{3,2,1,0:T(8,128)(2,1)S(1)}, bf16[2,1,512,512]{3,2,1,0:T(8,128)(2,1)}, u32[]{:S(2)}) copy-start(bf16[2,1,512,512]{3,2,1,0:T(8,128)(2,1)} %param.13) | copy-start | bytes 3145732
  0.8 1.8 %copy-start = (bf16[2,1,512,512]{3,2,1,0:T(8,128)(2,1)S(1)}, bf16[2,1,512,512]{3,2,1,0:T(8,128)(2,1)}, u32[]{:S(2)}) copy-start(bf16[2,1,512,512]{3,2,1,0:T(8,128)(2,1)} %param.15) | copy-start | bytes 3145732
  0.8 1.2 %collective-permute-start = (f32[2,512]{1,0:T(2,128)S(1)}, f32[2,512]{1,0:T(2,128)S(1)}, u32[]{:S(2)}, u32[]{:S(2)}) collective-permute-start(f32[2,512]{1,0:T(2,128)S(1)} %get-tuple-element.42), channel_id=1, source_target_pairs={{0,1},{1,0},{2,3},{3,2},{4,5},{5,4},{6,7},{7,6},{8,9},{9,8},{10,11... | collective-permute-start | bytes 12296 | tf_op jit(solution)/shard_map/ppermute | solution.py:169
  2.2 5.8 %collective-permute-start.1 = (f32[8,512]{1,0:T(8,128)S(1)}, f32[8,512]{1,0:T(8,128)S(1)}, u32[]{:S(2)}, u32[]{:S(2)}) collective-permute-start(f32[8,512]{1,0:T(8,128)S(1)} %get-tuple-element.43.refs_0_.after_ref), channel_id=1, source_target_pairs={{0,2},{1,3},{2,6},{3,7},{4,5},{5,4},{6,0},{7,1},{8,9},{9,8},{10,11... | collective-permute-start | bytes 49160 | tf_op jit(solution)/shard_map/ppermute | solution.py:576
  2.5 29.8 %collective-permute-start.11 = (f32[512,512]{1,0:T(8,128)S(1)}, f32[512,512]{1,0:T(8,128)S(1)}, u32[]{:S(2)}, u32[]{:S(2)}) collective-permute-start(f32[512,512]{1,0:T(8,128)S(1)} %compose.2), channel_id=1, source_target_pairs={{6,4},{12,10},{7,5},{13,11},{22,20},{28,26},{23,21},{29,27}} | collective-permute-start | bytes 3145736 | tf_op jit(solution)/shard_map/ppermute | solution.py:619
  6.4 1.5 %collective-permute-start.2 = (f32[2,512]{1,0:T(2,128)S(1)}, f32[2,512]{1,0:T(2,128)S(1)}, u32[]{:S(2)}, u32[]{:S(2)}) collective-permute-start(f32[2,512]{1,0:T(2,128)S(1)} %get-tuple-element.45), channel_id=1, source_target_pairs={{0,1},{1,0},{2,3},{3,2},{4,5},{5,4},{6,7},{7,6},{8,9},{9,8},{10,11... | collective-permute-start | bytes 12296 | tf_op jit(solution)/shard_map/ppermute | solution.py:169
  6.7 30.5 %collective-permute-start.15 = (f32[512,512]{1,0:T(8,128)S(1)}, f32[512,512]{1,0:T(8,128)S(1)}, u32[]{:S(2)}, u32[]{:S(2)}) collective-permute-start(f32[512,512]{1,0:T(8,128)S(1)} %compose.3), channel_id=1, source_target_pairs={{8,4},{9,5},{24,20},{25,21}} | collective-permute-start | bytes 3145736 | tf_op jit(solution)/shard_map/ppermute | solution.py:622
  8.0 2.7 %copy-start.2 = (bf16[1,512,512]{2,1,0:T(8,128)(2,1)S(1)}, bf16[1,512,512]{2,1,0:T(8,128)(2,1)}, u32[]{:S(2)}) copy-start(bf16[1,512,512]{2,1,0:T(8,128)(2,1)} %param.16) | copy-start | bytes 1572868
  8.4 4.7 %collective-permute-start.3 = (f32[1,512]{1,0:T(1,128)S(1)}, f32[1,512]{1,0:T(1,128)S(1)}, u32[]{:S(2)}, u32[]{:S(2)}) collective-permute-start(f32[1,512]{1,0:T(1,128)S(1)} %get-tuple-element.48), channel_id=1, source_target_pairs={{0,1},{1,0},{2,4},{3,5},{4,2},{5,3},{6,7},{7,6},{8,9},{9,8},{10,11... | collective-permute-start | bytes 6152 | tf_op jit(solution)/shard_map/ppermute | solution.py:576
  10.7 30.5 %collective-permute-start.18 = (f32[520,512]{1,0:T(8,128)S(1)}, f32[520,512]{1,0:T(8,128)S(1)}, u32[]{:S(2)}, u32[]{:S(2)}) collective-permute-start(f32[520,512]{1,0:T(8,128)S(1)} %late.1), channel_id=1, source_target_pairs={{2,0},{3,1},{18,16},{19,17}} | collective-permute-start | bytes 3194888 | tf_op jit(solution)/shard_map/ppermute | solution.py:637
  13.5 3.7 %collective-permute-start.4 = (f32[1,512]{1,0:T(1,128)S(1)}, f32[1,512]{1,0:T(1,128)S(1)}, u32[]{:S(2)}, u32[]{:S(2)}) collective-permute-start(f32[1,512]{1,0:T(1,128)S(1)} %get-tuple-element.51), channel_id=1, source_target_pairs={{0,4},{1,5},{2,3},{3,2},{4,6},{5,7},{6,0},{7,1},{8,9},{9,8},{10,11... | collective-permute-start | bytes 6152 | tf_op jit(solution)/shard_map/ppermute | solution.py:576
  17.2 1.2 %collective-permute-start.5 = (f32[1,512]{1,0:T(1,128)S(1)}, f32[1,512]{1,0:T(1,128)S(1)}, u32[]{:S(2)}, u32[]{:S(2)}) collective-permute-start(f32[1,512]{1,0:T(1,128)S(1)} %get-tuple-element.53), channel_id=1, source_target_pairs={{0,1},{1,0},{2,3},{3,2},{4,5},{5,4},{6,8},{7,9},{8,10},{9,11},{10,... | collective-permute-start | bytes 6152 | tf_op jit(solution)/shard_map/ppermute | solution.py:576
  18.4 5.5 %collective-permute-start.6 = (f32[1,512]{1,0:T(1,128)S(1)}, f32[1,512]{1,0:T(1,128)S(1)}, u32[]{:S(2)}, u32[]{:S(2)}) collective-permute-start(f32[1,512]{1,0:T(1,128)S(1)} %get-tuple-element.55), channel_id=1, source_target_pairs={{0,1},{1,0},{2,3},{3,2},{4,8},{5,9},{6,7},{7,6},{8,10},{9,11},{10,... | collective-permute-start | bytes 6152 | tf_op jit(solution)/shard_map/ppermute | solution.py:576
  23.8 1.2 %collective-permute-start.7 = (f32[1,512]{1,0:T(1,128)S(1)}, f32[1,512]{1,0:T(1,128)S(1)}, u32[]{:S(2)}, u32[]{:S(2)}) collective-permute-start(f32[1,512]{1,0:T(1,128)S(1)} %get-tuple-element.57), channel_id=1, source_target_pairs={{0,1},{1,0},{2,3},{3,2},{4,5},{5,4},{6,7},{7,6},{8,9},{9,8},{10,12... | collective-permute-start | bytes 6152 | tf_op jit(solution)/shard_map/ppermute | solution.py:576
  25.0 1.2 %collective-permute-start.8 = (f32[1,512]{1,0:T(1,128)S(1)}, f32[1,512]{1,0:T(1,128)S(1)}, u32[]{:S(2)}, u32[]{:S(2)}) collective-permute-start(f32[1,512]{1,0:T(1,128)S(1)} %get-tuple-element.59), channel_id=1, source_target_pairs={{0,1},{1,0},{2,3},{3,2},{4,5},{5,4},{6,7},{7,6},{8,9},{9,8},{10,11... | collective-permute-start | bytes 6152 | tf_op jit(solution)/shard_map/ppermute | solution.py:576
  25.8 6.5 %collective-permute-start.10 = (f32[1,512]{1,0:T(1,128)S(1)}, f32[1,512]{1,0:T(1,128)S(1)}, u32[]{:S(2)}, u32[]{:S(2)}) collective-permute-start(f32[1,512]{1,0:T(1,128)S(1)} %get-tuple-element.62.left_ref), channel_id=1, source_target_pairs={{0,1},{1,0},{2,3},{3,2},{4,6},{5,7},{6,4},{7,5},{8,9},{9,8},{10,12... | collective-permute-start | bytes 6152 | tf_op jit(solution)/shard_map/ppermute | solution.py:576
  26.1 6.2 %collective-permute-start.9 = (f32[1,512]{1,0:T(1,128)S(1)}, f32[1,512]{1,0:T(1,128)S(1)}, u32[]{:S(2)}, u32[]{:S(2)}) collective-permute-start(f32[1,512]{1,0:T(1,128)S(1)} %get-tuple-element.61.came_ref), channel_id=1, source_target_pairs={{0,1},{1,0},{2,3},{3,2},{4,5},{5,4},{6,7},{7,6},{8,9},{9,8},{10,14... | collective-permute-start | bytes 6152 | tf_op jit(solution)/shard_map/ppermute | solution.py:576
  32.4 6.5 %collective-permute-start.13 = (f32[1,512]{1,0:T(1,128)S(1)}, f32[1,512]{1,0:T(1,128)S(1)}, u32[]{:S(2)}, u32[]{:S(2)}) collective-permute-start(f32[1,512]{1,0:T(1,128)S(1)} %get-tuple-element.65.came_ref), channel_id=1, source_target_pairs={{0,1},{1,0},{2,3},{3,2},{4,5},{5,4},{6,7},{7,6},{8,10},{9,11},{10,... | collective-permute-start | bytes 6152 | tf_op jit(solution)/shard_map/ppermute | solution.py:576
  32.5 6.4 %collective-permute-start.12 = (f32[1,512]{1,0:T(1,128)S(1)}, f32[1,512]{1,0:T(1,128)S(1)}, u32[]{:S(2)}, u32[]{:S(2)}) collective-permute-start(f32[1,512]{1,0:T(1,128)S(1)} %get-tuple-element.65.came_ref), channel_id=1, source_target_pairs={{0,1},{1,0},{2,3},{3,2},{4,10},{5,11},{6,7},{7,6},{8,9},{9,8},{10,... | collective-permute-start | bytes 6152 | tf_op jit(solution)/shard_map/ppermute | solution.py:576
  36.7 3.6 %collective-permute-start.14 = (f32[1,512]{1,0:T(1,128)S(1)}, f32[1,512]{1,0:T(1,128)S(1)}, u32[]{:S(2)}, u32[]{:S(2)}) collective-permute-start(f32[1,512]{1,0:T(1,128)S(1)} %get-tuple-element.67), channel_id=1, source_target_pairs={{0,1},{1,0},{2,3},{3,2},{4,8},{5,9},{6,7},{7,6},{8,4},{9,5},{10,11... | collective-permute-start | bytes 6152 | tf_op jit(solution)/shard_map/ppermute | solution.py:576
  41.1 4.5 %collective-permute-start.17 = (f32[1,512]{1,0:T(1,128)S(1)}, f32[1,512]{1,0:T(1,128)S(1)}, u32[]{:S(2)}, u32[]{:S(2)}) collective-permute-start(f32[1,512]{1,0:T(1,128)S(1)} %get-tuple-element.73.after_ref), channel_id=1, source_target_pairs={{0,1},{1,0},{2,4},{3,5},{4,2},{5,3},{6,7},{7,6},{8,9},{9,8},{10,11... | collective-permute-start | bytes 6152 | tf_op jit(solution)/shard_map/ppermute | solution.py:576
  41.1 4.5 %collective-permute-start.16 = (f32[1,512]{1,0:T(1,128)S(1)}, f32[1,512]{1,0:T(1,128)S(1)}, u32[]{:S(2)}, u32[]{:S(2)}) collective-permute-start(f32[1,512]{1,0:T(1,128)S(1)} %get-tuple-element.73.after_ref), channel_id=1, source_target_pairs={{0,4},{1,5},{2,3},{3,2},{4,0},{5,1},{6,8},{7,9},{8,6},{9,7},{10,11... | collective-permute-start | bytes 6152 | tf_op jit(solution)/shard_map/ppermute | solution.py:576

commit v8 on v7

--- a/solution.py
+++ b/solution.py
@@ -328,9 +328,7 @@
         offset_ref[...] = late_ref[size : size + 1, :]
 
 
-def split_kernel(place, matrix_ref, left_ref, parts_ref, again_ref):
-    again_ref[...] = left_ref[...]
-
+def split_kernel(place, matrix_ref, parts_ref):
     @pl.when(lax.axis_index("tm") == place)
     def _():
         parts_ref[0], parts_ref[1] = halves(matrix_ref[...])
@@ -397,17 +395,17 @@
 def first_back_kernel(
     place, last_ref, far_offset_ref, far_parts_ref, own_parts_ref, left_ref, came_ref, entry_ref, send_ref
 ):
-    here = lax.axis_index("tm") == place
-
-    @pl.when(here)
+    here = lax.axis_index("tm")
+
+    @pl.when(here == place)
     def _():
         entry_ref[...] = parts_times(far_parts_ref, last_ref) + far_offset_ref[...]
         send_ref[...] = parts_times(own_parts_ref, entry_ref) + left_ref[...]
 
-    @pl.when(jnp.logical_not(here))
+    @pl.when(here != place)
     def _():
         entry_ref[...] = last_ref[...]
-        send_ref[...] = came_ref[...]
+        send_ref[...] = jnp.where(here == place - 1, left_ref[...], came_ref[...])
 
 
 def second_back_kernel(
@@ -415,7 +413,6 @@
     three_ref,
     one_ref,
     entry_ref,
-    skip_offset_ref,
     skip_parts_ref,
     pair_parts_ref,
     pair_offset_ref,
@@ -434,7 +431,7 @@
 
     @pl.when(here == last - 5)
     def _():
-        state = parts_times(skip_parts_ref, three_ref) + skip_offset_ref[...]
+        state = parts_times(skip_parts_ref, three_ref) + one_ref[...]
         next_ref[...] = state
         send_ref[...] = times([pair_parts_ref[0], pair_parts_ref[1]], state) + pair_offset_ref[...]
         states_ref[...] = kept_ref[...]
@@ -577,8 +574,6 @@
 
 
 def ring_up(place, places):
-    if place == 0:
-        return (0, 1, 3)
     if place % 2 and place >= places - 5 and place < places - 1:
         return (place, place + 1, place + 2)
     if place % 2 or place == places - 2:
@@ -621,14 +616,15 @@
     )
     skip = lax.ppermute(compose(send, last - 3), "tm", [(last - 3, last - 5)])
     for place in range(1, places):
-        came = pass_row(send, [ring_up(place - 1, places)], places)
         if place == 1:
+            came = lax.ppermute(send, "tm", [(0, 1)])
             mine, other = sensor_info((send,), *sensors)
             inputs, means, send = call(
                 first_hop_kernel, "forward", (many, many, one),
                 came, mine, other, covariance, operator, inputs, means, cost=COSTS[1],
             )
             continue
+        came = pass_row(send, [ring_up(place - 1, places)], places)
         if place == 2:
             late = call(
                 functools.partial(late_kernel, (1,)), "late", ((size + 8, size),), means, gain, matrix,
@@ -658,16 +654,13 @@
     )
     came = pass_row(send, [(last, last - 2)], places)
 
-    far_parts, again = call(
-        functools.partial(split_kernel, last - 2), "split", (parts, one), first, left, cost=0.05
-    )
-    skip_offset = pass_row(again, [(last - 3, last - 5)], places)
+    (far_parts,) = call(functools.partial(split_kernel, last - 2), "split", (parts,), first, cost=0.05)
     entry, send = call(
         functools.partial(first_back_kernel, last - 2), "first_back", (one, one),
         came, first_offset, far_parts, own_parts, left, send,
         cost=COSTS[3],
     )
-    one_up = pass_row(send, [(last - 2, last - 3)], places)
+    one_up = pass_row(send, [(last - 2, last - 3, last - 5, last - 4)], places)
     three = pass_row(send, [(last - 2, last - 5), (last, last - 1)], places)
     near_parts, pair_parts, pair_offset, skip_parts = call(
         functools.partial(pair_kernel, tuple(place - 1 for place in near_senders), last - 5),
@@ -687,7 +680,6 @@
         three,
         one_up,
         entry,
-        skip_offset,
         skip_parts,
         pair_parts,
         pair_offset,

time: 47.2 us -> 44.4 us (0.941)
  the two profiles are of different devices: /device:TPU:10 before, /device:TPU:0 now
where the time goes in v8:
time: 44.4 us; the launch traced here: 44.2 us
  starting transfers between devices  27.9 us (63%)
  waiting for transfers between devices  8.85 us (20%)
  Pallas kernels  5.81 us (13%)
  local copies, waits for them, and re-layouts  0.82 us (2%)
  between operations  0.81 us (2%)
    ppermute x12, starting transfers between devices, pass_row(): return lax.ppermute(row, ('tm', 'block'), sorted(route.items()))  23 us
    ppermute x12, waiting for transfers between devices, pass_row(): return lax.ppermute(row, ('tm', 'block'), sorted(route.items()))  7.62 us
    pallas_call x18, Pallas kernels, call(): pl.pallas_call(kernel, out_shape=[jax.ShapeDtypeStruct(shape, jnp.bfloat1...  2.97 us
    pallas_call x2, Pallas kernels, sensor_info(): pl.pallas_call(functools.partial(info_kernel, zero), out_shape=[jax.Shape...  2.84 us
    ppermute x1, starting transfers between devices, local(): came = lax.ppermute(send, 'tm', [(0, 1)])  1.62 us
    ppermute x1, starting transfers between devices, local(): late = lax.ppermute(late, 'tm', [(1, 0)])  1.28 us
    ppermute x2, waiting for transfers between devices, sensor_info(): return (mine, lax.ppermute(theirs, 'block', [(0, 1), (1, 0)]))  1.22 us
  transfers between devices with their start and end apart: 18, of which 11 were waited for; matrix products, arithmetic and copies ran while one was open for 0% of the time, Pallas kernels for 2%

profile of v8, /device:TPU:0, one launch (start us, length us, event | category | flops | bytes accessed | tf_op | source)
XLA Modules:
  0.0 44.2 jit_solution(7889417323217490166)
XLA Ops:
  0.7 2.7 %sensor_info.2 = (f32[2,512]{1,0:T(2,128)S(1)}, f32[2,512]{1,0:T(2,128)S(1)}) custom-call(bf16[2,1024,512]{2,1,0:T(8,128)(2,1)} %bitcast.28, bf16[7,7,16]{2,1,0:T(8,128)(2,1)} %bitcast.30, s32[2,64]{1,0:T(2,128)} %refs_3_.1, s32[1,2]{1,0:T(1,128)} %bitcast.32), custom_call_target="tpu_custom_call" | custom-call | flops 1000000 | bytes 4096 | tf_op jit(solution)/shard_map/sensor_info/pallas_call | solution.py:140
  3.4 0.5 %collective-permute-start = (f32[2,512]{1,0:T(2,128)S(1)}, f32[2,512]{1,0:T(2,128)S(1)}, u32[]{:S(2)}, u32[]{:S(2)}) collective-permute-start(f32[2,512]{1,0:T(2,128)S(1)} %get-tuple-element.40), channel_id=1, source_target_pairs={{0,1},{1,0},{2,3},{3,2},{4,5},{5,4},{6,7},{7,6},{8,9},{9,8},{10,11... | collective-permute-start | bytes 12296 | tf_op jit(solution)/shard_map/ppermute | solution.py:169
  3.9 0.8 %collective-permute-done.other_ref = f32[2,512]{1,0:T(2,128)S(1)} collective-permute-done((f32[2,512]{1,0:T(2,128)S(1)}, f32[2,512]{1,0:T(2,128)S(1)}, u32[]{:S(2)}, u32[]{:S(2)}) %collective-permute-start) | collective-permute-done | bytes 4128 | tf_op jit(solution)/shard_map/ppermute | solution.py:169
  4.8 0.7 %start.1 = (f32[2,512]{1,0:T(2,128)S(1)}, f32[2,512]{1,0:T(2,128)S(1)}, f32[8,512]{1,0:T(8,128)S(1)}) custom-call(f32[2,512]{1,0:T(2,128)S(1)} %get-tuple-element.39.mine_ref, f32[2,512]{1,0:T(2,128)S(1)} %collective-permute-done.other_ref, bf16[2,512,512]{2,1,0:T(8,128)(2,1)S(1)} %bitcast.26, bf16[2,512,512]{2,1,0:T(8,128)(2,1)S(1)} %bitcast.15, ...), custom_call_target="tpu_custom_call" | custom-call | flops 500000000 | bytes 4096 | tf_op jit(solution)/shard_map/start/pallas_call | solution.py:550
  5.4 1.6 %collective-permute-start.1 = (f32[8,512]{1,0:T(8,128)S(1)}, f32[8,512]{1,0:T(8,128)S(1)}, u32[]{:S(2)}, u32[]{:S(2)}) collective-permute-start(f32[8,512]{1,0:T(8,128)S(1)} %get-tuple-element.41.refs_0_.after_ref), channel_id=1, source_target_pairs={{0,2},{1,3},{16,18},{17,19}} | collective-permute-start | bytes 49160 | tf_op jit(solution)/shard_map/ppermute | solution.py:620
  7.1 0.7 %collective-permute-start.11 = (f32[512,512]{1,0:T(8,128)S(1)}, f32[512,512]{1,0:T(8,128)S(1)}, u32[]{:S(2)}, u32[]{:S(2)}) collective-permute-start(f32[512,512]{1,0:T(8,128)S(1)} %compose.2), channel_id=1, source_target_pairs={{6,4},{12,10},{7,5},{13,11},{22,20},{28,26},{23,21},{29,27}} | collective-permute-start | bytes 3145736 | tf_op jit(solution)/shard_map/ppermute | solution.py:614
  8.1 0.7 %collective-permute-start.14 = (f32[512,512]{1,0:T(8,128)S(1)}, f32[512,512]{1,0:T(8,128)S(1)}, u32[]{:S(2)}, u32[]{:S(2)}) collective-permute-start(f32[512,512]{1,0:T(8,128)S(1)} %compose.3), channel_id=1, source_target_pairs={{8,4},{9,5},{24,20},{25,21}} | collective-permute-start | bytes 3145736 | tf_op jit(solution)/shard_map/ppermute | solution.py:617
  8.8 0.4 collective-permute-done.2.other_ref
  9.2 0.2 collective-permute-start.3
  9.4 0.8 %copy-done.2 = bf16[1,512,512]{2,1,0:T(8,128)(2,1)S(1)} copy-done((bf16[1,512,512]{2,1,0:T(8,128)(2,1)S(1)}, bf16[1,512,512]{2,1,0:T(8,128)(2,1)}, u32[]{:S(2)}) %copy-start.2) | copy-done | bytes 524312
  10.2 1.3 %collective-permute-start.17 = (f32[520,512]{1,0:T(8,128)S(1)}, f32[520,512]{1,0:T(8,128)S(1)}, u32[]{:S(2)}, u32[]{:S(2)}) collective-permute-start(f32[520,512]{1,0:T(8,128)S(1)} %late.1), channel_id=1, source_target_pairs={{2,0},{3,1},{18,16},{19,17}} | collective-permute-start | bytes 3194888 | tf_op jit(solution)/shard_map/ppermute | solution.py:633
  11.6 5.2 %collective-permute-start.4 = (f32[1,512]{1,0:T(1,128)S(1)}, f32[1,512]{1,0:T(1,128)S(1)}, u32[]{:S(2)}, u32[]{:S(2)}) collective-permute-start(f32[1,512]{1,0:T(1,128)S(1)} %get-tuple-element.49), channel_id=1, source_target_pairs={{0,4},{1,5},{2,3},{3,2},{4,6},{5,7},{6,0},{7,1},{8,9},{9,8},{10,11... | collective-permute-start | bytes 6152 | tf_op jit(solution)/shard_map/ppermute | solution.py:573
  16.8 1.3 %collective-permute-done.4.came_ref = f32[1,512]{1,0:T(1,128)S(1)} collective-permute-done((f32[1,512]{1,0:T(1,128)S(1)}, f32[1,512]{1,0:T(1,128)S(1)}, u32[]{:S(2)}, u32[]{:S(2)}) %collective-permute-start.4) | collective-permute-done | bytes 2080 | tf_op jit(solution)/shard_map/ppermute | solution.py:573
  18.1 1.2 %collective-permute-done.5.came_ref = f32[1,512]{1,0:T(1,128)S(1)} collective-permute-done((f32[1,512]{1,0:T(1,128)S(1)}, f32[1,512]{1,0:T(1,128)S(1)}, u32[]{:S(2)}, u32[]{:S(2)}) %collective-permute-start.5) | collective-permute-done | bytes 2080 | tf_op jit(solution)/shard_map/ppermute | solution.py:573
  19.2 0.2 collective-permute-start.6
  19.4 1.0 %collective-permute-done.6.came_ref = f32[1,512]{1,0:T(1,128)S(1)} collective-permute-done((f32[1,512]{1,0:T(1,128)S(1)}, f32[1,512]{1,0:T(1,128)S(1)}, u32[]{:S(2)}, u32[]{:S(2)}) %collective-permute-start.6) | collective-permute-done | bytes 2080 | tf_op jit(solution)/shard_map/ppermute | solution.py:573
  20.4 0.2 collective-permute-start.7
  20.6 1.0 %collective-permute-done.7.came_ref = f32[1,512]{1,0:T(1,128)S(1)} collective-permute-done((f32[1,512]{1,0:T(1,128)S(1)}, f32[1,512]{1,0:T(1,128)S(1)}, u32[]{:S(2)}, u32[]{:S(2)}) %collective-permute-start.7) | collective-permute-done | bytes 2080 | tf_op jit(solution)/shard_map/ppermute | solution.py:573
  21.6 0.2 collective-permute-start.8
  21.7 0.7 %offsets.1 = (f32[2,512]{1,0:T(2,128)S(1)}, f32[1,512]{1,0:T(1,128)S(1)}, bf16[2,512,512]{2,1,0:T(8,128)(2,1)S(1)}) custom-call(f32[2,512]{1,0:T(2,128)S(1)} %get-tuple-element.58.kept_ref.means_ref, bf16[2,512,512]{2,1,0:T(8,128)(2,1)S(1)} %bitcast.10, bf16[512,512]{1,0:T(8,128)(2,1)S(1)} %bitcast.24), custom_call_target="tpu_custom_call" | custom-call | flops 1000000000 | bytes 4096 | tf_op jit(solution)/shard_map/offsets/pallas_call | solution.py:550
  22.4 0.4 collective-permute-start.10
  22.8 0.2 collective-permute-start.9
  23.0 0.6 %collective-permute-done.10.far_offset_ref.near_offset_ref = f32[1,512]{1,0:T(1,128)S(1)} collective-permute-done((f32[1,512]{1,0:T(1,128)S(1)}, f32[1,512]{1,0:T(1,128)S(1)}, u32[]{:S(2)}, u32[]{:S(2)}) %collective-permute-start.10) | collective-permute-done | bytes 2080 | tf_op jit(solution)/shard_map/ppermute | solution.py:573
  23.6 0.3 collective-permute-done.9.last_ref
  24.0 0.2 collective-permute-start.13
  24.2 0.3 collective-permute-start.12
  24.5 0.6 %collective-permute-done.13.one_ref = f32[1,512]{1,0:T(1,128)S(1)} collective-permute-done((f32[1,512]{1,0:T(1,128)S(1)}, f32[1,512]{1,0:T(1,128)S(1)}, u32[]{:S(2)}, u32[]{:S(2)}) %collective-permute-start.13) | collective-permute-done | bytes 2080 | tf_op jit(solution)/shard_map/ppermute | solution.py:573
  25.1 0.2 collective-permute-done.12.three_ref
  25.3 0.3 collective-permute-start.16
  25.7 15.6 %collective-permute-start.15 = (f32[1,512]{1,0:T(1,128)S(1)}, f32[1,512]{1,0:T(1,128)S(1)}, u32[]{:S(2)}, u32[]{:S(2)}) collective-permute-start(f32[1,512]{1,0:T(1,128)S(1)} %get-tuple-element.69.after_ref), channel_id=1, source_target_pairs={{0,4},{1,5},{2,3},{3,2},{4,0},{5,1},{6,8},{7,9},{8,6},{9,7},{10,11... | collective-permute-start | bytes 6152 | tf_op jit(solution)/shard_map/ppermute | solution.py:573
  41.4 1.4 %collective-permute-done.15.two_ref = f32[1,512]{1,0:T(1,128)S(1)} collective-permute-done((f32[1,512]{1,0:T(1,128)S(1)}, f32[1,512]{1,0:T(1,128)S(1)}, u32[]{:S(2)}, u32[]{:S(2)}) %collective-permute-start.15) | collective-permute-done | bytes 2080 | tf_op jit(solution)/shard_map/ppermute | solution.py:573
  42.8 1.4 %final.1 = (f32[2,1,512]{2,1,0:T(1,128)}, f32[2,1,512]{2,1,0:T(1,128)}) custom-call(f32[1,512]{1,0:T(1,128)S(1)} %collective-permute-done.15.two_ref, f32[1,512]{1,0:T(1,128)S(1)} %collective-permute-done.16.one_ref, f32[1,512]{1,0:T(1,128)S(1)} %get-tuple-element.70.entry_ref, f32[1,512]{1,0:T(1,128)S(1)} %collective-permute-done.10.far_offset_ref.near_offset_ref, ...), custom_call_target="tpu_custom_call" | custom-call | flops 1000000000 | bytes 4096 | tf_op jit(solution)/shard_map/final/pallas_call | solution.py:550
  (34 shorter events, 0.5 us)
Async XLA Ops:
  0.6 4.1 %copy-start.4 = (f32[1,512]{1,0:T(1,128)S(1)}, f32[1,512]{1,0:T(1,128)}, u32[]{:S(2)}) copy-start(f32[1,512]{1,0:T(1,128)} %start_ref.1) | copy-start | bytes 6148
  0.6 4.1 %copy-start.3 = (bf16[2,1,512,512]{3,2,1,0:T(8,128)(2,1)S(1)}, bf16[2,1,512,512]{3,2,1,0:T(8,128)(2,1)}, u32[]{:S(2)}) copy-start(bf16[2,1,512,512]{3,2,1,0:T(8,128)(2,1)} %param.14) | copy-start | bytes 3145732
  0.7 4.1 %copy-start.1 = (bf16[2,1,512,512]{3,2,1,0:T(8,128)(2,1)S(1)}, bf16[2,1,512,512]{3,2,1,0:T(8,128)(2,1)}, u32[]{:S(2)}) copy-start(bf16[2,1,512,512]{3,2,1,0:T(8,128)(2,1)} %param.13) | copy-start | bytes 3145732
  3.4 3.7 %copy-start = (bf16[2,1,512,512]{3,2,1,0:T(8,128)(2,1)S(1)}, bf16[2,1,512,512]{3,2,1,0:T(8,128)(2,1)}, u32[]{:S(2)}) copy-start(bf16[2,1,512,512]{3,2,1,0:T(8,128)(2,1)} %param.15) | copy-start | bytes 3145732
  3.4 1.3 %collective-permute-start = (f32[2,512]{1,0:T(2,128)S(1)}, f32[2,512]{1,0:T(2,128)S(1)}, u32[]{:S(2)}, u32[]{:S(2)}) collective-permute-start(f32[2,512]{1,0:T(2,128)S(1)} %get-tuple-element.40), channel_id=1, source_target_pairs={{0,1},{1,0},{2,3},{3,2},{4,5},{5,4},{6,7},{7,6},{8,9},{9,8},{10,11... | collective-permute-start | bytes 12296 | tf_op jit(solution)/shard_map/ppermute | solution.py:169
  5.4 3.8 %collective-permute-start.1 = (f32[8,512]{1,0:T(8,128)S(1)}, f32[8,512]{1,0:T(8,128)S(1)}, u32[]{:S(2)}, u32[]{:S(2)}) collective-permute-start(f32[8,512]{1,0:T(8,128)S(1)} %get-tuple-element.41.refs_0_.after_ref), channel_id=1, source_target_pairs={{0,2},{1,3},{16,18},{17,19}} | collective-permute-start | bytes 49160 | tf_op jit(solution)/shard_map/ppermute | solution.py:620
  7.1 15.9 %collective-permute-start.11 = (f32[512,512]{1,0:T(8,128)S(1)}, f32[512,512]{1,0:T(8,128)S(1)}, u32[]{:S(2)}, u32[]{:S(2)}) collective-permute-start(f32[512,512]{1,0:T(8,128)S(1)} %compose.2), channel_id=1, source_target_pairs={{6,4},{12,10},{7,5},{13,11},{22,20},{28,26},{23,21},{29,27}} | collective-permute-start | bytes 3145736 | tf_op jit(solution)/shard_map/ppermute | solution.py:614
  8.0 1.2 %collective-permute-start.2 = (f32[2,512]{1,0:T(2,128)S(1)}, f32[2,512]{1,0:T(2,128)S(1)}, u32[]{:S(2)}, u32[]{:S(2)}) collective-permute-start(f32[2,512]{1,0:T(2,128)S(1)} %get-tuple-element.43), channel_id=1, source_target_pairs={{0,1},{1,0},{2,3},{3,2},{4,5},{5,4},{6,7},{7,6},{8,9},{9,8},{10,11... | collective-permute-start | bytes 12296 | tf_op jit(solution)/shard_map/ppermute | solution.py:169
  8.1 16.4 %collective-permute-start.14 = (f32[512,512]{1,0:T(8,128)S(1)}, f32[512,512]{1,0:T(8,128)S(1)}, u32[]{:S(2)}, u32[]{:S(2)}) collective-permute-start(f32[512,512]{1,0:T(8,128)S(1)} %compose.3), channel_id=1, source_target_pairs={{8,4},{9,5},{24,20},{25,21}} | collective-permute-start | bytes 3145736 | tf_op jit(solution)/shard_map/ppermute | solution.py:617
  9.2 1.0 %copy-start.2 = (bf16[1,512,512]{2,1,0:T(8,128)(2,1)S(1)}, bf16[1,512,512]{2,1,0:T(8,128)(2,1)}, u32[]{:S(2)}) copy-start(bf16[1,512,512]{2,1,0:T(8,128)(2,1)} %param.16) | copy-start | bytes 1572868
  9.2 2.3 %collective-permute-start.3 = (f32[1,512]{1,0:T(1,128)S(1)}, f32[1,512]{1,0:T(1,128)S(1)}, u32[]{:S(2)}, u32[]{:S(2)}) collective-permute-start(f32[1,512]{1,0:T(1,128)S(1)} %get-tuple-element.46), channel_id=1, source_target_pairs={{0,1},{1,0},{2,4},{3,5},{4,2},{5,3},{6,7},{7,6},{8,9},{9,8},{10,11... | collective-permute-start | bytes 6152 | tf_op jit(solution)/shard_map/ppermute | solution.py:573
  10.2 31.0 %collective-permute-start.17 = (f32[520,512]{1,0:T(8,128)S(1)}, f32[520,512]{1,0:T(8,128)S(1)}, u32[]{:S(2)}, u32[]{:S(2)}) collective-permute-start(f32[520,512]{1,0:T(8,128)S(1)} %late.1), channel_id=1, source_target_pairs={{2,0},{3,1},{18,16},{19,17}} | collective-permute-start | bytes 3194888 | tf_op jit(solution)/shard_map/ppermute | solution.py:633
  11.6 6.5 %collective-permute-start.4 = (f32[1,512]{1,0:T(1,128)S(1)}, f32[1,512]{1,0:T(1,128)S(1)}, u32[]{:S(2)}, u32[]{:S(2)}) collective-permute-start(f32[1,512]{1,0:T(1,128)S(1)} %get-tuple-element.49), channel_id=1, source_target_pairs={{0,4},{1,5},{2,3},{3,2},{4,6},{5,7},{6,0},{7,1},{8,9},{9,8},{10,11... | collective-permute-start | bytes 6152 | tf_op jit(solution)/shard_map/ppermute | solution.py:573
  18.1 1.2 %collective-permute-start.5 = (f32[1,512]{1,0:T(1,128)S(1)}, f32[1,512]{1,0:T(1,128)S(1)}, u32[]{:S(2)}, u32[]{:S(2)}) collective-permute-start(f32[1,512]{1,0:T(1,128)S(1)} %get-tuple-element.51), channel_id=1, source_target_pairs={{0,1},{1,0},{2,3},{3,2},{4,5},{5,4},{6,8},{7,9},{8,10},{9,11},{10,... | collective-permute-start | bytes 6152 | tf_op jit(solution)/shard_map/ppermute | solution.py:573
  19.2 1.2 %collective-permute-start.6 = (f32[1,512]{1,0:T(1,128)S(1)}, f32[1,512]{1,0:T(1,128)S(1)}, u32[]{:S(2)}, u32[]{:S(2)}) collective-permute-start(f32[1,512]{1,0:T(1,128)S(1)} %get-tuple-element.53), channel_id=1, source_target_pairs={{0,1},{1,0},{2,3},{3,2},{4,8},{5,9},{6,7},{7,6},{8,10},{9,11},{10,... | collective-permute-start | bytes 6152 | tf_op jit(solution)/shard_map/ppermute | solution.py:573
  20.4 1.2 %collective-permute-start.7 = (f32[1,512]{1,0:T(1,128)S(1)}, f32[1,512]{1,0:T(1,128)S(1)}, u32[]{:S(2)}, u32[]{:S(2)}) collective-permute-start(f32[1,512]{1,0:T(1,128)S(1)} %get-tuple-element.55), channel_id=1, source_target_pairs={{0,1},{1,0},{2,3},{3,2},{4,5},{5,4},{6,7},{7,6},{8,9},{9,8},{10,12... | collective-permute-start | bytes 6152 | tf_op jit(solution)/shard_map/ppermute | solution.py:573
  21.6 1.3 %collective-permute-start.8 = (f32[1,512]{1,0:T(1,128)S(1)}, f32[1,512]{1,0:T(1,128)S(1)}, u32[]{:S(2)}, u32[]{:S(2)}) collective-permute-start(f32[1,512]{1,0:T(1,128)S(1)} %get-tuple-element.57), channel_id=1, source_target_pairs={{0,1},{1,0},{2,3},{3,2},{4,5},{5,4},{6,7},{7,6},{8,9},{9,8},{10,11... | collective-permute-start | bytes 6152 | tf_op jit(solution)/shard_map/ppermute | solution.py:573
  22.4 1.2 %collective-permute-start.10 = (f32[1,512]{1,0:T(1,128)S(1)}, f32[1,512]{1,0:T(1,128)S(1)}, u32[]{:S(2)}, u32[]{:S(2)}) collective-permute-start(f32[1,512]{1,0:T(1,128)S(1)} %get-tuple-element.60.left_ref), channel_id=1, source_target_pairs={{0,1},{1,0},{2,3},{3,2},{4,6},{5,7},{6,4},{7,5},{8,9},{9,8},{10,12... | collective-permute-start | bytes 6152 | tf_op jit(solution)/shard_map/ppermute | solution.py:573
  22.8 1.2 %collective-permute-start.9 = (f32[1,512]{1,0:T(1,128)S(1)}, f32[1,512]{1,0:T(1,128)S(1)}, u32[]{:S(2)}, u32[]{:S(2)}) collective-permute-start(f32[1,512]{1,0:T(1,128)S(1)} %get-tuple-element.59.came_ref), channel_id=1, source_target_pairs={{0,1},{1,0},{2,3},{3,2},{4,5},{5,4},{6,7},{7,6},{8,9},{9,8},{10,14... | collective-permute-start | bytes 6152 | tf_op jit(solution)/shard_map/ppermute | solution.py:573
  24.0 1.2 %collective-permute-start.13 = (f32[1,512]{1,0:T(1,128)S(1)}, f32[1,512]{1,0:T(1,128)S(1)}, u32[]{:S(2)}, u32[]{:S(2)}) collective-permute-start(f32[1,512]{1,0:T(1,128)S(1)} %get-tuple-element.62.came_ref), channel_id=1, source_target_pairs={{0,1},{1,0},{2,3},{3,2},{4,6},{5,7},{6,10},{7,11},{8,4},{9,5},{10,... | collective-permute-start | bytes 6152 | tf_op jit(solution)/shard_map/ppermute | solution.py:573
  24.2 1.2 %collective-permute-start.12 = (f32[1,512]{1,0:T(1,128)S(1)}, f32[1,512]{1,0:T(1,128)S(1)}, u32[]{:S(2)}, u32[]{:S(2)}) collective-permute-start(f32[1,512]{1,0:T(1,128)S(1)} %get-tuple-element.62.came_ref), channel_id=1, source_target_pairs={{0,1},{1,0},{2,3},{3,2},{4,10},{5,11},{6,7},{7,6},{8,9},{9,8},{10,... | collective-permute-start | bytes 6152 | tf_op jit(solution)/shard_map/ppermute | solution.py:573
  25.3 16.1 %collective-permute-start.16 = (f32[1,512]{1,0:T(1,128)S(1)}, f32[1,512]{1,0:T(1,128)S(1)}, u32[]{:S(2)}, u32[]{:S(2)}) collective-permute-start(f32[1,512]{1,0:T(1,128)S(1)} %get-tuple-element.69.after_ref), channel_id=1, source_target_pairs={{0,1},{1,0},{2,4},{3,5},{4,2},{5,3},{6,7},{7,6},{8,9},{9,8},{10,11... | collective-permute-start | bytes 6152 | tf_op jit(solution)/shard_map/ppermute | solution.py:573
  25.7 17.1 %collective-permute-start.15 = (f32[1,512]{1,0:T(1,128)S(1)}, f32[1,512]{1,0:T(1,128)S(1)}, u32[]{:S(2)}, u32[]{:S(2)}) collective-permute-start(f32[1,512]{1,0:T(1,128)S(1)} %get-tuple-element.69.after_ref), channel_id=1, source_target_pairs={{0,4},{1,5},{2,3},{3,2},{4,0},{5,1},{6,8},{7,9},{8,6},{9,7},{10,11... | collective-permute-start | bytes 6152 | tf_op jit(solution)/shard_map/ppermute | solution.py:573

commit v9 on v8

--- a/solution.py
+++ b/solution.py
@@ -8,7 +8,6 @@
 from jax.sharding import PartitionSpec as P
 
 GH = 16
-MAP_COPIES = 4
 COSTS = (60.0, 2.5, 2.5, 6.0, 0.5)
 VMEM = pl.BlockSpec(memory_space=pltpu.VMEM)
 PARAMS = pltpu.CompilerParams(vmem_limit_bytes=16 * 2**20)
@@ -36,46 +35,36 @@
     return found if len(rows) > 1 else found[0]
 
 
-def info_kernel(zero, *refs):
-    @pl.when((lax.axis_index("tm") == 0) == zero)
-    def _():
-        place_info(*(refs if zero else refs[1:]))
-
-
-def place_info(
-    maps_hbm,
-    stencil_hbm,
-    observed_hbm,
-    active_hbm,
-    mine_ref,
-    theirs_ref,
-    maps,
-    stencil_ref,
-    observed_ref,
-    active_ref,
-    taps,
-    map_sems,
-    sems,
-):
+def info_kernel(stencil_hbm, observed_hbm, active_hbm, maps_hbm, mine_ref, theirs_ref, *scratch):
+    stencil_ref, observed_ref, active_ref, maps, taps, sems = scratch
+
+    @pl.when(lax.axis_index("tm") == 0)
+    def _():
+        copies = []
+        for i, (source, target) in enumerate(
+            ((stencil_hbm, stencil_ref), (observed_hbm, observed_ref), (active_hbm, active_ref))
+        ):
+            copies.append(pltpu.make_async_copy(source, target, sems.at[i]))
+        for t in range(maps.shape[0]):
+            copies.append(pltpu.make_async_copy(maps_hbm.at[t], maps.at[t], sems.at[3 + t]))
+        for copy in copies:
+            copy.start()
+        place_info(stencil_ref, observed_ref, active_ref, maps, mine_ref, theirs_ref, taps, copies)
+
+
+def staged_info_kernel(after_ref, *refs):
+    del after_ref
+
+    @pl.when(lax.axis_index("tm") != 0)
+    def _():
+        place_info(*refs, [])
+
+
+def place_info(stencil_ref, observed_ref, active_ref, maps, mine_ref, theirs_ref, taps, copies):
     steps, rows, cells = maps.shape
     slots = observed_ref.shape[1]
     side, _, channels = stencil_ref.shape
     half = side // 2
-    small = []
-    for i, (source, target) in enumerate(
-        ((stencil_hbm, stencil_ref), (observed_hbm, observed_ref), (active_hbm, active_ref))
-    ):
-        small.append(pltpu.make_async_copy(source, target, sems.at[i]))
-        small[-1].start()
-    part = rows // MAP_COPIES
-    copies = []
-    for t in range(steps):
-        for i in range(MAP_COPIES):
-            at = pl.ds(i * part, part)
-            copies.append(
-                pltpu.make_async_copy(maps_hbm.at[t, at], maps.at[t, at], map_sems.at[t, i])
-            )
-            copies[-1].start()
 
     repeat = jnp.where(
         lax.broadcasted_iota(jnp.int32, (channels, rows), 1) % channels
@@ -99,7 +88,7 @@
     column = across - tap + half
     column_inside = (column >= 0) & (column < width) & (tap < side)
     me = lax.axis_index("block")
-    for copy in small:
+    for copy in copies[:3]:
         copy.wait()
     for p in range(side):
         taps[p * 8 : p * 8 + side, :] = jnp.dot(
@@ -113,7 +102,7 @@
             jnp.where(live, 1.0, 0.0).astype(jnp.bfloat16), spread, preferred_element_type=jnp.float32
         )
         left = jnp.concatenate([taps[...] * weight[b : b + 1, :] for b in range(2)], axis=0)
-        for copy in copies[t * MAP_COPIES : (t + 1) * MAP_COPIES]:
+        for copy in copies[3 + t : 4 + t]:
             copy.wait()
         shifted = jnp.dot(left.astype(jnp.bfloat16), maps[t], preferred_element_type=jnp.float32)
         found = []
@@ -134,38 +123,35 @@
 
 
 def sensor_info(after, scaled_residual_maps, measurement_stencil, observed_partition, active_probe_total):
-    zero = not after
     steps, slots, channels, cells = scaled_residual_maps.shape
     side = measurement_stencil.shape[1]
+    operands = (
+        measurement_stencil.transpose(1, 2, 0),
+        observed_partition,
+        active_probe_total.T,
+        scaled_residual_maps.reshape(steps, slots * channels, cells),
+    )
+    taps = pltpu.VMEM((side * 8, slots * channels), jnp.float32)
+    if after:
+        kernel, specs, scratch, cost = staged_info_kernel, [VMEM] * 5, [taps], int(COSTS[0] * 1e9)
+    else:
+        kernel, specs, cost = info_kernel, [pl.BlockSpec(memory_space=pltpu.HBM)] * 4, 10**6
+        scratch = [
+            *(pltpu.VMEM(array.shape, array.dtype) for array in operands),
+            taps,
+            pltpu.SemaphoreType.DMA((3 + steps,)),
+        ]
+        operands = [pltpu.with_memory_space_constraint(array, pltpu.HBM) for array in operands]
     mine, theirs = pl.pallas_call(
-        functools.partial(info_kernel, zero),
+        kernel,
         out_shape=[jax.ShapeDtypeStruct((steps, cells), jnp.float32)] * 2,
-        in_specs=[VMEM] * len(after) + [pl.BlockSpec(memory_space=pltpu.HBM)] * 4,
+        in_specs=specs,
         out_specs=[VMEM] * 2,
-        scratch_shapes=[
-            pltpu.VMEM((steps, slots * channels, cells), jnp.bfloat16),
-            pltpu.VMEM((side, side, channels), jnp.bfloat16),
-            pltpu.VMEM((steps, slots), jnp.int32),
-            pltpu.VMEM((1, steps), jnp.int32),
-            pltpu.VMEM((side * 8, slots * channels), jnp.float32),
-            pltpu.SemaphoreType.DMA((steps, MAP_COPIES)),
-            pltpu.SemaphoreType.DMA((3,)),
-        ],
+        scratch_shapes=scratch,
         compiler_params=PARAMS,
-        cost_estimate=pl.CostEstimate(flops=10**6 if zero else int(COSTS[0] * 1e9), bytes_accessed=2**12, transcendentals=0),
+        cost_estimate=pl.CostEstimate(flops=cost, bytes_accessed=2**12, transcendentals=0),
         name="sensor_info",
-    )(
-        *after,
-        *(
-            pltpu.with_memory_space_constraint(array, pltpu.HBM)
-            for array in (
-                scaled_residual_maps.reshape(steps, slots * channels, cells),
-                measurement_stencil.transpose(1, 2, 0),
-                observed_partition,
-                active_probe_total.T,
-            )
-        )
-    )
+    )(*after, *operands)
     return mine, lax.ppermute(theirs, "block", [(0, 1), (1, 0)])
 
 
@@ -576,6 +562,8 @@
 def ring_up(place, places):
     if place % 2 and place >= places - 5 and place < places - 1:
         return (place, place + 1, place + 2)
+    if place == 0:
+        return (0, 1, 3)
     if place % 2 or place == places - 2:
         return (place, place + 1)
     return (place, place + 1, place - 2)
@@ -617,7 +605,7 @@
     skip = lax.ppermute(compose(send, last - 3), "tm", [(last - 3, last - 5)])
     for place in range(1, places):
         if place == 1:
-            came = lax.ppermute(send, "tm", [(0, 1)])
+            came = pass_row(send, [ring_up(0, places)], places)
             mine, other = sensor_info((send,), *sensors)
             inputs, means, send = call(
                 first_hop_kernel, "forward", (many, many, one),

time: 44.4 us -> 43.7 us (0.984)
  starting transfers between devices: 27.9 us -> 24.3 us
  waiting for transfers between devices: 8.85 us -> 10.9 us
  local copies, waits for them, and re-layouts: 0.82 us -> 1.62 us
    ppermute x12 -> x13, starting transfers between devices: 23 us -> 20.5 us  [pass_row(): return lax.ppermute(row, ('tm', 'block'), sorted(route.items()))]
    ppermute x12 -> x13, waiting for transfers between devices: 7.62 us -> 9.94 us  [pass_row(): return lax.ppermute(row, ('tm', 'block'), sorted(route.items()))]
    ppermute x1 -> x0, starting transfers between devices: 1.62 us -> none  [local(): came = lax.ppermute(send, 'tm', [(0, 1)])]
    unnamed x10 -> x18, local copies, waits for them, and re-layouts: 0.82 us -> 1.62 us
  transfers between devices with their start and end apart: 18 -> 18, of which waited for: 11 -> 12; matrix products, arithmetic and copies ran while one was open for 0% -> 0% of each run, Pallas kernels for 2% -> 2%
where the time goes in v9:
time: 43.7 us; the launch traced here: 43.1 us
  starting transfers between devices  24.3 us (56%)
  waiting for transfers between devices  10.9 us (25%)
  Pallas kernels  5.47 us (13%)
  local copies, waits for them, and re-layouts  1.62 us (4%)
  between operations  0.83 us (2%)
    ppermute x13, starting transfers between devices, pass_row(): return lax.ppermute(row, ('tm', 'block'), sorted(route.items()))  20.5 us
    ppermute x13, waiting for transfers between devices, pass_row(): return lax.ppermute(row, ('tm', 'block'), sorted(route.items()))  9.94 us
    pallas_call x18, Pallas kernels, call(): pl.pallas_call(kernel, out_shape=[jax.ShapeDtypeStruct(shape, jnp.bfloat1...  2.97 us
    pallas_call x2, Pallas kernels, sensor_info(): pl.pallas_call(kernel, out_shape=[jax.ShapeDtypeStruct((steps, cells), jn...  2.5 us
    unnamed x18, local copies, waits for them, and re-layouts  1.62 us
    ppermute x1, starting transfers between devices, local(): late = lax.ppermute(late, 'tm', [(1, 0)])  1.28 us
    ppermute x2, starting transfers between devices, sensor_info(): return (mine, lax.ppermute(theirs, 'block', [(0, 1), (1, 0)]))  0.94 us
    ppermute x2, waiting for transfers between devices, sensor_info(): return (mine, lax.ppermute(theirs, 'block', [(0, 1), (1, 0)]))  0.92 us
  transfers between devices with their start and end apart: 18, of which 12 were waited for; matrix products, arithmetic and copies ran while one was open for 0% of the time, Pallas kernels for 2%

profile of v9, /device:TPU:0, one launch (start us, length us, event | category | flops | bytes accessed | tf_op | source)
XLA Modules:
  0.0 43.1 jit_solution(9578403244825152358)
XLA Ops:
  0.7 2.5 %sensor_info.2 = (f32[2,512]{1,0:T(2,128)S(1)}, f32[2,512]{1,0:T(2,128)S(1)}) custom-call(bf16[7,7,16]{2,1,0:T(8,128)(2,1)} %bitcast.30, s32[2,64]{1,0:T(2,128)} %refs_1_.1, s32[1,2]{1,0:T(1,128)} %bitcast.32, bf16[2,1024,512]{2,1,0:T(8,128)(2,1)} %bitcast.23), custom_call_target="tpu_custom_call" | custom-call | flops 1000000 | bytes 4096 | tf_op jit(solution)/shard_map/sensor_info/pallas_call | solution.py:145
  3.2 0.5 %collective-permute-start = (f32[2,512]{1,0:T(2,128)S(1)}, f32[2,512]{1,0:T(2,128)S(1)}, u32[]{:S(2)}, u32[]{:S(2)}) collective-permute-start(f32[2,512]{1,0:T(2,128)S(1)} %get-tuple-element.40), channel_id=1, source_target_pairs={{0,1},{1,0},{2,3},{3,2},{4,5},{5,4},{6,7},{7,6},{8,9},{9,8},{10,11... | collective-permute-start | bytes 12296 | tf_op jit(solution)/shard_map/ppermute | solution.py:155
  3.7 0.8 %collective-permute-done.other_ref = f32[2,512]{1,0:T(2,128)S(1)} collective-permute-done((f32[2,512]{1,0:T(2,128)S(1)}, f32[2,512]{1,0:T(2,128)S(1)}, u32[]{:S(2)}, u32[]{:S(2)}) %collective-permute-start) | collective-permute-done | bytes 4128 | tf_op jit(solution)/shard_map/ppermute | solution.py:155
  4.5 0.7 %start.1 = (f32[2,512]{1,0:T(2,128)S(1)}, f32[2,512]{1,0:T(2,128)S(1)}, f32[8,512]{1,0:T(8,128)S(1)}) custom-call(f32[2,512]{1,0:T(2,128)S(1)} %get-tuple-element.39.mine_ref, f32[2,512]{1,0:T(2,128)S(1)} %collective-permute-done.other_ref, bf16[2,512,512]{2,1,0:T(8,128)(2,1)S(1)} %bitcast.28, bf16[2,512,512]{2,1,0:T(8,128)(2,1)S(1)} %bitcast.15, ...), custom_call_target="tpu_custom_call" | custom-call | flops 500000000 | bytes 4096 | tf_op jit(solution)/shard_map/start/pallas_call | solution.py:536
  5.4 0.9 %collective-permute-start.11 = (f32[512,512]{1,0:T(8,128)S(1)}, f32[512,512]{1,0:T(8,128)S(1)}, u32[]{:S(2)}, u32[]{:S(2)}) collective-permute-start(f32[512,512]{1,0:T(8,128)S(1)} %compose.2), channel_id=1, source_target_pairs={{6,4},{12,10},{7,5},{13,11},{22,20},{28,26},{23,21},{29,27}} | collective-permute-start | bytes 3145736 | tf_op jit(solution)/shard_map/ppermute | solution.py:602
  6.2 0.6 %copy-done.2 = bf16[2,64,16,512]{3,2,1,0:T(8,128)(2,1)S(1)} copy-done((bf16[2,64,16,512]{3,2,1,0:T(8,128)(2,1)S(1)}, bf16[2,64,16,512]{3,2,1,0:T(8,128)(2,1)}, u32[]{:S(2)}) %copy-start.2) | copy-done | bytes 2097176
  6.8 0.4 collective-permute-start.2
  7.2 0.7 %collective-permute-start.14 = (f32[512,512]{1,0:T(8,128)S(1)}, f32[512,512]{1,0:T(8,128)S(1)}, u32[]{:S(2)}, u32[]{:S(2)}) collective-permute-start(f32[512,512]{1,0:T(8,128)S(1)} %compose.3), channel_id=1, source_target_pairs={{8,4},{9,5},{24,20},{25,21}} | collective-permute-start | bytes 3145736 | tf_op jit(solution)/shard_map/ppermute | solution.py:605
  8.1 1.9 %collective-permute-done.1.came_ref = f32[8,512]{1,0:T(8,128)S(1)} collective-permute-done((f32[8,512]{1,0:T(8,128)S(1)}, f32[8,512]{1,0:T(8,128)S(1)}, u32[]{:S(2)}, u32[]{:S(2)}) %collective-permute-start.1) | collective-permute-done | bytes 16416 | tf_op jit(solution)/shard_map/ppermute | solution.py:559
  10.0 1.0 %copy-done.3 = bf16[1,512,512]{2,1,0:T(8,128)(2,1)S(1)} copy-done((bf16[1,512,512]{2,1,0:T(8,128)(2,1)S(1)}, bf16[1,512,512]{2,1,0:T(8,128)(2,1)}, u32[]{:S(2)}) %copy-start.3) | copy-done | bytes 524312
  11.0 1.3 %collective-permute-start.17 = (f32[520,512]{1,0:T(8,128)S(1)}, f32[520,512]{1,0:T(8,128)S(1)}, u32[]{:S(2)}, u32[]{:S(2)}) collective-permute-start(f32[520,512]{1,0:T(8,128)S(1)} %late.1), channel_id=1, source_target_pairs={{2,0},{3,1},{18,16},{19,17}} | collective-permute-start | bytes 3194888 | tf_op jit(solution)/shard_map/ppermute | solution.py:621
  12.3 2.9 %collective-permute-start.4 = (f32[1,512]{1,0:T(1,128)S(1)}, f32[1,512]{1,0:T(1,128)S(1)}, u32[]{:S(2)}, u32[]{:S(2)}) collective-permute-start(f32[1,512]{1,0:T(1,128)S(1)} %get-tuple-element.49), channel_id=1, source_target_pairs={{0,4},{1,5},{2,3},{3,2},{4,6},{5,7},{6,0},{7,1},{8,9},{9,8},{10,11... | collective-permute-start | bytes 6152 | tf_op jit(solution)/shard_map/ppermute | solution.py:559
  15.3 1.7 %collective-permute-done.4.came_ref = f32[1,512]{1,0:T(1,128)S(1)} collective-permute-done((f32[1,512]{1,0:T(1,128)S(1)}, f32[1,512]{1,0:T(1,128)S(1)}, u32[]{:S(2)}, u32[]{:S(2)}) %collective-permute-start.4) | collective-permute-done | bytes 2080 | tf_op jit(solution)/shard_map/ppermute | solution.py:559
  17.0 1.2 %collective-permute-done.5.came_ref = f32[1,512]{1,0:T(1,128)S(1)} collective-permute-done((f32[1,512]{1,0:T(1,128)S(1)}, f32[1,512]{1,0:T(1,128)S(1)}, u32[]{:S(2)}, u32[]{:S(2)}) %collective-permute-start.5) | collective-permute-done | bytes 2080 | tf_op jit(solution)/shard_map/ppermute | solution.py:559
  18.2 0.2 collective-permute-start.6
  18.3 1.0 %collective-permute-done.6.came_ref = f32[1,512]{1,0:T(1,128)S(1)} collective-permute-done((f32[1,512]{1,0:T(1,128)S(1)}, f32[1,512]{1,0:T(1,128)S(1)}, u32[]{:S(2)}, u32[]{:S(2)}) %collective-permute-start.6) | collective-permute-done | bytes 2080 | tf_op jit(solution)/shard_map/ppermute | solution.py:559
  19.3 0.2 collective-permute-start.7
  19.5 1.0 %collective-permute-done.7.came_ref = f32[1,512]{1,0:T(1,128)S(1)} collective-permute-done((f32[1,512]{1,0:T(1,128)S(1)}, f32[1,512]{1,0:T(1,128)S(1)}, u32[]{:S(2)}, u32[]{:S(2)}) %collective-permute-start.7) | collective-permute-done | bytes 2080 | tf_op jit(solution)/shard_map/ppermute | solution.py:559
  20.5 0.2 collective-permute-start.8
  20.7 0.7 %offsets.1 = (f32[2,512]{1,0:T(2,128)S(1)}, f32[1,512]{1,0:T(1,128)S(1)}, bf16[2,512,512]{2,1,0:T(8,128)(2,1)S(1)}) custom-call(f32[2,512]{1,0:T(2,128)S(1)} %get-tuple-element.58.kept_ref.means_ref, bf16[2,512,512]{2,1,0:T(8,128)(2,1)S(1)} %bitcast.10, bf16[512,512]{1,0:T(8,128)(2,1)S(1)} %bitcast.26), custom_call_target="tpu_custom_call" | custom-call | flops 1000000000 | bytes 4096 | tf_op jit(solution)/shard_map/offsets/pallas_call | solution.py:536
  21.3 0.4 collective-permute-start.10
  21.8 0.2 collective-permute-start.9
  21.9 0.6 %collective-permute-done.10.far_offset_ref.near_offset_ref = f32[1,512]{1,0:T(1,128)S(1)} collective-permute-done((f32[1,512]{1,0:T(1,128)S(1)}, f32[1,512]{1,0:T(1,128)S(1)}, u32[]{:S(2)}, u32[]{:S(2)}) %collective-permute-start.10) | collective-permute-done | bytes 2080 | tf_op jit(solution)/shard_map/ppermute | solution.py:559
  22.6 0.3 collective-permute-done.9.last_ref
  22.9 0.2 collective-permute-start.13
  23.1 0.3 collective-permute-start.12
  23.4 0.6 %collective-permute-done.13.one_ref = f32[1,512]{1,0:T(1,128)S(1)} collective-permute-done((f32[1,512]{1,0:T(1,128)S(1)}, f32[1,512]{1,0:T(1,128)S(1)}, u32[]{:S(2)}, u32[]{:S(2)}) %collective-permute-start.13) | collective-permute-done | bytes 2080 | tf_op jit(solution)/shard_map/ppermute | solution.py:559
  24.1 0.2 collective-permute-done.12.three_ref
  24.3 0.3 collective-permute-start.16
  24.6 15.5 %collective-permute-start.15 = (f32[1,512]{1,0:T(1,128)S(1)}, f32[1,512]{1,0:T(1,128)S(1)}, u32[]{:S(2)}, u32[]{:S(2)}) collective-permute-start(f32[1,512]{1,0:T(1,128)S(1)} %get-tuple-element.69.after_ref), channel_id=1, source_target_pairs={{0,4},{1,5},{2,3},{3,2},{4,0},{5,1},{6,8},{7,9},{8,6},{9,7},{10,11... | collective-permute-start | bytes 6152 | tf_op jit(solution)/shard_map/ppermute | solution.py:559
  40.3 1.4 %collective-permute-done.15.two_ref = f32[1,512]{1,0:T(1,128)S(1)} collective-permute-done((f32[1,512]{1,0:T(1,128)S(1)}, f32[1,512]{1,0:T(1,128)S(1)}, u32[]{:S(2)}, u32[]{:S(2)}) %collective-permute-start.15) | collective-permute-done | bytes 2080 | tf_op jit(solution)/shard_map/ppermute | solution.py:559
  41.7 1.4 %final.1 = (f32[2,1,512]{2,1,0:T(1,128)}, f32[2,1,512]{2,1,0:T(1,128)}) custom-call(f32[1,512]{1,0:T(1,128)S(1)} %collective-permute-done.15.two_ref, f32[1,512]{1,0:T(1,128)S(1)} %collective-permute-done.16.one_ref, f32[1,512]{1,0:T(1,128)S(1)} %get-tuple-element.70.entry_ref, f32[1,512]{1,0:T(1,128)S(1)} %collective-permute-done.10.far_offset_ref.near_offset_ref, ...), custom_call_target="tpu_custom_call" | custom-call | flops 1000000000 | bytes 4096 | tf_op jit(solution)/shard_map/final/pallas_call | solution.py:536
  (42 shorter events, 0.5 us)
Async XLA Ops:
  0.6 3.9 %copy-start.6 = (f32[1,512]{1,0:T(1,128)S(1)}, f32[1,512]{1,0:T(1,128)}, u32[]{:S(2)}) copy-start(f32[1,512]{1,0:T(1,128)} %start_ref.1) | copy-start | bytes 6148
  0.6 3.9 %copy-start.4 = (bf16[2,1,512,512]{3,2,1,0:T(8,128)(2,1)S(1)}, bf16[2,1,512,512]{3,2,1,0:T(8,128)(2,1)}, u32[]{:S(2)}) copy-start(bf16[2,1,512,512]{3,2,1,0:T(8,128)(2,1)} %param.14) | copy-start | bytes 3145732
  0.7 3.9 %copy-start.1 = (bf16[2,1,512,512]{3,2,1,0:T(8,128)(2,1)S(1)}, bf16[2,1,512,512]{3,2,1,0:T(8,128)(2,1)}, u32[]{:S(2)}) copy-start(bf16[2,1,512,512]{3,2,1,0:T(8,128)(2,1)} %param.13) | copy-start | bytes 3145732
  3.2 2.2 %copy-start = (bf16[2,1,512,512]{3,2,1,0:T(8,128)(2,1)S(1)}, bf16[2,1,512,512]{3,2,1,0:T(8,128)(2,1)}, u32[]{:S(2)}) copy-start(bf16[2,1,512,512]{3,2,1,0:T(8,128)(2,1)} %param.15) | copy-start | bytes 3145732
  3.2 1.3 %collective-permute-start = (f32[2,512]{1,0:T(2,128)S(1)}, f32[2,512]{1,0:T(2,128)S(1)}, u32[]{:S(2)}, u32[]{:S(2)}) collective-permute-start(f32[2,512]{1,0:T(2,128)S(1)} %get-tuple-element.40), channel_id=1, source_target_pairs={{0,1},{1,0},{2,3},{3,2},{4,5},{5,4},{6,7},{7,6},{8,9},{9,8},{10,11... | collective-permute-start | bytes 12296 | tf_op jit(solution)/shard_map/ppermute | solution.py:155
  5.2 1.6 %copy-start.2 = (bf16[2,64,16,512]{3,2,1,0:T(8,128)(2,1)S(1)}, bf16[2,64,16,512]{3,2,1,0:T(8,128)(2,1)}, u32[]{:S(2)}) copy-start(bf16[2,64,16,512]{3,2,1,0:T(8,128)(2,1)} %param.9) | copy-start | bytes 6291460
  5.2 1.6 %copy-start.5 = (bf16[16,7,7]{0,2,1:T(8,128)(2,1)S(1)}, bf16[16,7,7]{0,2,1:T(8,128)(2,1)}, u32[]{:S(2)}) copy-start(bf16[16,7,7]{0,2,1:T(8,128)(2,1)} %param.10) | copy-start | bytes 4708
  5.2 1.6 %copy-start.7 = (s32[2,64]{1,0:T(2,128)S(1)}, s32[2,64]{1,0:T(2,128)}, u32[]{:S(2)}) copy-start(s32[2,64]{1,0:T(2,128)} %refs_1_.1) | copy-start | bytes 1540
  5.2 1.6 %copy-start.8 = (s32[2,1]{0,1:T(1,128)S(1)}, s32[2,1]{0,1:T(1,128)}, u32[]{:S(2)}) copy-start(s32[2,1]{0,1:T(1,128)} %param.12) | copy-start | bytes 28
  5.2 4.7 %collective-permute-start.1 = (f32[8,512]{1,0:T(8,128)S(1)}, f32[8,512]{1,0:T(8,128)S(1)}, u32[]{:S(2)}, u32[]{:S(2)}) collective-permute-start(f32[8,512]{1,0:T(8,128)S(1)} %get-tuple-element.41.after_ref), channel_id=1, source_target_pairs={{0,2},{1,3},{2,6},{3,7},{4,5},{5,4},{6,0},{7,1},{8,9},{9,8},{10,11... | collective-permute-start | bytes 49160 | tf_op jit(solution)/shard_map/ppermute | solution.py:559
  5.4 16.6 %collective-permute-start.11 = (f32[512,512]{1,0:T(8,128)S(1)}, f32[512,512]{1,0:T(8,128)S(1)}, u32[]{:S(2)}, u32[]{:S(2)}) collective-permute-start(f32[512,512]{1,0:T(8,128)S(1)} %compose.2), channel_id=1, source_target_pairs={{6,4},{12,10},{7,5},{13,11},{22,20},{28,26},{23,21},{29,27}} | collective-permute-start | bytes 3145736 | tf_op jit(solution)/shard_map/ppermute | solution.py:602
  6.8 1.2 %collective-permute-start.2 = (f32[2,512]{1,0:T(2,128)S(1)}, f32[2,512]{1,0:T(2,128)S(1)}, u32[]{:S(2)}, u32[]{:S(2)}) collective-permute-start(f32[2,512]{1,0:T(2,128)S(1)} %get-tuple-element.43), channel_id=1, source_target_pairs={{0,1},{1,0},{2,3},{3,2},{4,5},{5,4},{6,7},{7,6},{8,9},{9,8},{10,11... | collective-permute-start | bytes 12296 | tf_op jit(solution)/shard_map/ppermute | solution.py:155
  7.2 16.2 %collective-permute-start.14 = (f32[512,512]{1,0:T(8,128)S(1)}, f32[512,512]{1,0:T(8,128)S(1)}, u32[]{:S(2)}, u32[]{:S(2)}) collective-permute-start(f32[512,512]{1,0:T(8,128)S(1)} %compose.3), channel_id=1, source_target_pairs={{8,4},{9,5},{24,20},{25,21}} | collective-permute-start | bytes 3145736 | tf_op jit(solution)/shard_map/ppermute | solution.py:605
  10.0 1.0 %copy-start.3 = (bf16[1,512,512]{2,1,0:T(8,128)(2,1)S(1)}, bf16[1,512,512]{2,1,0:T(8,128)(2,1)}, u32[]{:S(2)}) copy-start(bf16[1,512,512]{2,1,0:T(8,128)(2,1)} %param.16) | copy-start | bytes 1572868
  10.0 2.3 %collective-permute-start.3 = (f32[1,512]{1,0:T(1,128)S(1)}, f32[1,512]{1,0:T(1,128)S(1)}, u32[]{:S(2)}, u32[]{:S(2)}) collective-permute-start(f32[1,512]{1,0:T(1,128)S(1)} %get-tuple-element.46), channel_id=1, source_target_pairs={{0,1},{1,0},{2,4},{3,5},{4,2},{5,3},{6,7},{7,6},{8,9},{9,8},{10,11... | collective-permute-start | bytes 6152 | tf_op jit(solution)/shard_map/ppermute | solution.py:559
  11.0 29.1 %collective-permute-start.17 = (f32[520,512]{1,0:T(8,128)S(1)}, f32[520,512]{1,0:T(8,128)S(1)}, u32[]{:S(2)}, u32[]{:S(2)}) collective-permute-start(f32[520,512]{1,0:T(8,128)S(1)} %late.1), channel_id=1, source_target_pairs={{2,0},{3,1},{18,16},{19,17}} | collective-permute-start | bytes 3194888 | tf_op jit(solution)/shard_map/ppermute | solution.py:621
  12.3 4.7 %collective-permute-start.4 = (f32[1,512]{1,0:T(1,128)S(1)}, f32[1,512]{1,0:T(1,128)S(1)}, u32[]{:S(2)}, u32[]{:S(2)}) collective-permute-start(f32[1,512]{1,0:T(1,128)S(1)} %get-tuple-element.49), channel_id=1, source_target_pairs={{0,4},{1,5},{2,3},{3,2},{4,6},{5,7},{6,0},{7,1},{8,9},{9,8},{10,11... | collective-permute-start | bytes 6152 | tf_op jit(solution)/shard_map/ppermute | solution.py:559
  17.0 1.2 %collective-permute-start.5 = (f32[1,512]{1,0:T(1,128)S(1)}, f32[1,512]{1,0:T(1,128)S(1)}, u32[]{:S(2)}, u32[]{:S(2)}) collective-permute-start(f32[1,512]{1,0:T(1,128)S(1)} %get-tuple-element.51), channel_id=1, source_target_pairs={{0,1},{1,0},{2,3},{3,2},{4,5},{5,4},{6,8},{7,9},{8,10},{9,11},{10,... | collective-permute-start | bytes 6152 | tf_op jit(solution)/shard_map/ppermute | solution.py:559
  18.2 1.2 %collective-permute-start.6 = (f32[1,512]{1,0:T(1,128)S(1)}, f32[1,512]{1,0:T(1,128)S(1)}, u32[]{:S(2)}, u32[]{:S(2)}) collective-permute-start(f32[1,512]{1,0:T(1,128)S(1)} %get-tuple-element.53), channel_id=1, source_target_pairs={{0,1},{1,0},{2,3},{3,2},{4,8},{5,9},{6,7},{7,6},{8,10},{9,11},{10,... | collective-permute-start | bytes 6152 | tf_op jit(solution)/shard_map/ppermute | solution.py:559
  19.3 1.2 %collective-permute-start.7 = (f32[1,512]{1,0:T(1,128)S(1)}, f32[1,512]{1,0:T(1,128)S(1)}, u32[]{:S(2)}, u32[]{:S(2)}) collective-permute-start(f32[1,512]{1,0:T(1,128)S(1)} %get-tuple-element.55), channel_id=1, source_target_pairs={{0,1},{1,0},{2,3},{3,2},{4,5},{5,4},{6,7},{7,6},{8,9},{9,8},{10,12... | collective-permute-start | bytes 6152 | tf_op jit(solution)/shard_map/ppermute | solution.py:559
  20.5 1.3 %collective-permute-start.8 = (f32[1,512]{1,0:T(1,128)S(1)}, f32[1,512]{1,0:T(1,128)S(1)}, u32[]{:S(2)}, u32[]{:S(2)}) collective-permute-start(f32[1,512]{1,0:T(1,128)S(1)} %get-tuple-element.57), channel_id=1, source_target_pairs={{0,1},{1,0},{2,3},{3,2},{4,5},{5,4},{6,7},{7,6},{8,9},{9,8},{10,11... | collective-permute-start | bytes 6152 | tf_op jit(solution)/shard_map/ppermute | solution.py:559
  21.3 1.2 %collective-permute-start.10 = (f32[1,512]{1,0:T(1,128)S(1)}, f32[1,512]{1,0:T(1,128)S(1)}, u32[]{:S(2)}, u32[]{:S(2)}) collective-permute-start(f32[1,512]{1,0:T(1,128)S(1)} %get-tuple-element.60.left_ref), channel_id=1, source_target_pairs={{0,1},{1,0},{2,3},{3,2},{4,6},{5,7},{6,4},{7,5},{8,9},{9,8},{10,12... | collective-permute-start | bytes 6152 | tf_op jit(solution)/shard_map/ppermute | solution.py:559
  21.8 1.2 %collective-permute-start.9 = (f32[1,512]{1,0:T(1,128)S(1)}, f32[1,512]{1,0:T(1,128)S(1)}, u32[]{:S(2)}, u32[]{:S(2)}) collective-permute-start(f32[1,512]{1,0:T(1,128)S(1)} %get-tuple-element.59.came_ref), channel_id=1, source_target_pairs={{0,1},{1,0},{2,3},{3,2},{4,5},{5,4},{6,7},{7,6},{8,9},{9,8},{10,14... | collective-permute-start | bytes 6152 | tf_op jit(solution)/shard_map/ppermute | solution.py:559
  22.9 1.2 %collective-permute-start.13 = (f32[1,512]{1,0:T(1,128)S(1)}, f32[1,512]{1,0:T(1,128)S(1)}, u32[]{:S(2)}, u32[]{:S(2)}) collective-permute-start(f32[1,512]{1,0:T(1,128)S(1)} %get-tuple-element.62.came_ref), channel_id=1, source_target_pairs={{0,1},{1,0},{2,3},{3,2},{4,6},{5,7},{6,10},{7,11},{8,4},{9,5},{10,... | collective-permute-start | bytes 6152 | tf_op jit(solution)/shard_map/ppermute | solution.py:559
  23.1 1.2 %collective-permute-start.12 = (f32[1,512]{1,0:T(1,128)S(1)}, f32[1,512]{1,0:T(1,128)S(1)}, u32[]{:S(2)}, u32[]{:S(2)}) collective-permute-start(f32[1,512]{1,0:T(1,128)S(1)} %get-tuple-element.62.came_ref), channel_id=1, source_target_pairs={{0,1},{1,0},{2,3},{3,2},{4,10},{5,11},{6,7},{7,6},{8,9},{9,8},{10,... | collective-permute-start | bytes 6152 | tf_op jit(solution)/shard_map/ppermute | solution.py:559
  24.3 16.0 %collective-permute-start.16 = (f32[1,512]{1,0:T(1,128)S(1)}, f32[1,512]{1,0:T(1,128)S(1)}, u32[]{:S(2)}, u32[]{:S(2)}) collective-permute-start(f32[1,512]{1,0:T(1,128)S(1)} %get-tuple-element.69.after_ref), channel_id=1, source_target_pairs={{0,1},{1,0},{2,4},{3,5},{4,2},{5,3},{6,7},{7,6},{8,9},{9,8},{10,11... | collective-permute-start | bytes 6152 | tf_op jit(solution)/shard_map/ppermute | solution.py:559
  24.6 17.1 %collective-permute-start.15 = (f32[1,512]{1,0:T(1,128)S(1)}, f32[1,512]{1,0:T(1,128)S(1)}, u32[]{:S(2)}, u32[]{:S(2)}) collective-permute-start(f32[1,512]{1,0:T(1,128)S(1)} %get-tuple-element.69.after_ref), channel_id=1, source_target_pairs={{0,4},{1,5},{2,3},{3,2},{4,0},{5,1},{6,8},{7,9},{8,6},{9,7},{10,11... | collective-permute-start | bytes 6152 | tf_op jit(solution)/shard_map/ppermute | solution.py:559

commit v10 on v9

--- a/solution.py
+++ b/solution.py
@@ -25,10 +25,12 @@
     return block.astype(jnp.bfloat16)
 
 
-def times(matrices, *rows):
+def times(matrices, *rows, turned=False):
     block = pieces(rows)
     product = sum(
-        lax.dot_general(block, matrix, (((1,), (1,)), ((), ())), preferred_element_type=jnp.float32)
+        lax.dot_general(
+            block, matrix, (((1,), (0 if turned else 1,)), ((), ())), preferred_element_type=jnp.float32
+        )
         for matrix in matrices
     )
     found = [jnp.sum(product[3 * k : 3 * k + 3, :], axis=0, keepdims=True) for k in range(len(rows))]
@@ -231,10 +233,12 @@
     product = gain_ref[0]
     for t in range(1, gain_ref.shape[0]):
         product = sum(
-            jnp.dot(part, gain_ref[t], preferred_element_type=jnp.float32)
+            lax.dot_general(
+                gain_ref[t], part, (((0,), (0 if t > 1 else 1,)), ((), ())), preferred_element_type=jnp.float32
+            )
             for part in (halves(product) if t > 1 else [product])
         )
-    return product.astype(jnp.float32)
+    return product.astype(jnp.float32) if gain_ref.shape[0] > 1 else product.astype(jnp.float32).T
 
 
 def compose_kernel(senders, after_ref, gain_ref, composed_ref):
@@ -293,11 +297,11 @@
         own = halves(composed(gain_ref))
         near_parts_ref[0], near_parts_ref[1] = near
         pair_parts_ref[0], pair_parts_ref[1] = halves(
-            jnp.dot(own[0], near[0], preferred_element_type=jnp.float32)
-            + jnp.dot(own[0], near[1], preferred_element_type=jnp.float32)
-            + jnp.dot(own[1], near[0], preferred_element_type=jnp.float32)
+            jnp.dot(near[0], own[0], preferred_element_type=jnp.float32)
+            + jnp.dot(near[1], own[0], preferred_element_type=jnp.float32)
+            + jnp.dot(near[0], own[1], preferred_element_type=jnp.float32)
         )
-        pair_offset_ref[...] = times(own, near_offset_ref[...]) + left_ref[...]
+        pair_offset_ref[...] = times(own, near_offset_ref[...], turned=True) + left_ref[...]
 
     @pl.when(here == skip_place)
     def _():
@@ -375,7 +379,7 @@
 
 
 def parts_times(parts_ref, row_ref):
-    return times([parts_ref[0], parts_ref[1]], row_ref[...])
+    return times([parts_ref[0], parts_ref[1]], row_ref[...], turned=True)
 
 
 def first_back_kernel(
@@ -419,7 +423,7 @@
     def _():
         state = parts_times(skip_parts_ref, three_ref) + one_ref[...]
         next_ref[...] = state
-        send_ref[...] = times([pair_parts_ref[0], pair_parts_ref[1]], state) + pair_offset_ref[...]
+        send_ref[...] = times([pair_parts_ref[0], pair_parts_ref[1]], state, turned=True) + pair_offset_ref[...]
         states_ref[...] = kept_ref[...]
 
     @pl.when(here != last - 5)
@@ -466,7 +470,7 @@
 
     @pl.when(here == target)
     def _():
-        send_ref[...] = times([pair_parts_ref[0], pair_parts_ref[1]], two_ref[...]) + pair_offset_ref[...]
+        send_ref[...] = parts_times(pair_parts_ref, two_ref) + pair_offset_ref[...]
         next_ref[...] = two_ref[...]
         states_ref[...] = kept_ref[...]
 
@@ -477,7 +481,7 @@
 
     @pl.when(here == target + 2)
     def _():
-        state = times([near_parts_ref[0], near_parts_ref[1]], entry_ref[...]) + near_offset_ref[...]
+        state = parts_times(near_parts_ref, entry_ref) + near_offset_ref[...]
         smooth(state, gain_ref, offsets_ref, put)
 
     @pl.when((here == target + 1) | (here == stray))
@@ -519,7 +523,7 @@
 
     @pl.when(here == 2)
     def _():
-        state = times([near_parts_ref[0], near_parts_ref[1]], entry_ref[...]) + near_offset_ref[...]
+        state = parts_times(near_parts_ref, entry_ref) + near_offset_ref[...]
         smooth(state, gain_ref, offsets_ref, put)
 
     @pl.when((here == 1) | (here == stray))

time: 43.7 us -> 43.4 us (level)
  the two profiles are of different devices: /device:TPU:0 before, /device:TPU:10 now
where the time goes in v10:
time: 43.4 us; the launch traced here: 43.2 us
  waiting for transfers between devices  21.3 us (49%)
  starting transfers between devices  14.4 us (33%)
  Pallas kernels  6.11 us (14%)
  between operations  0.9 us (2%)
  local copies, waits for them, and re-layouts  0.47 us (1%)
    ppermute x13, waiting for transfers between devices, pass_row(): return lax.ppermute(row, ('tm', 'block'), sorted(route.items()))  12.6 us
    ppermute x13, starting transfers between devices, pass_row(): return lax.ppermute(row, ('tm', 'block'), sorted(route.items()))  10.6 us
    ppermute x1, waiting for transfers between devices, local(): lax.ppermute(compose(send, last - 1, *near_senders), 'tm', [(place, place...  7.59 us
    pallas_call x18, Pallas kernels, call(): pl.pallas_call(kernel, out_shape=[jax.ShapeDtypeStruct(shape, jnp.bfloat1...  5.07 us
    ppermute x1, starting transfers between devices, local(): lax.ppermute(compose(send, last - 1, *near_senders), 'tm', [(place, place...  1.41 us
    ppermute x1, starting transfers between devices, local(): skip = lax.ppermute(compose(send, last - 3), 'tm', [(last - 3, last - 5)])  1.28 us
    ppermute x2, waiting for transfers between devices, sensor_info(): return (mine, lax.ppermute(theirs, 'block', [(0, 1), (1, 0)]))  1.16 us
    pallas_call x2, Pallas kernels, sensor_info(): pl.pallas_call(kernel, out_shape=[jax.ShapeDtypeStruct((steps, cells), jn...  1.04 us
  transfers between devices with their start and end apart: 18, of which 10 were waited for; matrix products, arithmetic and copies ran while one was open for 0% of the time, Pallas kernels for 11%

profile of v10, /device:TPU:10, one launch (start us, length us, event | category | flops | bytes accessed | tf_op | source)
XLA Modules:
  0.0 43.2 jit_solution(8480872074825643134)
XLA Ops:
  0.8 1.2 %collective-permute-done.other_ref = f32[2,512]{1,0:T(2,128)S(1)} collective-permute-done((f32[2,512]{1,0:T(2,128)S(1)}, f32[2,512]{1,0:T(2,128)S(1)}, u32[]{:S(2)}, u32[]{:S(2)}) %collective-permute-start) | collective-permute-done | bytes 4128 | tf_op jit(solution)/shard_map/ppermute | solution.py:157
  2.0 0.2 copy-done.1
  2.2 0.1 collective-permute-start.1
  2.3 0.2 copy-done
  2.5 1.4 %collective-permute-start.11 = (f32[512,512]{1,0:T(8,128)S(1)}, f32[512,512]{1,0:T(8,128)S(1)}, u32[]{:S(2)}, u32[]{:S(2)}) collective-permute-start(f32[512,512]{1,0:T(8,128)S(1)} %compose.2), channel_id=1, source_target_pairs={{6,4},{12,10},{7,5},{13,11},{22,20},{28,26},{23,21},{29,27}} | collective-permute-start | bytes 3145736 | tf_op jit(solution)/shard_map/ppermute | solution.py:606
  4.0 1.0 %sensor_info.3 = (f32[2,512]{1,0:T(2,128)S(1)}, f32[2,512]{1,0:T(2,128)S(1)}) custom-call(f32[8,512]{1,0:T(8,128)S(1)} %get-tuple-element.41.after_ref, bf16[7,7,16]{2,1,0:T(8,128)(2,1)S(1)} %bitcast.31, s32[2,64]{1,0:T(2,128)S(1)} %copy-done.7, s32[1,2]{1,0:T(1,128)S(1)} %bitcast.33, bf16[2,1024,512]{2,1,0:T(8,128)(2,1)S(1)} %bitcast.24), custom_call_target="tpu_custom_call" | custom-call | flops 60000002048 | bytes 4096 | tf_op jit(solution)/shard_map/sensor_info/pallas_call | solution.py:147
  5.0 0.3 collective-permute-start.2
  5.3 1.3 %collective-permute-start.14 = (f32[512,512]{1,0:T(8,128)S(1)}, f32[512,512]{1,0:T(8,128)S(1)}, u32[]{:S(2)}, u32[]{:S(2)}) collective-permute-start(f32[512,512]{1,0:T(8,128)S(1)} %compose.3), channel_id=1, source_target_pairs={{8,4},{9,5},{24,20},{25,21}} | collective-permute-start | bytes 3145736 | tf_op jit(solution)/shard_map/ppermute | solution.py:609
  6.6 0.4 forward.6
  7.1 2.7 %collective-permute-start.3 = (f32[1,512]{1,0:T(1,128)S(1)}, f32[1,512]{1,0:T(1,128)S(1)}, u32[]{:S(2)}, u32[]{:S(2)}) collective-permute-start(f32[1,512]{1,0:T(1,128)S(1)} %get-tuple-element.46), channel_id=1, source_target_pairs={{0,1},{1,0},{2,4},{3,5},{4,2},{5,3},{6,7},{7,6},{8,9},{9,8},{10,11... | collective-permute-start | bytes 6152 | tf_op jit(solution)/shard_map/ppermute | solution.py:563
  9.8 0.7 %collective-permute-start.17 = (f32[520,512]{1,0:T(8,128)S(1)}, f32[520,512]{1,0:T(8,128)S(1)}, u32[]{:S(2)}, u32[]{:S(2)}) collective-permute-start(f32[520,512]{1,0:T(8,128)S(1)} %late.1), channel_id=1, source_target_pairs={{2,0},{3,1},{18,16},{19,17}} | collective-permute-start | bytes 3194888 | tf_op jit(solution)/shard_map/ppermute | solution.py:625
  10.5 1.2 %collective-permute-done.3.came_ref = f32[1,512]{1,0:T(1,128)S(1)} collective-permute-done((f32[1,512]{1,0:T(1,128)S(1)}, f32[1,512]{1,0:T(1,128)S(1)}, u32[]{:S(2)}, u32[]{:S(2)}) %collective-permute-start.3) | collective-permute-done | bytes 2080 | tf_op jit(solution)/shard_map/ppermute | solution.py:563
  11.7 0.5 %forward.7 = (f32[2,512]{1,0:T(2,128)S(1)}, f32[1,512]{1,0:T(1,128)S(1)}) custom-call(f32[1,512]{1,0:T(1,128)S(1)} %collective-permute-done.3.came_ref, bf16[2,512,512]{2,1,0:T(8,128)(2,1)S(1)} %bitcast.17, f32[2,512]{1,0:T(2,128)S(1)} %get-tuple-element.47.offsets_ref.inputs_ref, f32[2,512]{1,0:T(2,128)S(1)} %get-tuple-element.48.kept_ref.means_ref), custom_call_target="tpu_custom_call" | custom-call | flops 2500000000 | bytes 4096 | tf_op jit(solution)/shard_map/forward/pallas_call | solution.py:540
  12.2 0.9 %collective-permute-start.4 = (f32[1,512]{1,0:T(1,128)S(1)}, f32[1,512]{1,0:T(1,128)S(1)}, u32[]{:S(2)}, u32[]{:S(2)}) collective-permute-start(f32[1,512]{1,0:T(1,128)S(1)} %get-tuple-element.49), channel_id=1, source_target_pairs={{0,4},{1,5},{2,3},{3,2},{4,6},{5,7},{6,0},{7,1},{8,9},{9,8},{10,11... | collective-permute-start | bytes 6152 | tf_op jit(solution)/shard_map/ppermute | solution.py:563
  13.1 2.7 %collective-permute-done.4.came_ref = f32[1,512]{1,0:T(1,128)S(1)} collective-permute-done((f32[1,512]{1,0:T(1,128)S(1)}, f32[1,512]{1,0:T(1,128)S(1)}, u32[]{:S(2)}, u32[]{:S(2)}) %collective-permute-start.4) | collective-permute-done | bytes 2080 | tf_op jit(solution)/shard_map/ppermute | solution.py:563
  15.9 1.2 %collective-permute-done.5.came_ref = f32[1,512]{1,0:T(1,128)S(1)} collective-permute-done((f32[1,512]{1,0:T(1,128)S(1)}, f32[1,512]{1,0:T(1,128)S(1)}, u32[]{:S(2)}, u32[]{:S(2)}) %collective-permute-start.5) | collective-permute-done | bytes 2080 | tf_op jit(solution)/shard_map/ppermute | solution.py:563
  17.0 3.8 %collective-permute-start.6 = (f32[1,512]{1,0:T(1,128)S(1)}, f32[1,512]{1,0:T(1,128)S(1)}, u32[]{:S(2)}, u32[]{:S(2)}) collective-permute-start(f32[1,512]{1,0:T(1,128)S(1)} %get-tuple-element.53), channel_id=1, source_target_pairs={{0,1},{1,0},{2,3},{3,2},{4,8},{5,9},{6,7},{7,6},{8,10},{9,11},{10,... | collective-permute-start | bytes 6152 | tf_op jit(solution)/shard_map/ppermute | solution.py:563
  20.8 1.3 %collective-permute-done.6.came_ref = f32[1,512]{1,0:T(1,128)S(1)} collective-permute-done((f32[1,512]{1,0:T(1,128)S(1)}, f32[1,512]{1,0:T(1,128)S(1)}, u32[]{:S(2)}, u32[]{:S(2)}) %collective-permute-start.6) | collective-permute-done | bytes 2080 | tf_op jit(solution)/shard_map/ppermute | solution.py:563
  22.1 1.2 %collective-permute-done.7.came_ref = f32[1,512]{1,0:T(1,128)S(1)} collective-permute-done((f32[1,512]{1,0:T(1,128)S(1)}, f32[1,512]{1,0:T(1,128)S(1)}, u32[]{:S(2)}, u32[]{:S(2)}) %collective-permute-start.7) | collective-permute-done | bytes 2080 | tf_op jit(solution)/shard_map/ppermute | solution.py:563
  23.2 0.2 collective-permute-start.8
  23.4 0.7 %offsets.1 = (f32[2,512]{1,0:T(2,128)S(1)}, f32[1,512]{1,0:T(1,128)S(1)}, bf16[2,512,512]{2,1,0:T(8,128)(2,1)S(1)}) custom-call(f32[2,512]{1,0:T(2,128)S(1)} %get-tuple-element.58.kept_ref.means_ref, bf16[2,512,512]{2,1,0:T(8,128)(2,1)S(1)} %bitcast.10, bf16[512,512]{1,0:T(8,128)(2,1)S(1)} %bitcast.26), custom_call_target="tpu_custom_call" | custom-call | flops 1000000000 | bytes 4096 | tf_op jit(solution)/shard_map/offsets/pallas_call | solution.py:540
  24.1 0.1 collective-permute-start.10
  24.2 0.2 collective-permute-done.8.came_ref
  24.4 0.2 collective-permute-start.9
  24.6 7.6 %collective-permute-done.11.matrix_ref.near_ref = f32[512,512]{1,0:T(8,128)S(1)} collective-permute-done((f32[512,512]{1,0:T(8,128)S(1)}, f32[512,512]{1,0:T(8,128)S(1)}, u32[]{:S(2)}, u32[]{:S(2)}) %collective-permute-start.11) | collective-permute-done | bytes 1048608 | tf_op jit(solution)/shard_map/ppermute | solution.py:606
  32.3 2.4 %collective-permute-start.12 = (f32[1,512]{1,0:T(1,128)S(1)}, f32[1,512]{1,0:T(1,128)S(1)}, u32[]{:S(2)}, u32[]{:S(2)}) collective-permute-start(f32[1,512]{1,0:T(1,128)S(1)} %get-tuple-element.62.came_ref), channel_id=1, source_target_pairs={{0,1},{1,0},{2,3},{3,2},{4,10},{5,11},{6,7},{7,6},{8,9},{9,8},{10,... | collective-permute-start | bytes 6152 | tf_op jit(solution)/shard_map/ppermute | solution.py:563
  34.7 1.7 %pair.1 = (bf16[2,512,512]{2,1,0:T(8,128)(2,1)S(1)}, bf16[2,512,512]{2,1,0:T(8,128)(2,1)S(1)}, f32[1,512]{1,0:T(1,128)S(1)}, bf16[2,512,512]{2,1,0:T(8,128)(2,1)S(1)}) custom-call(f32[512,512]{1,0:T(8,128)S(1)} %collective-permute-done.11.matrix_ref.near_ref, f32[512,512]{1,0:T(8,128)S(1)} %collective-permute-done.14.skip_ref, ...), custom_call_target="tpu_custom_call" | custom-call | flops 50000000 | bytes 4096 | tf_op jit(solution)/shard_map/pair/pallas_call | solution.py:540
  36.4 0.4 collective-permute-done.12.three_ref
  36.8 0.5 %second_back.1 = (f32[2,512]{1,0:T(2,128)S(1)}, f32[1,512]{1,0:T(1,128)S(1)}, f32[1,512]{1,0:T(1,128)S(1)}) custom-call(f32[1,512]{1,0:T(1,128)S(1)} %collective-permute-done.12.three_ref, f32[1,512]{1,0:T(1,128)S(1)} %collective-permute-done.13.one_ref, f32[1,512]{1,0:T(1,128)S(1)} %get-tuple-element.63.entry_ref, ...), custom_call_target="tpu_custom_call" | custom-call | flops 500000000 | bytes 4096 | tf_op jit(solution)/shard_map/second_back/pallas_call | solution.py:540
  37.4 0.1 collective-permute-start.16
  37.6 4.4 %collective-permute-done.16.one_ref = f32[1,512]{1,0:T(1,128)S(1)} collective-permute-done((f32[1,512]{1,0:T(1,128)S(1)}, f32[1,512]{1,0:T(1,128)S(1)}, u32[]{:S(2)}, u32[]{:S(2)}) %collective-permute-start.16) | collective-permute-done | bytes 2080 | tf_op jit(solution)/shard_map/ppermute | solution.py:563
  41.9 1.3 %final.1 = (f32[2,1,512]{2,1,0:T(1,128)}, f32[2,1,512]{2,1,0:T(1,128)}) custom-call(f32[1,512]{1,0:T(1,128)S(1)} %collective-permute-done.15.two_ref, f32[1,512]{1,0:T(1,128)S(1)} %collective-permute-done.16.one_ref, f32[1,512]{1,0:T(1,128)S(1)} %get-tuple-element.70.entry_ref, f32[1,512]{1,0:T(1,128)S(1)} %collective-permute-done.10.far_offset_ref.near_offset_ref, ...), custom_call_target="tpu_custom_call" | custom-call | flops 1000000000 | bytes 4096 | tf_op jit(solution)/shard_map/final/pallas_call | solution.py:540
  (42 shorter events, 0.4 us)
Async XLA Ops:
  0.6 1.3 %copy-start.6 = (f32[1,512]{1,0:T(1,128)S(1)}, f32[1,512]{1,0:T(1,128)}, u32[]{:S(2)}) copy-start(f32[1,512]{1,0:T(1,128)} %start_ref.1) | copy-start | bytes 6148
  0.6 1.3 %copy-start.4 = (bf16[2,1,512,512]{3,2,1,0:T(8,128)(2,1)S(1)}, bf16[2,1,512,512]{3,2,1,0:T(8,128)(2,1)}, u32[]{:S(2)}) copy-start(bf16[2,1,512,512]{3,2,1,0:T(8,128)(2,1)} %param.14) | copy-start | bytes 3145732
  0.7 1.5 %copy-start.1 = (bf16[2,1,512,512]{3,2,1,0:T(8,128)(2,1)S(1)}, bf16[2,1,512,512]{3,2,1,0:T(8,128)(2,1)}, u32[]{:S(2)}) copy-start(bf16[2,1,512,512]{3,2,1,0:T(8,128)(2,1)} %param.13) | copy-start | bytes 3145732
  0.7 1.8 %copy-start = (bf16[2,1,512,512]{3,2,1,0:T(8,128)(2,1)S(1)}, bf16[2,1,512,512]{3,2,1,0:T(8,128)(2,1)}, u32[]{:S(2)}) copy-start(bf16[2,1,512,512]{3,2,1,0:T(8,128)(2,1)} %param.15) | copy-start | bytes 3145732
  0.7 1.2 %collective-permute-start = (f32[2,512]{1,0:T(2,128)S(1)}, f32[2,512]{1,0:T(2,128)S(1)}, u32[]{:S(2)}, u32[]{:S(2)}) collective-permute-start(f32[2,512]{1,0:T(2,128)S(1)} %get-tuple-element.40), channel_id=1, source_target_pairs={{0,1},{1,0},{2,3},{3,2},{4,5},{5,4},{6,7},{7,6},{8,9},{9,8},{10,11... | collective-permute-start | bytes 12296 | tf_op jit(solution)/shard_map/ppermute | solution.py:157
  2.2 1.8 %copy-start.2 = (bf16[2,64,16,512]{3,2,1,0:T(8,128)(2,1)S(1)}, bf16[2,64,16,512]{3,2,1,0:T(8,128)(2,1)}, u32[]{:S(2)}) copy-start(bf16[2,64,16,512]{3,2,1,0:T(8,128)(2,1)} %param.9) | copy-start | bytes 6291460
  2.2 1.8 %copy-start.5 = (bf16[16,7,7]{0,2,1:T(8,128)(2,1)S(1)}, bf16[16,7,7]{0,2,1:T(8,128)(2,1)}, u32[]{:S(2)}) copy-start(bf16[16,7,7]{0,2,1:T(8,128)(2,1)} %param.10) | copy-start | bytes 4708
  2.2 1.8 %copy-start.7 = (s32[2,64]{1,0:T(2,128)S(1)}, s32[2,64]{1,0:T(2,128)}, u32[]{:S(2)}) copy-start(s32[2,64]{1,0:T(2,128)} %refs_1_.1) | copy-start | bytes 1540
  2.2 1.8 %copy-start.8 = (s32[2,1]{0,1:T(1,128)S(1)}, s32[2,1]{0,1:T(1,128)}, u32[]{:S(2)}) copy-start(s32[2,1]{0,1:T(1,128)} %param.12) | copy-start | bytes 28
  2.2 4.4 %collective-permute-start.1 = (f32[8,512]{1,0:T(8,128)S(1)}, f32[8,512]{1,0:T(8,128)S(1)}, u32[]{:S(2)}, u32[]{:S(2)}) collective-permute-start(f32[8,512]{1,0:T(8,128)S(1)} %get-tuple-element.41.after_ref), channel_id=1, source_target_pairs={{0,2},{1,3},{2,6},{3,7},{4,5},{5,4},{6,0},{7,1},{8,9},{9,8},{10,11... | collective-permute-start | bytes 49160 | tf_op jit(solution)/shard_map/ppermute | solution.py:563
  2.5 29.7 %collective-permute-start.11 = (f32[512,512]{1,0:T(8,128)S(1)}, f32[512,512]{1,0:T(8,128)S(1)}, u32[]{:S(2)}, u32[]{:S(2)}) collective-permute-start(f32[512,512]{1,0:T(8,128)S(1)} %compose.2), channel_id=1, source_target_pairs={{6,4},{12,10},{7,5},{13,11},{22,20},{28,26},{23,21},{29,27}} | collective-permute-start | bytes 3145736 | tf_op jit(solution)/shard_map/ppermute | solution.py:606
  5.0 1.6 %collective-permute-start.2 = (f32[2,512]{1,0:T(2,128)S(1)}, f32[2,512]{1,0:T(2,128)S(1)}, u32[]{:S(2)}, u32[]{:S(2)}) collective-permute-start(f32[2,512]{1,0:T(2,128)S(1)} %get-tuple-element.43), channel_id=1, source_target_pairs={{0,1},{1,0},{2,3},{3,2},{4,5},{5,4},{6,7},{7,6},{8,9},{9,8},{10,11... | collective-permute-start | bytes 12296 | tf_op jit(solution)/shard_map/ppermute | solution.py:157
  5.3 29.4 %collective-permute-start.14 = (f32[512,512]{1,0:T(8,128)S(1)}, f32[512,512]{1,0:T(8,128)S(1)}, u32[]{:S(2)}, u32[]{:S(2)}) collective-permute-start(f32[512,512]{1,0:T(8,128)S(1)} %compose.3), channel_id=1, source_target_pairs={{8,4},{9,5},{24,20},{25,21}} | collective-permute-start | bytes 3145736 | tf_op jit(solution)/shard_map/ppermute | solution.py:609
  6.6 3.2 %copy-start.3 = (bf16[1,512,512]{2,1,0:T(8,128)(2,1)S(1)}, bf16[1,512,512]{2,1,0:T(8,128)(2,1)}, u32[]{:S(2)}) copy-start(bf16[1,512,512]{2,1,0:T(8,128)(2,1)} %param.16) | copy-start | bytes 1572868
  7.1 4.7 %collective-permute-start.3 = (f32[1,512]{1,0:T(1,128)S(1)}, f32[1,512]{1,0:T(1,128)S(1)}, u32[]{:S(2)}, u32[]{:S(2)}) collective-permute-start(f32[1,512]{1,0:T(1,128)S(1)} %get-tuple-element.46), channel_id=1, source_target_pairs={{0,1},{1,0},{2,4},{3,5},{4,2},{5,3},{6,7},{7,6},{8,9},{9,8},{10,11... | collective-permute-start | bytes 6152 | tf_op jit(solution)/shard_map/ppermute | solution.py:563
  9.8 27.7 %collective-permute-start.17 = (f32[520,512]{1,0:T(8,128)S(1)}, f32[520,512]{1,0:T(8,128)S(1)}, u32[]{:S(2)}, u32[]{:S(2)}) collective-permute-start(f32[520,512]{1,0:T(8,128)S(1)} %late.1), channel_id=1, source_target_pairs={{2,0},{3,1},{18,16},{19,17}} | collective-permute-start | bytes 3194888 | tf_op jit(solution)/shard_map/ppermute | solution.py:625
  12.2 3.7 %collective-permute-start.4 = (f32[1,512]{1,0:T(1,128)S(1)}, f32[1,512]{1,0:T(1,128)S(1)}, u32[]{:S(2)}, u32[]{:S(2)}) collective-permute-start(f32[1,512]{1,0:T(1,128)S(1)} %get-tuple-element.49), channel_id=1, source_target_pairs={{0,4},{1,5},{2,3},{3,2},{4,6},{5,7},{6,0},{7,1},{8,9},{9,8},{10,11... | collective-permute-start | bytes 6152 | tf_op jit(solution)/shard_map/ppermute | solution.py:563
  15.9 1.2 %collective-permute-start.5 = (f32[1,512]{1,0:T(1,128)S(1)}, f32[1,512]{1,0:T(1,128)S(1)}, u32[]{:S(2)}, u32[]{:S(2)}) collective-permute-start(f32[1,512]{1,0:T(1,128)S(1)} %get-tuple-element.51), channel_id=1, source_target_pairs={{0,1},{1,0},{2,3},{3,2},{4,5},{5,4},{6,8},{7,9},{8,10},{9,11},{10,... | collective-permute-start | bytes 6152 | tf_op jit(solution)/shard_map/ppermute | solution.py:563
  17.0 5.1 %collective-permute-start.6 = (f32[1,512]{1,0:T(1,128)S(1)}, f32[1,512]{1,0:T(1,128)S(1)}, u32[]{:S(2)}, u32[]{:S(2)}) collective-permute-start(f32[1,512]{1,0:T(1,128)S(1)} %get-tuple-element.53), channel_id=1, source_target_pairs={{0,1},{1,0},{2,3},{3,2},{4,8},{5,9},{6,7},{7,6},{8,10},{9,11},{10,... | collective-permute-start | bytes 6152 | tf_op jit(solution)/shard_map/ppermute | solution.py:563
  22.1 1.2 %collective-permute-start.7 = (f32[1,512]{1,0:T(1,128)S(1)}, f32[1,512]{1,0:T(1,128)S(1)}, u32[]{:S(2)}, u32[]{:S(2)}) collective-permute-start(f32[1,512]{1,0:T(1,128)S(1)} %get-tuple-element.55), channel_id=1, source_target_pairs={{0,1},{1,0},{2,3},{3,2},{4,5},{5,4},{6,7},{7,6},{8,9},{9,8},{10,12... | collective-permute-start | bytes 6152 | tf_op jit(solution)/shard_map/ppermute | solution.py:563
  23.2 1.2 %collective-permute-start.8 = (f32[1,512]{1,0:T(1,128)S(1)}, f32[1,512]{1,0:T(1,128)S(1)}, u32[]{:S(2)}, u32[]{:S(2)}) collective-permute-start(f32[1,512]{1,0:T(1,128)S(1)} %get-tuple-element.57), channel_id=1, source_target_pairs={{0,1},{1,0},{2,3},{3,2},{4,5},{5,4},{6,7},{7,6},{8,9},{9,8},{10,11... | collective-permute-start | bytes 6152 | tf_op jit(solution)/shard_map/ppermute | solution.py:563
  24.1 8.1 %collective-permute-start.10 = (f32[1,512]{1,0:T(1,128)S(1)}, f32[1,512]{1,0:T(1,128)S(1)}, u32[]{:S(2)}, u32[]{:S(2)}) collective-permute-start(f32[1,512]{1,0:T(1,128)S(1)} %get-tuple-element.60.left_ref), channel_id=1, source_target_pairs={{0,1},{1,0},{2,3},{3,2},{4,6},{5,7},{6,4},{7,5},{8,9},{9,8},{10,12... | collective-permute-start | bytes 6152 | tf_op jit(solution)/shard_map/ppermute | solution.py:563
  24.4 7.8 %collective-permute-start.9 = (f32[1,512]{1,0:T(1,128)S(1)}, f32[1,512]{1,0:T(1,128)S(1)}, u32[]{:S(2)}, u32[]{:S(2)}) collective-permute-start(f32[1,512]{1,0:T(1,128)S(1)} %get-tuple-element.59.came_ref), channel_id=1, source_target_pairs={{0,1},{1,0},{2,3},{3,2},{4,5},{5,4},{6,7},{7,6},{8,9},{9,8},{10,14... | collective-permute-start | bytes 6152 | tf_op jit(solution)/shard_map/ppermute | solution.py:563
  32.2 4.2 %collective-permute-start.13 = (f32[1,512]{1,0:T(1,128)S(1)}, f32[1,512]{1,0:T(1,128)S(1)}, u32[]{:S(2)}, u32[]{:S(2)}) collective-permute-start(f32[1,512]{1,0:T(1,128)S(1)} %get-tuple-element.62.came_ref), channel_id=1, source_target_pairs={{0,1},{1,0},{2,3},{3,2},{4,6},{5,7},{6,10},{7,11},{8,4},{9,5},{10,... | collective-permute-start | bytes 6152 | tf_op jit(solution)/shard_map/ppermute | solution.py:563
  32.3 4.5 %collective-permute-start.12 = (f32[1,512]{1,0:T(1,128)S(1)}, f32[1,512]{1,0:T(1,128)S(1)}, u32[]{:S(2)}, u32[]{:S(2)}) collective-permute-start(f32[1,512]{1,0:T(1,128)S(1)} %get-tuple-element.62.came_ref), channel_id=1, source_target_pairs={{0,1},{1,0},{2,3},{3,2},{4,10},{5,11},{6,7},{7,6},{8,9},{9,8},{10,... | collective-permute-start | bytes 6152 | tf_op jit(solution)/shard_map/ppermute | solution.py:563
  37.4 4.5 %collective-permute-start.16 = (f32[1,512]{1,0:T(1,128)S(1)}, f32[1,512]{1,0:T(1,128)S(1)}, u32[]{:S(2)}, u32[]{:S(2)}) collective-permute-start(f32[1,512]{1,0:T(1,128)S(1)} %get-tuple-element.69.after_ref), channel_id=1, source_target_pairs={{0,1},{1,0},{2,4},{3,5},{4,2},{5,3},{6,7},{7,6},{8,9},{9,8},{10,11... | collective-permute-start | bytes 6152 | tf_op jit(solution)/shard_map/ppermute | solution.py:563
  37.4 4.5 %collective-permute-start.15 = (f32[1,512]{1,0:T(1,128)S(1)}, f32[1,512]{1,0:T(1,128)S(1)}, u32[]{:S(2)}, u32[]{:S(2)}) collective-permute-start(f32[1,512]{1,0:T(1,128)S(1)} %get-tuple-element.69.after_ref), channel_id=1, source_target_pairs={{0,4},{1,5},{2,3},{3,2},{4,0},{5,1},{6,8},{7,9},{8,6},{9,7},{10,11... | collective-permute-start | bytes 6152 | tf_op jit(solution)/shard_map/ppermute | solution.py:563

commit v11 on v10

--- a/solution.py
+++ b/solution.py
@@ -207,14 +207,14 @@
         send_ref[...] = came_ref[0:1, :]
 
 
-def hop_kernel(turn, came_ref, matrices_ref, offsets_ref, kept_ref, states_ref, send_ref):
+def hop_kernel(turn, turned, came_ref, matrices_ref, offsets_ref, kept_ref, states_ref, send_ref):
     here = lax.axis_index("tm") == turn
 
     @pl.when(here)
     def _():
         state = came_ref[...]
         for t in range(matrices_ref.shape[0]):
-            state = times([matrices_ref[t]], state) + offsets_ref[t : t + 1, :]
+            state = times([matrices_ref[t]], state, turned=turned) + offsets_ref[t : t + 1, :]
             states_ref[t : t + 1, :] = state
         send_ref[...] = state
 
@@ -251,16 +251,20 @@
         composed_ref[...] = composed(gain_ref)
 
 
-def late_kernel(senders, means_ref, gain_ref, propagator_ref, composed_ref):
+def late_kernel(place, means_ref, gain_ref, propagator_ref, operator_ref, composed_ref, turned_ref):
     size = gain_ref.shape[1]
     here = lax.axis_index("tm")
-    sends = functools.reduce(jnp.logical_or, [here == place for place in senders])
-
-    @pl.when(sends)
+
+    @pl.when(here == place)
     def _():
         composed_ref[:size, :] = composed(gain_ref)
         composed_ref[size:, :] = jnp.zeros((composed_ref.shape[0] - size, size), jnp.float32)
         composed_ref[size : size + 1, :] = offsets(means_ref, gain_ref, propagator_ref)[0]
+
+    @pl.when(here > place + 1)
+    def _():
+        for t in range(operator_ref.shape[0]):
+            turned_ref[t] = operator_ref[t].T
 
 
 def offsets(means_ref, gain_ref, propagator_ref):
@@ -281,7 +285,7 @@
     skip_place,
     near_ref,
     skip_ref,
-    gain_ref,
+    own_parts_ref,
     left_ref,
     near_offset_ref,
     near_parts_ref,
@@ -294,7 +298,7 @@
     @pl.when(functools.reduce(jnp.logical_or, [here == place for place in places]))
     def _():
         near = halves(near_ref[...])
-        own = halves(composed(gain_ref))
+        own = [own_parts_ref[0], own_parts_ref[1]]
         near_parts_ref[0], near_parts_ref[1] = near
         pair_parts_ref[0], pair_parts_ref[1] = halves(
             jnp.dot(near[0], own[0], preferred_element_type=jnp.float32)
@@ -308,15 +312,30 @@
         skip_parts_ref[0], skip_parts_ref[1] = halves(skip_ref[...])
 
 
-def late_split_kernel(place, late_ref, after_ref, parts_ref, offset_ref):
+def beside_kernel(
+    late_ref, after_ref, entry_ref, near_parts_ref, near_offset_ref, gain_ref, offsets_ref, kept_ref,
+    parts_ref, offset_ref, states_ref,
+):
     del after_ref
     size = late_ref.shape[1]
-
-    @pl.when(lax.axis_index("tm") == place)
+    here = lax.axis_index("tm")
+
+    @pl.when(here == 0)
     def _():
         parts_ref[0], parts_ref[1] = halves(late_ref[:size, :])
         offset_ref[...] = late_ref[size : size + 1, :]
 
+    @pl.when(here != 2)
+    def _():
+        states_ref[...] = kept_ref[...]
+
+    @pl.when(here == 2)
+    def _():
+        def put(t, state):
+            states_ref[t : t + 1, :] = state
+
+        smooth(parts_times(near_parts_ref, entry_ref) + near_offset_ref[...], gain_ref, offsets_ref, put)
+
 
 def split_kernel(place, matrix_ref, parts_ref):
     @pl.when(lax.axis_index("tm") == place)
@@ -327,12 +346,9 @@
 def offsets_kernel(last, means_ref, gain_ref, propagator_ref, offsets_ref, send_ref, own_parts_ref):
     here = lax.axis_index("tm") == last
 
-    @pl.when(lax.axis_index("tm") == last - 2)
+    @pl.when(jnp.logical_not(here))
     def _():
         own_parts_ref[0], own_parts_ref[1] = halves(composed(gain_ref))
-
-    @pl.when(jnp.logical_not(here))
-    def _():
         send_ref[...], found = offsets(means_ref, gain_ref, propagator_ref)
         for t, row in enumerate(found):
             offsets_ref[t : t + 1, :] = row
@@ -344,16 +360,16 @@
 
 
 def last_kernel(
-    last, came_ref, operator_ref, inputs_ref, kept_ref, gain_ref, propagator_ref,
+    last, came_ref, turned_ref, inputs_ref, kept_ref, gain_ref, propagator_ref,
     means_ref, states_ref, send_ref,
 ):
     @pl.when(lax.axis_index("tm") == last)
     def _():
-        steps = operator_ref.shape[0]
+        steps = turned_ref.shape[0]
         state = came_ref[...]
         means, moved = [], []
         for t in range(steps):
-            state = times([operator_ref[t]], state) + inputs_ref[t : t + 1, :]
+            state = times([turned_ref[t]], state, turned=True) + inputs_ref[t : t + 1, :]
             means_ref[t : t + 1, :] = state
             means.append(state)
             if t < steps - 1:
@@ -372,8 +388,8 @@
         send_ref[...] = came_ref[...]
 
 
-def smooth(state, gain_ref, offsets_ref, put):
-    for t in reversed(range(gain_ref.shape[0])):
+def smooth(state, gain_ref, offsets_ref, put, first=0):
+    for t in reversed(range(first, gain_ref.shape[0])):
         state = times([gain_ref[t]], state) + offsets_ref[t : t + 1, :]
         put(t, state)
 
@@ -498,11 +514,10 @@
     stray,
     two_ref,
     one_ref,
-    entry_ref,
-    near_offset_ref,
-    near_parts_ref,
+    late_parts_ref,
     late_offset_ref,
-    late_parts_ref,
+    own_parts_ref,
+    left_ref,
     gain_ref,
     offsets_ref,
     kept_ref,
@@ -519,18 +534,15 @@
 
     @pl.when(here == 0)
     def _():
-        smooth(parts_times(late_parts_ref, two_ref) + late_offset_ref[...], gain_ref, offsets_ref, put)
-
-    @pl.when(here == 2)
-    def _():
-        state = parts_times(near_parts_ref, entry_ref) + near_offset_ref[...]
-        smooth(state, gain_ref, offsets_ref, put)
+        state = parts_times(late_parts_ref, two_ref) + late_offset_ref[...]
+        smooth(state, gain_ref, offsets_ref, put, 1)
+        put(0, times([own_parts_ref[0], own_parts_ref[1]], state, turned=True) + left_ref[...])
 
     @pl.when((here == 1) | (here == stray))
     def _():
         smooth(jnp.where(here == stray, two_ref[...], one_ref[...]), gain_ref, offsets_ref, put)
 
-    @pl.when((here > 2) & (here != stray))
+    @pl.when((here > 1) & (here != stray))
     def _():
         for t in range(kept_ref.shape[0]):
             states_ref[t] = kept_ref[t : t + 1, :]
@@ -618,14 +630,20 @@
             continue
         came = pass_row(send, [ring_up(place - 1, places)], places)
         if place == 2:
-            late = call(
-                functools.partial(late_kernel, (1,)), "late", ((size + 8, size),), means, gain, matrix,
-                cost=0.5,
-            )[0]
+            late, turned = call(
+                functools.partial(late_kernel, 1), "late", ((size + 8, size), (steps, size, size)),
+                means, gain, matrix, operator, cost=0.5,
+            )
             late = lax.ppermute(late, "tm", [(1, 0)])
         if place < last:
             means, send = call(
-                functools.partial(hop_kernel, place), "forward", (many, one), came, operator, inputs, means,
+                functools.partial(hop_kernel, place, place > 2),
+                "forward",
+                (many, one),
+                came,
+                turned if place > 2 else operator,
+                inputs,
+                means,
                 cost=COSTS[2] if place == 2 else 0.5,
             )
     offset_rows, left, own_parts = call(
@@ -637,7 +655,7 @@
         "last",
         (many, many, one),
         came,
-        operator,
+        turned,
         inputs,
         means,
         gain,
@@ -660,7 +678,7 @@
         (parts, parts, one, parts),
         first,
         skip,
-        gain,
+        own_parts,
         left,
         first_offset,
         cost=0.05,
@@ -693,12 +711,13 @@
                 send,
             )
         else:
-            late_parts, late_offset = call(
-                functools.partial(late_split_kernel, 0), "late_split", (parts, one), late, send, cost=0.05
+            late_parts, late_offset, states = call(
+                beside_kernel, "beside", (parts, one, many),
+                late, send, entry, near_parts, first_offset, gain, offset_rows, states, cost=0.05,
             )
             means, states = call(
                 functools.partial(final_kernel, stray), "final", (result, result),
-                two, one_up, entry, first_offset, near_parts, late_offset, late_parts, gain, offset_rows, states, means,
+                two, one_up, late_parts, late_offset, own_parts, left, gain, offset_rows, states, means,
             )
         stray = -1
     return means, states

time: 43.4 us -> 42.7 us (0.984)
  the two profiles are of different devices: /device:TPU:10 before, /device:TPU:0 now
where the time goes in v11:
time: 42.7 us; the launch traced here: 42.3 us
  starting transfers between devices  23.4 us (55%)
  waiting for transfers between devices  10.9 us (26%)
  Pallas kernels  5.57 us (13%)
  local copies, waits for them, and re-layouts  1.62 us (4%)
  between operations  0.84 us (2%)
    ppermute x13, starting transfers between devices, pass_row(): return lax.ppermute(row, ('tm', 'block'), sorted(route.items()))  19.6 us
    ppermute x13, waiting for transfers between devices, pass_row(): return lax.ppermute(row, ('tm', 'block'), sorted(route.items()))  9.93 us
    pallas_call x18, Pallas kernels, call(): pl.pallas_call(kernel, out_shape=[jax.ShapeDtypeStruct(shape, jnp.bfloat1...  3.07 us
    pallas_call x2, Pallas kernels, sensor_info(): pl.pallas_call(kernel, out_shape=[jax.ShapeDtypeStruct((steps, cells), jn...  2.5 us
    unnamed x18, local copies, waits for them, and re-layouts  1.62 us
    ppermute x1, starting transfers between devices, local(): late = lax.ppermute(late, 'tm', [(1, 0)])  1.28 us
    ppermute x2, starting transfers between devices, sensor_info(): return (mine, lax.ppermute(theirs, 'block', [(0, 1), (1, 0)]))  0.94 us
    ppermute x2, waiting for transfers between devices, sensor_info(): return (mine, lax.ppermute(theirs, 'block', [(0, 1), (1, 0)]))  0.92 us
  transfers between devices with their start and end apart: 18, of which 12 were waited for; matrix products, arithmetic and copies ran while one was open for 0% of the time, Pallas kernels for 3%

profile of v11, /device:TPU:0, one launch (start us, length us, event | category | flops | bytes accessed | tf_op | source)
XLA Modules:
  0.0 42.3 jit_solution(17497888382350716105)
XLA Ops:
  0.7 2.5 %sensor_info.2 = (f32[2,512]{1,0:T(2,128)S(1)}, f32[2,512]{1,0:T(2,128)S(1)}) custom-call(bf16[7,7,16]{2,1,0:T(8,128)(2,1)} %bitcast.26, s32[2,64]{1,0:T(2,128)} %refs_1_.1, s32[1,2]{1,0:T(1,128)} %bitcast.28, bf16[2,1024,512]{2,1,0:T(8,128)(2,1)} %bitcast.19), custom_call_target="tpu_custom_call" | custom-call | flops 1000000 | bytes 4096 | tf_op jit(solution)/shard_map/sensor_info/pallas_call | solution.py:147
  3.2 0.5 %collective-permute-start = (f32[2,512]{1,0:T(2,128)S(1)}, f32[2,512]{1,0:T(2,128)S(1)}, u32[]{:S(2)}, u32[]{:S(2)}) collective-permute-start(f32[2,512]{1,0:T(2,128)S(1)} %get-tuple-element.43), channel_id=1, source_target_pairs={{0,1},{1,0},{2,3},{3,2},{4,5},{5,4},{6,7},{7,6},{8,9},{9,8},{10,11... | collective-permute-start | bytes 12296 | tf_op jit(solution)/shard_map/ppermute | solution.py:157
  3.7 0.8 %collective-permute-done.other_ref = f32[2,512]{1,0:T(2,128)S(1)} collective-permute-done((f32[2,512]{1,0:T(2,128)S(1)}, f32[2,512]{1,0:T(2,128)S(1)}, u32[]{:S(2)}, u32[]{:S(2)}) %collective-permute-start) | collective-permute-done | bytes 4128 | tf_op jit(solution)/shard_map/ppermute | solution.py:157
  4.5 0.7 %start.1 = (f32[2,512]{1,0:T(2,128)S(1)}, f32[2,512]{1,0:T(2,128)S(1)}, f32[8,512]{1,0:T(8,128)S(1)}) custom-call(f32[2,512]{1,0:T(2,128)S(1)} %get-tuple-element.42.mine_ref, f32[2,512]{1,0:T(2,128)S(1)} %collective-permute-done.other_ref, bf16[2,512,512]{2,1,0:T(8,128)(2,1)S(1)} %bitcast.24, bf16[2,512,512]{2,1,0:T(8,128)(2,1)S(1)} %bitcast.15, ...), custom_call_target="tpu_custom_call" | custom-call | flops 500000000 | bytes 4096 | tf_op jit(solution)/shard_map/start/pallas_call | solution.py:552
  5.4 0.9 %collective-permute-start.11 = (f32[512,512]{1,0:T(8,128)S(1)}, f32[512,512]{1,0:T(8,128)S(1)}, u32[]{:S(2)}, u32[]{:S(2)}) collective-permute-start(f32[512,512]{1,0:T(8,128)S(1)} %compose.2), channel_id=1, source_target_pairs={{6,4},{12,10},{7,5},{13,11},{22,20},{28,26},{23,21},{29,27}} | collective-permute-start | bytes 3145736 | tf_op jit(solution)/shard_map/ppermute | solution.py:618
  6.2 0.6 %copy-done.2 = bf16[2,64,16,512]{3,2,1,0:T(8,128)(2,1)S(1)} copy-done((bf16[2,64,16,512]{3,2,1,0:T(8,128)(2,1)S(1)}, bf16[2,64,16,512]{3,2,1,0:T(8,128)(2,1)}, u32[]{:S(2)}) %copy-start.2) | copy-done | bytes 2097176
  6.8 0.4 collective-permute-start.2
  7.2 0.7 %collective-permute-start.14 = (f32[512,512]{1,0:T(8,128)S(1)}, f32[512,512]{1,0:T(8,128)S(1)}, u32[]{:S(2)}, u32[]{:S(2)}) collective-permute-start(f32[512,512]{1,0:T(8,128)S(1)} %compose.3), channel_id=1, source_target_pairs={{8,4},{9,5},{24,20},{25,21}} | collective-permute-start | bytes 3145736 | tf_op jit(solution)/shard_map/ppermute | solution.py:621
  8.1 1.9 %collective-permute-done.1.came_ref = f32[8,512]{1,0:T(8,128)S(1)} collective-permute-done((f32[8,512]{1,0:T(8,128)S(1)}, f32[8,512]{1,0:T(8,128)S(1)}, u32[]{:S(2)}, u32[]{:S(2)}) %collective-permute-start.1) | collective-permute-done | bytes 16416 | tf_op jit(solution)/shard_map/ppermute | solution.py:575
  10.0 1.0 %copy-done.3 = bf16[1,512,512]{2,1,0:T(8,128)(2,1)S(1)} copy-done((bf16[1,512,512]{2,1,0:T(8,128)(2,1)S(1)}, bf16[1,512,512]{2,1,0:T(8,128)(2,1)}, u32[]{:S(2)}) %copy-start.3) | copy-done | bytes 524312
  11.0 1.3 %collective-permute-start.17 = (f32[520,512]{1,0:T(8,128)S(1)}, f32[520,512]{1,0:T(8,128)S(1)}, u32[]{:S(2)}, u32[]{:S(2)}) collective-permute-start(f32[520,512]{1,0:T(8,128)S(1)} %get-tuple-element.74), channel_id=1, source_target_pairs={{2,0},{3,1},{18,16},{19,17}} | collective-permute-start | bytes 3194888 | tf_op jit(solution)/shard_map/ppermute | solution.py:637
  12.3 2.9 %collective-permute-start.4 = (f32[1,512]{1,0:T(1,128)S(1)}, f32[1,512]{1,0:T(1,128)S(1)}, u32[]{:S(2)}, u32[]{:S(2)}) collective-permute-start(f32[1,512]{1,0:T(1,128)S(1)} %get-tuple-element.52), channel_id=1, source_target_pairs={{0,4},{1,5},{2,3},{3,2},{4,6},{5,7},{6,0},{7,1},{8,9},{9,8},{10,11... | collective-permute-start | bytes 6152 | tf_op jit(solution)/shard_map/ppermute | solution.py:575
  15.3 1.7 %collective-permute-done.4.came_ref = f32[1,512]{1,0:T(1,128)S(1)} collective-permute-done((f32[1,512]{1,0:T(1,128)S(1)}, f32[1,512]{1,0:T(1,128)S(1)}, u32[]{:S(2)}, u32[]{:S(2)}) %collective-permute-start.4) | collective-permute-done | bytes 2080 | tf_op jit(solution)/shard_map/ppermute | solution.py:575
  17.0 1.2 %collective-permute-done.5.came_ref = f32[1,512]{1,0:T(1,128)S(1)} collective-permute-done((f32[1,512]{1,0:T(1,128)S(1)}, f32[1,512]{1,0:T(1,128)S(1)}, u32[]{:S(2)}, u32[]{:S(2)}) %collective-permute-start.5) | collective-permute-done | bytes 2080 | tf_op jit(solution)/shard_map/ppermute | solution.py:575
  18.2 0.2 collective-permute-start.6
  18.3 1.0 %collective-permute-done.6.came_ref = f32[1,512]{1,0:T(1,128)S(1)} collective-permute-done((f32[1,512]{1,0:T(1,128)S(1)}, f32[1,512]{1,0:T(1,128)S(1)}, u32[]{:S(2)}, u32[]{:S(2)}) %collective-permute-start.6) | collective-permute-done | bytes 2080 | tf_op jit(solution)/shard_map/ppermute | solution.py:575
  19.3 0.2 collective-permute-start.7
  19.5 1.0 %collective-permute-done.7.came_ref = f32[1,512]{1,0:T(1,128)S(1)} collective-permute-done((f32[1,512]{1,0:T(1,128)S(1)}, f32[1,512]{1,0:T(1,128)S(1)}, u32[]{:S(2)}, u32[]{:S(2)}) %collective-permute-start.7) | collective-permute-done | bytes 2080 | tf_op jit(solution)/shard_map/ppermute | solution.py:575
  20.5 0.2 collective-permute-start.8
  20.7 1.0 %offsets.1 = (f32[2,512]{1,0:T(2,128)S(1)}, f32[1,512]{1,0:T(1,128)S(1)}, bf16[2,512,512]{2,1,0:T(8,128)(2,1)S(1)}) custom-call(f32[2,512]{1,0:T(2,128)S(1)} %get-tuple-element.62.kept_ref.means_ref, bf16[2,512,512]{2,1,0:T(8,128)(2,1)S(1)} %bitcast.10, bf16[512,512]{1,0:T(8,128)(2,1)S(1)} %bitcast.22), custom_call_target="tpu_custom_call" | custom-call | flops 1000000000 | bytes 4096 | tf_op jit(solution)/shard_map/offsets/pallas_call | solution.py:552
  21.6 0.4 collective-permute-start.10
  22.0 0.2 collective-permute-start.9
  22.2 0.6 %collective-permute-done.10.far_offset_ref.near_offset_ref = f32[1,512]{1,0:T(1,128)S(1)} collective-permute-done((f32[1,512]{1,0:T(1,128)S(1)}, f32[1,512]{1,0:T(1,128)S(1)}, u32[]{:S(2)}, u32[]{:S(2)}) %collective-permute-start.10) | collective-permute-done | bytes 2080 | tf_op jit(solution)/shard_map/ppermute | solution.py:575
  22.9 0.3 collective-permute-done.9.last_ref
  23.2 0.2 collective-permute-start.13
  23.4 0.3 collective-permute-start.12
  23.7 0.6 %collective-permute-done.13.one_ref = f32[1,512]{1,0:T(1,128)S(1)} collective-permute-done((f32[1,512]{1,0:T(1,128)S(1)}, f32[1,512]{1,0:T(1,128)S(1)}, u32[]{:S(2)}, u32[]{:S(2)}) %collective-permute-start.13) | collective-permute-done | bytes 2080 | tf_op jit(solution)/shard_map/ppermute | solution.py:575
  24.4 0.2 collective-permute-done.12.three_ref
  24.6 0.3 collective-permute-start.16
  24.9 14.6 %collective-permute-start.15 = (f32[1,512]{1,0:T(1,128)S(1)}, f32[1,512]{1,0:T(1,128)S(1)}, u32[]{:S(2)}, u32[]{:S(2)}) collective-permute-start(f32[1,512]{1,0:T(1,128)S(1)} %get-tuple-element.73.after_ref), channel_id=1, source_target_pairs={{0,4},{1,5},{2,3},{3,2},{4,0},{5,1},{6,8},{7,9},{8,6},{9,7},{10,11... | collective-permute-start | bytes 6152 | tf_op jit(solution)/shard_map/ppermute | solution.py:575
  39.7 1.4 %collective-permute-done.15.two_ref = f32[1,512]{1,0:T(1,128)S(1)} collective-permute-done((f32[1,512]{1,0:T(1,128)S(1)}, f32[1,512]{1,0:T(1,128)S(1)}, u32[]{:S(2)}, u32[]{:S(2)}) %collective-permute-start.15) | collective-permute-done | bytes 2080 | tf_op jit(solution)/shard_map/ppermute | solution.py:575
  41.1 1.2 %final.1 = (f32[2,1,512]{2,1,0:T(1,128)}, f32[2,1,512]{2,1,0:T(1,128)}) custom-call(f32[1,512]{1,0:T(1,128)S(1)} %collective-permute-done.15.two_ref, f32[1,512]{1,0:T(1,128)S(1)} %collective-permute-done.16.one_ref, bf16[2,512,512]{2,1,0:T(8,128)(2,1)S(1)} %get-tuple-element.78.late_parts_ref, f32[1,512]{1,0:T(1,128)S(1)} %get-tuple-element.79.late_offset_ref, ...), custom_call_target="tpu_custom_call" | custom-call | flops 1000000000 | bytes 4096 | tf_op jit(solution)/shard_map/final/pallas_call | solution.py:552
  (42 shorter events, 0.5 us)
Async XLA Ops:
  0.6 3.9 %copy-start.6 = (f32[1,512]{1,0:T(1,128)S(1)}, f32[1,512]{1,0:T(1,128)}, u32[]{:S(2)}) copy-start(f32[1,512]{1,0:T(1,128)} %start_ref.1) | copy-start | bytes 6148
  0.6 3.9 %copy-start.4 = (bf16[2,1,512,512]{3,2,1,0:T(8,128)(2,1)S(1)}, bf16[2,1,512,512]{3,2,1,0:T(8,128)(2,1)}, u32[]{:S(2)}) copy-start(bf16[2,1,512,512]{3,2,1,0:T(8,128)(2,1)} %param.14) | copy-start | bytes 3145732
  0.7 3.9 %copy-start.1 = (bf16[2,1,512,512]{3,2,1,0:T(8,128)(2,1)S(1)}, bf16[2,1,512,512]{3,2,1,0:T(8,128)(2,1)}, u32[]{:S(2)}) copy-start(bf16[2,1,512,512]{3,2,1,0:T(8,128)(2,1)} %param.13) | copy-start | bytes 3145732
  3.2 2.2 %copy-start = (bf16[2,1,512,512]{3,2,1,0:T(8,128)(2,1)S(1)}, bf16[2,1,512,512]{3,2,1,0:T(8,128)(2,1)}, u32[]{:S(2)}) copy-start(bf16[2,1,512,512]{3,2,1,0:T(8,128)(2,1)} %param.15) | copy-start | bytes 3145732
  3.2 1.3 %collective-permute-start = (f32[2,512]{1,0:T(2,128)S(1)}, f32[2,512]{1,0:T(2,128)S(1)}, u32[]{:S(2)}, u32[]{:S(2)}) collective-permute-start(f32[2,512]{1,0:T(2,128)S(1)} %get-tuple-element.43), channel_id=1, source_target_pairs={{0,1},{1,0},{2,3},{3,2},{4,5},{5,4},{6,7},{7,6},{8,9},{9,8},{10,11... | collective-permute-start | bytes 12296 | tf_op jit(solution)/shard_map/ppermute | solution.py:157
  5.2 1.6 %copy-start.2 = (bf16[2,64,16,512]{3,2,1,0:T(8,128)(2,1)S(1)}, bf16[2,64,16,512]{3,2,1,0:T(8,128)(2,1)}, u32[]{:S(2)}) copy-start(bf16[2,64,16,512]{3,2,1,0:T(8,128)(2,1)} %param.9) | copy-start | bytes 6291460
  5.2 1.6 %copy-start.5 = (bf16[16,7,7]{0,2,1:T(8,128)(2,1)S(1)}, bf16[16,7,7]{0,2,1:T(8,128)(2,1)}, u32[]{:S(2)}) copy-start(bf16[16,7,7]{0,2,1:T(8,128)(2,1)} %param.10) | copy-start | bytes 4708
  5.2 1.6 %copy-start.7 = (s32[2,64]{1,0:T(2,128)S(1)}, s32[2,64]{1,0:T(2,128)}, u32[]{:S(2)}) copy-start(s32[2,64]{1,0:T(2,128)} %refs_1_.1) | copy-start | bytes 1540
  5.2 1.6 %copy-start.8 = (s32[2,1]{0,1:T(1,128)S(1)}, s32[2,1]{0,1:T(1,128)}, u32[]{:S(2)}) copy-start(s32[2,1]{0,1:T(1,128)} %param.12) | copy-start | bytes 28
  5.2 4.7 %collective-permute-start.1 = (f32[8,512]{1,0:T(8,128)S(1)}, f32[8,512]{1,0:T(8,128)S(1)}, u32[]{:S(2)}, u32[]{:S(2)}) collective-permute-start(f32[8,512]{1,0:T(8,128)S(1)} %get-tuple-element.44.after_ref), channel_id=1, source_target_pairs={{0,2},{1,3},{2,6},{3,7},{4,5},{5,4},{6,0},{7,1},{8,9},{9,8},{10,11... | collective-permute-start | bytes 49160 | tf_op jit(solution)/shard_map/ppermute | solution.py:575
  5.4 16.9 %collective-permute-start.11 = (f32[512,512]{1,0:T(8,128)S(1)}, f32[512,512]{1,0:T(8,128)S(1)}, u32[]{:S(2)}, u32[]{:S(2)}) collective-permute-start(f32[512,512]{1,0:T(8,128)S(1)} %compose.2), channel_id=1, source_target_pairs={{6,4},{12,10},{7,5},{13,11},{22,20},{28,26},{23,21},{29,27}} | collective-permute-start | bytes 3145736 | tf_op jit(solution)/shard_map/ppermute | solution.py:618
  6.8 1.2 %collective-permute-start.2 = (f32[2,512]{1,0:T(2,128)S(1)}, f32[2,512]{1,0:T(2,128)S(1)}, u32[]{:S(2)}, u32[]{:S(2)}) collective-permute-start(f32[2,512]{1,0:T(2,128)S(1)} %get-tuple-element.46), channel_id=1, source_target_pairs={{0,1},{1,0},{2,3},{3,2},{4,5},{5,4},{6,7},{7,6},{8,9},{9,8},{10,11... | collective-permute-start | bytes 12296 | tf_op jit(solution)/shard_map/ppermute | solution.py:157
  7.2 16.5 %collective-permute-start.14 = (f32[512,512]{1,0:T(8,128)S(1)}, f32[512,512]{1,0:T(8,128)S(1)}, u32[]{:S(2)}, u32[]{:S(2)}) collective-permute-start(f32[512,512]{1,0:T(8,128)S(1)} %compose.3), channel_id=1, source_target_pairs={{8,4},{9,5},{24,20},{25,21}} | collective-permute-start | bytes 3145736 | tf_op jit(solution)/shard_map/ppermute | solution.py:621
  10.0 1.0 %copy-start.3 = (bf16[1,512,512]{2,1,0:T(8,128)(2,1)S(1)}, bf16[1,512,512]{2,1,0:T(8,128)(2,1)}, u32[]{:S(2)}) copy-start(bf16[1,512,512]{2,1,0:T(8,128)(2,1)} %param.16) | copy-start | bytes 1572868
  10.0 2.3 %collective-permute-start.3 = (f32[1,512]{1,0:T(1,128)S(1)}, f32[1,512]{1,0:T(1,128)S(1)}, u32[]{:S(2)}, u32[]{:S(2)}) collective-permute-start(f32[1,512]{1,0:T(1,128)S(1)} %get-tuple-element.49), channel_id=1, source_target_pairs={{0,1},{1,0},{2,4},{3,5},{4,2},{5,3},{6,7},{7,6},{8,9},{9,8},{10,11... | collective-permute-start | bytes 6152 | tf_op jit(solution)/shard_map/ppermute | solution.py:575
  11.0 28.5 %collective-permute-start.17 = (f32[520,512]{1,0:T(8,128)S(1)}, f32[520,512]{1,0:T(8,128)S(1)}, u32[]{:S(2)}, u32[]{:S(2)}) collective-permute-start(f32[520,512]{1,0:T(8,128)S(1)} %get-tuple-element.74), channel_id=1, source_target_pairs={{2,0},{3,1},{18,16},{19,17}} | collective-permute-start | bytes 3194888 | tf_op jit(solution)/shard_map/ppermute | solution.py:637
  12.3 4.7 %collective-permute-start.4 = (f32[1,512]{1,0:T(1,128)S(1)}, f32[1,512]{1,0:T(1,128)S(1)}, u32[]{:S(2)}, u32[]{:S(2)}) collective-permute-start(f32[1,512]{1,0:T(1,128)S(1)} %get-tuple-element.52), channel_id=1, source_target_pairs={{0,4},{1,5},{2,3},{3,2},{4,6},{5,7},{6,0},{7,1},{8,9},{9,8},{10,11... | collective-permute-start | bytes 6152 | tf_op jit(solution)/shard_map/ppermute | solution.py:575
  17.0 1.2 %collective-permute-start.5 = (f32[1,512]{1,0:T(1,128)S(1)}, f32[1,512]{1,0:T(1,128)S(1)}, u32[]{:S(2)}, u32[]{:S(2)}) collective-permute-start(f32[1,512]{1,0:T(1,128)S(1)} %get-tuple-element.55), channel_id=1, source_target_pairs={{0,1},{1,0},{2,3},{3,2},{4,5},{5,4},{6,8},{7,9},{8,10},{9,11},{10,... | collective-permute-start | bytes 6152 | tf_op jit(solution)/shard_map/ppermute | solution.py:575
  18.2 1.2 %collective-permute-start.6 = (f32[1,512]{1,0:T(1,128)S(1)}, f32[1,512]{1,0:T(1,128)S(1)}, u32[]{:S(2)}, u32[]{:S(2)}) collective-permute-start(f32[1,512]{1,0:T(1,128)S(1)} %get-tuple-element.57), channel_id=1, source_target_pairs={{0,1},{1,0},{2,3},{3,2},{4,8},{5,9},{6,7},{7,6},{8,10},{9,11},{10,... | collective-permute-start | bytes 6152 | tf_op jit(solution)/shard_map/ppermute | solution.py:575
  19.3 1.2 %collective-permute-start.7 = (f32[1,512]{1,0:T(1,128)S(1)}, f32[1,512]{1,0:T(1,128)S(1)}, u32[]{:S(2)}, u32[]{:S(2)}) collective-permute-start(f32[1,512]{1,0:T(1,128)S(1)} %get-tuple-element.59), channel_id=1, source_target_pairs={{0,1},{1,0},{2,3},{3,2},{4,5},{5,4},{6,7},{7,6},{8,9},{9,8},{10,12... | collective-permute-start | bytes 6152 | tf_op jit(solution)/shard_map/ppermute | solution.py:575
  20.5 1.6 %collective-permute-start.8 = (f32[1,512]{1,0:T(1,128)S(1)}, f32[1,512]{1,0:T(1,128)S(1)}, u32[]{:S(2)}, u32[]{:S(2)}) collective-permute-start(f32[1,512]{1,0:T(1,128)S(1)} %get-tuple-element.61), channel_id=1, source_target_pairs={{0,1},{1,0},{2,3},{3,2},{4,5},{5,4},{6,7},{7,6},{8,9},{9,8},{10,11... | collective-permute-start | bytes 6152 | tf_op jit(solution)/shard_map/ppermute | solution.py:575
  21.6 1.2 %collective-permute-start.10 = (f32[1,512]{1,0:T(1,128)S(1)}, f32[1,512]{1,0:T(1,128)S(1)}, u32[]{:S(2)}, u32[]{:S(2)}) collective-permute-start(f32[1,512]{1,0:T(1,128)S(1)} %get-tuple-element.64.left_ref), channel_id=1, source_target_pairs={{0,1},{1,0},{2,3},{3,2},{4,6},{5,7},{6,4},{7,5},{8,9},{9,8},{10,12... | collective-permute-start | bytes 6152 | tf_op jit(solution)/shard_map/ppermute | solution.py:575
  22.0 1.2 %collective-permute-start.9 = (f32[1,512]{1,0:T(1,128)S(1)}, f32[1,512]{1,0:T(1,128)S(1)}, u32[]{:S(2)}, u32[]{:S(2)}) collective-permute-start(f32[1,512]{1,0:T(1,128)S(1)} %get-tuple-element.63.came_ref), channel_id=1, source_target_pairs={{0,1},{1,0},{2,3},{3,2},{4,5},{5,4},{6,7},{7,6},{8,9},{9,8},{10,14... | collective-permute-start | bytes 6152 | tf_op jit(solution)/shard_map/ppermute | solution.py:575
  23.2 1.2 %collective-permute-start.13 = (f32[1,512]{1,0:T(1,128)S(1)}, f32[1,512]{1,0:T(1,128)S(1)}, u32[]{:S(2)}, u32[]{:S(2)}) collective-permute-start(f32[1,512]{1,0:T(1,128)S(1)} %get-tuple-element.66.came_ref), channel_id=1, source_target_pairs={{0,1},{1,0},{2,3},{3,2},{4,6},{5,7},{6,10},{7,11},{8,4},{9,5},{10,... | collective-permute-start | bytes 6152 | tf_op jit(solution)/shard_map/ppermute | solution.py:575
  23.4 1.2 %collective-permute-start.12 = (f32[1,512]{1,0:T(1,128)S(1)}, f32[1,512]{1,0:T(1,128)S(1)}, u32[]{:S(2)}, u32[]{:S(2)}) collective-permute-start(f32[1,512]{1,0:T(1,128)S(1)} %get-tuple-element.66.came_ref), channel_id=1, source_target_pairs={{0,1},{1,0},{2,3},{3,2},{4,10},{5,11},{6,7},{7,6},{8,9},{9,8},{10,... | collective-permute-start | bytes 6152 | tf_op jit(solution)/shard_map/ppermute | solution.py:575
  24.6 15.1 %collective-permute-start.16 = (f32[1,512]{1,0:T(1,128)S(1)}, f32[1,512]{1,0:T(1,128)S(1)}, u32[]{:S(2)}, u32[]{:S(2)}) collective-permute-start(f32[1,512]{1,0:T(1,128)S(1)} %get-tuple-element.73.after_ref), channel_id=1, source_target_pairs={{0,1},{1,0},{2,4},{3,5},{4,2},{5,3},{6,7},{7,6},{8,9},{9,8},{10,11... | collective-permute-start | bytes 6152 | tf_op jit(solution)/shard_map/ppermute | solution.py:575
  24.9 16.2 %collective-permute-start.15 = (f32[1,512]{1,0:T(1,128)S(1)}, f32[1,512]{1,0:T(1,128)S(1)}, u32[]{:S(2)}, u32[]{:S(2)}) collective-permute-start(f32[1,512]{1,0:T(1,128)S(1)} %get-tuple-element.73.after_ref), channel_id=1, source_target_pairs={{0,4},{1,5},{2,3},{3,2},{4,0},{5,1},{6,8},{7,9},{8,6},{9,7},{10,11... | collective-permute-start | bytes 6152 | tf_op jit(solution)/shard_map/ppermute | solution.py:575

commit v12 on v11

--- a/solution.py
+++ b/solution.py
@@ -177,24 +177,21 @@
         send_ref[...] = jnp.zeros_like(send_ref)
 
 
+def drive(mine_ref, other_ref, covariance_ref, inputs_ref):
+    for t in range(mine_ref.shape[0]):
+        info = mine_ref[t : t + 1, :] + other_ref[t : t + 1, :]
+        inputs_ref[t : t + 1, :] = times([covariance_ref[t]], info)
+
+
 def first_hop_kernel(
     came_ref, mine_ref, other_ref, covariance_ref, operator_ref, kept_inputs_ref, kept_ref,
     inputs_ref, states_ref, send_ref,
 ):
     here = lax.axis_index("tm")
 
-    @pl.when(here == 0)
-    def _():
-        inputs_ref[...] = kept_inputs_ref[...]
-
-    @pl.when(here != 0)
-    def _():
-        for t in range(mine_ref.shape[0]):
-            info = mine_ref[t : t + 1, :] + other_ref[t : t + 1, :]
-            inputs_ref[t : t + 1, :] = times([covariance_ref[t]], info)
-
     @pl.when(here == 1)
     def _():
+        drive(mine_ref, other_ref, covariance_ref, inputs_ref)
         state = came_ref[0:1, :]
         for t in range(operator_ref.shape[0]):
             state = times([operator_ref[t]], state) + inputs_ref[t : t + 1, :]
@@ -203,6 +200,7 @@
 
     @pl.when(here != 1)
     def _():
+        inputs_ref[...] = kept_inputs_ref[...]
         states_ref[...] = kept_ref[...]
         send_ref[...] = came_ref[0:1, :]
 
@@ -251,7 +249,10 @@
         composed_ref[...] = composed(gain_ref)
 
 
-def late_kernel(place, means_ref, gain_ref, propagator_ref, operator_ref, composed_ref, turned_ref):
+def late_kernel(
+    place, means_ref, gain_ref, propagator_ref, operator_ref, mine_ref, other_ref, covariance_ref, kept_inputs_ref,
+    composed_ref, turned_ref, inputs_ref,
+):
     size = gain_ref.shape[1]
     here = lax.axis_index("tm")
 
@@ -260,6 +261,14 @@
         composed_ref[:size, :] = composed(gain_ref)
         composed_ref[size:, :] = jnp.zeros((composed_ref.shape[0] - size, size), jnp.float32)
         composed_ref[size : size + 1, :] = offsets(means_ref, gain_ref, propagator_ref)[0]
+
+    @pl.when(here <= place)
+    def _():
+        inputs_ref[...] = kept_inputs_ref[...]
+
+    @pl.when(here > place)
+    def _():
+        drive(mine_ref, other_ref, covariance_ref, inputs_ref)
 
     @pl.when(here > place + 1)
     def _():
@@ -579,7 +588,7 @@
     if place % 2 and place >= places - 5 and place < places - 1:
         return (place, place + 1, place + 2)
     if place == 0:
-        return (0, 1, 3)
+        return (0, 1, 3, places - 1)
     if place % 2 or place == places - 2:
         return (place, place + 1)
     return (place, place + 1, place - 2)
@@ -630,9 +639,9 @@
             continue
         came = pass_row(send, [ring_up(place - 1, places)], places)
         if place == 2:
-            late, turned = call(
-                functools.partial(late_kernel, 1), "late", ((size + 8, size), (steps, size, size)),
-                means, gain, matrix, operator, cost=0.5,
+            late, turned, inputs = call(
+                functools.partial(late_kernel, 1), "late", ((size + 8, size), (steps, size, size), many),
+                means, gain, matrix, operator, mine, other, covariance, inputs, cost=0.5,
             )
             late = lax.ppermute(late, "tm", [(1, 0)])
         if place < last:

time: 42.7 us -> 42.6 us (level)
  waiting for transfers between devices: 10.9 us -> 14.8 us
  starting transfers between devices: 23.4 us -> 19.5 us
    ppermute x13, waiting for transfers between devices: 9.93 us -> 13.9 us  [pass_row(): return lax.ppermute(row, ('tm', 'block'), sorted(route.items()))]
    ppermute x13, starting transfers between devices: 19.6 us -> 15.7 us  [pass_row(): return lax.ppermute(row, ('tm', 'block'), sorted(route.items()))]
where the time goes in v12:
time: 42.6 us; the launch traced here: 42.4 us
  starting transfers between devices  19.5 us (46%)
  waiting for transfers between devices  14.8 us (35%)
  Pallas kernels  5.56 us (13%)
  local copies, waits for them, and re-layouts  1.65 us (4%)
  between operations  0.83 us (2%)
    ppermute x13, starting transfers between devices, pass_row(): return lax.ppermute(row, ('tm', 'block'), sorted(route.items()))  15.7 us
    ppermute x13, waiting for transfers between devices, pass_row(): return lax.ppermute(row, ('tm', 'block'), sorted(route.items()))  13.9 us
    pallas_call x18, Pallas kernels, call(): pl.pallas_call(kernel, out_shape=[jax.ShapeDtypeStruct(shape, jnp.bfloat1...  3.06 us
    pallas_call x2, Pallas kernels, sensor_info(): pl.pallas_call(kernel, out_shape=[jax.ShapeDtypeStruct((steps, cells), jn...  2.5 us
    unnamed x18, local copies, waits for them, and re-layouts  1.65 us
    ppermute x1, starting transfers between devices, local(): late = lax.ppermute(late, 'tm', [(1, 0)])  1.28 us
    ppermute x2, starting transfers between devices, sensor_info(): return (mine, lax.ppermute(theirs, 'block', [(0, 1), (1, 0)]))  0.94 us
    ppermute x2, waiting for transfers between devices, sensor_info(): return (mine, lax.ppermute(theirs, 'block', [(0, 1), (1, 0)]))  0.92 us
  transfers between devices with their start and end apart: 18, of which 12 were waited for; matrix products, arithmetic and copies ran while one was open for 0% of the time, Pallas kernels for 3%

profile of v12, /device:TPU:0, one launch (start us, length us, event | category | flops | bytes accessed | tf_op | source)
XLA Modules:
  0.0 42.4 jit_solution(1801037323832169687)
XLA Ops:
  0.7 2.5 %sensor_info.2 = (f32[2,512]{1,0:T(2,128)S(1)}, f32[2,512]{1,0:T(2,128)S(1)}) custom-call(bf16[7,7,16]{2,1,0:T(8,128)(2,1)} %bitcast.27, s32[2,64]{1,0:T(2,128)} %refs_1_.1, s32[1,2]{1,0:T(1,128)} %bitcast.29, bf16[2,1024,512]{2,1,0:T(8,128)(2,1)} %bitcast.22), custom_call_target="tpu_custom_call" | custom-call | flops 1000000 | bytes 4096 | tf_op jit(solution)/shard_map/sensor_info/pallas_call | solution.py:147
  3.2 0.5 %collective-permute-start = (f32[2,512]{1,0:T(2,128)S(1)}, f32[2,512]{1,0:T(2,128)S(1)}, u32[]{:S(2)}, u32[]{:S(2)}) collective-permute-start(f32[2,512]{1,0:T(2,128)S(1)} %get-tuple-element.44), channel_id=1, source_target_pairs={{0,1},{1,0},{2,3},{3,2},{4,5},{5,4},{6,7},{7,6},{8,9},{9,8},{10,11... | collective-permute-start | bytes 12296 | tf_op jit(solution)/shard_map/ppermute | solution.py:157
  3.7 0.8 %collective-permute-done.other_ref = f32[2,512]{1,0:T(2,128)S(1)} collective-permute-done((f32[2,512]{1,0:T(2,128)S(1)}, f32[2,512]{1,0:T(2,128)S(1)}, u32[]{:S(2)}, u32[]{:S(2)}) %collective-permute-start) | collective-permute-done | bytes 4128 | tf_op jit(solution)/shard_map/ppermute | solution.py:157
  4.5 0.7 %start.1 = (f32[2,512]{1,0:T(2,128)S(1)}, f32[2,512]{1,0:T(2,128)S(1)}, f32[8,512]{1,0:T(8,128)S(1)}) custom-call(f32[2,512]{1,0:T(2,128)S(1)} %get-tuple-element.43.mine_ref, f32[2,512]{1,0:T(2,128)S(1)} %collective-permute-done.other_ref, bf16[2,512,512]{2,1,0:T(8,128)(2,1)S(1)} %bitcast.15, bf16[2,512,512]{2,1,0:T(8,128)(2,1)S(1)} %bitcast.18, ...), custom_call_target="tpu_custom_call" | custom-call | flops 500000000 | bytes 4096 | tf_op jit(solution)/shard_map/start/pallas_call | solution.py:561
  5.3 0.9 %collective-permute-start.11 = (f32[512,512]{1,0:T(8,128)S(1)}, f32[512,512]{1,0:T(8,128)S(1)}, u32[]{:S(2)}, u32[]{:S(2)}) collective-permute-start(f32[512,512]{1,0:T(8,128)S(1)} %compose.2), channel_id=1, source_target_pairs={{6,4},{12,10},{7,5},{13,11},{22,20},{28,26},{23,21},{29,27}} | collective-permute-start | bytes 3145736 | tf_op jit(solution)/shard_map/ppermute | solution.py:627
  6.2 0.6 %copy-done.3 = bf16[2,64,16,512]{3,2,1,0:T(8,128)(2,1)S(1)} copy-done((bf16[2,64,16,512]{3,2,1,0:T(8,128)(2,1)S(1)}, bf16[2,64,16,512]{3,2,1,0:T(8,128)(2,1)}, u32[]{:S(2)}) %copy-start.3) | copy-done | bytes 2097176
  6.8 0.4 collective-permute-start.2
  7.2 0.7 %collective-permute-start.14 = (f32[512,512]{1,0:T(8,128)S(1)}, f32[512,512]{1,0:T(8,128)S(1)}, u32[]{:S(2)}, u32[]{:S(2)}) collective-permute-start(f32[512,512]{1,0:T(8,128)S(1)} %compose.3), channel_id=1, source_target_pairs={{8,4},{9,5},{24,20},{25,21}} | collective-permute-start | bytes 3145736 | tf_op jit(solution)/shard_map/ppermute | solution.py:630
  8.1 3.7 %collective-permute-done.1.came_ref = f32[8,512]{1,0:T(8,128)S(1)} collective-permute-done((f32[8,512]{1,0:T(8,128)S(1)}, f32[8,512]{1,0:T(8,128)S(1)}, u32[]{:S(2)}, u32[]{:S(2)}) %collective-permute-start.1) | collective-permute-done | bytes 16416 | tf_op jit(solution)/shard_map/ppermute | solution.py:584
  11.8 1.0 %copy-done.4 = bf16[1,512,512]{2,1,0:T(8,128)(2,1)S(1)} copy-done((bf16[1,512,512]{2,1,0:T(8,128)(2,1)S(1)}, bf16[1,512,512]{2,1,0:T(8,128)(2,1)}, u32[]{:S(2)}) %copy-start.4) | copy-done | bytes 524312
  12.8 1.3 %collective-permute-start.17 = (f32[520,512]{1,0:T(8,128)S(1)}, f32[520,512]{1,0:T(8,128)S(1)}, u32[]{:S(2)}, u32[]{:S(2)}) collective-permute-start(f32[520,512]{1,0:T(8,128)S(1)} %get-tuple-element.76), channel_id=1, source_target_pairs={{2,0},{3,1},{18,16},{19,17}} | collective-permute-start | bytes 3194888 | tf_op jit(solution)/shard_map/ppermute | solution.py:646
  14.1 0.7 %collective-permute-start.4 = (f32[1,512]{1,0:T(1,128)S(1)}, f32[1,512]{1,0:T(1,128)S(1)}, u32[]{:S(2)}, u32[]{:S(2)}) collective-permute-start(f32[1,512]{1,0:T(1,128)S(1)} %get-tuple-element.54), channel_id=1, source_target_pairs={{0,4},{1,5},{2,3},{3,2},{4,6},{5,7},{6,0},{7,1},{8,9},{9,8},{10,11... | collective-permute-start | bytes 6152 | tf_op jit(solution)/shard_map/ppermute | solution.py:584
  14.9 3.9 %collective-permute-done.4.came_ref = f32[1,512]{1,0:T(1,128)S(1)} collective-permute-done((f32[1,512]{1,0:T(1,128)S(1)}, f32[1,512]{1,0:T(1,128)S(1)}, u32[]{:S(2)}, u32[]{:S(2)}) %collective-permute-start.4) | collective-permute-done | bytes 2080 | tf_op jit(solution)/shard_map/ppermute | solution.py:584
  18.8 1.2 %collective-permute-done.5.came_ref = f32[1,512]{1,0:T(1,128)S(1)} collective-permute-done((f32[1,512]{1,0:T(1,128)S(1)}, f32[1,512]{1,0:T(1,128)S(1)}, u32[]{:S(2)}, u32[]{:S(2)}) %collective-permute-start.5) | collective-permute-done | bytes 2080 | tf_op jit(solution)/shard_map/ppermute | solution.py:584
  19.9 0.2 collective-permute-start.6
  20.1 1.0 %collective-permute-done.6.came_ref = f32[1,512]{1,0:T(1,128)S(1)} collective-permute-done((f32[1,512]{1,0:T(1,128)S(1)}, f32[1,512]{1,0:T(1,128)S(1)}, u32[]{:S(2)}, u32[]{:S(2)}) %collective-permute-start.6) | collective-permute-done | bytes 2080 | tf_op jit(solution)/shard_map/ppermute | solution.py:584
  21.1 0.2 collective-permute-start.7
  21.3 1.0 %collective-permute-done.7.came_ref = f32[1,512]{1,0:T(1,128)S(1)} collective-permute-done((f32[1,512]{1,0:T(1,128)S(1)}, f32[1,512]{1,0:T(1,128)S(1)}, u32[]{:S(2)}, u32[]{:S(2)}) %collective-permute-start.7) | collective-permute-done | bytes 2080 | tf_op jit(solution)/shard_map/ppermute | solution.py:584
  22.3 0.2 collective-permute-start.8
  22.4 1.0 %offsets.1 = (f32[2,512]{1,0:T(2,128)S(1)}, f32[1,512]{1,0:T(1,128)S(1)}, bf16[2,512,512]{2,1,0:T(8,128)(2,1)S(1)}) custom-call(f32[2,512]{1,0:T(2,128)S(1)} %get-tuple-element.64.kept_ref.means_ref, bf16[2,512,512]{2,1,0:T(8,128)(2,1)S(1)} %bitcast.10, bf16[512,512]{1,0:T(8,128)(2,1)S(1)} %bitcast.25), custom_call_target="tpu_custom_call" | custom-call | flops 1000000000 | bytes 4096 | tf_op jit(solution)/shard_map/offsets/pallas_call | solution.py:561
  23.4 0.4 collective-permute-start.10
  23.8 0.2 collective-permute-start.9
  24.0 0.6 %collective-permute-done.10.far_offset_ref.near_offset_ref = f32[1,512]{1,0:T(1,128)S(1)} collective-permute-done((f32[1,512]{1,0:T(1,128)S(1)}, f32[1,512]{1,0:T(1,128)S(1)}, u32[]{:S(2)}, u32[]{:S(2)}) %collective-permute-start.10) | collective-permute-done | bytes 2080 | tf_op jit(solution)/shard_map/ppermute | solution.py:584
  24.6 0.3 collective-permute-done.9.last_ref
  25.0 0.2 collective-permute-start.13
  25.2 0.3 collective-permute-start.12
  25.5 0.6 %collective-permute-done.13.one_ref = f32[1,512]{1,0:T(1,128)S(1)} collective-permute-done((f32[1,512]{1,0:T(1,128)S(1)}, f32[1,512]{1,0:T(1,128)S(1)}, u32[]{:S(2)}, u32[]{:S(2)}) %collective-permute-start.13) | collective-permute-done | bytes 2080 | tf_op jit(solution)/shard_map/ppermute | solution.py:584
  26.1 0.2 collective-permute-done.12.three_ref
  26.3 0.3 collective-permute-start.16
  26.7 13.0 %collective-permute-start.15 = (f32[1,512]{1,0:T(1,128)S(1)}, f32[1,512]{1,0:T(1,128)S(1)}, u32[]{:S(2)}, u32[]{:S(2)}) collective-permute-start(f32[1,512]{1,0:T(1,128)S(1)} %get-tuple-element.75.after_ref), channel_id=1, source_target_pairs={{0,4},{1,5},{2,3},{3,2},{4,0},{5,1},{6,8},{7,9},{8,6},{9,7},{10,11... | collective-permute-start | bytes 6152 | tf_op jit(solution)/shard_map/ppermute | solution.py:584
  39.8 1.4 %collective-permute-done.15.two_ref = f32[1,512]{1,0:T(1,128)S(1)} collective-permute-done((f32[1,512]{1,0:T(1,128)S(1)}, f32[1,512]{1,0:T(1,128)S(1)}, u32[]{:S(2)}, u32[]{:S(2)}) %collective-permute-start.15) | collective-permute-done | bytes 2080 | tf_op jit(solution)/shard_map/ppermute | solution.py:584
  41.2 1.2 %final.1 = (f32[2,1,512]{2,1,0:T(1,128)}, f32[2,1,512]{2,1,0:T(1,128)}) custom-call(f32[1,512]{1,0:T(1,128)S(1)} %collective-permute-done.15.two_ref, f32[1,512]{1,0:T(1,128)S(1)} %collective-permute-done.16.one_ref, bf16[2,512,512]{2,1,0:T(8,128)(2,1)S(1)} %get-tuple-element.80.late_parts_ref, f32[1,512]{1,0:T(1,128)S(1)} %get-tuple-element.81.late_offset_ref, ...), custom_call_target="tpu_custom_call" | custom-call | flops 1000000000 | bytes 4096 | tf_op jit(solution)/shard_map/final/pallas_call | solution.py:561
  (42 shorter events, 0.5 us)
Async XLA Ops:
  0.6 3.9 %copy-start.6 = (f32[1,512]{1,0:T(1,128)S(1)}, f32[1,512]{1,0:T(1,128)}, u32[]{:S(2)}) copy-start(f32[1,512]{1,0:T(1,128)} %start_ref.1) | copy-start | bytes 6148
  0.6 3.9 %copy-start.1 = (bf16[2,1,512,512]{3,2,1,0:T(8,128)(2,1)S(1)}, bf16[2,1,512,512]{3,2,1,0:T(8,128)(2,1)}, u32[]{:S(2)}) copy-start(bf16[2,1,512,512]{3,2,1,0:T(8,128)(2,1)} %param.14) | copy-start | bytes 3145732
  0.7 3.9 %copy-start.2 = (bf16[2,1,512,512]{3,2,1,0:T(8,128)(2,1)S(1)}, bf16[2,1,512,512]{3,2,1,0:T(8,128)(2,1)}, u32[]{:S(2)}) copy-start(bf16[2,1,512,512]{3,2,1,0:T(8,128)(2,1)} %param.13) | copy-start | bytes 3145732
  3.2 2.2 %copy-start = (bf16[2,1,512,512]{3,2,1,0:T(8,128)(2,1)S(1)}, bf16[2,1,512,512]{3,2,1,0:T(8,128)(2,1)}, u32[]{:S(2)}) copy-start(bf16[2,1,512,512]{3,2,1,0:T(8,128)(2,1)} %param.15) | copy-start | bytes 3145732
  3.2 1.3 %collective-permute-start = (f32[2,512]{1,0:T(2,128)S(1)}, f32[2,512]{1,0:T(2,128)S(1)}, u32[]{:S(2)}, u32[]{:S(2)}) collective-permute-start(f32[2,512]{1,0:T(2,128)S(1)} %get-tuple-element.44), channel_id=1, source_target_pairs={{0,1},{1,0},{2,3},{3,2},{4,5},{5,4},{6,7},{7,6},{8,9},{9,8},{10,11... | collective-permute-start | bytes 12296 | tf_op jit(solution)/shard_map/ppermute | solution.py:157
  5.2 1.6 %copy-start.3 = (bf16[2,64,16,512]{3,2,1,0:T(8,128)(2,1)S(1)}, bf16[2,64,16,512]{3,2,1,0:T(8,128)(2,1)}, u32[]{:S(2)}) copy-start(bf16[2,64,16,512]{3,2,1,0:T(8,128)(2,1)} %param.9) | copy-start | bytes 6291460
  5.2 1.6 %copy-start.5 = (bf16[16,7,7]{0,2,1:T(8,128)(2,1)S(1)}, bf16[16,7,7]{0,2,1:T(8,128)(2,1)}, u32[]{:S(2)}) copy-start(bf16[16,7,7]{0,2,1:T(8,128)(2,1)} %param.10) | copy-start | bytes 4708
  5.2 1.6 %copy-start.7 = (s32[2,64]{1,0:T(2,128)S(1)}, s32[2,64]{1,0:T(2,128)}, u32[]{:S(2)}) copy-start(s32[2,64]{1,0:T(2,128)} %refs_1_.1) | copy-start | bytes 1540
  5.2 1.6 %copy-start.8 = (s32[2,1]{0,1:T(1,128)S(1)}, s32[2,1]{0,1:T(1,128)}, u32[]{:S(2)}) copy-start(s32[2,1]{0,1:T(1,128)} %param.12) | copy-start | bytes 28
  5.2 6.5 %collective-permute-start.1 = (f32[8,512]{1,0:T(8,128)S(1)}, f32[8,512]{1,0:T(8,128)S(1)}, u32[]{:S(2)}, u32[]{:S(2)}) collective-permute-start(f32[8,512]{1,0:T(8,128)S(1)} %get-tuple-element.45.after_ref), channel_id=1, source_target_pairs={{0,2},{1,3},{2,6},{3,7},{4,5},{5,4},{6,14},{7,15},{8,9},{9,8},{10,... | collective-permute-start | bytes 49160 | tf_op jit(solution)/shard_map/ppermute | solution.py:584
  5.3 18.7 %collective-permute-start.11 = (f32[512,512]{1,0:T(8,128)S(1)}, f32[512,512]{1,0:T(8,128)S(1)}, u32[]{:S(2)}, u32[]{:S(2)}) collective-permute-start(f32[512,512]{1,0:T(8,128)S(1)} %compose.2), channel_id=1, source_target_pairs={{6,4},{12,10},{7,5},{13,11},{22,20},{28,26},{23,21},{29,27}} | collective-permute-start | bytes 3145736 | tf_op jit(solution)/shard_map/ppermute | solution.py:627
  6.8 1.2 %collective-permute-start.2 = (f32[2,512]{1,0:T(2,128)S(1)}, f32[2,512]{1,0:T(2,128)S(1)}, u32[]{:S(2)}, u32[]{:S(2)}) collective-permute-start(f32[2,512]{1,0:T(2,128)S(1)} %get-tuple-element.47), channel_id=1, source_target_pairs={{0,1},{1,0},{2,3},{3,2},{4,5},{5,4},{6,7},{7,6},{8,9},{9,8},{10,11... | collective-permute-start | bytes 12296 | tf_op jit(solution)/shard_map/ppermute | solution.py:157
  7.2 18.3 %collective-permute-start.14 = (f32[512,512]{1,0:T(8,128)S(1)}, f32[512,512]{1,0:T(8,128)S(1)}, u32[]{:S(2)}, u32[]{:S(2)}) collective-permute-start(f32[512,512]{1,0:T(8,128)S(1)} %compose.3), channel_id=1, source_target_pairs={{8,4},{9,5},{24,20},{25,21}} | collective-permute-start | bytes 3145736 | tf_op jit(solution)/shard_map/ppermute | solution.py:630
  11.7 1.0 %copy-start.4 = (bf16[1,512,512]{2,1,0:T(8,128)(2,1)S(1)}, bf16[1,512,512]{2,1,0:T(8,128)(2,1)}, u32[]{:S(2)}) copy-start(bf16[1,512,512]{2,1,0:T(8,128)(2,1)} %param.16) | copy-start | bytes 1572868
  11.8 2.3 %collective-permute-start.3 = (f32[1,512]{1,0:T(1,128)S(1)}, f32[1,512]{1,0:T(1,128)S(1)}, u32[]{:S(2)}, u32[]{:S(2)}) collective-permute-start(f32[1,512]{1,0:T(1,128)S(1)} %get-tuple-element.50), channel_id=1, source_target_pairs={{0,1},{1,0},{2,4},{3,5},{4,2},{5,3},{6,7},{7,6},{8,9},{9,8},{10,11... | collective-permute-start | bytes 6152 | tf_op jit(solution)/shard_map/ppermute | solution.py:584
  12.8 26.8 %collective-permute-start.17 = (f32[520,512]{1,0:T(8,128)S(1)}, f32[520,512]{1,0:T(8,128)S(1)}, u32[]{:S(2)}, u32[]{:S(2)}) collective-permute-start(f32[520,512]{1,0:T(8,128)S(1)} %get-tuple-element.76), channel_id=1, source_target_pairs={{2,0},{3,1},{18,16},{19,17}} | collective-permute-start | bytes 3194888 | tf_op jit(solution)/shard_map/ppermute | solution.py:646
  14.1 4.7 %collective-permute-start.4 = (f32[1,512]{1,0:T(1,128)S(1)}, f32[1,512]{1,0:T(1,128)S(1)}, u32[]{:S(2)}, u32[]{:S(2)}) collective-permute-start(f32[1,512]{1,0:T(1,128)S(1)} %get-tuple-element.54), channel_id=1, source_target_pairs={{0,4},{1,5},{2,3},{3,2},{4,6},{5,7},{6,0},{7,1},{8,9},{9,8},{10,11... | collective-permute-start | bytes 6152 | tf_op jit(solution)/shard_map/ppermute | solution.py:584
  18.8 1.2 %collective-permute-start.5 = (f32[1,512]{1,0:T(1,128)S(1)}, f32[1,512]{1,0:T(1,128)S(1)}, u32[]{:S(2)}, u32[]{:S(2)}) collective-permute-start(f32[1,512]{1,0:T(1,128)S(1)} %get-tuple-element.57), channel_id=1, source_target_pairs={{0,1},{1,0},{2,3},{3,2},{4,5},{5,4},{6,8},{7,9},{8,10},{9,11},{10,... | collective-permute-start | bytes 6152 | tf_op jit(solution)/shard_map/ppermute | solution.py:584
  19.9 1.2 %collective-permute-start.6 = (f32[1,512]{1,0:T(1,128)S(1)}, f32[1,512]{1,0:T(1,128)S(1)}, u32[]{:S(2)}, u32[]{:S(2)}) collective-permute-start(f32[1,512]{1,0:T(1,128)S(1)} %get-tuple-element.59), channel_id=1, source_target_pairs={{0,1},{1,0},{2,3},{3,2},{4,8},{5,9},{6,7},{7,6},{8,10},{9,11},{10,... | collective-permute-start | bytes 6152 | tf_op jit(solution)/shard_map/ppermute | solution.py:584
  21.1 1.2 %collective-permute-start.7 = (f32[1,512]{1,0:T(1,128)S(1)}, f32[1,512]{1,0:T(1,128)S(1)}, u32[]{:S(2)}, u32[]{:S(2)}) collective-permute-start(f32[1,512]{1,0:T(1,128)S(1)} %get-tuple-element.61), channel_id=1, source_target_pairs={{0,1},{1,0},{2,3},{3,2},{4,5},{5,4},{6,7},{7,6},{8,9},{9,8},{10,12... | collective-permute-start | bytes 6152 | tf_op jit(solution)/shard_map/ppermute | solution.py:584
  22.3 1.6 %collective-permute-start.8 = (f32[1,512]{1,0:T(1,128)S(1)}, f32[1,512]{1,0:T(1,128)S(1)}, u32[]{:S(2)}, u32[]{:S(2)}) collective-permute-start(f32[1,512]{1,0:T(1,128)S(1)} %get-tuple-element.63), channel_id=1, source_target_pairs={{0,1},{1,0},{2,3},{3,2},{4,5},{5,4},{6,7},{7,6},{8,9},{9,8},{10,11... | collective-permute-start | bytes 6152 | tf_op jit(solution)/shard_map/ppermute | solution.py:584
  23.4 1.2 %collective-permute-start.10 = (f32[1,512]{1,0:T(1,128)S(1)}, f32[1,512]{1,0:T(1,128)S(1)}, u32[]{:S(2)}, u32[]{:S(2)}) collective-permute-start(f32[1,512]{1,0:T(1,128)S(1)} %get-tuple-element.66.left_ref), channel_id=1, source_target_pairs={{0,1},{1,0},{2,3},{3,2},{4,6},{5,7},{6,4},{7,5},{8,9},{9,8},{10,12... | collective-permute-start | bytes 6152 | tf_op jit(solution)/shard_map/ppermute | solution.py:584
  23.8 1.2 %collective-permute-start.9 = (f32[1,512]{1,0:T(1,128)S(1)}, f32[1,512]{1,0:T(1,128)S(1)}, u32[]{:S(2)}, u32[]{:S(2)}) collective-permute-start(f32[1,512]{1,0:T(1,128)S(1)} %get-tuple-element.65.came_ref), channel_id=1, source_target_pairs={{0,1},{1,0},{2,3},{3,2},{4,5},{5,4},{6,7},{7,6},{8,9},{9,8},{10,14... | collective-permute-start | bytes 6152 | tf_op jit(solution)/shard_map/ppermute | solution.py:584
  25.0 1.2 %collective-permute-start.13 = (f32[1,512]{1,0:T(1,128)S(1)}, f32[1,512]{1,0:T(1,128)S(1)}, u32[]{:S(2)}, u32[]{:S(2)}) collective-permute-start(f32[1,512]{1,0:T(1,128)S(1)} %get-tuple-element.68.came_ref), channel_id=1, source_target_pairs={{0,1},{1,0},{2,3},{3,2},{4,6},{5,7},{6,10},{7,11},{8,4},{9,5},{10,... | collective-permute-start | bytes 6152 | tf_op jit(solution)/shard_map/ppermute | solution.py:584
  25.2 1.2 %collective-permute-start.12 = (f32[1,512]{1,0:T(1,128)S(1)}, f32[1,512]{1,0:T(1,128)S(1)}, u32[]{:S(2)}, u32[]{:S(2)}) collective-permute-start(f32[1,512]{1,0:T(1,128)S(1)} %get-tuple-element.68.came_ref), channel_id=1, source_target_pairs={{0,1},{1,0},{2,3},{3,2},{4,10},{5,11},{6,7},{7,6},{8,9},{9,8},{10,... | collective-permute-start | bytes 6152 | tf_op jit(solution)/shard_map/ppermute | solution.py:584
  26.3 13.5 %collective-permute-start.16 = (f32[1,512]{1,0:T(1,128)S(1)}, f32[1,512]{1,0:T(1,128)S(1)}, u32[]{:S(2)}, u32[]{:S(2)}) collective-permute-start(f32[1,512]{1,0:T(1,128)S(1)} %get-tuple-element.75.after_ref), channel_id=1, source_target_pairs={{0,1},{1,0},{2,4},{3,5},{4,2},{5,3},{6,7},{7,6},{8,9},{9,8},{10,11... | collective-permute-start | bytes 6152 | tf_op jit(solution)/shard_map/ppermute | solution.py:584
  26.7 14.5 %collective-permute-start.15 = (f32[1,512]{1,0:T(1,128)S(1)}, f32[1,512]{1,0:T(1,128)S(1)}, u32[]{:S(2)}, u32[]{:S(2)}) collective-permute-start(f32[1,512]{1,0:T(1,128)S(1)} %get-tuple-element.75.after_ref), channel_id=1, source_target_pairs={{0,4},{1,5},{2,3},{3,2},{4,0},{5,1},{6,8},{7,9},{8,6},{9,7},{10,11... | collective-permute-start | bytes 6152 | tf_op jit(solution)/shard_map/ppermute | solution.py:584
